TPU v7x, 32 devices: a whole 2x2x4 slice. The times are simulated.
32 devices in a mesh: blk: 4 (over y, x), tones: 8 (over z, core).
Axes of the slice: x: 2, y: 2, z: 4, core: 2. Of those that a mesh axis runs over, the one named last changes fastest.
Arguments:
- channel: float32 [256, 2, 256, 1024], P('tones', None, None, 'blk'), may hold values from -0.25 to 0.25
- received: float32 [256, 2, 448, 1024], P('tones', None, None, 'blk'), may hold values from -6 to 6
- step_sizes: float32 [4, 2], P('blk'), may hold values from 0.1 to 0.4
- hop_offset: int32 [8], replicated, may hold values from 0 to 3
- user_order: int32 [256], replicated, may hold values from 0 to 255, each once
Outputs:
- soft_symbols: float32 [256, 2, 448, 256], P(('blk', 'tones'))
Inputs may be any that keep to these rules, and one draw needn't show every extreme that they name: `user_order`: each user appears exactly once.
All inputs are finite; a program needn't handle non-finite values.
Results may differ from a plain program's by a relative error of at most 0.0003.
Values sent between devices are 32-bit elements; how exact they have to be, the bound alone decides.
No kernel may reach another device: no remote copies, remote signals or barrier semaphores. Data moves between devices by JAX's collectives and lax.ppermute only.
A program may use at most 192 MiB of HBM per device.

v0:
```python
import jax
import jax.numpy as jnp
from jax import lax
from jax.sharding import PartitionSpec as P


def shifted(value, axis, steps):
    count = lax.axis_size(axis)
    pairs = [(source, (source + steps) % count) for source in range(count)]
    return lax.ppermute(value, axis, pairs)


def forward(left, right):
    return jnp.einsum("...su,...ub->...sb", left, right, precision=lax.Precision.HIGHEST)


def adjoint(left, right):
    return jnp.einsum("...sb,...ub->...su", left, right, precision=lax.Precision.HIGHEST)


def gradient_step(estimate, chan, recv, step_rate):
    est_real = estimate[..., 0, :, :]
    est_imag = estimate[..., 1, :, :]
    chan_real = chan[..., 0, :, :]
    channel_imaginary = chan[..., 1, :, :]
    res_real = recv[..., 0, :, :] - (
        forward(est_real, chan_real) - forward(est_imag, channel_imaginary)
    )
    res_imag = recv[..., 1, :, :] - (
        forward(est_real, channel_imaginary) + forward(est_imag, chan_real)
    )
    grad_real = adjoint(res_real, chan_real) + adjoint(res_imag, channel_imaginary)
    grad_imag = adjoint(res_imag, chan_real) - adjoint(res_real, channel_imaginary)
    return jnp.tanh(
        jnp.stack([est_real + step_rate * grad_real, est_imag + step_rate * grad_imag], axis=-3)
    )


def tables(length):
    index_row = jnp.arange(length, dtype=jnp.int32)
    products = index_row[:, None] * index_row[None, :] % length
    angle = 2.0 * jnp.pi / length * products.astype(jnp.float32)
    scale = 1.0 / jnp.sqrt(jnp.float32(length))
    return (jnp.cos(angle) * scale, jnp.sin(angle) * scale)


def despread(spread):
    cosine_table, sine_table = tables(spread.shape[-1])
    spread_real = spread[:, 0]
    spread_imag = spread[:, 1]
    highest = lax.Precision.HIGHEST
    out_real = jnp.einsum("isk,kn->isn", spread_real, cosine_table, precision=highest) - jnp.einsum(
        "isk,kn->isn", spread_imag, sine_table, precision=highest
    )
    out_imag = jnp.einsum("isk,kn->isn", spread_real, sine_table, precision=highest) + jnp.einsum(
        "isk,kn->isn", spread_imag, cosine_table, precision=highest
    )
    return jnp.tanh(jnp.stack([out_real, out_imag], axis=1))


def on_device(channel, received, step_sizes, hop_offset, user_order):
    chain_len = lax.axis_size("blk")
    tone_groups = lax.axis_size("tones")
    position = lax.axis_index("blk")
    tone_group = lax.axis_index("tones")
    tones_dev = channel.shape[0]
    users = channel.shape[2]
    symbols = received.shape[2]
    block_rows = symbols // chain_len
    offset = hop_offset[tone_group]
    step_rates = step_sizes[0]

    def advance(estimate, hop_index, first_row, row_count):
        block_index = (position - offset - hop_index) % chain_len
        received_block = lax.dynamic_slice_in_dim(
            received, block_index * block_rows + first_row, row_count, 2
        )
        for substep in range(2):
            estimate = gradient_step(estimate, channel, received_block, step_rates[substep])
        return estimate

    start_est = jnp.zeros((tones_dev, 2, block_rows, users), jnp.float32)

    def one_hop(hop_index, estimate):
        return shifted(advance(estimate, hop_index, 0, block_rows), "blk", 1)

    estimate = lax.fori_loop(0, chain_len - 1, one_hop, start_est)
    estimate = advance(estimate, chain_len - 1, 0, block_rows)
    owners = chain_len * tone_groups
    per_owner = users // owners
    ordered = jnp.take(estimate, user_order, axis=3)
    packed = jnp.transpose(ordered, (3, 1, 2, 0)).reshape(
        chain_len, tone_groups, per_owner, 2 * block_rows * tones_dev
    )
    pieces = lax.all_to_all(
        packed.reshape(owners, per_owner, -1),
        ("blk", "tones"),
        split_axis=0,
        concat_axis=0,
        tiled=True,
    )
    item_count = pieces.shape[1]
    arranged = pieces.reshape(chain_len, tone_groups, item_count, 2, block_rows, tones_dev)
    source = (jnp.arange(chain_len, dtype=jnp.int32)[:, None] + hop_offset[None, :] - 1) % chain_len
    aligned = jnp.take_along_axis(arranged, source[:, :, None, None, None, None], axis=0)
    spread = jnp.transpose(aligned, (2, 3, 0, 4, 1, 5)).reshape(
        item_count, 2, chain_len * block_rows, tone_groups * tones_dev
    )
    return despread(spread)


def solution(mesh):
    in_specs = (
        P("tones", None, None, "blk"),
        P("tones", None, None, "blk"),
        P("blk", None),
        P(),
        P(),
    )
    out_specs = P(("blk", "tones"), None, None, None)
    return jax.shard_map(
        on_device, mesh=mesh, in_specs=in_specs, out_specs=out_specs, check_vma=False
    )
```

profile of v0, /device:TPU:0, one launch (start us, length us, event | category | flops | bytes accessed | tf_op | source)
XLA Modules:
  0.0 1749.8 jit_solution(10081130209439884025)
XLA Ops:
  1.9 22.5 %copy.12 = f32[32,2,448,256]{3,2,0,1:T(8,128)} copy(f32[32,2,448,256]{3,2,1,0:T(8,128)} %param.8) | data formatting | bytes 58720256 | tf_op jit(solution)/shard_map/while | solution.py:87
  36.5 1136.1 %while.15 = (s32[]{:T(128)}, f32[32,2,112,256]{3,2,0,1:T(8,128)}, f32[2]{0:T(128)S(1)}, s32[]{:T(128)}, f32[32,2,448,256]{3,2,0,1:T(8,128)}, /*index=5*/f32[32,2...) while((s32[]{:T(128)}, f32[32,2,112,256]{3,2,0,1:T(8,128)}, ...), condition=%wide.region_1.2_spmd, body=%wide.region_0.1_spmd.sunk | while | flops 45119176704 | bytes 463471072 | solution.py:87
  117.8 15.3 fusion.264
  133.1 15.2 fusion.266
  229.3 15.1 add_bitcast_fusion.8
  254.4 159.4 %collective-permute-done = f32[32,2,112,256]{3,2,0,1:T(8,128)} collective-permute-done((f32[32,2,112,256]{3,2,0,1:T(8,128)}, f32[32,2,112,256]{3,2,0,1:T(8,128)}, u32[]{:S(2)}, u32[]{:S(2)}) %collective-permute-start) | collective-permute-done | bytes 7340064 | tf_op jit(solution)/shard_map/while/body/eval_jaxpr/ppermute | solution.py:10
  494.9 15.3 fusion.264
  510.2 15.2 fusion.266
  606.4 15.1 add_bitcast_fusion.8
  629.5 159.8 %collective-permute-done = f32[32,2,112,256]{3,2,0,1:T(8,128)} collective-permute-done((f32[32,2,112,256]{3,2,0,1:T(8,128)}, f32[32,2,112,256]{3,2,0,1:T(8,128)}, u32[]{:S(2)}, u32[]{:S(2)}) %collective-permute-start) | collective-permute-done | bytes 7340064 | tf_op jit(solution)/shard_map/while/body/eval_jaxpr/ppermute | solution.py:10
  870.4 15.3 fusion.264
  885.7 15.2 fusion.266
  982.0 15.1 add_bitcast_fusion.8
  1004.3 159.6 %collective-permute-done = f32[32,2,112,256]{3,2,0,1:T(8,128)} collective-permute-done((f32[32,2,112,256]{3,2,0,1:T(8,128)}, f32[32,2,112,256]{3,2,0,1:T(8,128)}, u32[]{:S(2)}, u32[]{:S(2)}) %collective-permute-start) | collective-permute-done | bytes 7340064 | tf_op jit(solution)/shard_map/while/body/eval_jaxpr/ppermute | solution.py:10
  1249.3 15.1 fusion.100
  1264.4 15.3 fusion.103
  1361.1 15.5 add_bitcast_fusion.4
  1407.4 17.3 copy.18
  1424.8 22.5 %reshape_reshape.3 = f32[32,8,7168]{2,1,0:T(8,128)} reshape(f32[256,2,112,32]{3,2,1,0:T(8,128)} %copy.18) | data formatting | bytes 14680064 | tf_op jit(solution)/shard_map/reshape;reshape | solution.py:96
  1451.4 162.3 %all-to-all-done = f32[32,8,7168]{2,1,0:T(8,128)} async-done(((f32[32,8,7168]{2,1,0:T(8,128)}), f32[32,8,7168]{2,1,0:T(8,128)}, u32[]{:S(2)}, u32[]{:S(2)}) %all-to-all-start) | async-done | bytes 7340064 | tf_op jit(solution)/shard_map/all_to_all | solution.py:95
  1613.7 18.8 %reshape.117 = f32[4,8,8,2,112,32]{5,4,3,2,1,0:T(8,128)} reshape(f32[32,8,7168]{2,1,0:T(8,128)} %all-to-all-done) | data formatting | bytes 14680064 | tf_op jit(solution)/shard_map/reshape | solution.py:103
  1632.5 21.5 %gather_fusion.1 = f32[32,8,2,112,32]{4,3,2,1,0:T(8,128)} fusion(f32[4,8,8,2,112,32]{5,4,3,2,1,0:T(8,128)} %reshape.117, s32[32]{0:T(128)S(1)} %reshape.127), kind=kCustom, calls=%fused_computation.1 | custom fusion | bytes 14680320 | tf_op jit(solution)/shard_map/jit(take_along_axis)/gather | solution.py:105
  1654.0 19.9 %copy.19 = f32[32,8,2,112,32]{3,4,2,1,0:T(8,128)} copy(f32[32,8,2,112,32]{4,3,2,1,0:T(8,128)} %gather_fusion.1) | data formatting | bytes 14680064 | tf_op jit(solution)/shard_map/jit(take_along_axis)/gather | solution.py:105
  1682.7 14.9 copy.20
  (151 shorter events, 777.2 us)
Async XLA Ops:
  1.9 24.5 %copy-start.1 = (f32[32,2,256,256]{3,2,1,0:T(8,128)S(1)}, f32[32,2,256,256]{3,2,1,0:T(8,128)}, u32[]{:S(2)}) copy-start(f32[32,2,256,256]{3,2,1,0:T(8,128)} %param.7) | copy-start | bytes 50331652
  88.8 28.9 %slice-start = ((s8[16777216]{0:T(1024)(128)(4,1)}), s8[4194304]{0:T(1024)(128)(4,1)S(1)}, s32[]{:S(2)}) async-start(s8[16777216]{0:T(1024)(128)(4,1)} %bitcast.353), calls=%async_computation.1 | async-start | bytes 8388608 | tf_op jit(solution)/shard_map/while
  88.8 28.9 %slice-start.1 = ((s8[16777216]{0:T(1024)(128)(4,1)}), s8[4194304]{0:T(1024)(128)(4,1)S(1)}, s32[]{:S(2)}) async-start(s8[16777216]{0:T(1024)(128)(4,1)} %bitcast.353), calls=%async_computation.2 | async-start | bytes 8388608 | tf_op jit(solution)/shard_map/while
  88.8 28.9 %slice-start.2 = ((s8[16777216]{0:T(1024)(128)(4,1)}), s8[4194304]{0:T(1024)(128)(4,1)S(1)}, s32[]{:S(2)}) async-start(s8[16777216]{0:T(1024)(128)(4,1)} %bitcast.353), calls=%async_computation.3 | async-start | bytes 8388608 | tf_op jit(solution)/shard_map/while
  103.0 14.8 slice-start.3
  251.5 162.3 %collective-permute-start = (f32[32,2,112,256]{3,2,0,1:T(8,128)}, f32[32,2,112,256]{3,2,0,1:T(8,128)}, u32[]{:S(2)}, u32[]{:S(2)}) collective-permute-start(f32[32,2,112,256]{3,2,0,1:T(8,128)} %maximum_tanh_fusion.8), channel_id=1, source_target_pairs={{0,8},{8,16},{16,24},{24,0},{1,9},{9,17},{17,25},{25,1},{2,10},{10... | collective-permute-start | bytes 22020104 | tf_op jit(solution)/shard_map/while/body/eval_jaxpr/ppermute | solution.py:10
  465.9 28.9 %slice-start = ((s8[16777216]{0:T(1024)(128)(4,1)}), s8[4194304]{0:T(1024)(128)(4,1)S(1)}, s32[]{:S(2)}) async-start(s8[16777216]{0:T(1024)(128)(4,1)} %bitcast.353), calls=%async_computation.1 | async-start | bytes 8388608 | tf_op jit(solution)/shard_map/while
  465.9 28.9 %slice-start.1 = ((s8[16777216]{0:T(1024)(128)(4,1)}), s8[4194304]{0:T(1024)(128)(4,1)S(1)}, s32[]{:S(2)}) async-start(s8[16777216]{0:T(1024)(128)(4,1)} %bitcast.353), calls=%async_computation.2 | async-start | bytes 8388608 | tf_op jit(solution)/shard_map/while
  465.9 28.9 %slice-start.2 = ((s8[16777216]{0:T(1024)(128)(4,1)}), s8[4194304]{0:T(1024)(128)(4,1)S(1)}, s32[]{:S(2)}) async-start(s8[16777216]{0:T(1024)(128)(4,1)} %bitcast.353), calls=%async_computation.3 | async-start | bytes 8388608 | tf_op jit(solution)/shard_map/while
  480.1 14.8 slice-start.3
  628.7 160.6 %collective-permute-start = (f32[32,2,112,256]{3,2,0,1:T(8,128)}, f32[32,2,112,256]{3,2,0,1:T(8,128)}, u32[]{:S(2)}, u32[]{:S(2)}) collective-permute-start(f32[32,2,112,256]{3,2,0,1:T(8,128)} %maximum_tanh_fusion.8), channel_id=1, source_target_pairs={{0,8},{8,16},{16,24},{24,0},{1,9},{9,17},{17,25},{25,1},{2,10},{10... | collective-permute-start | bytes 22020104 | tf_op jit(solution)/shard_map/while/body/eval_jaxpr/ppermute | solution.py:10
  841.4 28.9 %slice-start = ((s8[16777216]{0:T(1024)(128)(4,1)}), s8[4194304]{0:T(1024)(128)(4,1)S(1)}, s32[]{:S(2)}) async-start(s8[16777216]{0:T(1024)(128)(4,1)} %bitcast.353), calls=%async_computation.1 | async-start | bytes 8388608 | tf_op jit(solution)/shard_map/while
  841.4 28.9 %slice-start.1 = ((s8[16777216]{0:T(1024)(128)(4,1)}), s8[4194304]{0:T(1024)(128)(4,1)S(1)}, s32[]{:S(2)}) async-start(s8[16777216]{0:T(1024)(128)(4,1)} %bitcast.353), calls=%async_computation.2 | async-start | bytes 8388608 | tf_op jit(solution)/shard_map/while
  841.4 28.9 %slice-start.2 = ((s8[16777216]{0:T(1024)(128)(4,1)}), s8[4194304]{0:T(1024)(128)(4,1)S(1)}, s32[]{:S(2)}) async-start(s8[16777216]{0:T(1024)(128)(4,1)} %bitcast.353), calls=%async_computation.3 | async-start | bytes 8388608 | tf_op jit(solution)/shard_map/while
  855.6 14.8 slice-start.3
  1004.3 159.6 %collective-permute-start = (f32[32,2,112,256]{3,2,0,1:T(8,128)}, f32[32,2,112,256]{3,2,0,1:T(8,128)}, u32[]{:S(2)}, u32[]{:S(2)}) collective-permute-start(f32[32,2,112,256]{3,2,0,1:T(8,128)} %maximum_tanh_fusion.8), channel_id=1, source_target_pairs={{0,8},{8,16},{16,24},{24,0},{1,9},{9,17},{17,25},{25,1},{2,10},{10... | collective-permute-start | bytes 22020104 | tf_op jit(solution)/shard_map/while/body/eval_jaxpr/ppermute | solution.py:10
  1196.3 28.9 %slice-start.4 = ((s8[16777216]{0:T(1024)(128)(4,1)}), s8[4194304]{0:T(1024)(128)(4,1)S(1)}, s32[]{:S(2)}) async-start(s8[16777216]{0:T(1024)(128)(4,1)} %bitcast.355), calls=%async_computation.5 | async-start | bytes 8388608
  1196.3 28.9 %slice-start.5 = ((s8[16777216]{0:T(1024)(128)(4,1)}), s8[4194304]{0:T(1024)(128)(4,1)S(1)}, s32[]{:S(2)}) async-start(s8[16777216]{0:T(1024)(128)(4,1)} %bitcast.355), calls=%async_computation.6 | async-start | bytes 8388608
  1196.3 28.9 %slice-start.6 = ((s8[16777216]{0:T(1024)(128)(4,1)}), s8[4194304]{0:T(1024)(128)(4,1)S(1)}, s32[]{:S(2)}) async-start(s8[16777216]{0:T(1024)(128)(4,1)} %bitcast.355), calls=%async_computation.7 | async-start | bytes 8388608
  1210.5 14.6 slice-start.7
  1290.9 7.5 copy-start.5
  1447.2 166.5 %all-to-all-start = ((f32[32,8,7168]{2,1,0:T(8,128)}), f32[32,8,7168]{2,1,0:T(8,128)}, u32[]{:S(2)}, u32[]{:S(2)}) async-start(f32[32,8,7168]{2,1,0:T(8,128)} %reshape_reshape.3), calls=%async_computation | async-start | bytes 14680064 | tf_op jit(solution)/shard_map/all_to_all | solution.py:95
  1708.1 21.2 %slice-start.8 = ((s8[8388608]{0:T(1024)(128)(4,1)}), s8[4194304]{0:T(1024)(128)(4,1)S(1)}, s32[]{:S(2)}) async-start(s8[8388608]{0:T(1024)(128)(4,1)} %bitcast.357), calls=%async_computation.9 | async-start | bytes 8388608
  1718.7 10.6 slice-start.9
  (9 other events, 41.6 us)
where the time goes:
time: 1750 us
  matrix products  838 us (48%)
  waiting for transfers between devices  641 us (37%)
  local copies, waits for them, and re-layouts  191 us (11%)
  other arithmetic  60.9 us (3%)
    ppermute x3, waiting for transfers between devices, shifted(): return lax.ppermute(value, axis, pairs)  479 us
    dot_general x32, matrix products, adjoint(): jnp.einsum('...sb,...ub->...su', left, right, precision=lax.Precision.HIG...  452 us
    dot_general x32, matrix products, forward(): jnp.einsum('...su,...ub->...sb', left, right, precision=lax.Precision.HIG...  349 us
    all_to_all x1, waiting for transfers between devices, on_device(): lax.all_to_all(packed.reshape(owners, per_owner, -1), ('blk', 'tones'), s...  162 us
    tanh x8, other arithmetic, gradient_step(): jnp.tanh(jnp.stack([est_real + step_rate * grad_real, est_imag + step_rat...  45 us
    gather x3, local copies, waits for them, and re-layouts, on_device(): jnp.take_along_axis(arranged, source[:, :, None, None, None, None], axis=0)  41.5 us
  transfers between devices with their start and end apart: 4, of which 4 were waited for; matrix products, arithmetic and copies ran while one was open for 0% of the time, Pallas kernels for 0%

commit v1 on v0

v1 whole, which is shorter than its diff:
```python
import functools

import jax
import jax.numpy as jnp
import ml_dtypes
import numpy as np
from jax import lax
from jax.experimental import pallas as pl
from jax.experimental.pallas import tpu as pltpu
from jax.sharding import PartitionSpec as P

F32 = jnp.float32
BF16 = jnp.bfloat16
VMEM_LIMIT = 56 * 1024 * 1024
ANY = pl.BlockSpec(memory_space=pl.ANY)
SMEM = pl.BlockSpec(memory_space=pltpu.SMEM)


def split(value):
    high = value.astype(BF16)
    return high, (value - high.astype(F32)).astype(BF16)


def dot(left, right, contract):
    return lax.dot_general(left, right, ((contract[:1], contract[1:]), ((), ())), preferred_element_type=F32)


def dot3(left, right, contract):
    left_high, left_low = left
    right_high, right_low = right
    return (
        dot(left_high, right_high, contract)
        + dot(left_high, right_low, contract)
        + dot(left_low, right_high, contract)
    )


def triangle(users):
    row = lax.broadcasted_iota(jnp.int32, (users, users), 0)
    column = lax.broadcasted_iota(jnp.int32, (users, users), 1)
    return row, column


def prepare_body(start, chan, recv, *refs):
    out = refs[-1]
    users = chan.shape[2]
    symbols = recv.shape[2]
    left_real = split(jnp.concatenate([chan[0, 0], recv[0, 0]], 0))
    left_imag = split(jnp.concatenate([chan[0, 1], recv[0, 1]], 0))
    right = tuple(
        jnp.concatenate([real[:users], imag[:users]], 1) for real, imag in zip(left_real, left_imag)
    )
    real = dot3(tuple(jnp.concatenate(pair, 1) for pair in zip(left_real, left_imag)), right, (1, 1))
    imag = dot3(
        tuple(jnp.concatenate([b, -a], 1) for a, b in zip(left_real, left_imag)), right, (1, 1)
    )
    row, column = triangle(users)
    out[0, :users] = jnp.where(row <= column, real[:users], imag[:users])
    out[0, users : users + symbols] = real[users:]
    out[0, users + symbols :] = imag[users:]


def prepare(channel, received, start, count, after):
    _, _, users, width = channel.shape
    symbols = received.shape[2]
    rows = users + 2 * symbols
    return pl.pallas_call(
        prepare_body,
        out_shape=jax.ShapeDtypeStruct((count, rows, users), F32),
        grid_spec=pltpu.PrefetchScalarGridSpec(
            num_scalar_prefetch=1,
            grid=(count,),
            in_specs=[
                pl.BlockSpec((1, 2, users, width), lambda i, start: (start[0] + i, 0, 0, 0)),
                pl.BlockSpec((1, 2, symbols, width), lambda i, start: (start[0] + i, 0, 0, 0)),
            ]
            + [ANY] * len(after),
            out_specs=pl.BlockSpec((1, rows, users), lambda i, start: (i, 0, 0)),
        ),
        compiler_params=pltpu.CompilerParams(vmem_limit_bytes=VMEM_LIMIT),
        cost_estimate=pl.CostEstimate(
            flops=count * 2 * 12 * (users + symbols) * width * users,
            bytes_accessed=4 * count * (2 * (users + symbols) * width + rows * users),
            transcendentals=0,
        ),
        name="prepare",
    )(start, channel, received, *after)


def unpack(packed, gram, sub):
    users = packed.shape[0]
    row, column = triangle(users)
    turned = packed.T
    real = split(jnp.where(row <= column, packed, turned))
    imag = split(jnp.where(row > column, packed, jnp.where(row < column, -turned, 0.0)))
    for part in range(2):
        gram[sub, part, :users, :users] = real[part]
        gram[sub, part, :users, users:] = imag[part]
        gram[sub, part, users:, :users] = -imag[part]
        gram[sub, part, users:, users:] = real[part]


def step(estimate, matched, gram, sub, rate):
    product = dot3(split(estimate), (gram[sub, 0], gram[sub, 1]), (1, 0))
    return jnp.tanh(estimate + rate * (matched - product))


def filtered(ref, users, symbols, rows, block):
    parts = []
    for part in range(2):
        first = pl.multiple_of(users + part * symbols + block * rows, 8)
        parts.append(ref[0, pl.ds(first, rows), :])
    return jnp.concatenate(parts, 1)


def chain_body(round_index, kind, symbols, scalars, rates, own, peer, *refs):
    users = own.shape[2]
    rows = symbols // kind["blocks"]
    side = scalars[0]
    even_block = scalars[1 + 2 * round_index]
    odd_block = scalars[2 + 2 * round_index]
    gram, matched = refs[-2:]
    for ref, sub in ((own, side), (peer, 1 - side)):
        unpack(ref[0, :users], gram, sub)
        for slot, block in enumerate((even_block, odd_block)):
            matched[sub, slot * rows : (slot + 1) * rows] = filtered(ref, users, symbols, rows, block)

    if round_index == 0:
        out = refs[-3:-2]
        even = jnp.tanh(rates[0, 0] * matched[0, :rows])
        even = step(even, matched[0, :rows], gram, 0, rates[0, 1])
        even = step(even, matched[1, :rows], gram, 1, rates[1, 0])
        odd = jnp.tanh(rates[1, 0] * matched[1, rows:])
        both = step(jnp.concatenate([even, odd], 0), matched[1], gram, 1, rates[1, 1])
    else:
        out = refs[-4:-2] if kind["last"] else refs[-3:-2]
        came = refs[0]
        both = jnp.concatenate(
            [jnp.concatenate([came[0, slot, 0], came[0, slot, 1]], 1) for slot in range(2)], 0
        )
        for sub in range(2):
            for substep in range(2):
                both = step(both, matched[sub], gram, sub, rates[sub, substep])
    for slot in range(2):
        for part in range(2):
            piece = both[slot * rows : (slot + 1) * rows, part * users : (part + 1) * users]
            if len(out) == 2:
                out[slot][0, part] = piece
            else:
                out[0][0, slot, part] = piece


def chain(round_index, last, blocks, scalars, rates, own, peer, came, after):
    count, packed_rows, users = own.shape
    symbols = (packed_rows - users) // 2
    rows = symbols // blocks
    packed_spec = pl.BlockSpec((1, packed_rows, users), lambda i, s: (i, 0, 0))
    both_spec = pl.BlockSpec((1, 2, 2, rows, users), lambda i, s: (i, 0, 0, 0, 0))
    one_spec = pl.BlockSpec((1, 2, rows, users), lambda i, s: (i, 0, 0, 0))
    both_shape = jax.ShapeDtypeStruct((count, 2, 2, rows, users), F32)
    one_shape = jax.ShapeDtypeStruct((count, 2, rows, users), F32)
    return pl.pallas_call(
        functools.partial(chain_body, round_index, {"blocks": blocks, "last": last}, symbols),
        out_shape=[one_shape, one_shape] if last else both_shape,
        grid_spec=pltpu.PrefetchScalarGridSpec(
            num_scalar_prefetch=1,
            grid=(count,),
            in_specs=[SMEM, packed_spec, packed_spec] + [both_spec] * len(came) + [ANY] * len(after),
            out_specs=[one_spec, one_spec] if last else both_spec,
            scratch_shapes=[
                pltpu.VMEM((2, 2, 2 * users, 2 * users), BF16),
                pltpu.VMEM((2, 2 * rows, 2 * users), F32),
            ],
        ),
        compiler_params=pltpu.CompilerParams(vmem_limit_bytes=VMEM_LIMIT),
        cost_estimate=pl.CostEstimate(
            flops=count * 2 * 12 * 8 * rows * users * users,
            bytes_accessed=4 * count * (2 * packed_rows + 8 * rows) * users,
            transcendentals=count * 16 * rows * users,
        ),
        name="chain%d" % round_index,
    )(scalars, rates, own, peer, *came, *after)


def finish_body(round_index, count, rows, symbols, scalars, rates, own, peer, even, odd, order, *refs):
    users = own.shape[2]
    out, gram, gathered = refs[-3:]
    tone = pl.program_id(0)
    side = scalars[0]
    block = scalars[2 + 2 * round_index]
    even_slot = scalars[1 + 2 * (round_index + 1)]

    @pl.when(side == 0)
    def _():
        unpack(own[0, :users], gram, 0)

    @pl.when(side != 0)
    def _():
        unpack(peer[0, :users], gram, 0)

    matched = jnp.where(
        side == 0,
        filtered(own, users, symbols, rows, block),
        filtered(peer, users, symbols, rows, block),
    )
    estimate = jnp.concatenate([odd[0, 0], odd[0, 1]], 1)
    for substep in range(2):
        estimate = step(estimate, matched, gram, 0, rates[0, substep])
    for part in range(2):
        first = (tone * 2 + part) * 2
        odd_row = pl.multiple_of((first + 1 - even_slot) * rows, 8)
        even_row = pl.multiple_of((first + even_slot) * rows, 8)
        gathered[pl.ds(odd_row, rows), :] = estimate[:, part * users : (part + 1) * users]
        gathered[pl.ds(even_row, rows), :] = even[0, part]

    @pl.when(tone == count - 1)
    def _():
        high, low = split(gathered[...])
        turned = dot(order[...], high, (1, 1)) + dot(order[...], low, (1, 1))
        out[...] = turned.reshape(out.shape)


def finish(round_index, blocks, owners, scalars, rates, own, peer, even, odd, order, after):
    count, packed_rows, users = own.shape
    symbols = (packed_rows - users) // 2
    rows = symbols // blocks
    packed_spec = pl.BlockSpec((1, packed_rows, users), lambda i, s: (i, 0, 0))
    one_spec = pl.BlockSpec((1, 2, rows, users), lambda i, s: (i, 0, 0, 0))
    shape = (owners, users // owners, count * 4 * rows)
    return pl.pallas_call(
        functools.partial(finish_body, round_index, count, rows, symbols),
        out_shape=jax.ShapeDtypeStruct(shape, F32),
        grid_spec=pltpu.PrefetchScalarGridSpec(
            num_scalar_prefetch=1,
            grid=(count,),
            in_specs=[
                SMEM,
                packed_spec,
                packed_spec,
                one_spec,
                one_spec,
                pl.BlockSpec((users, users), lambda i, s: (0, 0)),
            ]
            + [ANY] * len(after),
            out_specs=pl.BlockSpec(shape, lambda i, s: (0, 0, 0)),
            scratch_shapes=[
                pltpu.VMEM((1, 2, 2 * users, 2 * users), BF16),
                pltpu.VMEM((count * 4 * rows, users), F32),
            ],
        ),
        compiler_params=pltpu.CompilerParams(vmem_limit_bytes=VMEM_LIMIT),
        cost_estimate=pl.CostEstimate(
            flops=count * 2 * 12 * 3 * rows * users * users,
            bytes_accessed=4 * count * (2 * packed_rows + 8 * rows) * users,
            transcendentals=count * 4 * rows * users,
        ),
        name="finish",
    )(scalars, rates, own, peer, even, odd, order, *after)


def despread_body(groups, half, sizes, rows, source, table, *refs):
    pieces = refs[: len(sizes)]
    out, tones_first, symbols_first = refs[len(sizes) :]
    items = out.shape[0]
    length = groups * 2 * half
    pair = pl.program_id(0)
    for slot in range(2):
        block = 2 * pair + slot

        def gather(group, carry):
            position = source[block * groups + group]
            for side in range(2):
                start = group * 2 * half + side * half
                for piece, size in zip(pieces, sizes):
                    src = (2 * position + side) * groups + group
                    for tone in range(size):
                        for part in range(2):
                            lane = ((tone * 2 + part) * 2 + slot) * rows
                            tones_first[part, start + tone, :, :rows] = piece[src, :, lane : lane + rows]
                    start = start + size
            return carry

        lax.fori_loop(0, groups, gather, 0)
        for item in range(items):
            for part in range(2):
                turned = split(tones_first[part, :, item, :].T[:rows])
                for precision in range(2):
                    symbols_first[
                        precision, item * rows : (item + 1) * rows, part * length : (part + 1) * length
                    ] = turned[precision]
        result = jnp.tanh(
            dot3((symbols_first[0], symbols_first[1]), (table[0], table[1]), (1, 0))
        )
        for item in range(items):
            for part in range(2):
                out[item, part, slot * rows : (slot + 1) * rows, :] = result[
                    item * rows : (item + 1) * rows, part * length : (part + 1) * length
                ]


def despread(pieces, sizes, groups, half, blocks, rows, source):
    items = pieces[0].shape[1]
    length = groups * 2 * half
    lanes = -(-rows // 128) * 128
    index = np.arange(length)
    angle = 2.0 * np.pi / length * (index[:, None] * index[None, :] % length)
    cosine, sine = np.cos(angle) / np.sqrt(length), np.sin(angle) / np.sqrt(length)
    table = np.block([[cosine, sine], [-sine, cosine]])
    high = table.astype(ml_dtypes.bfloat16)
    table = np.stack([high, (table - high.astype(np.float64)).astype(ml_dtypes.bfloat16)])
    return pl.pallas_call(
        functools.partial(despread_body, groups, half, sizes, rows),
        out_shape=jax.ShapeDtypeStruct((items, 2, blocks * rows, length), F32),
        grid_spec=pltpu.PrefetchScalarGridSpec(
            num_scalar_prefetch=1,
            grid=(blocks // 2,),
            in_specs=[pl.BlockSpec(table.shape, lambda i, s: (0, 0, 0))]
            + [pl.BlockSpec(piece.shape, lambda i, s: (0, 0, 0)) for piece in pieces],
            out_specs=pl.BlockSpec((items, 2, 2 * rows, length), lambda i, s: (0, 0, i, 0)),
            scratch_shapes=[
                pltpu.VMEM((2, length, items, lanes), F32),
                pltpu.VMEM((2, items * rows, 2 * length), BF16),
            ],
        ),
        compiler_params=pltpu.CompilerParams(vmem_limit_bytes=VMEM_LIMIT),
        cost_estimate=pl.CostEstimate(
            flops=2 * 12 * items * blocks * rows * length * length,
            bytes_accessed=16 * items * blocks * rows * length,
            transcendentals=2 * items * blocks * rows * length,
        ),
        name="despread",
    )(source, jnp.asarray(table), *pieces)


def on_device(channel, received, step_sizes, hop_offset, user_order):
    blocks = lax.axis_size("blk")
    groups = lax.axis_size("tones")
    pairs = blocks // 2
    half = channel.shape[0] // 2
    users = channel.shape[2]
    rows = received.shape[2] // blocks
    owners = blocks * groups
    position = lax.axis_index("blk")
    offset = hop_offset[lax.axis_index("tones")]
    side = position % 2
    pair = position // 2

    swap = [(p, p ^ 1) for p in range(blocks)]
    onward = [(p, (p + 2) % blocks) for p in range(blocks)]

    size = 2 if half % 2 == 0 else 1
    sizes = [size] * (half // size)
    starts = [sum(sizes[:c]) for c in range(len(sizes))]
    chunks = len(sizes)

    scalars = [side]
    for r in range(pairs + 1):
        scalars += [(2 * (pair - r) - offset) % blocks, (2 * (pair - r) + 1 - offset) % blocks]
    scalars.append((offset + 0) % 2)
    scalars = jnp.stack(scalars).astype(jnp.int32)
    peer_rates = lax.ppermute(step_sizes, "blk", swap)
    rates = jnp.where(
        side == 0,
        jnp.concatenate([step_sizes, peer_rates], 0),
        jnp.concatenate([peer_rates, step_sizes], 0),
    )
    order = (user_order[:, None] == jnp.arange(users, dtype=jnp.int32)[None, :]).astype(BF16)

    begins = (jnp.arange(blocks, dtype=jnp.int32)[:, None] + hop_offset[None, :]) % blocks
    source = jnp.where(begins % 2 == 0, begins // 2 + pairs - 1, begins // 2) % pairs

    own, peer, came, pieces = {}, {}, {}, []

    def ready_peer(c, after):
        start = ((1 - side) * half + starts[c]).astype(jnp.int32).reshape(1)
        sent = prepare(channel, received, start, sizes[c], after)
        peer[c] = lax.ppermute(sent, "blk", swap)
        return sent

    def ready_own(c, after):
        start = (side * half + starts[c]).astype(jnp.int32).reshape(1)
        own[c] = prepare(channel, received, start, sizes[c], after)
        return own[c]

    last = ready_peer(0, [])
    if chunks > 1:
        last = ready_peer(1, [last])
    last = ready_own(0, [last])
    for c in range(chunks):
        last = chain(0, False, blocks, scalars, rates, own[c], peer[c], [], [last])
        both = lax.ppermute(last, "blk", onward)
        if c + 2 < chunks:
            last = ready_peer(c + 2, [last])
        if c + 1 < chunks:
            last = ready_own(c + 1, [last])
        for r in range(1, pairs):
            done = chain(r, r == pairs - 1, blocks, scalars, rates, own[c], peer[c], [both], [last])
            if r < pairs - 1:
                both = lax.ppermute(done, "blk", onward)
                last = done
        even, odd = done
        odd = lax.ppermute(odd, "blk", onward)
        last = finish(pairs, blocks, owners, scalars, rates, own[c], peer[c], even, odd, order, [])
        pieces.append(
            lax.all_to_all(last, ("blk", "tones"), split_axis=0, concat_axis=0, tiled=True)
        )
    return despread(pieces, sizes, groups, half, blocks, rows, source.reshape(-1))


def solution(mesh):
    in_specs = (
        P("tones", None, None, "blk"),
        P("tones", None, None, "blk"),
        P("blk", None),
        P(),
        P(),
    )
    out_specs = P(("blk", "tones"), None, None, None)
    return jax.shard_map(
        on_device, mesh=mesh, in_specs=in_specs, out_specs=out_specs, check_vma=False
    )
```

time: 1750 us -> 694 us (0.40)
  matrix products: 838 us -> 0 us
  waiting for transfers between devices: 641 us -> 321 us
  Pallas kernels: 0 us -> 265 us
  local copies, waits for them, and re-layouts: 191 us -> 13.8 us
  starting transfers between devices: 7.69 us -> 77.3 us
  other arithmetic: 60.9 us -> 1.9 us
    dot_general x68 -> x0, matrix products: 838 us -> none  [the longest x32 452 us: adjoint(): jnp.einsum('...sb,...ub->...su', left, right, precision=lax.Precision.HIG...]
    pallas_call x0 -> x41, Pallas kernels: none -> 265 us  [the longest x16 114 us: chain(): pl.pallas_call(functools.partial(chain_body, round_index, {'blocks': bloc...]
    ppermute x3 -> x25, waiting for transfers between devices: 479 us -> 297 us  [the longest x8 133 us: on_device(): both = lax.ppermute(last, 'blk', onward)]
    all_to_all x1 -> x8, waiting for transfers between devices: 162 us -> 24.1 us  [on_device(): lax.all_to_all(last, ('blk', 'tones'), split_axis=0, concat_axis=0, tiled...]
    gather x4 -> x0, local copies, waits for them, and re-layouts: 49.4 us -> none  [the longest x3 41.5 us: on_device(): jnp.take_along_axis(arranged, source[:, :, None, None, None, None], axis=0)]
    tanh x9 -> x0, other arithmetic: 46 us -> none  [the longest x8 45 us: gradient_step(): jnp.tanh(jnp.stack([est_real + step_rate * grad_real, est_imag + step_rat...]
    all_to_all x1 -> x8, starting transfers between devices: 4.04 us -> 40.6 us  [on_device(): lax.all_to_all(last, ('blk', 'tones'), split_axis=0, concat_axis=0, tiled...]
    while x38 -> x0, local copies, waits for them, and re-layouts: 34.3 us -> none  [the longest x2 28.9 us: on_device(): estimate = lax.fori_loop(0, chain_len - 1, one_hop, start_est)]
  transfers between devices with their start and end apart: 4 -> 33, of which waited for: 4 -> 18; matrix products, arithmetic and copies ran while one was open for 0% -> 0% of each run, Pallas kernels for 0% -> 35%
where the time goes in v1:
time: 694 us; the launch traced here: 686 us
  waiting for transfers between devices  321 us (46%)
  Pallas kernels  265 us (38%)
  starting transfers between devices  77.3 us (11%)
  local copies, waits for them, and re-layouts  13.8 us (2%)
    ppermute x8, waiting for transfers between devices, on_device(): both = lax.ppermute(last, 'blk', onward)  133 us
    pallas_call x16, Pallas kernels, chain(): pl.pallas_call(functools.partial(chain_body, round_index, {'blocks': bloc...  114 us
    ppermute x1, waiting for transfers between devices, on_device(): peer_rates = lax.ppermute(step_sizes, 'blk', swap)  83.1 us
    ppermute x8, waiting for transfers between devices, on_device(): odd = lax.ppermute(odd, 'blk', onward)  81.5 us
    pallas_call x16, Pallas kernels, prepare(): pl.pallas_call(prepare_body, out_shape=jax.ShapeDtypeStruct((count, rows,...  80.6 us
    pallas_call x8, Pallas kernels, finish(): pl.pallas_call(functools.partial(finish_body, round_index, count, rows, s...  49.4 us
    all_to_all x8, starting transfers between devices, on_device(): lax.all_to_all(last, ('blk', 'tones'), split_axis=0, concat_axis=0, tiled...  40.6 us
    all_to_all x8, waiting for transfers between devices, on_device(): lax.all_to_all(last, ('blk', 'tones'), split_axis=0, concat_axis=0, tiled...  24.1 us
  transfers between devices with their start and end apart: 33, of which 18 were waited for; matrix products, arithmetic and copies ran while one was open for 0% of the time, Pallas kernels for 35%

profile of v1, /device:TPU:0, one launch (start us, length us, event | category | flops | bytes accessed | tf_op | source)
XLA Modules:
  0.0 685.7 jit_solution(5218380374945102251)
XLA Ops:
  26.9 83.1 %collective-permute-done = f32[1,2]{1,0:T(1,128)S(1)} collective-permute-done((f32[1,2]{1,0:T(1,128)S(1)}, f32[1,2]{1,0:T(1,128)S(1)}, u32[]{:S(2)}, u32[]{:S(2)}) %collective-permute-start) | collective-permute-done | bytes 40 | tf_op jit(solution)/shard_map/ppermute | solution.py:361
  128.8 9.9 %collective-permute-done.2.refs_0_ = f32[2,2,2,112,256]{4,3,2,1,0:T(8,128)S(1)} collective-permute-done((f32[2,2,2,112,256]{4,3,2,1,0:T(8,128)}, f32[2,2,2,112,256]{4,3,2,1,0:T(8,128)S(1)}, u32[]{:S(2)}, u32[]{:S(2)}) %collective-permute-start.2) | collective-permute-done | bytes 917536 | tf_op jit(solution)/shard_map/ppermute | solution.py:391
  139.6 7.8 %chain1.8 = (f32[2,2,112,256]{3,2,1,0:T(8,128)}, f32[2,2,112,256]{3,2,1,0:T(8,128)}) custom-call(s32[8]{0:T(128)} %stack.35.scalars, f32[2,2]{1,0:T(2,128)} %maximum_select_fusion.rates, f32[2,1152,256]{2,1,0:T(8,128)} %prepare.18.own.refs_0_, f32[2,1152,256]{2,1,0:T(8,128)} %collective-permute-done.1.peer, f32[2,2,2,112,256]{4,3,2,1,0:T(8,128)} %copy-done.20, ...), custom_call_target="tpu_custom_call" | custom-call | flops 2818572288 | bytes 6553600 | tf_op jit(solution)/shard_map/chain1/pallas_call | solution.py:162
  191.0 14.9 %collective-permute-done.5.refs_0_ = f32[2,2,2,112,256]{4,3,2,1,0:T(8,128)} collective-permute-done((f32[2,2,2,112,256]{4,3,2,1,0:T(8,128)}, f32[2,2,2,112,256]{4,3,2,1,0:T(8,128)}, u32[]{:S(2)}, u32[]{:S(2)}) %collective-permute-start.5) | collective-permute-done | bytes 917536 | tf_op jit(solution)/shard_map/ppermute | solution.py:391
  205.9 7.8 %chain1.9 = (f32[2,2,112,256]{3,2,1,0:T(8,128)}, f32[2,2,112,256]{3,2,1,0:T(8,128)}) custom-call(s32[8]{0:T(128)} %stack.35.scalars, f32[2,2]{1,0:T(2,128)} %maximum_select_fusion.rates, f32[2,1152,256]{2,1,0:T(8,128)} %prepare.20.refs_1_.own, f32[2,1152,256]{2,1,0:T(8,128)} %copy-done.2, f32[2,2,2,112,256]{4,3,2,1,0:T(8,128)} %collective-permute-done.5.refs_0_, ...), custom_call_target="tpu_custom_call" | custom-call | flops 2818572288 | bytes 6553600 | tf_op jit(solution)/shard_map/chain1/pallas_call | solution.py:162
  216.4 9.4 %collective-permute-done.6.odd = f32[2,2,112,256]{3,2,1,0:T(8,128)S(1)} collective-permute-done((f32[2,2,112,256]{3,2,1,0:T(8,128)}, f32[2,2,112,256]{3,2,1,0:T(8,128)S(1)}, u32[]{:S(2)}, u32[]{:S(2)}) %collective-permute-start.6) | collective-permute-done | bytes 458784 | tf_op jit(solution)/shard_map/ppermute | solution.py:402
  257.4 15.4 %collective-permute-done.8.refs_0_ = f32[2,2,2,112,256]{4,3,2,1,0:T(8,128)} collective-permute-done((f32[2,2,2,112,256]{4,3,2,1,0:T(8,128)}, f32[2,2,2,112,256]{4,3,2,1,0:T(8,128)}, u32[]{:S(2)}, u32[]{:S(2)}) %collective-permute-start.8) | collective-permute-done | bytes 917536 | tf_op jit(solution)/shard_map/ppermute | solution.py:391
  272.8 7.8 %chain1.10 = (f32[2,2,112,256]{3,2,1,0:T(8,128)}, f32[2,2,112,256]{3,2,1,0:T(8,128)}) custom-call(s32[8]{0:T(128)} %stack.35.scalars, f32[2,2]{1,0:T(2,128)} %maximum_select_fusion.rates, f32[2,1152,256]{2,1,0:T(8,128)} %prepare.22.refs_1_.own, f32[2,1152,256]{2,1,0:T(8,128)} %collective-permute-done.7.peer, ...), custom_call_target="tpu_custom_call" | custom-call | flops 2818572288 | bytes 6553600 | tf_op jit(solution)/shard_map/chain1/pallas_call | solution.py:162
  283.1 10.2 %collective-permute-done.9.odd = f32[2,2,112,256]{3,2,1,0:T(8,128)S(1)} collective-permute-done((f32[2,2,112,256]{3,2,1,0:T(8,128)}, f32[2,2,112,256]{3,2,1,0:T(8,128)S(1)}, u32[]{:S(2)}, u32[]{:S(2)}) %collective-permute-start.9) | collective-permute-done | bytes 458784 | tf_op jit(solution)/shard_map/ppermute | solution.py:402
  323.6 15.4 %collective-permute-done.11.refs_0_ = f32[2,2,2,112,256]{4,3,2,1,0:T(8,128)S(1)} collective-permute-done((f32[2,2,2,112,256]{4,3,2,1,0:T(8,128)}, f32[2,2,2,112,256]{4,3,2,1,0:T(8,128)S(1)}, u32[]{:S(2)}, u32[]{:S(2)}) %collective-permute-start.11) | collective-permute-done | bytes 917536 | tf_op jit(solution)/shard_map/ppermute | solution.py:391
  340.0 7.9 %chain1.11 = (f32[2,2,112,256]{3,2,1,0:T(8,128)}, f32[2,2,112,256]{3,2,1,0:T(8,128)}) custom-call(s32[8]{0:T(128)} %stack.35.scalars, f32[2,2]{1,0:T(2,128)} %maximum_select_fusion.rates, f32[2,1152,256]{2,1,0:T(8,128)} %prepare.24.refs_1_.own, f32[2,1152,256]{2,1,0:T(8,128)} %collective-permute-done.10.peer, f32[2,2,2,112,256]{4,3,2,1,0:T(8,128)} %copy-done.21, ...), custom_call_target="tpu_custom_call" | custom-call | flops 2818572288 | bytes 6553600 | tf_op jit(solution)/shard_map/chain1/pallas_call | solution.py:162
  350.3 10.4 %collective-permute-done.12.odd = f32[2,2,112,256]{3,2,1,0:T(8,128)S(1)} collective-permute-done((f32[2,2,112,256]{3,2,1,0:T(8,128)}, f32[2,2,112,256]{3,2,1,0:T(8,128)S(1)}, u32[]{:S(2)}, u32[]{:S(2)}) %collective-permute-start.12) | collective-permute-done | bytes 458784 | tf_op jit(solution)/shard_map/ppermute | solution.py:402
  390.8 15.4 %collective-permute-done.14.refs_0_ = f32[2,2,2,112,256]{4,3,2,1,0:T(8,128)} collective-permute-done((f32[2,2,2,112,256]{4,3,2,1,0:T(8,128)}, f32[2,2,2,112,256]{4,3,2,1,0:T(8,128)}, u32[]{:S(2)}, u32[]{:S(2)}) %collective-permute-start.14) | collective-permute-done | bytes 917536 | tf_op jit(solution)/shard_map/ppermute | solution.py:391
  416.5 10.2 %collective-permute-done.15.odd = f32[2,2,112,256]{3,2,1,0:T(8,128)S(1)} collective-permute-done((f32[2,2,112,256]{3,2,1,0:T(8,128)}, f32[2,2,112,256]{3,2,1,0:T(8,128)S(1)}, u32[]{:S(2)}, u32[]{:S(2)}) %collective-permute-start.15) | collective-permute-done | bytes 458784 | tf_op jit(solution)/shard_map/ppermute | solution.py:402
  456.7 15.6 %collective-permute-done.17.refs_0_ = f32[2,2,2,112,256]{4,3,2,1,0:T(8,128)} collective-permute-done((f32[2,2,2,112,256]{4,3,2,1,0:T(8,128)}, f32[2,2,2,112,256]{4,3,2,1,0:T(8,128)}, u32[]{:S(2)}, u32[]{:S(2)}) %collective-permute-start.17) | collective-permute-done | bytes 917536 | tf_op jit(solution)/shard_map/ppermute | solution.py:391
  472.3 7.8 %chain1.13 = (f32[2,2,112,256]{3,2,1,0:T(8,128)}, f32[2,2,112,256]{3,2,1,0:T(8,128)}) custom-call(s32[8]{0:T(128)} %stack.35.scalars, f32[2,2]{1,0:T(2,128)} %maximum_select_fusion.rates, f32[2,1152,256]{2,1,0:T(8,128)} %prepare.28.refs_1_.own, f32[2,1152,256]{2,1,0:T(8,128)} %collective-permute-done.16.peer, ...), custom_call_target="tpu_custom_call" | custom-call | flops 2818572288 | bytes 6553600 | tf_op jit(solution)/shard_map/chain1/pallas_call | solution.py:162
  482.5 10.3 %collective-permute-done.18.odd = f32[2,2,112,256]{3,2,1,0:T(8,128)S(1)} collective-permute-done((f32[2,2,112,256]{3,2,1,0:T(8,128)}, f32[2,2,112,256]{3,2,1,0:T(8,128)S(1)}, u32[]{:S(2)}, u32[]{:S(2)}) %collective-permute-start.18) | collective-permute-done | bytes 458784 | tf_op jit(solution)/shard_map/ppermute | solution.py:402
  517.5 20.5 %collective-permute-done.20.refs_0_ = f32[2,2,2,112,256]{4,3,2,1,0:T(8,128)S(1)} collective-permute-done((f32[2,2,2,112,256]{4,3,2,1,0:T(8,128)}, f32[2,2,2,112,256]{4,3,2,1,0:T(8,128)S(1)}, u32[]{:S(2)}, u32[]{:S(2)}) %collective-permute-start.20) | collective-permute-done | bytes 917536 | tf_op jit(solution)/shard_map/ppermute | solution.py:391
  539.0 7.9 %chain1.14 = (f32[2,2,112,256]{3,2,1,0:T(8,128)}, f32[2,2,112,256]{3,2,1,0:T(8,128)}) custom-call(s32[8]{0:T(128)} %stack.35.scalars, f32[2,2]{1,0:T(2,128)} %maximum_select_fusion.rates, f32[2,1152,256]{2,1,0:T(8,128)} %prepare.30.refs_1_.own, f32[2,1152,256]{2,1,0:T(8,128)} %collective-permute-done.19.peer, f32[2,2,2,112,256]{4,3,2,1,0:T(8,128)} %copy-done.22, ...), custom_call_target="tpu_custom_call" | custom-call | flops 2818572288 | bytes 6553600 | tf_op jit(solution)/shard_map/chain1/pallas_call | solution.py:162
  547.7 12.0 %collective-permute-done.21.odd = f32[2,2,112,256]{3,2,1,0:T(8,128)S(1)} collective-permute-done((f32[2,2,112,256]{3,2,1,0:T(8,128)}, f32[2,2,112,256]{3,2,1,0:T(8,128)S(1)}, u32[]{:S(2)}, u32[]{:S(2)}) %collective-permute-start.21) | collective-permute-done | bytes 458784 | tf_op jit(solution)/shard_map/ppermute | solution.py:402
  579.8 25.5 %collective-permute-done.23.refs_0_ = f32[2,2,2,112,256]{4,3,2,1,0:T(8,128)S(1)} collective-permute-done((f32[2,2,2,112,256]{4,3,2,1,0:T(8,128)}, f32[2,2,2,112,256]{4,3,2,1,0:T(8,128)S(1)}, u32[]{:S(2)}, u32[]{:S(2)}) %collective-permute-start.23) | collective-permute-done | bytes 917536 | tf_op jit(solution)/shard_map/ppermute | solution.py:391
  614.9 11.8 %collective-permute-done.24.odd = f32[2,2,112,256]{3,2,1,0:T(8,128)S(1)} collective-permute-done((f32[2,2,112,256]{3,2,1,0:T(8,128)}, f32[2,2,112,256]{3,2,1,0:T(8,128)S(1)}, u32[]{:S(2)}, u32[]{:S(2)}) %collective-permute-start.24) | collective-permute-done | bytes 458784 | tf_op jit(solution)/shard_map/ppermute | solution.py:402
  639.1 24.1 %all-to-all-done.7.refs_7_ = f32[32,8,896]{2,1,0:T(8,128)S(1)} async-done(((f32[32,8,896]{2,1,0:T(8,128)}), f32[32,8,896]{2,1,0:T(8,128)S(1)}, u32[]{:S(2)}, u32[]{:S(2)}) %all-to-all-start.7) | async-done | bytes 917536 | tf_op jit(solution)/shard_map/all_to_all | solution.py:405
  664.1 21.2 %despread.1 = f32[8,2,448,256]{3,2,1,0:T(8,128)} custom-call(s32[32]{0:T(128)} %and_select_fusion.source, bf16[2,512,512]{2,1,0:T(8,128)(2,1)} %constant.119.clone.table, f32[32,8,896]{2,1,0:T(8,128)} %copy-done.3, f32[32,8,896]{2,1,0:T(8,128)} %all-to-all-done.1.refs_1_, f32[32,8,896]{2,1,0:T(8,128)} %copy-done.4, f32[32,8,896]{2,1,0:T(8,128)} %all-to-all-done.3.refs_3_, ...), custom_call_target="tpu_custom_call" | custom-call | flops 5637144576 | bytes 14680064 | tf_op jit(solution)/shard_map/despread/pallas_call | solution.py:311
  (138 shorter events, 297.2 us)
Async XLA Ops:
  5.0 105.6 %collective-permute-start.1 = (f32[2,1152,256]{2,1,0:T(8,128)}, f32[2,1152,256]{2,1,0:T(8,128)}, u32[]{:S(2)}, u32[]{:S(2)}) collective-permute-start(f32[2,1152,256]{2,1,0:T(8,128)} %prepare.16.refs_0_), channel_id=1, source_target_pairs={{0,8},{8,0},{16,24},{24,16},{1,9},{9,1},{17,25},{25,17},{2,10},{10... | collective-permute-start | bytes 7077896 | tf_op jit(solution)/shard_map/ppermute | solution.py:377
  13.0 158.1 %collective-permute-start.4 = (f32[2,1152,256]{2,1,0:T(8,128)}, f32[2,1152,256]{2,1,0:T(8,128)S(1)}, u32[]{:S(2)}, u32[]{:S(2)}) collective-permute-start(f32[2,1152,256]{2,1,0:T(8,128)} %prepare.17.refs_0_), channel_id=1, source_target_pairs={{0,8},{8,0},{16,24},{24,16},{1,9},{9,1},{17,25},{25,17},{2,10},{10... | collective-permute-start | bytes 7077896 | tf_op jit(solution)/shard_map/ppermute | solution.py:377
  13.1 97.0 %collective-permute-start = (f32[1,2]{1,0:T(1,128)S(1)}, f32[1,2]{1,0:T(1,128)S(1)}, u32[]{:S(2)}, u32[]{:S(2)}) collective-permute-start(f32[1,2]{1,0:T(1,128)S(1)} %copy-done.17), channel_id=1, source_target_pairs={{0,8},{8,0},{16,24},{24,16},{1,9},{9,1},{17,25},{25,17},{2,10},{10... | collective-permute-start | bytes 32 | tf_op jit(solution)/shard_map/ppermute | solution.py:361
  149.0 90.1 %collective-permute-start.7 = (f32[2,1152,256]{2,1,0:T(8,128)}, f32[2,1152,256]{2,1,0:T(8,128)}, u32[]{:S(2)}, u32[]{:S(2)}) collective-permute-start(f32[2,1152,256]{2,1,0:T(8,128)} %prepare.19.refs_0_), channel_id=1, source_target_pairs={{0,8},{8,0},{16,24},{24,16},{1,9},{9,1},{17,25},{25,17},{2,10},{10... | collective-permute-start | bytes 7077896 | tf_op jit(solution)/shard_map/ppermute | solution.py:377
  165.4 67.3 %all-to-all-start = ((f32[32,8,896]{2,1,0:T(8,128)}), f32[32,8,896]{2,1,0:T(8,128)S(1)}, u32[]{:S(2)}, u32[]{:S(2)}) async-start(f32[32,8,896]{2,1,0:T(8,128)} %finish.8.refs_0_), calls=%async_computation | async-start | bytes 1835008 | tf_op jit(solution)/shard_map/all_to_all | solution.py:405
  179.0 26.9 %collective-permute-start.5 = (f32[2,2,2,112,256]{4,3,2,1,0:T(8,128)}, f32[2,2,2,112,256]{4,3,2,1,0:T(8,128)}, u32[]{:S(2)}, u32[]{:S(2)}) collective-permute-start(f32[2,2,2,112,256]{4,3,2,1,0:T(8,128)} %chain0.9.refs_0_), channel_id=1, source_target_pairs={{0,16},{8,24},{16,0},{24,8},{1,17},{9,25},{17,1},{25,9},{2,18},{10... | collective-permute-start | bytes 2752520 | tf_op jit(solution)/shard_map/ppermute | solution.py:391
  215.3 90.0 %collective-permute-start.10 = (f32[2,1152,256]{2,1,0:T(8,128)S(1)}, f32[2,1152,256]{2,1,0:T(8,128)}, u32[]{:S(2)}, u32[]{:S(2)}) collective-permute-start(f32[2,1152,256]{2,1,0:T(8,128)S(1)} %copy-done.1), channel_id=1, source_target_pairs={{0,8},{8,0},{16,24},{24,16},{1,9},{9,1},{17,25},{25,17},{2,10},{10... | collective-permute-start | bytes 7077896 | tf_op jit(solution)/shard_map/ppermute | solution.py:377
  232.7 67.6 %all-to-all-start.1 = ((f32[32,8,896]{2,1,0:T(8,128)}), f32[32,8,896]{2,1,0:T(8,128)}, u32[]{:S(2)}, u32[]{:S(2)}) async-start(f32[32,8,896]{2,1,0:T(8,128)} %finish.9.refs_0_), calls=%async_computation.1 | async-start | bytes 1835008 | tf_op jit(solution)/shard_map/all_to_all | solution.py:405
  245.5 27.3 %collective-permute-start.8 = (f32[2,2,2,112,256]{4,3,2,1,0:T(8,128)}, f32[2,2,2,112,256]{4,3,2,1,0:T(8,128)}, u32[]{:S(2)}, u32[]{:S(2)}) collective-permute-start(f32[2,2,2,112,256]{4,3,2,1,0:T(8,128)} %chain0.10.refs_0_), channel_id=1, source_target_pairs={{0,16},{8,24},{16,0},{24,8},{1,17},{9,25},{17,1},{25,9},{2,18},{10... | collective-permute-start | bytes 2752520 | tf_op jit(solution)/shard_map/ppermute | solution.py:391
  281.6 90.8 %collective-permute-start.13 = (f32[2,1152,256]{2,1,0:T(8,128)}, f32[2,1152,256]{2,1,0:T(8,128)}, u32[]{:S(2)}, u32[]{:S(2)}) collective-permute-start(f32[2,1152,256]{2,1,0:T(8,128)} %prepare.23.refs_0_), channel_id=1, source_target_pairs={{0,8},{8,0},{16,24},{24,16},{1,9},{9,1},{17,25},{25,17},{2,10},{10... | collective-permute-start | bytes 7077896 | tf_op jit(solution)/shard_map/ppermute | solution.py:377
  300.3 67.3 %all-to-all-start.2 = ((f32[32,8,896]{2,1,0:T(8,128)}), f32[32,8,896]{2,1,0:T(8,128)S(1)}, u32[]{:S(2)}, u32[]{:S(2)}) async-start(f32[32,8,896]{2,1,0:T(8,128)} %finish.10.refs_0_), calls=%async_computation.2 | async-start | bytes 1835008 | tf_op jit(solution)/shard_map/all_to_all | solution.py:405
  311.7 27.3 %collective-permute-start.11 = (f32[2,2,2,112,256]{4,3,2,1,0:T(8,128)}, f32[2,2,2,112,256]{4,3,2,1,0:T(8,128)S(1)}, u32[]{:S(2)}, u32[]{:S(2)}) collective-permute-start(f32[2,2,2,112,256]{4,3,2,1,0:T(8,128)} %chain0.11.refs_0_), channel_id=1, source_target_pairs={{0,16},{8,24},{16,0},{24,8},{1,17},{9,25},{17,1},{25,9},{2,18},{10... | collective-permute-start | bytes 2752520 | tf_op jit(solution)/shard_map/ppermute | solution.py:391
  348.7 89.7 %collective-permute-start.16 = (f32[2,1152,256]{2,1,0:T(8,128)}, f32[2,1152,256]{2,1,0:T(8,128)}, u32[]{:S(2)}, u32[]{:S(2)}) collective-permute-start(f32[2,1152,256]{2,1,0:T(8,128)} %prepare.25.refs_0_), channel_id=1, source_target_pairs={{0,8},{8,0},{16,24},{24,16},{1,9},{9,1},{17,25},{25,17},{2,10},{10... | collective-permute-start | bytes 7077896 | tf_op jit(solution)/shard_map/ppermute | solution.py:377
  367.6 66.0 %all-to-all-start.3 = ((f32[32,8,896]{2,1,0:T(8,128)}), f32[32,8,896]{2,1,0:T(8,128)}, u32[]{:S(2)}, u32[]{:S(2)}) async-start(f32[32,8,896]{2,1,0:T(8,128)} %finish.11.refs_0_), calls=%async_computation.3 | async-start | bytes 1835008 | tf_op jit(solution)/shard_map/all_to_all | solution.py:405
  378.8 27.4 %collective-permute-start.14 = (f32[2,2,2,112,256]{4,3,2,1,0:T(8,128)}, f32[2,2,2,112,256]{4,3,2,1,0:T(8,128)}, u32[]{:S(2)}, u32[]{:S(2)}) collective-permute-start(f32[2,2,2,112,256]{4,3,2,1,0:T(8,128)} %chain0.12.refs_0_), channel_id=1, source_target_pairs={{0,16},{8,24},{16,0},{24,8},{1,17},{9,25},{17,1},{25,9},{2,18},{10... | collective-permute-start | bytes 2752520 | tf_op jit(solution)/shard_map/ppermute | solution.py:391
  414.9 89.4 %collective-permute-start.19 = (f32[2,1152,256]{2,1,0:T(8,128)S(1)}, f32[2,1152,256]{2,1,0:T(8,128)}, u32[]{:S(2)}, u32[]{:S(2)}) collective-permute-start(f32[2,1152,256]{2,1,0:T(8,128)S(1)} %copy-done), channel_id=1, source_target_pairs={{0,8},{8,0},{16,24},{24,16},{1,9},{9,1},{17,25},{25,17},{2,10},{10... | collective-permute-start | bytes 7077896 | tf_op jit(solution)/shard_map/ppermute | solution.py:377
  433.6 66.1 %all-to-all-start.4 = ((f32[32,8,896]{2,1,0:T(8,128)}), f32[32,8,896]{2,1,0:T(8,128)S(1)}, u32[]{:S(2)}, u32[]{:S(2)}) async-start(f32[32,8,896]{2,1,0:T(8,128)} %finish.12.refs_0_), calls=%async_computation.4 | async-start | bytes 1835008 | tf_op jit(solution)/shard_map/all_to_all | solution.py:405
  444.8 27.5 %collective-permute-start.17 = (f32[2,2,2,112,256]{4,3,2,1,0:T(8,128)}, f32[2,2,2,112,256]{4,3,2,1,0:T(8,128)}, u32[]{:S(2)}, u32[]{:S(2)}) collective-permute-start(f32[2,2,2,112,256]{4,3,2,1,0:T(8,128)} %chain0.13.refs_0_), channel_id=1, source_target_pairs={{0,16},{8,24},{16,0},{24,8},{1,17},{9,25},{17,1},{25,9},{2,18},{10... | collective-permute-start | bytes 2752520 | tf_op jit(solution)/shard_map/ppermute | solution.py:391
  480.9 90.6 %collective-permute-start.22 = (f32[2,1152,256]{2,1,0:T(8,128)}, f32[2,1152,256]{2,1,0:T(8,128)}, u32[]{:S(2)}, u32[]{:S(2)}) collective-permute-start(f32[2,1152,256]{2,1,0:T(8,128)} %prepare.29.refs_0_), channel_id=1, source_target_pairs={{0,8},{8,0},{16,24},{24,16},{1,9},{9,1},{17,25},{25,17},{2,10},{10... | collective-permute-start | bytes 7077896 | tf_op jit(solution)/shard_map/ppermute | solution.py:377
  499.8 66.9 %all-to-all-start.5 = ((f32[32,8,896]{2,1,0:T(8,128)}), f32[32,8,896]{2,1,0:T(8,128)}, u32[]{:S(2)}, u32[]{:S(2)}) async-start(f32[32,8,896]{2,1,0:T(8,128)} %finish.13.refs_0_), calls=%async_computation.5 | async-start | bytes 1835008 | tf_op jit(solution)/shard_map/all_to_all | solution.py:405
  510.8 27.3 %collective-permute-start.20 = (f32[2,2,2,112,256]{4,3,2,1,0:T(8,128)}, f32[2,2,2,112,256]{4,3,2,1,0:T(8,128)S(1)}, u32[]{:S(2)}, u32[]{:S(2)}) collective-permute-start(f32[2,2,2,112,256]{4,3,2,1,0:T(8,128)} %chain0.14.refs_0_), channel_id=1, source_target_pairs={{0,16},{8,24},{16,0},{24,8},{1,17},{9,25},{17,1},{25,9},{2,18},{10... | collective-permute-start | bytes 2752520 | tf_op jit(solution)/shard_map/ppermute | solution.py:391
  566.7 67.1 %all-to-all-start.6 = ((f32[32,8,896]{2,1,0:T(8,128)}), f32[32,8,896]{2,1,0:T(8,128)S(1)}, u32[]{:S(2)}, u32[]{:S(2)}) async-start(f32[32,8,896]{2,1,0:T(8,128)} %finish.14.refs_0_), calls=%async_computation.6 | async-start | bytes 1835008 | tf_op jit(solution)/shard_map/all_to_all | solution.py:405
  577.9 27.4 %collective-permute-start.23 = (f32[2,2,2,112,256]{4,3,2,1,0:T(8,128)}, f32[2,2,2,112,256]{4,3,2,1,0:T(8,128)S(1)}, u32[]{:S(2)}, u32[]{:S(2)}) collective-permute-start(f32[2,2,2,112,256]{4,3,2,1,0:T(8,128)} %chain0.15.refs_1_), channel_id=1, source_target_pairs={{0,16},{8,24},{16,0},{24,8},{1,17},{9,25},{17,1},{25,9},{2,18},{10... | collective-permute-start | bytes 2752520 | tf_op jit(solution)/shard_map/ppermute | solution.py:391
  633.8 29.4 %all-to-all-start.7 = ((f32[32,8,896]{2,1,0:T(8,128)}), f32[32,8,896]{2,1,0:T(8,128)S(1)}, u32[]{:S(2)}, u32[]{:S(2)}) async-start(f32[32,8,896]{2,1,0:T(8,128)} %finish.15), calls=%async_computation.7 | async-start | bytes 1835008 | tf_op jit(solution)/shard_map/all_to_all | solution.py:405
  (33 other events, 291.0 us)

commit v2 on v1

--- a/solution.py
+++ b/solution.py
@@ -41,7 +41,7 @@
     return row, column
 
 
-def prepare_body(start, chan, recv, *refs):
+def prepare_body(carry, start, rates, chan, recv, *refs):
     out = refs[-1]
     users = chan.shape[2]
     symbols = recv.shape[2]
@@ -56,21 +56,26 @@
     )
     row, column = triangle(users)
     out[0, :users] = jnp.where(row <= column, real[:users], imag[:users])
+    rows = users + 2 * symbols
     out[0, users : users + symbols] = real[users:]
-    out[0, users + symbols :] = imag[users:]
-
-
-def prepare(channel, received, start, count, after):
+    out[0, users + symbols : rows] = imag[users:]
+    if carry:
+        lane = lax.broadcasted_iota(jnp.int32, (carry, users), 1)
+        out[0, rows:] = jnp.where(lane == 0, rates[0, 0], rates[0, 1])
+
+
+def prepare(channel, received, step_sizes, start, count, carry, after):
     _, _, users, width = channel.shape
     symbols = received.shape[2]
-    rows = users + 2 * symbols
+    rows = users + 2 * symbols + carry
     return pl.pallas_call(
-        prepare_body,
+        functools.partial(prepare_body, carry),
         out_shape=jax.ShapeDtypeStruct((count, rows, users), F32),
         grid_spec=pltpu.PrefetchScalarGridSpec(
             num_scalar_prefetch=1,
             grid=(count,),
             in_specs=[
+                SMEM,
                 pl.BlockSpec((1, 2, users, width), lambda i, start: (start[0] + i, 0, 0, 0)),
                 pl.BlockSpec((1, 2, symbols, width), lambda i, start: (start[0] + i, 0, 0, 0)),
             ]
@@ -84,7 +89,7 @@
             transcendentals=0,
         ),
         name="prepare",
-    )(start, channel, received, *after)
+    )(start, step_sizes, channel, received, *after)
 
 
 def unpack(packed, gram, sub):
@@ -258,11 +263,14 @@
     )(scalars, rates, own, peer, even, odd, order, *after)
 
 
-def despread_body(groups, half, sizes, rows, source, table, *refs):
+def despread_body(groups, sizes, rows, folded, first, last, source, table, *refs):
     pieces = refs[: len(sizes)]
-    out, tones_first, symbols_first = refs[len(sizes) :]
+    if not first:
+        total = refs[len(sizes)]
+    out, tones_first, symbols_first = refs[-3:]
     items = out.shape[0]
-    length = groups * 2 * half
+    length = out.shape[3]
+    tones = sum(sizes)
     pair = pl.program_id(0)
     for slot in range(2):
         block = 2 * pair + slot
@@ -270,66 +278,80 @@
         def gather(group, carry):
             position = source[block * groups + group]
             for side in range(2):
-                start = group * 2 * half + side * half
+                place = (group * 2 + side) * tones * 2
+                src = (2 * position + side) * groups + group
                 for piece, size in zip(pieces, sizes):
-                    src = (2 * position + side) * groups + group
-                    for tone in range(size):
-                        for part in range(2):
-                            lane = ((tone * 2 + part) * 2 + slot) * rows
-                            tones_first[part, start + tone, :, :rows] = piece[src, :, lane : lane + rows]
-                    start = start + size
+                    for tone in range(2 * size):
+                        lane = (tone * 2 + slot) * rows
+                        tones_first[place + tone, :, :rows] = piece[src, :, lane : lane + rows]
+                    place = place + 2 * size
             return carry
 
         lax.fori_loop(0, groups, gather, 0)
         for item in range(items):
-            for part in range(2):
-                turned = split(tones_first[part, :, item, :].T[:rows])
-                for precision in range(2):
-                    symbols_first[
-                        precision, item * rows : (item + 1) * rows, part * length : (part + 1) * length
-                    ] = turned[precision]
-        result = jnp.tanh(
-            dot3((symbols_first[0], symbols_first[1]), (table[0], table[1]), (1, 0))
-        )
+            high, low = split(tones_first[:, item, :])
+            if folded:
+                high = high.astype(F32)
+                joined = jnp.concatenate([high, high, low.astype(F32)], 0)
+                parts = [joined.T[:rows].astype(BF16)]
+            else:
+                parts = [high.astype(F32).T[:rows].astype(BF16), low.astype(F32).T[:rows].astype(BF16)]
+            for k, value in enumerate(parts):
+                symbols_first[k, item * rows : (item + 1) * rows, :] = value
+        if folded:
+            result = dot(symbols_first[0], table[0], (1, 0))
+        else:
+            result = dot3((symbols_first[0], symbols_first[1]), (table[0], table[1]), (1, 0))
         for item in range(items):
             for part in range(2):
-                out[item, part, slot * rows : (slot + 1) * rows, :] = result[
-                    item * rows : (item + 1) * rows, part * length : (part + 1) * length
-                ]
-
-
-def despread(pieces, sizes, groups, half, blocks, rows, source):
+                value = result[item * rows : (item + 1) * rows, part * length : (part + 1) * length]
+                if not first:
+                    value = value + total[item, part, slot * rows : (slot + 1) * rows, :]
+                out[item, part, slot * rows : (slot + 1) * rows, :] = jnp.tanh(value) if last else value
+
+
+def despread(pieces, starts, groups, half, blocks, rows, source, total, last, after):
     items = pieces[0].shape[1]
     length = groups * 2 * half
     lanes = -(-rows // 128) * 128
-    index = np.arange(length)
-    angle = 2.0 * np.pi / length * (index[:, None] * index[None, :] % length)
+    sizes = [piece.shape[2] // (4 * rows) for piece in pieces]
+    local = np.concatenate([np.arange(begin, begin + size) for begin, size in zip(starts, sizes)])
+    index = (np.arange(groups * 2)[:, None] * half + local[None, :]).reshape(-1)
+    angle = 2.0 * np.pi / length * (index[:, None] * np.arange(length)[None, :] % length)
     cosine, sine = np.cos(angle) / np.sqrt(length), np.sin(angle) / np.sqrt(length)
-    table = np.block([[cosine, sine], [-sine, cosine]])
+    real, imag = np.concatenate([cosine, sine], 1), np.concatenate([-sine, cosine], 1)
+    table = np.stack([real, imag], 1).reshape(2 * len(index), 2 * length)
     high = table.astype(ml_dtypes.bfloat16)
-    table = np.stack([high, (table - high.astype(np.float64)).astype(ml_dtypes.bfloat16)])
+    low = (table - high.astype(np.float64)).astype(ml_dtypes.bfloat16)
+    depth = len(table)
+    folded = 3 * depth <= 256
+    table = np.concatenate([high, low, high])[None] if folded else np.stack([high, low])
+    block_spec = pl.BlockSpec((items, 2, 2 * rows, length), lambda i, s: (0, 0, i, 0))
+    totals = [] if total is None else [total]
     return pl.pallas_call(
-        functools.partial(despread_body, groups, half, sizes, rows),
+        functools.partial(despread_body, groups, sizes, rows, folded, total is None, last),
         out_shape=jax.ShapeDtypeStruct((items, 2, blocks * rows, length), F32),
         grid_spec=pltpu.PrefetchScalarGridSpec(
             num_scalar_prefetch=1,
             grid=(blocks // 2,),
             in_specs=[pl.BlockSpec(table.shape, lambda i, s: (0, 0, 0))]
-            + [pl.BlockSpec(piece.shape, lambda i, s: (0, 0, 0)) for piece in pieces],
-            out_specs=pl.BlockSpec((items, 2, 2 * rows, length), lambda i, s: (0, 0, i, 0)),
+            + [pl.BlockSpec(piece.shape, lambda i, s: (0, 0, 0)) for piece in pieces]
+            + [block_spec] * len(totals)
+            + [ANY] * len(after),
+            out_specs=block_spec,
             scratch_shapes=[
-                pltpu.VMEM((2, length, items, lanes), F32),
-                pltpu.VMEM((2, items * rows, 2 * length), BF16),
+                pltpu.VMEM((depth, items, lanes), F32),
+                pltpu.VMEM((table.shape[0], items * rows, table.shape[1]), BF16),
             ],
         ),
         compiler_params=pltpu.CompilerParams(vmem_limit_bytes=VMEM_LIMIT),
         cost_estimate=pl.CostEstimate(
-            flops=2 * 12 * items * blocks * rows * length * length,
+            flops=2 * 6 * items * blocks * rows * depth * length,
             bytes_accessed=16 * items * blocks * rows * length,
             transcendentals=2 * items * blocks * rows * length,
         ),
         name="despread",
-    )(source, jnp.asarray(table), *pieces)
+    )(source, jnp.asarray(table), *pieces, *totals, *after)
 
 
 def on_device(channel, received, step_sizes, hop_offset, user_order):
@@ -348,8 +370,8 @@
     swap = [(p, p ^ 1) for p in range(blocks)]
     onward = [(p, (p + 2) % blocks) for p in range(blocks)]
 
-    size = 2 if half % 2 == 0 else 1
-    sizes = [size] * (half // size)
+    sizes = [1] + [2] * ((half - 2) // 2) + [1]
+    sizes += [1] * (half - sum(sizes))
     starts = [sum(sizes[:c]) for c in range(len(sizes))]
     chunks = len(sizes)
 
@@ -358,53 +380,85 @@
         scalars += [(2 * (pair - r) - offset) % blocks, (2 * (pair - r) + 1 - offset) % blocks]
     scalars.append((offset + 0) % 2)
     scalars = jnp.stack(scalars).astype(jnp.int32)
-    peer_rates = lax.ppermute(step_sizes, "blk", swap)
+    order = (user_order[:, None] == jnp.arange(users, dtype=jnp.int32)[None, :]).astype(BF16)
+
+    begins = (jnp.arange(blocks, dtype=jnp.int32)[:, None] + hop_offset[None, :]) % blocks
+    source = jnp.where(begins % 2 == 0, begins // 2 + pairs - 1, begins // 2) % pairs
+
+    own, peer, odd, pieces = {}, {}, {}, []
+
+    def ready_peer(c, after):
+        start = ((1 - side) * half + starts[c]).astype(jnp.int32).reshape(1)
+        carry = 8 if c == 0 else 0
+        sent = prepare(channel, received, step_sizes, start, sizes[c], carry, after)
+        peer[c] = lax.ppermute(sent, "blk", swap)
+        return sent
+
+    def ready_own(c, after):
+        start = (side * half + starts[c]).astype(jnp.int32).reshape(1)
+        own[c] = prepare(channel, received, step_sizes, start, sizes[c], 0, after)
+        return own[c]
+
+    def complete(c, after):
+        even, moved = odd[c]
+        done = finish(
+            pairs, blocks, owners, scalars, rates, own[c], peer[c], even, moved, order, after
+        )
+        pieces.append(
+            lax.all_to_all(done, ("blk", "tones"), split_axis=0, concat_axis=0, tiled=True)
+        )
+        return done
+
+    def bring_together(begin, end, total, last, after):
+        return despread(
+            pieces[begin:end],
+            starts[begin:end],
+            groups,
+            half,
+            blocks,
+            rows,
+            source.reshape(-1),
+            total,
+            last,
+            after,
+        )
+
+    before = ready_peer(0, [])
+    if chunks > 1:
+        before = ready_peer(1, [before])
+    before = ready_own(0, [before])
+    peer_rates = peer[0][0, users + 2 * received.shape[2], :2].reshape(1, 2)
     rates = jnp.where(
         side == 0,
         jnp.concatenate([step_sizes, peer_rates], 0),
         jnp.concatenate([peer_rates, step_sizes], 0),
     )
-    order = (user_order[:, None] == jnp.arange(users, dtype=jnp.int32)[None, :]).astype(BF16)
-
-    begins = (jnp.arange(blocks, dtype=jnp.int32)[:, None] + hop_offset[None, :]) % blocks
-    source = jnp.where(begins % 2 == 0, begins // 2 + pairs - 1, begins // 2) % pairs
-
-    own, peer, came, pieces = {}, {}, {}, []
-
-    def ready_peer(c, after):
-        start = ((1 - side) * half + starts[c]).astype(jnp.int32).reshape(1)
-        sent = prepare(channel, received, start, sizes[c], after)
-        peer[c] = lax.ppermute(sent, "blk", swap)
-        return sent
-
-    def ready_own(c, after):
-        start = (side * half + starts[c]).astype(jnp.int32).reshape(1)
-        own[c] = prepare(channel, received, start, sizes[c], after)
-        return own[c]
-
-    last = ready_peer(0, [])
-    if chunks > 1:
-        last = ready_peer(1, [last])
-    last = ready_own(0, [last])
+    early = max(chunks - 4, 0)
+    total = None
     for c in range(chunks):
-        last = chain(0, False, blocks, scalars, rates, own[c], peer[c], [], [last])
-        both = lax.ppermute(last, "blk", onward)
+        before = chain(0, False, blocks, scalars, rates, own[c], peer[c], [], [before])
+        both = lax.ppermute(before, "blk", onward)
         if c + 2 < chunks:
-            last = ready_peer(c + 2, [last])
+            before = ready_peer(c + 2, [before])
+        if c > 0:
+            before = complete(c - 1, [before])
         if c + 1 < chunks:
-            last = ready_own(c + 1, [last])
+            before = ready_own(c + 1, [before])
         for r in range(1, pairs):
-            done = chain(r, r == pairs - 1, blocks, scalars, rates, own[c], peer[c], [both], [last])
+            done = chain(r, r == pairs - 1, blocks, scalars, rates, own[c], peer[c], [both], [before])
             if r < pairs - 1:
                 both = lax.ppermute(done, "blk", onward)
-                last = done
-        even, odd = done
-        odd = lax.ppermute(odd, "blk", onward)
-        last = finish(pairs, blocks, owners, scalars, rates, own[c], peer[c], even, odd, order, [])
-        pieces.append(
-            lax.all_to_all(last, ("blk", "tones"), split_axis=0, concat_axis=0, tiled=True)
-        )
-    return despread(pieces, sizes, groups, half, blocks, rows, source.reshape(-1))
+                before = done
+        even, moving = done
+        odd[c] = (even, lax.ppermute(moving, "blk", onward))
+        before = even
+        if early and c == early + 1:
+            total = bring_together(0, early, None, False, [before])
+            before = total
+    before = complete(chunks - 1, [before])
+    if early < chunks - 1:
+        total = bring_together(early, chunks - 1, total, False, [before])
+    return bring_together(chunks - 1, chunks, total, True, [])
 
 
 def solution(mesh):

time: 694 us -> 677 us (0.976)
  waiting for transfers between devices: 321 us -> 244 us
  Pallas kernels: 265 us -> 312 us
  starting transfers between devices: 77.3 us -> 86 us
    ppermute x17 -> x18, waiting for transfers between devices: 297 us -> 184 us  [the longest x9 152 us: on_device(): both = lax.ppermute(before, 'blk', onward)]
    pallas_call x17 -> x21, Pallas kernels: 102 us -> 139 us  [the longest x18 86 us: prepare(): pl.pallas_call(functools.partial(prepare_body, carry), out_shape=jax.Shap...]
    ppermute x8 -> x9, waiting for transfers between devices: 0.02 us -> 32.3 us  [ready_peer(): peer[c] = lax.ppermute(sent, 'blk', swap)]
    all_to_all x8 -> x9, starting transfers between devices: 40.6 us -> 49.8 us  [complete(): lax.all_to_all(done, ('blk', 'tones'), split_axis=0, concat_axis=0, tiled...]
    pallas_call x16 -> x18, Pallas kernels: 114 us -> 120 us  [chain(): pl.pallas_call(functools.partial(chain_body, round_index, {'blocks': bloc...]
    all_to_all x8 -> x9, waiting for transfers between devices: 24.1 us -> 27.9 us  [complete(): lax.all_to_all(done, ('blk', 'tones'), split_axis=0, concat_axis=0, tiled...]
    pallas_call x8 -> x9, Pallas kernels: 49.4 us -> 52.5 us  [finish(): pl.pallas_call(functools.partial(finish_body, round_index, count, rows, s...]
    ppermute x17 -> x18, starting transfers between devices: 24.9 us -> 22 us  [the longest x9 16.6 us: on_device(): both = lax.ppermute(before, 'blk', onward)]
  transfers between devices with their start and end apart: 33 -> 36, of which waited for: 18 -> 18; matrix products, arithmetic and copies ran while one was open for 0% -> 1% of each run, Pallas kernels for 35% -> 45%
where the time goes in v2:
time: 677 us; the launch traced here: 668 us
  Pallas kernels  312 us (46%)
  waiting for transfers between devices  244 us (36%)
  starting transfers between devices  86 us (13%)
  local copies, waits for them, and re-layouts  16.6 us (2%)
  between operations  6.9 us (1%)
    ppermute x9, waiting for transfers between devices, on_device(): both = lax.ppermute(before, 'blk', onward)  152 us
    pallas_call x18, Pallas kernels, chain(): pl.pallas_call(functools.partial(chain_body, round_index, {'blocks': bloc...  120 us
    pallas_call x18, Pallas kernels, prepare(): pl.pallas_call(functools.partial(prepare_body, carry), out_shape=jax.Shap...  86 us
    pallas_call x3, Pallas kernels, despread(): pl.pallas_call(functools.partial(despread_body, groups, sizes, rows, fold...  53 us
    pallas_call x9, Pallas kernels, finish(): pl.pallas_call(functools.partial(finish_body, round_index, count, rows, s...  52.5 us
    all_to_all x9, starting transfers between devices, complete(): lax.all_to_all(done, ('blk', 'tones'), split_axis=0, concat_axis=0, tiled...  49.8 us
    ppermute x9, waiting for transfers between devices, ready_peer(): peer[c] = lax.ppermute(sent, 'blk', swap)  32.3 us
    ppermute x9, waiting for transfers between devices, on_device(): odd[c] = (even, lax.ppermute(moving, 'blk', onward))  32.3 us
  transfers between devices with their start and end apart: 36, of which 18 were waited for; matrix products, arithmetic and copies ran while one was open for 1% of the time, Pallas kernels for 45%

profile of v2, /device:TPU:0, one launch (start us, length us, event | category | flops | bytes accessed | tf_op | source)
XLA Modules:
  0.0 667.6 jit_solution(10138285529201768143)
XLA Ops:
  22.9 10.9 %collective-permute-done.peer = f32[1,1160,256]{2,1,0:T(8,128)S(1)} collective-permute-done((f32[1,1160,256]{2,1,0:T(8,128)}, f32[1,1160,256]{2,1,0:T(8,128)S(1)}, u32[]{:S(2)}, u32[]{:S(2)}) %collective-permute-start) | collective-permute-done | bytes 1187872 | tf_op jit(solution)/shard_map/ppermute | solution.py:394
  63.0 21.4 %collective-permute-done.3.peer = f32[2,1152,256]{2,1,0:T(8,128)S(1)} collective-permute-done((f32[2,1152,256]{2,1,0:T(8,128)}, f32[2,1152,256]{2,1,0:T(8,128)S(1)}, u32[]{:S(2)}, u32[]{:S(2)}) %collective-permute-start.3) | collective-permute-done | bytes 2359328 | tf_op jit(solution)/shard_map/ppermute | solution.py:394
  102.3 15.9 %collective-permute-done.2.odd = f32[1,2,112,256]{3,2,1,0:T(8,128)S(1)} collective-permute-done((f32[1,2,112,256]{3,2,1,0:T(8,128)S(1)}, f32[1,2,112,256]{3,2,1,0:T(8,128)S(1)}, u32[]{:S(2)}, u32[]{:S(2)}) %collective-permute-start.2) | collective-permute-done | bytes 229408 | tf_op jit(solution)/shard_map/ppermute | solution.py:453
  135.4 7.8 %chain1.10 = (f32[2,2,112,256]{3,2,1,0:T(8,128)}, f32[2,2,112,256]{3,2,1,0:T(8,128)}) custom-call(s32[8]{0:T(128)} %stack.35.scalars, f32[2,2]{1,0:T(2,128)} %maximum_select_fusion.rates, f32[2,1152,256]{2,1,0:T(8,128)} %prepare.22.refs_1_.own, f32[2,1152,256]{2,1,0:T(8,128)} %copy-done.8, f32[2,2,2,112,256]{4,3,2,1,0:T(8,128)} %copy-done.28, ...), custom_call_target="tpu_custom_call" | custom-call | flops 2818572288 | bytes 6553600 | tf_op jit(solution)/shard_map/chain1/pallas_call | solution.py:167
  163.7 27.9 %all-to-all-done.refs_0_ = f32[32,8,448]{2,1,0:T(8,128)S(1)} async-done(((f32[32,8,448]{2,1,0:T(8,128)}), f32[32,8,448]{2,1,0:T(8,128)S(1)}, u32[]{:S(2)}, u32[]{:S(2)}) %all-to-all-start) | async-done | bytes 458784 | tf_op jit(solution)/shard_map/all_to_all | solution.py:408
  205.9 24.1 %collective-permute-done.6.refs_0_ = f32[2,2,2,112,256]{4,3,2,1,0:T(8,128)} collective-permute-done((f32[2,2,2,112,256]{4,3,2,1,0:T(8,128)}, f32[2,2,2,112,256]{4,3,2,1,0:T(8,128)}, u32[]{:S(2)}, u32[]{:S(2)}) %collective-permute-start.6) | collective-permute-done | bytes 917536 | tf_op jit(solution)/shard_map/ppermute | solution.py:440
  230.0 7.8 %chain1.11 = (f32[2,2,112,256]{3,2,1,0:T(8,128)}, f32[2,2,112,256]{3,2,1,0:T(8,128)}) custom-call(s32[8]{0:T(128)} %stack.35.scalars, f32[2,2]{1,0:T(2,128)} %maximum_select_fusion.rates, f32[2,1152,256]{2,1,0:T(8,128)} %prepare.24.refs_1_.own, f32[2,1152,256]{2,1,0:T(8,128)} %collective-permute-done.4.peer, ...), custom_call_target="tpu_custom_call" | custom-call | flops 2818572288 | bytes 6553600 | tf_op jit(solution)/shard_map/chain1/pallas_call | solution.py:167
  271.1 24.1 %collective-permute-done.11.refs_0_ = f32[2,2,2,112,256]{4,3,2,1,0:T(8,128)} collective-permute-done((f32[2,2,2,112,256]{4,3,2,1,0:T(8,128)}, f32[2,2,2,112,256]{4,3,2,1,0:T(8,128)}, u32[]{:S(2)}, u32[]{:S(2)}) %collective-permute-start.11) | collective-permute-done | bytes 917536 | tf_op jit(solution)/shard_map/ppermute | solution.py:440
  295.2 7.8 %chain1.12 = (f32[2,2,112,256]{3,2,1,0:T(8,128)}, f32[2,2,112,256]{3,2,1,0:T(8,128)}) custom-call(s32[8]{0:T(128)} %stack.35.scalars, f32[2,2]{1,0:T(2,128)} %maximum_select_fusion.rates, f32[2,1152,256]{2,1,0:T(8,128)} %prepare.26.refs_1_.own, f32[2,1152,256]{2,1,0:T(8,128)} %collective-permute-done.9.peer, ...), custom_call_target="tpu_custom_call" | custom-call | flops 2818572288 | bytes 6553600 | tf_op jit(solution)/shard_map/chain1/pallas_call | solution.py:167
  336.3 24.0 %collective-permute-done.12.refs_0_ = f32[2,2,2,112,256]{4,3,2,1,0:T(8,128)S(1)} collective-permute-done((f32[2,2,2,112,256]{4,3,2,1,0:T(8,128)S(1)}, f32[2,2,2,112,256]{4,3,2,1,0:T(8,128)S(1)}, u32[]{:S(2)}, u32[]{:S(2)}) %collective-permute-start.12) | collective-permute-done | bytes 917536 | tf_op jit(solution)/shard_map/ppermute | solution.py:440
  361.3 7.8 %chain1.13 = (f32[2,2,112,256]{3,2,1,0:T(8,128)}, f32[2,2,112,256]{3,2,1,0:T(8,128)}) custom-call(s32[8]{0:T(128)} %stack.35.scalars, f32[2,2]{1,0:T(2,128)} %maximum_select_fusion.rates, f32[2,1152,256]{2,1,0:T(8,128)} %prepare.28.refs_1_.own, f32[2,1152,256]{2,1,0:T(8,128)} %collective-permute-done.10.peer, f32[2,2,2,112,256]{4,3,2,1,0:T(8,128)} %copy-done.29, ...), custom_call_target="tpu_custom_call" | custom-call | flops 2818572288 | bytes 6553600 | tf_op jit(solution)/shard_map/chain1/pallas_call | solution.py:167
  402.3 24.0 %collective-permute-done.17.refs_0_ = f32[2,2,2,112,256]{4,3,2,1,0:T(8,128)} collective-permute-done((f32[2,2,2,112,256]{4,3,2,1,0:T(8,128)}, f32[2,2,2,112,256]{4,3,2,1,0:T(8,128)}, u32[]{:S(2)}, u32[]{:S(2)}) %collective-permute-start.17) | collective-permute-done | bytes 917536 | tf_op jit(solution)/shard_map/ppermute | solution.py:440
  426.3 7.8 %chain1.14 = (f32[2,2,112,256]{3,2,1,0:T(8,128)}, f32[2,2,112,256]{3,2,1,0:T(8,128)}) custom-call(s32[8]{0:T(128)} %stack.35.scalars, f32[2,2]{1,0:T(2,128)} %maximum_select_fusion.rates, f32[2,1152,256]{2,1,0:T(8,128)} %prepare.30.refs_1_.own, f32[2,1152,256]{2,1,0:T(8,128)} %collective-permute-done.15.peer, ...), custom_call_target="tpu_custom_call" | custom-call | flops 2818572288 | bytes 6553600 | tf_op jit(solution)/shard_map/chain1/pallas_call | solution.py:167
  465.0 7.0 %collective-permute-done.18.refs_0_ = f32[2,2,2,112,256]{4,3,2,1,0:T(8,128)} collective-permute-done((f32[2,2,2,112,256]{4,3,2,1,0:T(8,128)}, f32[2,2,2,112,256]{4,3,2,1,0:T(8,128)}, u32[]{:S(2)}, u32[]{:S(2)}) %collective-permute-start.18) | collective-permute-done | bytes 917536 | tf_op jit(solution)/shard_map/ppermute | solution.py:440
  472.1 7.8 %chain1.15 = (f32[2,2,112,256]{3,2,1,0:T(8,128)}, f32[2,2,112,256]{3,2,1,0:T(8,128)}) custom-call(s32[8]{0:T(128)} %stack.35.scalars, f32[2,2]{1,0:T(2,128)} %maximum_select_fusion.rates, f32[2,1152,256]{2,1,0:T(8,128)} %prepare.32.refs_1_.own, f32[2,1152,256]{2,1,0:T(8,128)} %collective-permute-done.16.peer, ...), custom_call_target="tpu_custom_call" | custom-call | flops 2818572288 | bytes 6553600 | tf_op jit(solution)/shard_map/chain1/pallas_call | solution.py:167
  480.6 24.2 %despread.3.refs_0_.refs_3_ = f32[8,2,448,256]{3,2,1,0:T(8,128)} custom-call(s32[32]{0:T(128)} %and_select_fusion.source, bf16[2,288,512]{2,1,0:T(8,128)(2,1)} %constant.128.clone.table, f32[32,8,448]{2,1,0:T(8,128)} %copy-done.9, f32[32,8,896]{2,1,0:T(8,128)} %copy-done.3, f32[32,8,896]{2,1,0:T(8,128)} %all-to-all-done.2.refs_2_, f32[32,8,896]{2,1,0:T(8,128)} %copy-done.4, ...), custom_call_target="tpu_custom_call" | custom-call | flops 3170893824 | bytes 14680064 | tf_op jit(solution)/shard_map/despread/pallas_call | solution.py:331
  519.9 6.8 %all-to-all-start.7 = ((f32[32,8,896]{2,1,0:T(8,128)}), f32[32,8,896]{2,1,0:T(8,128)}, u32[]{:S(2)}, u32[]{:S(2)}) async-start(f32[32,8,896]{2,1,0:T(8,128)} %finish.15.refs_0_), calls=%async_computation.7 | async-start | bytes 1835008 | tf_op jit(solution)/shard_map/all_to_all | solution.py:408
  533.7 25.4 %collective-permute-done.23.refs_0_ = f32[2,2,2,112,256]{4,3,2,1,0:T(8,128)} collective-permute-done((f32[2,2,2,112,256]{4,3,2,1,0:T(8,128)S(1)}, f32[2,2,2,112,256]{4,3,2,1,0:T(8,128)}, u32[]{:S(2)}, u32[]{:S(2)}) %collective-permute-start.23) | collective-permute-done | bytes 917536 | tf_op jit(solution)/shard_map/ppermute | solution.py:440
  559.0 7.8 %chain1.16 = (f32[2,2,112,256]{3,2,1,0:T(8,128)}, f32[2,2,112,256]{3,2,1,0:T(8,128)}) custom-call(s32[8]{0:T(128)} %stack.35.scalars, f32[2,2]{1,0:T(2,128)} %maximum_select_fusion.rates, f32[2,1152,256]{2,1,0:T(8,128)} %prepare.34.refs_1_.own, f32[2,1152,256]{2,1,0:T(8,128)} %copy-done, f32[2,2,2,112,256]{4,3,2,1,0:T(8,128)} %collective-permute-done.23.refs_0_, ...), custom_call_target="tpu_custom_call" | custom-call | flops 2818572288 | bytes 6553600 | tf_op jit(solution)/shard_map/chain1/pallas_call | solution.py:167
  572.2 7.0 %collective-permute-done.25.odd = f32[2,2,112,256]{3,2,1,0:T(8,128)S(1)} collective-permute-done((f32[2,2,112,256]{3,2,1,0:T(8,128)}, f32[2,2,112,256]{3,2,1,0:T(8,128)S(1)}, u32[]{:S(2)}, u32[]{:S(2)}) %collective-permute-start.25) | collective-permute-done | bytes 458784 | tf_op jit(solution)/shard_map/ppermute | solution.py:453
  592.8 19.8 %collective-permute-done.24.refs_0_ = f32[1,2,2,112,256]{4,3,2,1,0:T(8,128)S(1)} collective-permute-done((f32[1,2,2,112,256]{4,3,2,1,0:T(8,128)S(1)}, f32[1,2,2,112,256]{4,3,2,1,0:T(8,128)S(1)}, u32[]{:S(2)}, u32[]{:S(2)}) %collective-permute-start.24) | collective-permute-done | bytes 458784 | tf_op jit(solution)/shard_map/ppermute | solution.py:440
  619.3 6.6 collective-permute-done.26.odd
  637.5 19.1 %despread.4.refs_1_ = f32[8,2,448,256]{3,2,1,0:T(8,128)} custom-call(s32[32]{0:T(128)} %and_select_fusion.source, bf16[2,192,512]{2,1,0:T(8,128)(2,1)} %constant.129.clone.table, f32[32,8,896]{2,1,0:T(8,128)} %copy-done.6, f32[32,8,896]{2,1,0:T(8,128)} %all-to-all-done.7.refs_1_, f32[32,8,896]{2,1,0:T(8,128)} %copy-done.7, ...), custom_call_target="tpu_custom_call" | custom-call | flops 2113929216 | bytes 14680064 | tf_op jit(solution)/shard_map/despread/pallas_call | solution.py:331
  657.4 9.7 %despread.5 = f32[8,2,448,256]{3,2,1,0:T(8,128)} custom-call(s32[32]{0:T(128)} %and_select_fusion.source, bf16[1,96,512]{2,1,0:T(8,128)(2,1)} %constant.130.clone.table, f32[32,8,448]{2,1,0:T(8,128)} %copy-done.10, f32[8,2,448,256]{3,2,1,0:T(8,128)} %despread.4.refs_1_), custom_call_target="tpu_custom_call" | custom-call | flops 352321536 | bytes 14680064 | tf_op jit(solution)/shard_map/despread/pallas_call | solution.py:331
  (170 shorter events, 307.9 us)
Async XLA Ops:
  11.7 72.7 %collective-permute-start.3 = (f32[2,1152,256]{2,1,0:T(8,128)}, f32[2,1152,256]{2,1,0:T(8,128)S(1)}, u32[]{:S(2)}, u32[]{:S(2)}) collective-permute-start(f32[2,1152,256]{2,1,0:T(8,128)} %prepare.19.refs_0_), channel_id=1, source_target_pairs={{0,8},{8,0},{16,24},{24,16},{1,9},{9,1},{17,25},{25,17},{2,10},{10... | collective-permute-start | bytes 7077896 | tf_op jit(solution)/shard_map/ppermute | solution.py:394
  44.7 100.4 %collective-permute-start.4 = (f32[2,1152,256]{2,1,0:T(8,128)}, f32[2,1152,256]{2,1,0:T(8,128)}, u32[]{:S(2)}, u32[]{:S(2)}) collective-permute-start(f32[2,1152,256]{2,1,0:T(8,128)} %prepare.21.refs_0_), channel_id=1, source_target_pairs={{0,8},{8,0},{16,24},{24,16},{1,9},{9,1},{17,25},{25,17},{2,10},{10... | collective-permute-start | bytes 7077896 | tf_op jit(solution)/shard_map/ppermute | solution.py:394
  92.3 42.1 %collective-permute-start.5 = (f32[2,2,2,112,256]{4,3,2,1,0:T(8,128)}, f32[2,2,2,112,256]{4,3,2,1,0:T(8,128)S(1)}, u32[]{:S(2)}, u32[]{:S(2)}) collective-permute-start(f32[2,2,2,112,256]{4,3,2,1,0:T(8,128)} %chain0.10.refs_0_), channel_id=1, source_target_pairs={{0,16},{8,24},{16,0},{24,8},{1,17},{9,25},{17,1},{25,9},{2,18},{10... | collective-permute-start | bytes 2752520 | tf_op jit(solution)/shard_map/ppermute | solution.py:440
  99.7 138.7 %collective-permute-start.9 = (f32[2,1152,256]{2,1,0:T(8,128)}, f32[2,1152,256]{2,1,0:T(8,128)}, u32[]{:S(2)}, u32[]{:S(2)}) collective-permute-start(f32[2,1152,256]{2,1,0:T(8,128)} %prepare.23.refs_0_), channel_id=1, source_target_pairs={{0,8},{8,0},{16,24},{24,16},{1,9},{9,1},{17,25},{25,17},{2,10},{10... | collective-permute-start | bytes 7077896 | tf_op jit(solution)/shard_map/ppermute | solution.py:394
  123.4 68.1 %all-to-all-start = ((f32[32,8,448]{2,1,0:T(8,128)}), f32[32,8,448]{2,1,0:T(8,128)S(1)}, u32[]{:S(2)}, u32[]{:S(2)}) async-start(f32[32,8,448]{2,1,0:T(8,128)} %finish.9.refs_0_), calls=%async_computation | async-start | bytes 1048576 | tf_op jit(solution)/shard_map/all_to_all | solution.py:408
  192.3 64.9 %all-to-all-start.1 = ((f32[32,8,896]{2,1,0:T(8,128)}), f32[32,8,896]{2,1,0:T(8,128)S(1)}, u32[]{:S(2)}, u32[]{:S(2)}) async-start(f32[32,8,896]{2,1,0:T(8,128)} %finish.10.refs_0_), calls=%async_computation.1 | async-start | bytes 1835008 | tf_op jit(solution)/shard_map/all_to_all | solution.py:408
  197.4 32.6 %collective-permute-start.6 = (f32[2,2,2,112,256]{4,3,2,1,0:T(8,128)}, f32[2,2,2,112,256]{4,3,2,1,0:T(8,128)}, u32[]{:S(2)}, u32[]{:S(2)}) collective-permute-start(f32[2,2,2,112,256]{4,3,2,1,0:T(8,128)} %chain0.11.refs_0_), channel_id=1, source_target_pairs={{0,16},{8,24},{16,0},{24,8},{1,17},{9,25},{17,1},{25,9},{2,18},{10... | collective-permute-start | bytes 2752520 | tf_op jit(solution)/shard_map/ppermute | solution.py:440
  199.4 104.1 %collective-permute-start.10 = (f32[2,1152,256]{2,1,0:T(8,128)S(1)}, f32[2,1152,256]{2,1,0:T(8,128)}, u32[]{:S(2)}, u32[]{:S(2)}) collective-permute-start(f32[2,1152,256]{2,1,0:T(8,128)S(1)} %copy-done.1), channel_id=1, source_target_pairs={{0,8},{8,0},{16,24},{24,16},{1,9},{9,1},{17,25},{25,17},{2,10},{10... | collective-permute-start | bytes 7077896 | tf_op jit(solution)/shard_map/ppermute | solution.py:394
  257.2 65.2 %all-to-all-start.2 = ((f32[32,8,896]{2,1,0:T(8,128)}), f32[32,8,896]{2,1,0:T(8,128)}, u32[]{:S(2)}, u32[]{:S(2)}) async-start(f32[32,8,896]{2,1,0:T(8,128)} %finish.11.refs_0_), calls=%async_computation.2 | async-start | bytes 1835008 | tf_op jit(solution)/shard_map/all_to_all | solution.py:408
  262.7 32.5 %collective-permute-start.11 = (f32[2,2,2,112,256]{4,3,2,1,0:T(8,128)}, f32[2,2,2,112,256]{4,3,2,1,0:T(8,128)}, u32[]{:S(2)}, u32[]{:S(2)}) collective-permute-start(f32[2,2,2,112,256]{4,3,2,1,0:T(8,128)} %chain0.12.refs_0_), channel_id=1, source_target_pairs={{0,16},{8,24},{16,0},{24,8},{1,17},{9,25},{17,1},{25,9},{2,18},{10... | collective-permute-start | bytes 2752520 | tf_op jit(solution)/shard_map/ppermute | solution.py:440
  264.6 104.9 %collective-permute-start.15 = (f32[2,1152,256]{2,1,0:T(8,128)}, f32[2,1152,256]{2,1,0:T(8,128)}, u32[]{:S(2)}, u32[]{:S(2)}) collective-permute-start(f32[2,1152,256]{2,1,0:T(8,128)} %prepare.27.refs_0_), channel_id=1, source_target_pairs={{0,8},{8,0},{16,24},{24,16},{1,9},{9,1},{17,25},{25,17},{2,10},{10... | collective-permute-start | bytes 7077896 | tf_op jit(solution)/shard_map/ppermute | solution.py:394
  322.4 66.1 %all-to-all-start.3 = ((f32[32,8,896]{2,1,0:T(8,128)}), f32[32,8,896]{2,1,0:T(8,128)S(1)}, u32[]{:S(2)}, u32[]{:S(2)}) async-start(f32[32,8,896]{2,1,0:T(8,128)} %finish.12.refs_0_), calls=%async_computation.3 | async-start | bytes 1835008 | tf_op jit(solution)/shard_map/all_to_all | solution.py:408
  327.9 32.5 %collective-permute-start.12 = (f32[2,2,2,112,256]{4,3,2,1,0:T(8,128)S(1)}, f32[2,2,2,112,256]{4,3,2,1,0:T(8,128)S(1)}, u32[]{:S(2)}, u32[]{:S(2)}) collective-permute-start(f32[2,2,2,112,256]{4,3,2,1,0:T(8,128)S(1)} %copy-done.12), channel_id=1, source_target_pairs={{0,16},{8,24},{16,0},{24,8},{1,17},{9,25},{17,1},{25,9},{2,18},{10... | collective-permute-start | bytes 2752520 | tf_op jit(solution)/shard_map/ppermute | solution.py:440
  329.8 104.8 %collective-permute-start.16 = (f32[2,1152,256]{2,1,0:T(8,128)}, f32[2,1152,256]{2,1,0:T(8,128)}, u32[]{:S(2)}, u32[]{:S(2)}) collective-permute-start(f32[2,1152,256]{2,1,0:T(8,128)} %prepare.29.refs_0_), channel_id=1, source_target_pairs={{0,8},{8,0},{16,24},{24,16},{1,9},{9,1},{17,25},{25,17},{2,10},{10... | collective-permute-start | bytes 7077896 | tf_op jit(solution)/shard_map/ppermute | solution.py:394
  388.5 66.2 %all-to-all-start.4 = ((f32[32,8,896]{2,1,0:T(8,128)}), f32[32,8,896]{2,1,0:T(8,128)}, u32[]{:S(2)}, u32[]{:S(2)}) async-start(f32[32,8,896]{2,1,0:T(8,128)} %finish.13.refs_0_), calls=%async_computation.4 | async-start | bytes 1835008 | tf_op jit(solution)/shard_map/all_to_all | solution.py:408
  393.8 32.5 %collective-permute-start.17 = (f32[2,2,2,112,256]{4,3,2,1,0:T(8,128)}, f32[2,2,2,112,256]{4,3,2,1,0:T(8,128)}, u32[]{:S(2)}, u32[]{:S(2)}) collective-permute-start(f32[2,2,2,112,256]{4,3,2,1,0:T(8,128)} %chain0.14.refs_0_), channel_id=1, source_target_pairs={{0,16},{8,24},{16,0},{24,8},{1,17},{9,25},{17,1},{25,9},{2,18},{10... | collective-permute-start | bytes 2752520 | tf_op jit(solution)/shard_map/ppermute | solution.py:440
  395.7 109.0 %collective-permute-start.21 = (f32[2,1152,256]{2,1,0:T(8,128)}, f32[2,1152,256]{2,1,0:T(8,128)S(1)}, u32[]{:S(2)}, u32[]{:S(2)}) collective-permute-start(f32[2,1152,256]{2,1,0:T(8,128)} %prepare.31.refs_0_), channel_id=1, source_target_pairs={{0,8},{8,0},{16,24},{24,16},{1,9},{9,1},{17,25},{25,17},{2,10},{10... | collective-permute-start | bytes 7077896 | tf_op jit(solution)/shard_map/ppermute | solution.py:394
  441.0 31.0 %collective-permute-start.18 = (f32[2,2,2,112,256]{4,3,2,1,0:T(8,128)}, f32[2,2,2,112,256]{4,3,2,1,0:T(8,128)}, u32[]{:S(2)}, u32[]{:S(2)}) collective-permute-start(f32[2,2,2,112,256]{4,3,2,1,0:T(8,128)} %chain0.15.refs_0_), channel_id=1, source_target_pairs={{0,16},{8,24},{16,0},{24,8},{1,17},{9,25},{17,1},{25,9},{2,18},{10... | collective-permute-start | bytes 2752520 | tf_op jit(solution)/shard_map/ppermute | solution.py:440
  454.7 65.1 %all-to-all-start.6 = ((f32[32,8,896]{2,1,0:T(8,128)}), f32[32,8,896]{2,1,0:T(8,128)S(1)}, u32[]{:S(2)}, u32[]{:S(2)}) async-start(f32[32,8,896]{2,1,0:T(8,128)} %finish.14.refs_0_), calls=%async_computation.6 | async-start | bytes 1835008 | tf_op jit(solution)/shard_map/all_to_all | solution.py:408
  479.9 32.7 %collective-permute-start.20 = (f32[2,2,112,256]{3,2,1,0:T(8,128)}, f32[2,2,112,256]{3,2,1,0:T(8,128)S(1)}, u32[]{:S(2)}, u32[]{:S(2)}) collective-permute-start(f32[2,2,112,256]{3,2,1,0:T(8,128)} %get-tuple-element.36), channel_id=1, source_target_pairs={{0,16},{8,24},{16,0},{24,8},{1,17},{9,25},{17,1},{25,9},{2,18},{10... | collective-permute-start | bytes 1376264 | tf_op jit(solution)/shard_map/ppermute | solution.py:453
  519.9 66.2 %all-to-all-start.7 = ((f32[32,8,896]{2,1,0:T(8,128)}), f32[32,8,896]{2,1,0:T(8,128)}, u32[]{:S(2)}, u32[]{:S(2)}) async-start(f32[32,8,896]{2,1,0:T(8,128)} %finish.15.refs_0_), calls=%async_computation.7 | async-start | bytes 1835008 | tf_op jit(solution)/shard_map/all_to_all | solution.py:408
  526.7 32.4 %collective-permute-start.23 = (f32[2,2,2,112,256]{4,3,2,1,0:T(8,128)S(1)}, f32[2,2,2,112,256]{4,3,2,1,0:T(8,128)}, u32[]{:S(2)}, u32[]{:S(2)}) collective-permute-start(f32[2,2,2,112,256]{4,3,2,1,0:T(8,128)S(1)} %copy-done.5), channel_id=1, source_target_pairs={{0,16},{8,24},{16,0},{24,8},{1,17},{9,25},{17,1},{25,9},{2,18},{10... | collective-permute-start | bytes 2752520 | tf_op jit(solution)/shard_map/ppermute | solution.py:440
  528.5 38.9 %collective-permute-start.22 = (f32[1,1152,256]{2,1,0:T(8,128)S(1)}, f32[1,1152,256]{2,1,0:T(8,128)}, u32[]{:S(2)}, u32[]{:S(2)}) collective-permute-start(f32[1,1152,256]{2,1,0:T(8,128)S(1)} %copy-done.2), channel_id=1, source_target_pairs={{0,8},{8,0},{16,24},{24,16},{1,9},{9,1},{17,25},{25,17},{2,10},{10... | collective-permute-start | bytes 3538952 | tf_op jit(solution)/shard_map/ppermute | solution.py:394
  586.1 45.0 %all-to-all-start.8 = ((f32[32,8,896]{2,1,0:T(8,128)}), f32[32,8,896]{2,1,0:T(8,128)S(1)}, u32[]{:S(2)}, u32[]{:S(2)}) async-start(f32[32,8,896]{2,1,0:T(8,128)} %finish.16.refs_1_), calls=%async_computation.8 | async-start | bytes 1835008 | tf_op jit(solution)/shard_map/all_to_all | solution.py:408
  (45 other events, 418.1 us)

commit v3 on v2

--- a/solution.py
+++ b/solution.py
@@ -12,6 +12,7 @@
 F32 = jnp.float32
 BF16 = jnp.bfloat16
 VMEM_LIMIT = 56 * 1024 * 1024
+HEAVY = pl.CostEstimate(flops=10**13, bytes_accessed=10**10, transcendentals=0)
 ANY = pl.BlockSpec(memory_space=pl.ANY)
 SMEM = pl.BlockSpec(memory_space=pltpu.SMEM)
 
@@ -83,11 +84,7 @@
             out_specs=pl.BlockSpec((1, rows, users), lambda i, start: (i, 0, 0)),
         ),
         compiler_params=pltpu.CompilerParams(vmem_limit_bytes=VMEM_LIMIT),
-        cost_estimate=pl.CostEstimate(
-            flops=count * 2 * 12 * (users + symbols) * width * users,
-            bytes_accessed=4 * count * (2 * (users + symbols) * width + rows * users),
-            transcendentals=0,
-        ),
+        cost_estimate=HEAVY,
         name="prepare",
     )(start, step_sizes, channel, received, *after)
 
@@ -178,11 +175,7 @@
             ],
         ),
         compiler_params=pltpu.CompilerParams(vmem_limit_bytes=VMEM_LIMIT),
-        cost_estimate=pl.CostEstimate(
-            flops=count * 2 * 12 * 8 * rows * users * users,
-            bytes_accessed=4 * count * (2 * packed_rows + 8 * rows) * users,
-            transcendentals=count * 16 * rows * users,
-        ),
+        cost_estimate=HEAVY,
         name="chain%d" % round_index,
     )(scalars, rates, own, peer, *came, *after)
 
@@ -254,11 +247,7 @@
             ],
         ),
         compiler_params=pltpu.CompilerParams(vmem_limit_bytes=VMEM_LIMIT),
-        cost_estimate=pl.CostEstimate(
-            flops=count * 2 * 12 * 3 * rows * users * users,
-            bytes_accessed=4 * count * (2 * packed_rows + 8 * rows) * users,
-            transcendentals=count * 4 * rows * users,
-        ),
+        cost_estimate=HEAVY,
         name="finish",
     )(scalars, rates, own, peer, even, odd, order, *after)
 
@@ -289,15 +278,15 @@
 
         lax.fori_loop(0, groups, gather, 0)
         for item in range(items):
-            high, low = split(tones_first[:, item, :])
+            high, low = split(tones_first[:, item, :].T[:rows])
+            here = slice(item * rows, (item + 1) * rows)
             if folded:
-                high = high.astype(F32)
-                joined = jnp.concatenate([high, high, low.astype(F32)], 0)
-                parts = [joined.T[:rows].astype(BF16)]
+                depth = high.shape[1]
+                for k, value in enumerate((high, high, low)):
+                    symbols_first[0, here, k * depth : (k + 1) * depth] = value
             else:
-                parts = [high.astype(F32).T[:rows].astype(BF16), low.astype(F32).T[:rows].astype(BF16)]
-            for k, value in enumerate(parts):
-                symbols_first[k, item * rows : (item + 1) * rows, :] = value
+                symbols_first[0, here] = high
+                symbols_first[1, here] = low
         if folded:
             result = dot(symbols_first[0], table[0], (1, 0))
         else:
@@ -345,11 +334,7 @@
             ],
         ),
         compiler_params=pltpu.CompilerParams(vmem_limit_bytes=VMEM_LIMIT),
-        cost_estimate=pl.CostEstimate(
-            flops=2 * 6 * items * blocks * rows * depth * length,
-            bytes_accessed=16 * items * blocks * rows * length,
-            transcendentals=2 * items * blocks * rows * length,
-        ),
+        cost_estimate=HEAVY,
         name="despread",
     )(source, jnp.asarray(table), *pieces, *totals, *after)
 
@@ -436,7 +421,8 @@
     early = max(chunks - 4, 0)
     total = None
     for c in range(chunks):
-        before = chain(0, False, blocks, scalars, rates, own[c], peer[c], [], [before])
+        after = [before] + pieces[max(c - 2, 0) : c - 1]
+        before = chain(0, False, blocks, scalars, rates, own[c], peer[c], [], after)
         both = lax.ppermute(before, "blk", onward)
         if c + 2 < chunks:
             before = ready_peer(c + 2, [before])
@@ -455,7 +441,7 @@
         if early and c == early + 1:
             total = bring_together(0, early, None, False, [before])
             before = total
-    before = complete(chunks - 1, [before])
+    before = complete(chunks - 1, [before] + pieces[-1:])
     if early < chunks - 1:
         total = bring_together(early, chunks - 1, total, False, [before])
     return bring_together(chunks - 1, chunks, total, True, [])

time: 677 us -> 685 us (1.012)
  waiting for transfers between devices: 244 us -> 281 us
  local copies, waits for them, and re-layouts: 16.6 us -> 2.06 us
  Pallas kernels: 312 us -> 299 us
    all_to_all x9, waiting for transfers between devices: 27.9 us -> 225 us  [complete(): lax.all_to_all(done, ('blk', 'tones'), split_axis=0, concat_axis=0, tiled...]
    ppermute x9, waiting for transfers between devices: 152 us -> 10.8 us  [on_device(): both = lax.ppermute(before, 'blk', onward)]
    ppermute x9, waiting for transfers between devices: 32.3 us -> 10.1 us  [on_device(): odd[c] = (even, lax.ppermute(moving, 'blk', onward))]
    unnamed x66 -> x8, local copies, waits for them, and re-layouts: 15.2 us -> 0.02 us
    pallas_call x3, Pallas kernels: 53 us -> 41 us  [despread(): pl.pallas_call(functools.partial(despread_body, groups, sizes, rows, fold...]
    ppermute x9, starting transfers between devices: 16.6 us -> 8.83 us  [on_device(): both = lax.ppermute(before, 'blk', onward)]
    ppermute x9, starting transfers between devices: 5.4 us -> 13.2 us  [on_device(): odd[c] = (even, lax.ppermute(moving, 'blk', onward))]
  transfers between devices with their start and end apart: 36 -> 36, of which waited for: 18 -> 13; matrix products, arithmetic and copies ran while one was open for 1% -> 1% of each run, Pallas kernels for 45% -> 42%
where the time goes in v3:
time: 685 us; the launch traced here: 675 us
  Pallas kernels  299 us (44%)
  waiting for transfers between devices  281 us (41%)
  starting transfers between devices  84.5 us (12%)
  between operations  6.88 us (1%)
    all_to_all x9, waiting for transfers between devices, complete(): lax.all_to_all(done, ('blk', 'tones'), split_axis=0, concat_axis=0, tiled...  225 us
    pallas_call x18, Pallas kernels, chain(): pl.pallas_call(functools.partial(chain_body, round_index, {'blocks': bloc...  120 us
    pallas_call x18, Pallas kernels, prepare(): pl.pallas_call(functools.partial(prepare_body, carry), out_shape=jax.Shap...  85.8 us
    pallas_call x9, Pallas kernels, finish(): pl.pallas_call(functools.partial(finish_body, round_index, count, rows, s...  52 us
    all_to_all x9, starting transfers between devices, complete(): lax.all_to_all(done, ('blk', 'tones'), split_axis=0, concat_axis=0, tiled...  48.8 us
    pallas_call x3, Pallas kernels, despread(): pl.pallas_call(functools.partial(despread_body, groups, sizes, rows, fold...  41 us
    ppermute x9, waiting for transfers between devices, ready_peer(): peer[c] = lax.ppermute(sent, 'blk', swap)  34.5 us
    ppermute x9, starting transfers between devices, ready_peer(): peer[c] = lax.ppermute(sent, 'blk', swap)  13.7 us
  transfers between devices with their start and end apart: 36, of which 13 were waited for; matrix products, arithmetic and copies ran while one was open for 1% of the time, Pallas kernels for 42%

profile of v3, /device:TPU:0, one launch (start us, length us, event | category | flops | bytes accessed | tf_op | source)
XLA Modules:
  0.0 674.8 jit_solution(13277222236764334390)
XLA Ops:
  24.4 9.5 %collective-permute-done.peer = f32[1,1160,256]{2,1,0:T(8,128)} collective-permute-done((f32[1,1160,256]{2,1,0:T(8,128)}, f32[1,1160,256]{2,1,0:T(8,128)}, u32[]{:S(2)}, u32[]{:S(2)}) %collective-permute-start) | collective-permute-done | bytes 1187872 | tf_op jit(solution)/shard_map/ppermute | solution.py:379
  59.5 25.0 %collective-permute-done.3.peer = f32[2,1152,256]{2,1,0:T(8,128)} collective-permute-done((f32[2,1152,256]{2,1,0:T(8,128)}, f32[2,1152,256]{2,1,0:T(8,128)}, u32[]{:S(2)}, u32[]{:S(2)}) %collective-permute-start.3) | collective-permute-done | bytes 2359328 | tf_op jit(solution)/shard_map/ppermute | solution.py:379
  113.5 7.8 %chain1.10 = (f32[2,2,112,256]{3,2,1,0:T(8,128)}, f32[2,2,112,256]{3,2,1,0:T(8,128)}) custom-call(s32[8]{0:T(128)} %stack.35.scalars, f32[2,2]{1,0:T(2,128)} %maximum_select_fusion.rates, f32[2,1152,256]{2,1,0:T(8,128)} %prepare.22.refs_1_.own, f32[2,1152,256]{2,1,0:T(8,128)} %collective-permute-done.3.peer, ...), custom_call_target="tpu_custom_call" | custom-call | flops 9999999827968 | bytes 10000000000 | tf_op jit(solution)/shard_map/chain1/pallas_call | solution.py:164
  123.2 68.5 %all-to-all-done.refs_1_.refs_0_ = f32[32,8,448]{2,1,0:T(8,128)} async-done(((f32[32,8,448]{2,1,0:T(8,128)}), f32[32,8,448]{2,1,0:T(8,128)}, u32[]{:S(2)}, u32[]{:S(2)}) %all-to-all-start) | async-done | bytes 458784 | tf_op jit(solution)/shard_map/all_to_all | solution.py:393
  191.7 6.4 chain0.11.refs_0_
  221.6 7.8 %chain1.11 = (f32[2,2,112,256]{3,2,1,0:T(8,128)}, f32[2,2,112,256]{3,2,1,0:T(8,128)}) custom-call(s32[8]{0:T(128)} %stack.35.scalars, f32[2,2]{1,0:T(2,128)} %maximum_select_fusion.rates, f32[2,1152,256]{2,1,0:T(8,128)} %prepare.24.refs_1_.own, f32[2,1152,256]{2,1,0:T(8,128)} %collective-permute-done.4.peer, ...), custom_call_target="tpu_custom_call" | custom-call | flops 9999999827968 | bytes 10000000000 | tf_op jit(solution)/shard_map/chain1/pallas_call | solution.py:164
  231.3 35.8 %all-to-all-done.1.refs_1_ = f32[32,8,896]{2,1,0:T(8,128)} async-done(((f32[32,8,896]{2,1,0:T(8,128)}), f32[32,8,896]{2,1,0:T(8,128)}, u32[]{:S(2)}, u32[]{:S(2)}) %all-to-all-start.1) | async-done | bytes 917536 | tf_op jit(solution)/shard_map/all_to_all | solution.py:393
  267.1 6.4 chain0.12.refs_0_
  297.0 7.9 %chain1.12 = (f32[2,2,112,256]{3,2,1,0:T(8,128)}, f32[2,2,112,256]{3,2,1,0:T(8,128)}) custom-call(s32[8]{0:T(128)} %stack.35.scalars, f32[2,2]{1,0:T(2,128)} %maximum_select_fusion.rates, f32[2,1152,256]{2,1,0:T(8,128)} %prepare.26.refs_1_.own, f32[2,1152,256]{2,1,0:T(8,128)} %collective-permute-done.9.peer, ...), custom_call_target="tpu_custom_call" | custom-call | flops 9999999827968 | bytes 10000000000 | tf_op jit(solution)/shard_map/chain1/pallas_call | solution.py:164
  306.8 35.6 %all-to-all-done.2.refs_1_.refs_2_ = f32[32,8,896]{2,1,0:T(8,128)} async-done(((f32[32,8,896]{2,1,0:T(8,128)}), f32[32,8,896]{2,1,0:T(8,128)}, u32[]{:S(2)}, u32[]{:S(2)}) %all-to-all-start.2) | async-done | bytes 917536 | tf_op jit(solution)/shard_map/all_to_all | solution.py:393
  372.7 7.8 %chain1.13 = (f32[2,2,112,256]{3,2,1,0:T(8,128)}, f32[2,2,112,256]{3,2,1,0:T(8,128)}) custom-call(s32[8]{0:T(128)} %stack.35.scalars, f32[2,2]{1,0:T(2,128)} %maximum_select_fusion.rates, f32[2,1152,256]{2,1,0:T(8,128)} %prepare.28.refs_1_.own, f32[2,1152,256]{2,1,0:T(8,128)} %collective-permute-done.10.peer, ...), custom_call_target="tpu_custom_call" | custom-call | flops 9999999827968 | bytes 10000000000 | tf_op jit(solution)/shard_map/chain1/pallas_call | solution.py:164
  382.4 35.5 %all-to-all-done.3.refs_1_.refs_3_ = f32[32,8,896]{2,1,0:T(8,128)} async-done(((f32[32,8,896]{2,1,0:T(8,128)}), f32[32,8,896]{2,1,0:T(8,128)}, u32[]{:S(2)}, u32[]{:S(2)}) %all-to-all-start.3) | async-done | bytes 917536 | tf_op jit(solution)/shard_map/all_to_all | solution.py:393
  447.8 7.8 %chain1.14 = (f32[2,2,112,256]{3,2,1,0:T(8,128)}, f32[2,2,112,256]{3,2,1,0:T(8,128)}) custom-call(s32[8]{0:T(128)} %stack.35.scalars, f32[2,2]{1,0:T(2,128)} %maximum_select_fusion.rates, f32[2,1152,256]{2,1,0:T(8,128)} %prepare.30.refs_1_.own, f32[2,1152,256]{2,1,0:T(8,128)} %collective-permute-done.15.peer, ...), custom_call_target="tpu_custom_call" | custom-call | flops 9999999827968 | bytes 10000000000 | tf_op jit(solution)/shard_map/chain1/pallas_call | solution.py:164
  457.5 35.9 %all-to-all-done.4.refs_1_.refs_4_ = f32[32,8,896]{2,1,0:T(8,128)} async-done(((f32[32,8,896]{2,1,0:T(8,128)}), f32[32,8,896]{2,1,0:T(8,128)}, u32[]{:S(2)}, u32[]{:S(2)}) %all-to-all-start.4) | async-done | bytes 917536 | tf_op jit(solution)/shard_map/all_to_all | solution.py:393
  523.7 7.9 %chain1.15 = (f32[2,2,112,256]{3,2,1,0:T(8,128)}, f32[2,2,112,256]{3,2,1,0:T(8,128)}) custom-call(s32[8]{0:T(128)} %stack.35.scalars, f32[2,2]{1,0:T(2,128)} %maximum_select_fusion.rates, f32[2,1152,256]{2,1,0:T(8,128)} %prepare.32.refs_1_.own, f32[2,1152,256]{2,1,0:T(8,128)} %collective-permute-done.16.peer, ...), custom_call_target="tpu_custom_call" | custom-call | flops 9999999827968 | bytes 10000000000 | tf_op jit(solution)/shard_map/chain1/pallas_call | solution.py:164
  532.7 17.2 %despread.3.refs_0_.refs_3_ = f32[8,2,448,256]{3,2,1,0:T(8,128)} custom-call(s32[32]{0:T(128)} %and_select_fusion.source, bf16[2,288,512]{2,1,0:T(8,128)(2,1)} %constant.128.clone.table, f32[32,8,448]{2,1,0:T(8,128)} %all-to-all-done.refs_1_.refs_0_, f32[32,8,896]{2,1,0:T(8,128)} %all-to-all-done.1.refs_1_, f32[32,8,896]{2,1,0:T(8,128)} %all-to-all-done.2.refs_1_.refs_2_, ...), custom_call_target="tpu_custom_call" | custom-call | flops 9999999827968 | bytes 10000000000 | tf_op jit(solution)/shard_map/despread/pallas_call | solution.py:320
  563.3 7.4 %all-to-all-start.6 = ((f32[32,8,896]{2,1,0:T(8,128)}), f32[32,8,896]{2,1,0:T(8,128)}, u32[]{:S(2)}, u32[]{:S(2)}) async-start(f32[32,8,896]{2,1,0:T(8,128)} %finish.15.refs_0_), calls=%async_computation.6 | async-start | bytes 1835008 | tf_op jit(solution)/shard_map/all_to_all | solution.py:393
  574.4 9.1 %collective-permute-done.23.refs_0_ = f32[2,2,2,112,256]{4,3,2,1,0:T(8,128)} collective-permute-done((f32[2,2,2,112,256]{4,3,2,1,0:T(8,128)}, f32[2,2,2,112,256]{4,3,2,1,0:T(8,128)}, u32[]{:S(2)}, u32[]{:S(2)}) %collective-permute-start.23) | collective-permute-done | bytes 917536 | tf_op jit(solution)/shard_map/ppermute | solution.py:426
  583.5 7.9 %chain1.16 = (f32[2,2,112,256]{3,2,1,0:T(8,128)}, f32[2,2,112,256]{3,2,1,0:T(8,128)}) custom-call(s32[8]{0:T(128)} %stack.35.scalars, f32[2,2]{1,0:T(2,128)} %maximum_select_fusion.rates, f32[2,1152,256]{2,1,0:T(8,128)} %prepare.34.refs_1_.own, f32[2,1152,256]{2,1,0:T(8,128)} %collective-permute-done.21.peer, ...), custom_call_target="tpu_custom_call" | custom-call | flops 9999999827968 | bytes 10000000000 | tf_op jit(solution)/shard_map/chain1/pallas_call | solution.py:164
  606.8 8.4 %all-to-all-start.7 = ((f32[32,8,896]{2,1,0:T(8,128)}), f32[32,8,896]{2,1,0:T(8,128)}, u32[]{:S(2)}, u32[]{:S(2)}) async-start(f32[32,8,896]{2,1,0:T(8,128)} %finish.16.refs_1_), calls=%async_computation.7 | async-start | bytes 1835008 | tf_op jit(solution)/shard_map/all_to_all | solution.py:393
  622.4 10.1 %collective-permute-done.26.odd = f32[1,2,112,256]{3,2,1,0:T(8,128)S(1)} collective-permute-done((f32[1,2,112,256]{3,2,1,0:T(8,128)}, f32[1,2,112,256]{3,2,1,0:T(8,128)S(1)}, u32[]{:S(2)}, u32[]{:S(2)}) %collective-permute-start.26) | collective-permute-done | bytes 229408 | tf_op jit(solution)/shard_map/ppermute | solution.py:439
  632.5 7.5 %all-to-all-done.7.refs_1_.refs_2_ = f32[32,8,896]{2,1,0:T(8,128)} async-done(((f32[32,8,896]{2,1,0:T(8,128)}), f32[32,8,896]{2,1,0:T(8,128)}, u32[]{:S(2)}, u32[]{:S(2)}) %all-to-all-start.7) | async-done | bytes 917536 | tf_op jit(solution)/shard_map/all_to_all | solution.py:393
  647.9 13.6 %despread.4.refs_1_ = f32[8,2,448,256]{3,2,1,0:T(8,128)} custom-call(s32[32]{0:T(128)} %and_select_fusion.source, bf16[2,192,512]{2,1,0:T(8,128)(2,1)} %constant.129.clone.table, f32[32,8,896]{2,1,0:T(8,128)} %all-to-all-done.5.refs_1_.refs_0_, f32[32,8,896]{2,1,0:T(8,128)} %all-to-all-done.6.refs_1_, f32[32,8,896]{2,1,0:T(8,128)} %all-to-all-done.7.refs_1_.refs_2_, ...), custom_call_target="tpu_custom_call" | custom-call | flops 9999999827968 | bytes 10000000000 | tf_op jit(solution)/shard_map/despread/pallas_call | solution.py:320
  664.2 10.1 %despread.5 = f32[8,2,448,256]{3,2,1,0:T(8,128)} custom-call(s32[32]{0:T(128)} %and_select_fusion.source, bf16[1,96,512]{2,1,0:T(8,128)(2,1)} %constant.130.clone.table, f32[32,8,448]{2,1,0:T(8,128)} %all-to-all-done.8.refs_0_, f32[8,2,448,256]{3,2,1,0:T(8,128)} %despread.4.refs_1_), custom_call_target="tpu_custom_call" | custom-call | flops 9999999827968 | bytes 10000000000 | tf_op jit(solution)/shard_map/despread/pallas_call | solution.py:320
  (112 shorter events, 271.0 us)
Async XLA Ops:
  3.7 30.2 %collective-permute-start = (f32[1,1160,256]{2,1,0:T(8,128)}, f32[1,1160,256]{2,1,0:T(8,128)}, u32[]{:S(2)}, u32[]{:S(2)}) collective-permute-start(f32[1,1160,256]{2,1,0:T(8,128)} %prepare.18.refs_0_), channel_id=1, source_target_pairs={{0,8},{8,0},{16,24},{24,16},{1,9},{9,1},{17,25},{25,17},{2,10},{10... | collective-permute-start | bytes 3563528 | tf_op jit(solution)/shard_map/ppermute | solution.py:379
  11.7 72.8 %collective-permute-start.3 = (f32[2,1152,256]{2,1,0:T(8,128)}, f32[2,1152,256]{2,1,0:T(8,128)}, u32[]{:S(2)}, u32[]{:S(2)}) collective-permute-start(f32[2,1152,256]{2,1,0:T(8,128)} %prepare.19.refs_0_), channel_id=1, source_target_pairs={{0,8},{8,0},{16,24},{24,16},{1,9},{9,1},{17,25},{25,17},{2,10},{10... | collective-permute-start | bytes 7077896 | tf_op jit(solution)/shard_map/ppermute | solution.py:379
  47.1 144.6 %collective-permute-start.4 = (f32[2,1152,256]{2,1,0:T(8,128)}, f32[2,1152,256]{2,1,0:T(8,128)}, u32[]{:S(2)}, u32[]{:S(2)}) collective-permute-start(f32[2,1152,256]{2,1,0:T(8,128)} %prepare.21.refs_0_), channel_id=1, source_target_pairs={{0,8},{8,0},{16,24},{24,16},{1,9},{9,1},{17,25},{25,17},{2,10},{10... | collective-permute-start | bytes 7077896 | tf_op jit(solution)/shard_map/ppermute | solution.py:379
  59.0 40.6 %collective-permute-start.2 = (f32[1,2,112,256]{3,2,1,0:T(8,128)}, f32[1,2,112,256]{3,2,1,0:T(8,128)}, u32[]{:S(2)}, u32[]{:S(2)}) collective-permute-start(f32[1,2,112,256]{3,2,1,0:T(8,128)} %get-tuple-element.24), channel_id=1, source_target_pairs={{0,16},{8,24},{16,0},{24,8},{1,17},{9,25},{17,1},{25,9},{2,18},{10... | collective-permute-start | bytes 688136 | tf_op jit(solution)/shard_map/ppermute | solution.py:439
  98.1 133.2 %collective-permute-start.9 = (f32[2,1152,256]{2,1,0:T(8,128)}, f32[2,1152,256]{2,1,0:T(8,128)}, u32[]{:S(2)}, u32[]{:S(2)}) collective-permute-start(f32[2,1152,256]{2,1,0:T(8,128)} %prepare.23.refs_0_), channel_id=1, source_target_pairs={{0,8},{8,0},{16,24},{24,16},{1,9},{9,1},{17,25},{25,17},{2,10},{10... | collective-permute-start | bytes 7077896 | tf_op jit(solution)/shard_map/ppermute | solution.py:379
  104.0 87.6 %all-to-all-start = ((f32[32,8,448]{2,1,0:T(8,128)}), f32[32,8,448]{2,1,0:T(8,128)}, u32[]{:S(2)}, u32[]{:S(2)}) async-start(f32[32,8,448]{2,1,0:T(8,128)} %finish.9.refs_0_), calls=%async_computation | async-start | bytes 1048576 | tf_op jit(solution)/shard_map/all_to_all | solution.py:393
  121.3 83.9 %collective-permute-start.7 = (f32[2,2,112,256]{3,2,1,0:T(8,128)}, f32[2,2,112,256]{3,2,1,0:T(8,128)}, u32[]{:S(2)}, u32[]{:S(2)}) collective-permute-start(f32[2,2,112,256]{3,2,1,0:T(8,128)} %get-tuple-element.26), channel_id=1, source_target_pairs={{0,16},{8,24},{16,0},{24,8},{1,17},{9,25},{17,1},{25,9},{2,18},{10... | collective-permute-start | bytes 1376264 | tf_op jit(solution)/shard_map/ppermute | solution.py:439
  203.4 103.4 %collective-permute-start.10 = (f32[2,1152,256]{2,1,0:T(8,128)}, f32[2,1152,256]{2,1,0:T(8,128)}, u32[]{:S(2)}, u32[]{:S(2)}) collective-permute-start(f32[2,1152,256]{2,1,0:T(8,128)} %prepare.25.refs_0_), channel_id=1, source_target_pairs={{0,8},{8,0},{16,24},{24,16},{1,9},{9,1},{17,25},{25,17},{2,10},{10... | collective-permute-start | bytes 7077896 | tf_op jit(solution)/shard_map/ppermute | solution.py:379
  211.3 55.8 %all-to-all-start.1 = ((f32[32,8,896]{2,1,0:T(8,128)}), f32[32,8,896]{2,1,0:T(8,128)}, u32[]{:S(2)}, u32[]{:S(2)}) async-start(f32[32,8,896]{2,1,0:T(8,128)} %finish.10.refs_0_), calls=%async_computation.1 | async-start | bytes 1835008 | tf_op jit(solution)/shard_map/all_to_all | solution.py:393
  229.4 51.3 %collective-permute-start.8 = (f32[2,2,112,256]{3,2,1,0:T(8,128)}, f32[2,2,112,256]{3,2,1,0:T(8,128)}, u32[]{:S(2)}, u32[]{:S(2)}) collective-permute-start(f32[2,2,112,256]{3,2,1,0:T(8,128)} %get-tuple-element.28), channel_id=1, source_target_pairs={{0,16},{8,24},{16,0},{24,8},{1,17},{9,25},{17,1},{25,9},{2,18},{10... | collective-permute-start | bytes 1376264 | tf_op jit(solution)/shard_map/ppermute | solution.py:439
  279.4 103.0 %collective-permute-start.15 = (f32[2,1152,256]{2,1,0:T(8,128)}, f32[2,1152,256]{2,1,0:T(8,128)}, u32[]{:S(2)}, u32[]{:S(2)}) collective-permute-start(f32[2,1152,256]{2,1,0:T(8,128)} %prepare.27.refs_0_), channel_id=1, source_target_pairs={{0,8},{8,0},{16,24},{24,16},{1,9},{9,1},{17,25},{25,17},{2,10},{10... | collective-permute-start | bytes 7077896 | tf_op jit(solution)/shard_map/ppermute | solution.py:379
  286.9 55.5 %all-to-all-start.2 = ((f32[32,8,896]{2,1,0:T(8,128)}), f32[32,8,896]{2,1,0:T(8,128)}, u32[]{:S(2)}, u32[]{:S(2)}) async-start(f32[32,8,896]{2,1,0:T(8,128)} %finish.11.refs_0_), calls=%async_computation.2 | async-start | bytes 1835008 | tf_op jit(solution)/shard_map/all_to_all | solution.py:393
  304.9 51.3 %collective-permute-start.13 = (f32[2,2,112,256]{3,2,1,0:T(8,128)}, f32[2,2,112,256]{3,2,1,0:T(8,128)}, u32[]{:S(2)}, u32[]{:S(2)}) collective-permute-start(f32[2,2,112,256]{3,2,1,0:T(8,128)} %get-tuple-element.30), channel_id=1, source_target_pairs={{0,16},{8,24},{16,0},{24,8},{1,17},{9,25},{17,1},{25,9},{2,18},{10... | collective-permute-start | bytes 1376264 | tf_op jit(solution)/shard_map/ppermute | solution.py:439
  354.6 102.9 %collective-permute-start.16 = (f32[2,1152,256]{2,1,0:T(8,128)}, f32[2,1152,256]{2,1,0:T(8,128)}, u32[]{:S(2)}, u32[]{:S(2)}) collective-permute-start(f32[2,1152,256]{2,1,0:T(8,128)} %prepare.29.refs_0_), channel_id=1, source_target_pairs={{0,8},{8,0},{16,24},{24,16},{1,9},{9,1},{17,25},{25,17},{2,10},{10... | collective-permute-start | bytes 7077896 | tf_op jit(solution)/shard_map/ppermute | solution.py:379
  362.4 55.5 %all-to-all-start.3 = ((f32[32,8,896]{2,1,0:T(8,128)}), f32[32,8,896]{2,1,0:T(8,128)}, u32[]{:S(2)}, u32[]{:S(2)}) async-start(f32[32,8,896]{2,1,0:T(8,128)} %finish.12.refs_0_), calls=%async_computation.3 | async-start | bytes 1835008 | tf_op jit(solution)/shard_map/all_to_all | solution.py:393
  380.5 51.2 %collective-permute-start.14 = (f32[2,2,112,256]{3,2,1,0:T(8,128)}, f32[2,2,112,256]{3,2,1,0:T(8,128)}, u32[]{:S(2)}, u32[]{:S(2)}) collective-permute-start(f32[2,2,112,256]{3,2,1,0:T(8,128)} %get-tuple-element.32), channel_id=1, source_target_pairs={{0,16},{8,24},{16,0},{24,8},{1,17},{9,25},{17,1},{25,9},{2,18},{10... | collective-permute-start | bytes 1376264 | tf_op jit(solution)/shard_map/ppermute | solution.py:439
  429.9 120.0 %collective-permute-start.21 = (f32[2,1152,256]{2,1,0:T(8,128)}, f32[2,1152,256]{2,1,0:T(8,128)}, u32[]{:S(2)}, u32[]{:S(2)}) collective-permute-start(f32[2,1152,256]{2,1,0:T(8,128)} %prepare.31.refs_0_), channel_id=1, source_target_pairs={{0,8},{8,0},{16,24},{24,16},{1,9},{9,1},{17,25},{25,17},{2,10},{10... | collective-permute-start | bytes 7077896 | tf_op jit(solution)/shard_map/ppermute | solution.py:379
  437.9 55.5 %all-to-all-start.4 = ((f32[32,8,896]{2,1,0:T(8,128)}), f32[32,8,896]{2,1,0:T(8,128)}, u32[]{:S(2)}, u32[]{:S(2)}) async-start(f32[32,8,896]{2,1,0:T(8,128)} %finish.13.refs_0_), calls=%async_computation.4 | async-start | bytes 1835008 | tf_op jit(solution)/shard_map/all_to_all | solution.py:393
  455.6 50.2 %collective-permute-start.19 = (f32[2,2,112,256]{3,2,1,0:T(8,128)}, f32[2,2,112,256]{3,2,1,0:T(8,128)}, u32[]{:S(2)}, u32[]{:S(2)}) collective-permute-start(f32[2,2,112,256]{3,2,1,0:T(8,128)} %get-tuple-element.34), channel_id=1, source_target_pairs={{0,16},{8,24},{16,0},{24,8},{1,17},{9,25},{17,1},{25,9},{2,18},{10... | collective-permute-start | bytes 1376264 | tf_op jit(solution)/shard_map/ppermute | solution.py:439
  504.4 87.4 %collective-permute-start.22 = (f32[1,1152,256]{2,1,0:T(8,128)}, f32[1,1152,256]{2,1,0:T(8,128)}, u32[]{:S(2)}, u32[]{:S(2)}) collective-permute-start(f32[1,1152,256]{2,1,0:T(8,128)} %prepare.33.refs_0_), channel_id=1, source_target_pairs={{0,8},{8,0},{16,24},{24,16},{1,9},{9,1},{17,25},{25,17},{2,10},{10... | collective-permute-start | bytes 3538952 | tf_op jit(solution)/shard_map/ppermute | solution.py:379
  511.9 38.0 %all-to-all-start.5 = ((f32[32,8,896]{2,1,0:T(8,128)}), f32[32,8,896]{2,1,0:T(8,128)}, u32[]{:S(2)}, u32[]{:S(2)}) async-start(f32[32,8,896]{2,1,0:T(8,128)} %finish.14.refs_0_), calls=%async_computation.5 | async-start | bytes 1835008 | tf_op jit(solution)/shard_map/all_to_all | solution.py:393
  556.3 27.2 %collective-permute-start.23 = (f32[2,2,2,112,256]{4,3,2,1,0:T(8,128)}, f32[2,2,2,112,256]{4,3,2,1,0:T(8,128)}, u32[]{:S(2)}, u32[]{:S(2)}) collective-permute-start(f32[2,2,2,112,256]{4,3,2,1,0:T(8,128)} %chain0.16.refs_0_), channel_id=1, source_target_pairs={{0,16},{8,24},{16,0},{24,8},{1,17},{9,25},{17,1},{25,9},{2,18},{10... | collective-permute-start | bytes 2752520 | tf_op jit(solution)/shard_map/ppermute | solution.py:426
  563.3 32.1 %all-to-all-start.6 = ((f32[32,8,896]{2,1,0:T(8,128)}), f32[32,8,896]{2,1,0:T(8,128)}, u32[]{:S(2)}, u32[]{:S(2)}) async-start(f32[32,8,896]{2,1,0:T(8,128)} %finish.15.refs_0_), calls=%async_computation.6 | async-start | bytes 1835008 | tf_op jit(solution)/shard_map/all_to_all | solution.py:393
  606.8 33.2 %all-to-all-start.7 = ((f32[32,8,896]{2,1,0:T(8,128)}), f32[32,8,896]{2,1,0:T(8,128)}, u32[]{:S(2)}, u32[]{:S(2)}) async-start(f32[32,8,896]{2,1,0:T(8,128)} %finish.16.refs_1_), calls=%async_computation.7 | async-start | bytes 1835008 | tf_op jit(solution)/shard_map/all_to_all | solution.py:393
  (16 other events, 282.2 us)

commit v4 on v3

v4 whole, which is shorter than its diff:
```python
import functools

import jax
import jax.numpy as jnp
import ml_dtypes
import numpy as np
from jax import lax
from jax.experimental import pallas as pl
from jax.experimental.pallas import tpu as pltpu
from jax.sharding import PartitionSpec as P

F32 = jnp.float32
BF16 = jnp.bfloat16
VMEM_LIMIT = 56 * 1024 * 1024
HEAVY = pl.CostEstimate(flops=10**13, bytes_accessed=10**10, transcendentals=0)
ANY = pl.BlockSpec(memory_space=pl.ANY)
SMEM = pl.BlockSpec(memory_space=pltpu.SMEM)


def split(value):
    high = value.astype(BF16)
    return high, (value - high.astype(F32)).astype(BF16)


def dot(left, right, contract):
    return lax.dot_general(left, right, ((contract[:1], contract[1:]), ((), ())), preferred_element_type=F32)


def dot3(left, right, contract):
    left_high, left_low = left
    right_high, right_low = right
    return (
        dot(left_high, right_high, contract)
        + dot(left_high, right_low, contract)
        + dot(left_low, right_high, contract)
    )


def triangle(users):
    row = lax.broadcasted_iota(jnp.int32, (users, users), 0)
    column = lax.broadcasted_iota(jnp.int32, (users, users), 1)
    return row, column


def prepare_body(carry, blocks, scalars, rates, chan, recv, *refs):
    outs = refs[len(refs) - blocks // 2 :]
    users = chan.shape[2]
    rows = recv.shape[2] // blocks

    def stacked(part):
        pieces = [chan[0, part]]
        for place in range(blocks):
            first = pl.multiple_of(scalars[1 + place] * rows, 8)
            pieces.append(recv[0, part, pl.ds(first, rows), :])
        return split(jnp.concatenate(pieces, 0))

    left_real = stacked(0)
    left_imag = stacked(1)
    right = tuple(
        jnp.concatenate([real[:users], imag[:users]], 1) for real, imag in zip(left_real, left_imag)
    )
    real = dot3(tuple(jnp.concatenate(pair, 1) for pair in zip(left_real, left_imag)), right, (1, 1))
    imag = dot3(
        tuple(jnp.concatenate([b, -a], 1) for a, b in zip(left_real, left_imag)), right, (1, 1)
    )
    row, column = triangle(users)
    outs[0][0, :users] = jnp.where(row <= column, real[:users], imag[:users])
    for place in range(blocks):
        base = users if place < 2 else 0
        first = users + place * rows
        for part, value in enumerate((real, imag)):
            to = base + (2 * (place % 2) + part) * rows
            outs[place // 2][0, to : to + rows] = value[first : first + rows]
    if carry:
        lane = lax.broadcasted_iota(jnp.int32, (carry, users), 1)
        outs[0][0, users + 4 * rows :] = jnp.where(lane == 0, rates[0, 0], rates[0, 1])


def prepare(channel, received, step_sizes, scalars, count, blocks, carry, after):
    _, _, users, width = channel.shape
    symbols = received.shape[2]
    rows = symbols // blocks
    heights = [users + 4 * rows + carry] + [4 * rows] * (blocks // 2 - 1)
    return pl.pallas_call(
        functools.partial(prepare_body, carry, blocks),
        out_shape=[jax.ShapeDtypeStruct((count, height, users), F32) for height in heights],
        grid_spec=pltpu.PrefetchScalarGridSpec(
            num_scalar_prefetch=1,
            grid=(count,),
            in_specs=[
                SMEM,
                pl.BlockSpec((1, 2, users, width), lambda i, s: (s[0] + i, 0, 0, 0)),
                pl.BlockSpec((1, 2, symbols, width), lambda i, s: (s[0] + i, 0, 0, 0)),
            ]
            + [ANY] * len(after),
            out_specs=[pl.BlockSpec((1, height, users), lambda i, s: (i, 0, 0)) for height in heights],
        ),
        compiler_params=pltpu.CompilerParams(vmem_limit_bytes=VMEM_LIMIT),
        cost_estimate=HEAVY,
        name="prepare",
    )(scalars, step_sizes, channel, received, *after)


def unpack(packed, gram, sub):
    users = packed.shape[0]
    row, column = triangle(users)
    turned = packed.T
    real = split(jnp.where(row <= column, packed, turned))
    imag = split(jnp.where(row > column, packed, jnp.where(row < column, -turned, 0.0)))
    for part in range(2):
        gram[sub, part, :users, :users] = real[part]
        gram[sub, part, :users, users:] = imag[part]
        gram[sub, part, users:, :users] = -imag[part]
        gram[sub, part, users:, users:] = real[part]


def step(estimate, matched, gram, sub, rate):
    product = dot3(split(estimate), (gram[sub, 0], gram[sub, 1]), (1, 0))
    return jnp.tanh(estimate + rate * (matched - product))


def filtered(ref, base, rows, slot):
    first = base + 2 * slot * rows
    return jnp.concatenate([ref[0, first : first + rows], ref[0, first + rows : first + 2 * rows]], 1)


def chain_body(round_index, last, rows, side, rates, *refs):
    own, peer = refs[:2]
    users = own.shape[2]
    rest = refs[2:]
    base = users
    grams = (own, peer)
    if round_index:
        own, peer, came = rest[:3]
        base = 0
    gram, matched = refs[-2:]
    for packed, samples, sub in ((grams[0], own, side[0]), (grams[1], peer, 1 - side[0])):
        unpack(packed[0, :users], gram, sub)
        for slot in range(2):
            matched[sub, slot * rows : (slot + 1) * rows] = filtered(samples, base, rows, slot)

    if round_index == 0:
        even = jnp.tanh(rates[0, 0] * matched[0, :rows])
        even = step(even, matched[0, :rows], gram, 0, rates[0, 1])
        even = step(even, matched[1, :rows], gram, 1, rates[1, 0])
        odd = jnp.tanh(rates[1, 0] * matched[1, rows:])
        both = step(jnp.concatenate([even, odd], 0), matched[1], gram, 1, rates[1, 1])
    else:
        both = jnp.concatenate(
            [jnp.concatenate([came[0, slot, 0], came[0, slot, 1]], 1) for slot in range(2)], 0
        )
        for sub in range(2):
            for substep in range(2):
                both = step(both, matched[sub], gram, sub, rates[sub, substep])
    out = refs[-4:-2] if last else refs[-3:-2]
    for slot in range(2):
        for part in range(2):
            piece = both[slot * rows : (slot + 1) * rows, part * users : (part + 1) * users]
            if last:
                out[slot][0, part] = piece
            else:
                out[0][0, slot, part] = piece


def chain(round_index, last, rows, side, rates, own, peer, came, after):
    count, _, users = own[0].shape
    both_spec = pl.BlockSpec((1, 2, 2, rows, users), lambda i, s: (i, 0, 0, 0, 0))
    one_spec = pl.BlockSpec((1, 2, rows, users), lambda i, s: (i, 0, 0, 0))
    both_shape = jax.ShapeDtypeStruct((count, 2, 2, rows, users), F32)
    one_shape = jax.ShapeDtypeStruct((count, 2, rows, users), F32)
    inputs = [own[0], peer[0]]
    heights = [users if round_index else users + 4 * rows] * 2
    if round_index:
        inputs += [own[round_index], peer[round_index]]
        heights += [4 * rows] * 2
    specs = [pl.BlockSpec((1, height, users), lambda i, s: (i, 0, 0)) for height in heights]
    return pl.pallas_call(
        functools.partial(chain_body, round_index, last, rows),
        out_shape=[one_shape, one_shape] if last else both_shape,
        grid_spec=pltpu.PrefetchScalarGridSpec(
            num_scalar_prefetch=1,
            grid=(count,),
            in_specs=[SMEM] + specs + [both_spec] * len(came) + [ANY] * len(after),
            out_specs=[one_spec, one_spec] if last else both_spec,
            scratch_shapes=[
                pltpu.VMEM((2, 2, 2 * users, 2 * users), BF16),
                pltpu.VMEM((2, 2 * rows, 2 * users), F32),
            ],
        ),
        compiler_params=pltpu.CompilerParams(vmem_limit_bytes=VMEM_LIMIT),
        cost_estimate=HEAVY,
        name="chain%d" % round_index,
    )(side, rates, *inputs, *came, *after)


def finish_body(count, rows, scalars, rates, own, peer, even, odd, order, *refs):
    users = own.shape[2]
    out, gram, gathered = refs[-3:]
    tone = pl.program_id(0)
    side = scalars[0]
    even_slot = scalars[1]

    @pl.when(side == 0)
    def _():
        unpack(own[0, :users], gram, 0)

    @pl.when(side != 0)
    def _():
        unpack(peer[0, :users], gram, 0)

    matched = jnp.where(side == 0, filtered(own, users, rows, 1), filtered(peer, users, rows, 1))
    estimate = jnp.concatenate([odd[0, 0], odd[0, 1]], 1)
    for substep in range(2):
        estimate = step(estimate, matched, gram, 0, rates[0, substep])
    for part in range(2):
        first = (tone * 2 + part) * 2
        odd_row = pl.multiple_of((first + 1 - even_slot) * rows, 8)
        even_row = pl.multiple_of((first + even_slot) * rows, 8)
        gathered[pl.ds(odd_row, rows), :] = estimate[:, part * users : (part + 1) * users]
        gathered[pl.ds(even_row, rows), :] = even[0, part]

    @pl.when(tone == count - 1)
    def _():
        high, low = split(gathered[...])
        turned = dot(order[...], high, (1, 1)) + dot(order[...], low, (1, 1))
        out[...] = turned.reshape(out.shape)


def finish(rows, owners, scalars, rates, own, peer, even, odd, order, after):
    count, _, users = own[0].shape
    packed_spec = pl.BlockSpec((1, users + 4 * rows, users), lambda i, s: (i, 0, 0))
    one_spec = pl.BlockSpec((1, 2, rows, users), lambda i, s: (i, 0, 0, 0))
    shape = (owners, users // owners, count * 4 * rows)
    return pl.pallas_call(
        functools.partial(finish_body, count, rows),
        out_shape=jax.ShapeDtypeStruct(shape, F32),
        grid_spec=pltpu.PrefetchScalarGridSpec(
            num_scalar_prefetch=1,
            grid=(count,),
            in_specs=[
                SMEM,
                packed_spec,
                packed_spec,
                one_spec,
                one_spec,
                pl.BlockSpec((users, users), lambda i, s: (0, 0)),
            ]
            + [ANY] * len(after),
            out_specs=pl.BlockSpec(shape, lambda i, s: (0, 0, 0)),
            scratch_shapes=[
                pltpu.VMEM((1, 2, 2 * users, 2 * users), BF16),
                pltpu.VMEM((count * 4 * rows, users), F32),
            ],
        ),
        compiler_params=pltpu.CompilerParams(vmem_limit_bytes=VMEM_LIMIT),
        cost_estimate=HEAVY,
        name="finish",
    )(scalars, rates, own[0], peer[0], even, odd, order, *after)


def despread_body(groups, sizes, rows, folded, first, last, source, table, *refs):
    pieces = refs[: len(sizes)]
    if not first:
        total = refs[len(sizes)]
    out, tones_first, symbols_first = refs[-3:]
    items = out.shape[0]
    tones = sum(sizes)
    depth = tones_first.shape[0]
    pair = pl.program_id(0)
    part = pl.program_id(1)

    def turn(slot):
        block = 2 * pair + slot

        def gather(group, carry):
            position = source[block * groups + group]
            for side in range(2):
                place = (group * 2 + side) * tones * 2
                src = (2 * position + side) * groups + group
                for piece, size in zip(pieces, sizes):
                    for tone in range(2 * size):
                        lane = (tone * 2 + slot) * rows
                        tones_first[place + tone, :, :rows] = piece[src, :, lane : lane + rows]
                    place = place + 2 * size
            return carry

        lax.fori_loop(0, groups, gather, 0)
        for item in range(items):
            high, low = split(tones_first[:, item, :].T[:rows])
            here = slice((slot * items + item) * rows, (slot * items + item + 1) * rows)
            if folded:
                for k, value in enumerate((high, high, low)):
                    symbols_first[0, here, k * depth : (k + 1) * depth] = value
            else:
                symbols_first[0, here] = high
                symbols_first[1, here] = low

    @pl.when(part == 0)
    def _():
        for slot in range(2):
            turn(slot)

    if folded:
        result = dot(symbols_first[0], table[part, 0], (1, 0))
    else:
        result = dot3((symbols_first[0], symbols_first[1]), (table[part, 0], table[part, 1]), (1, 0))
    for slot in range(2):
        for item in range(items):
            value = result[(slot * items + item) * rows : (slot * items + item + 1) * rows]
            if not first:
                value = value + total[item, 0, slot * rows : (slot + 1) * rows, :]
            out[item, 0, slot * rows : (slot + 1) * rows, :] = jnp.tanh(value) if last else value


def despread(pieces, starts, groups, half, blocks, rows, source, total, last, after):
    items = pieces[0].shape[1]
    length = groups * 2 * half
    lanes = -(-rows // 128) * 128
    sizes = [piece.shape[2] // (4 * rows) for piece in pieces]
    local = np.concatenate([np.arange(begin, begin + size) for begin, size in zip(starts, sizes)])
    index = (np.arange(groups * 2)[:, None] * half + local[None, :]).reshape(-1)
    angle = 2.0 * np.pi / length * (index[:, None] * np.arange(length)[None, :] % length)
    cosine, sine = np.cos(angle) / np.sqrt(length), np.sin(angle) / np.sqrt(length)
    table = np.stack([np.stack([cosine, -sine], 1), np.stack([sine, cosine], 1)])
    table = table.reshape(2, 1, 2 * len(index), length)
    high = table.astype(ml_dtypes.bfloat16)
    low = (table - high.astype(np.float64)).astype(ml_dtypes.bfloat16)
    depth = table.shape[2]
    folded = 3 * depth <= 256
    table = np.concatenate([high, low, high], 2) if folded else np.concatenate([high, low], 1)
    block_spec = pl.BlockSpec((items, 1, 2 * rows, length), lambda i, part, s: (0, part, i, 0))
    totals = [] if total is None else [total]
    return pl.pallas_call(
        functools.partial(despread_body, groups, sizes, rows, folded, total is None, last),
        out_shape=jax.ShapeDtypeStruct((items, 2, blocks * rows, length), F32),
        grid_spec=pltpu.PrefetchScalarGridSpec(
            num_scalar_prefetch=1,
            grid=(blocks // 2, 2),
            in_specs=[pl.BlockSpec(table.shape, lambda i, part, s: (0, 0, 0, 0))]
            + [pl.BlockSpec(piece.shape, lambda i, part, s: (0, 0, 0)) for piece in pieces]
            + [block_spec] * len(totals)
            + [ANY] * len(after),
            out_specs=block_spec,
            scratch_shapes=[
                pltpu.VMEM((depth, items, lanes), F32),
                pltpu.VMEM((table.shape[1], 2 * items * rows, table.shape[2]), BF16),
            ],
        ),
        compiler_params=pltpu.CompilerParams(vmem_limit_bytes=VMEM_LIMIT),
        cost_estimate=HEAVY,
        name="despread",
    )(source, jnp.asarray(table), *pieces, *totals, *after)


def on_device(channel, received, step_sizes, hop_offset, user_order):
    blocks = lax.axis_size("blk")
    groups = lax.axis_size("tones")
    pairs = blocks // 2
    half = channel.shape[0] // 2
    users = channel.shape[2]
    rows = received.shape[2] // blocks
    owners = blocks * groups
    position = lax.axis_index("blk")
    offset = hop_offset[lax.axis_index("tones")]
    side = position % 2
    pair = position // 2

    swap = [(p, p ^ 1) for p in range(blocks)]
    onward = [(p, (p + 2) % blocks) for p in range(blocks)]

    sizes = [1] + [2] * ((half - 2) // 2) + [1]
    sizes += [1] * (half - sum(sizes))
    starts = [sum(sizes[:c]) for c in range(len(sizes))]
    chunks = len(sizes)

    order_of_blocks = []
    for r in range(pairs):
        order_of_blocks += [(2 * (pair - r) - offset) % blocks, (2 * (pair - r) + 1 - offset) % blocks]
    side_alone = side.reshape(1)
    side_and_slot = jnp.stack([side, offset % 2])
    order = (user_order[:, None] == jnp.arange(users, dtype=jnp.int32)[None, :]).astype(BF16)

    begins = (jnp.arange(blocks, dtype=jnp.int32)[:, None] + hop_offset[None, :]) % blocks
    source = jnp.where(begins % 2 == 0, begins // 2 + pairs - 1, begins // 2) % pairs

    own, peer, odd, pieces = {}, {}, {}, []

    def ready(c, first_tone, carry, after):
        scalars = jnp.stack([first_tone + starts[c]] + order_of_blocks)
        return prepare(channel, received, step_sizes, scalars, sizes[c], blocks, carry, after)

    def ready_peer(c, after):
        sent = ready(c, (1 - side) * half, 8 if c == 0 else 0, after)
        peer[c] = [lax.ppermute(value, "blk", swap) for value in sent]
        return sent[0]

    def ready_own(c, after):
        own[c] = ready(c, side * half, 0, after)
        return own[c][0]

    def complete(c, after):
        even, moved = odd[c]
        done = finish(rows, owners, side_and_slot, rates, own[c], peer[c], even, moved, order, after)
        pieces.append(
            lax.all_to_all(done, ("blk", "tones"), split_axis=0, concat_axis=0, tiled=True)
        )
        return done

    def bring_together(begin, end, total, last, after):
        return despread(
            pieces[begin:end],
            starts[begin:end],
            groups,
            half,
            blocks,
            rows,
            source.reshape(-1),
            total,
            last,
            after,
        )

    before = ready_peer(0, [])
    if chunks > 1:
        before = ready_peer(1, [before])
    before = ready_own(0, [before])
    peer_rates = peer[0][0][0, users + 4 * rows, :2].reshape(1, 2)
    rates = jnp.where(
        side == 0,
        jnp.concatenate([step_sizes, peer_rates], 0),
        jnp.concatenate([peer_rates, step_sizes], 0),
    )
    early = max(chunks - 4, 0)
    total = None
    for c in range(chunks):
        before = chain(0, False, rows, side_alone, rates, own[c], peer[c], [], [before])
        both = lax.ppermute(before, "blk", onward)
        if c > 0:
            before = complete(c - 1, [before] + pieces[-1:])
        if c + 2 < chunks:
            before = ready_peer(c + 2, [before])
        if c + 1 < chunks:
            before = ready_own(c + 1, [before])
        for r in range(1, pairs):
            done = chain(r, r == pairs - 1, rows, side_alone, rates, own[c], peer[c], [both], [before])
            if r < pairs - 1:
                both = lax.ppermute(done, "blk", onward)
                before = done
        even, moving = done
        odd[c] = (even, lax.ppermute(moving, "blk", onward))
        before = even
        if early and c == early + 1:
            total = bring_together(0, early, None, False, [before])
            before = total
    before = complete(chunks - 1, [before] + pieces[-1:])
    if early < chunks - 1:
        total = bring_together(early, chunks - 1, total, False, [before])
    return bring_together(chunks - 1, chunks, total, True, [])


def solution(mesh):
    in_specs = (
        P("tones", None, None, "blk"),
        P("tones", None, None, "blk"),
        P("blk", None),
        P(),
        P(),
    )
    out_specs = P(("blk", "tones"), None, None, None)
    return jax.shard_map(
        on_device, mesh=mesh, in_specs=in_specs, out_specs=out_specs, check_vma=False
    )
```

time: 685 us -> 575 us (0.84)
  waiting for transfers between devices: 281 us -> 157 us
  local copies, waits for them, and re-layouts: 2.06 us -> 13.2 us
  starting transfers between devices: 84.5 us -> 92.3 us
    all_to_all x9, waiting for transfers between devices: 225 us -> 86.8 us  [complete(): lax.all_to_all(done, ('blk', 'tones'), split_axis=0, concat_axis=0, tiled...]
    ppermute x9, waiting for transfers between devices: 10.1 us -> 24.1 us  [on_device(): odd[c] = (even, lax.ppermute(moving, 'blk', onward))]
    another operation x2 -> x19, local copies, waits for them, and re-layouts: 1.3 us -> 11.9 us  [the longest x18 11.2 us: ready(): scalars = jnp.stack([first_tone + starts[c]] + order_of_blocks)]
    pallas_call x45, Pallas kernels: 258 us -> 249 us  [the longest x18 103 us: chain(): pl.pallas_call(functools.partial(chain_body, round_index, last, rows), ou...]
    ppermute x9 -> x18, starting transfers between devices: 13.7 us -> 19.4 us  [ready_peer(): peer[c] = [lax.ppermute(value, 'blk', swap) for value in sent]]
    ppermute x9 -> x18, waiting for transfers between devices: 34.5 us -> 39.6 us  [ready_peer(): peer[c] = [lax.ppermute(value, 'blk', swap) for value in sent]]
  transfers between devices with their start and end apart: 36 -> 45, of which waited for: 13 -> 21; matrix products, arithmetic and copies ran while one was open for 1% -> 2% of each run, Pallas kernels for 42% -> 48%
where the time goes in v4:
time: 575 us; the launch traced here: 565 us
  Pallas kernels  294 us (51%)
  waiting for transfers between devices  157 us (27%)
  starting transfers between devices  92.3 us (16%)
  local copies, waits for them, and re-layouts  13.2 us (2%)
    pallas_call x18, Pallas kernels, chain(): pl.pallas_call(functools.partial(chain_body, round_index, last, rows), ou...  103 us
    pallas_call x18, Pallas kernels, prepare(): pl.pallas_call(functools.partial(prepare_body, carry, blocks), out_shape=...  97.2 us
    all_to_all x9, waiting for transfers between devices, complete(): lax.all_to_all(done, ('blk', 'tones'), split_axis=0, concat_axis=0, tiled...  86.8 us
    pallas_call x9, Pallas kernels, finish(): pl.pallas_call(functools.partial(finish_body, count, rows), out_shape=jax...  48.7 us
    pallas_call x3, Pallas kernels, despread(): pl.pallas_call(functools.partial(despread_body, groups, sizes, rows, fold...  45.4 us
    all_to_all x9, starting transfers between devices, complete(): lax.all_to_all(done, ('blk', 'tones'), split_axis=0, concat_axis=0, tiled...  45.1 us
    ppermute x18, waiting for transfers between devices, ready_peer(): peer[c] = [lax.ppermute(value, 'blk', swap) for value in sent]  39.6 us
    ppermute x9, waiting for transfers between devices, on_device(): odd[c] = (even, lax.ppermute(moving, 'blk', onward))  24.1 us
  transfers between devices with their start and end apart: 45, of which 21 were waited for; matrix products, arithmetic and copies ran while one was open for 2% of the time, Pallas kernels for 48%

profile of v4, /device:TPU:0, one launch (start us, length us, event | category | flops | bytes accessed | tf_op | source)
XLA Modules:
  0.0 564.6 jit_solution(1363269859563374220)
XLA Ops:
  64.1 25.5 %collective-permute-done.4.refs_1_.peer = f32[2,704,256]{2,1,0:T(8,128)} collective-permute-done((f32[2,704,256]{2,1,0:T(8,128)}, f32[2,704,256]{2,1,0:T(8,128)}, u32[]{:S(2)}, u32[]{:S(2)}) %collective-permute-start.4) | collective-permute-done | bytes 1441824 | tf_op jit(solution)/shard_map/ppermute | solution.py:394
  120.0 6.9 %chain1.10 = (f32[2,2,112,256]{3,2,1,0:T(8,128)}, f32[2,2,112,256]{3,2,1,0:T(8,128)}) custom-call(s32[1]{0:T(128)} %bitcast.side, f32[2,2]{1,0:T(2,128)} %maximum_select_fusion.rates, f32[2,704,256]{2,1,0:T(8,128)} %get-tuple-element.65.refs_5_.refs_0_.own, f32[2,704,256]{2,1,0:T(8,128)} %collective-permute-done.4.refs_1_.peer, ...), custom_call_target="tpu_custom_call" | custom-call | flops 9999999827968 | bytes 10000000000 | tf_op jit(solution)/shard_map/chain1/pallas_call | solution.py:177
  134.4 12.9 %all-to-all-done.refs_1_.refs_0_ = f32[32,8,448]{2,1,0:T(8,128)} async-done(((f32[32,8,448]{2,1,0:T(8,128)}), f32[32,8,448]{2,1,0:T(8,128)}, u32[]{:S(2)}, u32[]{:S(2)}) %all-to-all-start) | async-done | bytes 458784 | tf_op jit(solution)/shard_map/all_to_all | solution.py:405
  147.3 5.8 %finish.10.refs_0_ = f32[32,8,896]{2,1,0:T(8,128)} custom-call(s32[2]{0:T(128)} %pad_add_fusion.scalars, f32[2,2]{1,0:T(2,128)} %maximum_select_fusion.rates, f32[2,704,256]{2,1,0:T(8,128)} %get-tuple-element.65.refs_5_.refs_0_.own, f32[2,704,256]{2,1,0:T(8,128)} %collective-permute-done.4.refs_1_.peer, f32[2,2,112,256]{3,2,1,0:T(8,128)} %get-tuple-element.74.refs_2_.even, ...), custom_call_target="tpu_custom_call" | custom-call | flops 9999999827968 | bytes 10000000000 | tf_op jit(solution)/shard_map/finish/pallas_call | solution.py:234
  171.8 6.9 %chain1.11 = (f32[2,2,112,256]{3,2,1,0:T(8,128)}, f32[2,2,112,256]{3,2,1,0:T(8,128)}) custom-call(s32[1]{0:T(128)} %bitcast.side, f32[2,2]{1,0:T(2,128)} %maximum_select_fusion.rates, f32[2,704,256]{2,1,0:T(8,128)} %get-tuple-element.69.refs_5_.refs_0_.own, f32[2,704,256]{2,1,0:T(8,128)} %collective-permute-done.5.refs_1_.peer, ...), custom_call_target="tpu_custom_call" | custom-call | flops 9999999827968 | bytes 10000000000 | tf_op jit(solution)/shard_map/chain1/pallas_call | solution.py:177
  192.7 15.0 %all-to-all-done.1.refs_1_ = f32[32,8,896]{2,1,0:T(8,128)} async-done(((f32[32,8,896]{2,1,0:T(8,128)}), f32[32,8,896]{2,1,0:T(8,128)}, u32[]{:S(2)}, u32[]{:S(2)}) %all-to-all-start.1) | async-done | bytes 917536 | tf_op jit(solution)/shard_map/all_to_all | solution.py:405
  232.3 6.9 %chain1.12 = (f32[2,2,112,256]{3,2,1,0:T(8,128)}, f32[2,2,112,256]{3,2,1,0:T(8,128)}) custom-call(s32[1]{0:T(128)} %bitcast.side, f32[2,2]{1,0:T(2,128)} %maximum_select_fusion.rates, f32[2,704,256]{2,1,0:T(8,128)} %get-tuple-element.77.refs_5_.refs_0_.own, f32[2,704,256]{2,1,0:T(8,128)} %collective-permute-done.12.refs_1_.peer, ...), custom_call_target="tpu_custom_call" | custom-call | flops 9999999827968 | bytes 10000000000 | tf_op jit(solution)/shard_map/chain1/pallas_call | solution.py:177
  253.2 14.9 %all-to-all-done.2.refs_1_.refs_2_ = f32[32,8,896]{2,1,0:T(8,128)} async-done(((f32[32,8,896]{2,1,0:T(8,128)}), f32[32,8,896]{2,1,0:T(8,128)}, u32[]{:S(2)}, u32[]{:S(2)}) %all-to-all-start.2) | async-done | bytes 917536 | tf_op jit(solution)/shard_map/all_to_all | solution.py:405
  268.1 5.8 %finish.12.refs_0_ = f32[32,8,896]{2,1,0:T(8,128)} custom-call(s32[2]{0:T(128)} %pad_add_fusion.scalars, f32[2,2]{1,0:T(2,128)} %maximum_select_fusion.rates, f32[2,704,256]{2,1,0:T(8,128)} %get-tuple-element.77.refs_5_.refs_0_.own, f32[2,704,256]{2,1,0:T(8,128)} %collective-permute-done.12.refs_1_.peer, f32[2,2,112,256]{3,2,1,0:T(8,128)} %get-tuple-element.86.refs_2_.even, ...), custom_call_target="tpu_custom_call" | custom-call | flops 9999999827968 | bytes 10000000000 | tf_op jit(solution)/shard_map/finish/pallas_call | solution.py:234
  292.9 6.9 %chain1.13 = (f32[2,2,112,256]{3,2,1,0:T(8,128)}, f32[2,2,112,256]{3,2,1,0:T(8,128)}) custom-call(s32[1]{0:T(128)} %bitcast.side, f32[2,2]{1,0:T(2,128)} %maximum_select_fusion.rates, f32[2,704,256]{2,1,0:T(8,128)} %get-tuple-element.81.refs_5_.refs_0_.own, f32[2,704,256]{2,1,0:T(8,128)} %collective-permute-done.13.refs_1_.peer, ...), custom_call_target="tpu_custom_call" | custom-call | flops 9999999827968 | bytes 10000000000 | tf_op jit(solution)/shard_map/chain1/pallas_call | solution.py:177
  313.8 14.7 %all-to-all-done.3.refs_1_.refs_3_ = f32[32,8,896]{2,1,0:T(8,128)} async-done(((f32[32,8,896]{2,1,0:T(8,128)}), f32[32,8,896]{2,1,0:T(8,128)}, u32[]{:S(2)}, u32[]{:S(2)}) %all-to-all-start.3) | async-done | bytes 917536 | tf_op jit(solution)/shard_map/all_to_all | solution.py:405
  328.5 5.8 %finish.13.refs_0_ = f32[32,8,896]{2,1,0:T(8,128)} custom-call(s32[2]{0:T(128)} %pad_add_fusion.scalars, f32[2,2]{1,0:T(2,128)} %maximum_select_fusion.rates, f32[2,704,256]{2,1,0:T(8,128)} %get-tuple-element.81.refs_5_.refs_0_.own, f32[2,704,256]{2,1,0:T(8,128)} %collective-permute-done.13.refs_1_.peer, f32[2,2,112,256]{3,2,1,0:T(8,128)} %get-tuple-element.90.refs_2_.even, ...), custom_call_target="tpu_custom_call" | custom-call | flops 9999999827968 | bytes 10000000000 | tf_op jit(solution)/shard_map/finish/pallas_call | solution.py:234
  352.9 6.9 %chain1.14 = (f32[2,2,112,256]{3,2,1,0:T(8,128)}, f32[2,2,112,256]{3,2,1,0:T(8,128)}) custom-call(s32[1]{0:T(128)} %bitcast.side, f32[2,2]{1,0:T(2,128)} %maximum_select_fusion.rates, f32[2,704,256]{2,1,0:T(8,128)} %get-tuple-element.89.refs_5_.refs_0_.own, f32[2,704,256]{2,1,0:T(8,128)} %collective-permute-done.20.refs_1_.peer, ...), custom_call_target="tpu_custom_call" | custom-call | flops 9999999827968 | bytes 10000000000 | tf_op jit(solution)/shard_map/chain1/pallas_call | solution.py:177
  373.8 15.1 %all-to-all-done.4.refs_1_.refs_4_ = f32[32,8,896]{2,1,0:T(8,128)} async-done(((f32[32,8,896]{2,1,0:T(8,128)}), f32[32,8,896]{2,1,0:T(8,128)}, u32[]{:S(2)}, u32[]{:S(2)}) %all-to-all-start.4) | async-done | bytes 917536 | tf_op jit(solution)/shard_map/all_to_all | solution.py:405
  388.9 5.8 %finish.14.refs_0_ = f32[32,8,896]{2,1,0:T(8,128)} custom-call(s32[2]{0:T(128)} %pad_add_fusion.scalars, f32[2,2]{1,0:T(2,128)} %maximum_select_fusion.rates, f32[2,704,256]{2,1,0:T(8,128)} %get-tuple-element.89.refs_5_.refs_0_.own, f32[2,704,256]{2,1,0:T(8,128)} %collective-permute-done.20.refs_1_.peer, f32[2,2,112,256]{3,2,1,0:T(8,128)} %get-tuple-element.98.refs_2_.even, ...), custom_call_target="tpu_custom_call" | custom-call | flops 9999999827968 | bytes 10000000000 | tf_op jit(solution)/shard_map/finish/pallas_call | solution.py:234
  412.0 6.9 %chain1.15 = (f32[2,2,112,256]{3,2,1,0:T(8,128)}, f32[2,2,112,256]{3,2,1,0:T(8,128)}) custom-call(s32[1]{0:T(128)} %bitcast.side, f32[2,2]{1,0:T(2,128)} %maximum_select_fusion.rates, f32[2,704,256]{2,1,0:T(8,128)} %get-tuple-element.93.refs_5_.refs_0_.own, f32[2,704,256]{2,1,0:T(8,128)} %collective-permute-done.21.refs_1_.peer, ...), custom_call_target="tpu_custom_call" | custom-call | flops 9999999827968 | bytes 10000000000 | tf_op jit(solution)/shard_map/chain1/pallas_call | solution.py:177
  420.8 17.9 %despread.3.refs_2_.refs_3_ = f32[8,2,448,256]{3,2,1,0:T(8,128)} custom-call(s32[32]{0:T(128)} %and_select_fusion.source, bf16[2,2,288,256]{3,2,1,0:T(8,128)(2,1)} %constant.118.clone.table, f32[32,8,448]{2,1,0:T(8,128)} %all-to-all-done.refs_1_.refs_0_, f32[32,8,896]{2,1,0:T(8,128)} %all-to-all-done.1.refs_1_, ...), custom_call_target="tpu_custom_call" | custom-call | flops 9999999827968 | bytes 10000000000 | tf_op jit(solution)/shard_map/despread/pallas_call | solution.py:333
  464.6 6.6 %collective-permute-done.32.refs_4_ = f32[2,2,2,112,256]{4,3,2,1,0:T(8,128)} collective-permute-done((f32[2,2,2,112,256]{4,3,2,1,0:T(8,128)}, f32[2,2,2,112,256]{4,3,2,1,0:T(8,128)}, u32[]{:S(2)}, u32[]{:S(2)}) %collective-permute-start.32) | collective-permute-done | bytes 917536 | tf_op jit(solution)/shard_map/ppermute | solution.py:437
  471.3 6.9 %chain1.16 = (f32[2,2,112,256]{3,2,1,0:T(8,128)}, f32[2,2,112,256]{3,2,1,0:T(8,128)}) custom-call(s32[1]{0:T(128)} %bitcast.side, f32[2,2]{1,0:T(2,128)} %maximum_select_fusion.rates, f32[2,704,256]{2,1,0:T(8,128)} %get-tuple-element.101.refs_5_.refs_0_.own, f32[2,704,256]{2,1,0:T(8,128)} %collective-permute-done.28.refs_1_.peer, ...), custom_call_target="tpu_custom_call" | custom-call | flops 9999999827968 | bytes 10000000000 | tf_op jit(solution)/shard_map/chain1/pallas_call | solution.py:177
  484.0 9.2 %collective-permute-done.34.odd = f32[2,2,112,256]{3,2,1,0:T(8,128)} collective-permute-done((f32[2,2,112,256]{3,2,1,0:T(8,128)}, f32[2,2,112,256]{3,2,1,0:T(8,128)}, u32[]{:S(2)}, u32[]{:S(2)}) %collective-permute-start.34) | collective-permute-done | bytes 458784 | tf_op jit(solution)/shard_map/ppermute | solution.py:450
  509.8 10.1 %collective-permute-done.35.odd = f32[1,2,112,256]{3,2,1,0:T(8,128)S(1)} collective-permute-done((f32[1,2,112,256]{3,2,1,0:T(8,128)}, f32[1,2,112,256]{3,2,1,0:T(8,128)S(1)}, u32[]{:S(2)}, u32[]{:S(2)}) %collective-permute-start.35) | collective-permute-done | bytes 229408 | tf_op jit(solution)/shard_map/ppermute | solution.py:450
  519.9 8.4 %all-to-all-done.7.refs_1_.refs_2_ = f32[32,8,896]{2,1,0:T(8,128)} async-done(((f32[32,8,896]{2,1,0:T(8,128)}), f32[32,8,896]{2,1,0:T(8,128)}, u32[]{:S(2)}, u32[]{:S(2)}) %all-to-all-start.7) | async-done | bytes 917536 | tf_op jit(solution)/shard_map/all_to_all | solution.py:405
  535.8 15.4 %despread.4.refs_1_ = f32[8,2,448,256]{3,2,1,0:T(8,128)} custom-call(s32[32]{0:T(128)} %and_select_fusion.source, bf16[2,2,192,256]{3,2,1,0:T(8,128)(2,1)} %constant.119.clone.table, f32[32,8,896]{2,1,0:T(8,128)} %all-to-all-done.5.refs_1_.refs_0_, f32[32,8,896]{2,1,0:T(8,128)} %all-to-all-done.6.refs_1_, f32[32,8,896]{2,1,0:T(8,128)} %all-to-all-done.7.refs_1_.refs_2_, ...), custom_call_target="tpu_custom_call" | custom-call | flops 9999999827968 | bytes 10000000000 | tf_op jit(solution)/shard_map/despread/pallas_call | solution.py:333
  552.2 12.0 %despread.5 = f32[8,2,448,256]{3,2,1,0:T(8,128)} custom-call(s32[32]{0:T(128)} %and_select_fusion.source, bf16[2,1,96,256]{3,2,1,0:T(8,128)(2,1)} %constant.120.clone.table, f32[32,8,448]{2,1,0:T(8,128)} %all-to-all-done.8.refs_0_, f32[8,2,448,256]{3,2,1,0:T(8,128)} %despread.4.refs_1_), custom_call_target="tpu_custom_call" | custom-call | flops 9999999827968 | bytes 10000000000 | tf_op jit(solution)/shard_map/despread/pallas_call | solution.py:333
  (148 shorter events, 310.3 us)
Async XLA Ops:
  8.8 50.2 %collective-permute-start.1 = (f32[1,448,256]{2,1,0:T(8,128)}, f32[1,448,256]{2,1,0:T(8,128)}, u32[]{:S(2)}, u32[]{:S(2)}) collective-permute-start(f32[1,448,256]{2,1,0:T(8,128)} %get-tuple-element.63), channel_id=1, source_target_pairs={{0,8},{8,0},{16,24},{24,16},{1,9},{9,1},{17,25},{25,17},{2,10},{10... | collective-permute-start | bytes 1376264 | tf_op jit(solution)/shard_map/ppermute | solution.py:394
  18.1 101.8 %collective-permute-start.7 = (f32[2,448,256]{2,1,0:T(8,128)}, f32[2,448,256]{2,1,0:T(8,128)}, u32[]{:S(2)}, u32[]{:S(2)}) collective-permute-start(f32[2,448,256]{2,1,0:T(8,128)} %get-tuple-element.73), channel_id=1, source_target_pairs={{0,8},{8,0},{16,24},{24,16},{1,9},{9,1},{17,25},{25,17},{2,10},{10... | collective-permute-start | bytes 2752520 | tf_op jit(solution)/shard_map/ppermute | solution.py:394
  20.1 69.5 %collective-permute-start.4 = (f32[2,704,256]{2,1,0:T(8,128)}, f32[2,704,256]{2,1,0:T(8,128)}, u32[]{:S(2)}, u32[]{:S(2)}) collective-permute-start(f32[2,704,256]{2,1,0:T(8,128)} %get-tuple-element.60.refs_0_), channel_id=1, source_target_pairs={{0,8},{8,0},{16,24},{24,16},{1,9},{9,1},{17,25},{25,17},{2,10},{10... | collective-permute-start | bytes 4325384 | tf_op jit(solution)/shard_map/ppermute | solution.py:394
  51.8 77.0 %collective-permute-start.5 = (f32[2,704,256]{2,1,0:T(8,128)}, f32[2,704,256]{2,1,0:T(8,128)}, u32[]{:S(2)}, u32[]{:S(2)}) collective-permute-start(f32[2,704,256]{2,1,0:T(8,128)} %get-tuple-element.64.refs_0_), channel_id=1, source_target_pairs={{0,8},{8,0},{16,24},{24,16},{1,9},{9,1},{17,25},{25,17},{2,10},{10... | collective-permute-start | bytes 4325384 | tf_op jit(solution)/shard_map/ppermute | solution.py:394
  59.0 112.7 %collective-permute-start.6 = (f32[2,448,256]{2,1,0:T(8,128)}, f32[2,448,256]{2,1,0:T(8,128)}, u32[]{:S(2)}, u32[]{:S(2)}) collective-permute-start(f32[2,448,256]{2,1,0:T(8,128)} %get-tuple-element.71), channel_id=1, source_target_pairs={{0,8},{8,0},{16,24},{24,16},{1,9},{9,1},{17,25},{25,17},{2,10},{10... | collective-permute-start | bytes 2752520 | tf_op jit(solution)/shard_map/ppermute | solution.py:394
  101.4 46.0 %all-to-all-start = ((f32[32,8,448]{2,1,0:T(8,128)}), f32[32,8,448]{2,1,0:T(8,128)}, u32[]{:S(2)}, u32[]{:S(2)}) async-start(f32[32,8,448]{2,1,0:T(8,128)} %finish.9.refs_0_), calls=%async_computation | async-start | bytes 1048576 | tf_op jit(solution)/shard_map/all_to_all | solution.py:405
  112.2 71.8 %collective-permute-start.12 = (f32[2,704,256]{2,1,0:T(8,128)}, f32[2,704,256]{2,1,0:T(8,128)}, u32[]{:S(2)}, u32[]{:S(2)}) collective-permute-start(f32[2,704,256]{2,1,0:T(8,128)} %get-tuple-element.68.refs_0_), channel_id=1, source_target_pairs={{0,8},{8,0},{16,24},{24,16},{1,9},{9,1},{17,25},{25,17},{2,10},{10... | collective-permute-start | bytes 4325384 | tf_op jit(solution)/shard_map/ppermute | solution.py:394
  119.9 112.2 %collective-permute-start.15 = (f32[2,448,256]{2,1,0:T(8,128)}, f32[2,448,256]{2,1,0:T(8,128)}, u32[]{:S(2)}, u32[]{:S(2)}) collective-permute-start(f32[2,448,256]{2,1,0:T(8,128)} %get-tuple-element.85), channel_id=1, source_target_pairs={{0,8},{8,0},{16,24},{24,16},{1,9},{9,1},{17,25},{25,17},{2,10},{10... | collective-permute-start | bytes 2752520 | tf_op jit(solution)/shard_map/ppermute | solution.py:394
  153.1 54.6 %all-to-all-start.1 = ((f32[32,8,896]{2,1,0:T(8,128)}), f32[32,8,896]{2,1,0:T(8,128)}, u32[]{:S(2)}, u32[]{:S(2)}) async-start(f32[32,8,896]{2,1,0:T(8,128)} %finish.10.refs_0_), calls=%async_computation.1 | async-start | bytes 1835008 | tf_op jit(solution)/shard_map/all_to_all | solution.py:405
  164.1 80.4 %collective-permute-start.13 = (f32[2,704,256]{2,1,0:T(8,128)}, f32[2,704,256]{2,1,0:T(8,128)}, u32[]{:S(2)}, u32[]{:S(2)}) collective-permute-start(f32[2,704,256]{2,1,0:T(8,128)} %get-tuple-element.76.refs_0_), channel_id=1, source_target_pairs={{0,8},{8,0},{16,24},{24,16},{1,9},{9,1},{17,25},{25,17},{2,10},{10... | collective-permute-start | bytes 4325384 | tf_op jit(solution)/shard_map/ppermute | solution.py:394
  171.7 121.0 %collective-permute-start.14 = (f32[2,448,256]{2,1,0:T(8,128)}, f32[2,448,256]{2,1,0:T(8,128)}, u32[]{:S(2)}, u32[]{:S(2)}) collective-permute-start(f32[2,448,256]{2,1,0:T(8,128)} %get-tuple-element.83), channel_id=1, source_target_pairs={{0,8},{8,0},{16,24},{24,16},{1,9},{9,1},{17,25},{25,17},{2,10},{10... | collective-permute-start | bytes 2752520 | tf_op jit(solution)/shard_map/ppermute | solution.py:394
  213.5 54.6 %all-to-all-start.2 = ((f32[32,8,896]{2,1,0:T(8,128)}), f32[32,8,896]{2,1,0:T(8,128)}, u32[]{:S(2)}, u32[]{:S(2)}) async-start(f32[32,8,896]{2,1,0:T(8,128)} %finish.11.refs_0_), calls=%async_computation.2 | async-start | bytes 1835008 | tf_op jit(solution)/shard_map/all_to_all | solution.py:405
  224.5 80.3 %collective-permute-start.20 = (f32[2,704,256]{2,1,0:T(8,128)}, f32[2,704,256]{2,1,0:T(8,128)}, u32[]{:S(2)}, u32[]{:S(2)}) collective-permute-start(f32[2,704,256]{2,1,0:T(8,128)} %get-tuple-element.80.refs_0_), channel_id=1, source_target_pairs={{0,8},{8,0},{16,24},{24,16},{1,9},{9,1},{17,25},{25,17},{2,10},{10... | collective-permute-start | bytes 4325384 | tf_op jit(solution)/shard_map/ppermute | solution.py:394
  232.1 120.6 %collective-permute-start.23 = (f32[2,448,256]{2,1,0:T(8,128)}, f32[2,448,256]{2,1,0:T(8,128)}, u32[]{:S(2)}, u32[]{:S(2)}) collective-permute-start(f32[2,448,256]{2,1,0:T(8,128)} %get-tuple-element.97), channel_id=1, source_target_pairs={{0,8},{8,0},{16,24},{24,16},{1,9},{9,1},{17,25},{25,17},{2,10},{10... | collective-permute-start | bytes 2752520 | tf_op jit(solution)/shard_map/ppermute | solution.py:394
  249.9 43.0 %collective-permute-start.17 = (f32[2,2,2,112,256]{4,3,2,1,0:T(8,128)}, f32[2,2,2,112,256]{4,3,2,1,0:T(8,128)}, u32[]{:S(2)}, u32[]{:S(2)}) collective-permute-start(f32[2,2,2,112,256]{4,3,2,1,0:T(8,128)} %chain0.13.refs_0_), channel_id=1, source_target_pairs={{0,16},{8,24},{16,0},{24,8},{1,17},{9,25},{17,1},{25,9},{2,18},{10... | collective-permute-start | bytes 2752520 | tf_op jit(solution)/shard_map/ppermute | solution.py:437
  273.9 54.6 %all-to-all-start.3 = ((f32[32,8,896]{2,1,0:T(8,128)}), f32[32,8,896]{2,1,0:T(8,128)}, u32[]{:S(2)}, u32[]{:S(2)}) async-start(f32[32,8,896]{2,1,0:T(8,128)} %finish.12.refs_0_), calls=%async_computation.3 | async-start | bytes 1835008 | tf_op jit(solution)/shard_map/all_to_all | solution.py:405
  285.1 80.1 %collective-permute-start.21 = (f32[2,704,256]{2,1,0:T(8,128)}, f32[2,704,256]{2,1,0:T(8,128)}, u32[]{:S(2)}, u32[]{:S(2)}) collective-permute-start(f32[2,704,256]{2,1,0:T(8,128)} %get-tuple-element.88.refs_0_), channel_id=1, source_target_pairs={{0,8},{8,0},{16,24},{24,16},{1,9},{9,1},{17,25},{25,17},{2,10},{10... | collective-permute-start | bytes 4325384 | tf_op jit(solution)/shard_map/ppermute | solution.py:394
  292.7 119.1 %collective-permute-start.22 = (f32[2,448,256]{2,1,0:T(8,128)}, f32[2,448,256]{2,1,0:T(8,128)}, u32[]{:S(2)}, u32[]{:S(2)}) collective-permute-start(f32[2,448,256]{2,1,0:T(8,128)} %get-tuple-element.95), channel_id=1, source_target_pairs={{0,8},{8,0},{16,24},{24,16},{1,9},{9,1},{17,25},{25,17},{2,10},{10... | collective-permute-start | bytes 2752520 | tf_op jit(solution)/shard_map/ppermute | solution.py:394
  334.3 54.6 %all-to-all-start.4 = ((f32[32,8,896]{2,1,0:T(8,128)}), f32[32,8,896]{2,1,0:T(8,128)}, u32[]{:S(2)}, u32[]{:S(2)}) async-start(f32[32,8,896]{2,1,0:T(8,128)} %finish.13.refs_0_), calls=%async_computation.4 | async-start | bytes 1835008 | tf_op jit(solution)/shard_map/all_to_all | solution.py:405
  345.1 93.6 %collective-permute-start.28 = (f32[2,704,256]{2,1,0:T(8,128)}, f32[2,704,256]{2,1,0:T(8,128)}, u32[]{:S(2)}, u32[]{:S(2)}) collective-permute-start(f32[2,704,256]{2,1,0:T(8,128)} %get-tuple-element.92.refs_0_), channel_id=1, source_target_pairs={{0,8},{8,0},{16,24},{24,16},{1,9},{9,1},{17,25},{25,17},{2,10},{10... | collective-permute-start | bytes 4325384 | tf_op jit(solution)/shard_map/ppermute | solution.py:394
  352.7 111.9 %collective-permute-start.31 = (f32[2,448,256]{2,1,0:T(8,128)}, f32[2,448,256]{2,1,0:T(8,128)}, u32[]{:S(2)}, u32[]{:S(2)}) collective-permute-start(f32[2,448,256]{2,1,0:T(8,128)} %get-tuple-element.108), channel_id=1, source_target_pairs={{0,8},{8,0},{16,24},{24,16},{1,9},{9,1},{17,25},{25,17},{2,10},{10... | collective-permute-start | bytes 2752520 | tf_op jit(solution)/shard_map/ppermute | solution.py:394
  394.7 54.6 %all-to-all-start.5 = ((f32[32,8,896]{2,1,0:T(8,128)}), f32[32,8,896]{2,1,0:T(8,128)}, u32[]{:S(2)}, u32[]{:S(2)}) async-start(f32[32,8,896]{2,1,0:T(8,128)} %finish.14.refs_0_), calls=%async_computation.5 | async-start | bytes 1835008 | tf_op jit(solution)/shard_map/all_to_all | solution.py:405
  404.2 74.3 %collective-permute-start.29 = (f32[1,704,256]{2,1,0:T(8,128)}, f32[1,704,256]{2,1,0:T(8,128)}, u32[]{:S(2)}, u32[]{:S(2)}) collective-permute-start(f32[1,704,256]{2,1,0:T(8,128)} %get-tuple-element.100.refs_0_), channel_id=1, source_target_pairs={{0,8},{8,0},{16,24},{24,16},{1,9},{9,1},{17,25},{25,17},{2,10},{10... | collective-permute-start | bytes 2162696 | tf_op jit(solution)/shard_map/ppermute | solution.py:394
  411.8 91.7 %collective-permute-start.30 = (f32[1,448,256]{2,1,0:T(8,128)}, f32[1,448,256]{2,1,0:T(8,128)}, u32[]{:S(2)}, u32[]{:S(2)}) collective-permute-start(f32[1,448,256]{2,1,0:T(8,128)} %get-tuple-element.106), channel_id=1, source_target_pairs={{0,8},{8,0},{16,24},{24,16},{1,9},{9,1},{17,25},{25,17},{2,10},{10... | collective-permute-start | bytes 1376264 | tf_op jit(solution)/shard_map/ppermute | solution.py:394
  (25 other events, 555.6 us)

commit v5 on v4

--- a/solution.py
+++ b/solution.py
@@ -42,7 +42,7 @@
     return row, column
 
 
-def prepare_body(carry, blocks, scalars, rates, chan, recv, *refs):
+def prepare_body(carry, blocks, base, pair, group, hop_offset, rates, chan, recv, *refs):
     outs = refs[len(refs) - blocks // 2 :]
     users = chan.shape[2]
     rows = recv.shape[2] // blocks
@@ -50,7 +50,9 @@
     def stacked(part):
         pieces = [chan[0, part]]
         for place in range(blocks):
-            first = pl.multiple_of(scalars[1 + place] * rows, 8)
+            first_hop = 2 * pair[0] + (place % 2) - 2 * (place // 2)
+            block = lax.rem(first_hop - hop_offset[group[0]] + 4 * blocks, blocks)
+            first = pl.multiple_of(block * rows, 8)
             pieces.append(recv[0, part, pl.ds(first, rows), :])
         return split(jnp.concatenate(pieces, 0))
 
@@ -76,7 +78,7 @@
         outs[0][0, users + 4 * rows :] = jnp.where(lane == 0, rates[0, 0], rates[0, 1])
 
 
-def prepare(channel, received, step_sizes, scalars, count, blocks, carry, after):
+def prepare(channel, received, step_sizes, scalars, start, count, blocks, carry, after):
     _, _, users, width = channel.shape
     symbols = received.shape[2]
     rows = symbols // blocks
@@ -85,20 +87,20 @@
         functools.partial(prepare_body, carry, blocks),
         out_shape=[jax.ShapeDtypeStruct((count, height, users), F32) for height in heights],
         grid_spec=pltpu.PrefetchScalarGridSpec(
-            num_scalar_prefetch=1,
+            num_scalar_prefetch=4,
             grid=(count,),
             in_specs=[
                 SMEM,
-                pl.BlockSpec((1, 2, users, width), lambda i, s: (s[0] + i, 0, 0, 0)),
-                pl.BlockSpec((1, 2, symbols, width), lambda i, s: (s[0] + i, 0, 0, 0)),
+                pl.BlockSpec((1, 2, users, width), lambda i, s, *_: (s[0] + start + i, 0, 0, 0)),
+                pl.BlockSpec((1, 2, symbols, width), lambda i, s, *_: (s[0] + start + i, 0, 0, 0)),
             ]
             + [ANY] * len(after),
-            out_specs=[pl.BlockSpec((1, height, users), lambda i, s: (i, 0, 0)) for height in heights],
+            out_specs=[pl.BlockSpec((1, height, users), lambda i, *_: (i, 0, 0)) for height in heights],
         ),
         compiler_params=pltpu.CompilerParams(vmem_limit_bytes=VMEM_LIMIT),
         cost_estimate=HEAVY,
         name="prepare",
-    )(scalars, step_sizes, channel, received, *after)
+    )(*scalars, step_sizes, channel, received, *after)
 
 
 def unpack(packed, gram, sub):
@@ -265,7 +267,6 @@
     out, tones_first, symbols_first = refs[-3:]
     items = out.shape[0]
     tones = sum(sizes)
-    depth = tones_first.shape[0]
     pair = pl.program_id(0)
     part = pl.program_id(1)
 
@@ -286,12 +287,14 @@
 
         lax.fori_loop(0, groups, gather, 0)
         for item in range(items):
-            high, low = split(tones_first[:, item, :].T[:rows])
+            value = tones_first[:, item, :]
             here = slice((slot * items + item) * rows, (slot * items + item + 1) * rows)
             if folded:
-                for k, value in enumerate((high, high, low)):
-                    symbols_first[0, here, k * depth : (k + 1) * depth] = value
+                high = value.astype(BF16).astype(F32)
+                joined = jnp.concatenate([high, high, value - high], 0)
+                symbols_first[0, here] = joined.T[:rows].astype(BF16)
             else:
+                high, low = split(value.T[:rows])
                 symbols_first[0, here] = high
                 symbols_first[1, here] = low
 
@@ -368,14 +371,12 @@
     swap = [(p, p ^ 1) for p in range(blocks)]
     onward = [(p, (p + 2) % blocks) for p in range(blocks)]
 
-    sizes = [1] + [2] * ((half - 2) // 2) + [1]
-    sizes += [1] * (half - sum(sizes))
+    doubles = max((half - 4) // 2, 0)
+    sizes = [1] + [2] * doubles + [1] * (half - 1 - 2 * doubles)
     starts = [sum(sizes[:c]) for c in range(len(sizes))]
     chunks = len(sizes)
 
-    order_of_blocks = []
-    for r in range(pairs):
-        order_of_blocks += [(2 * (pair - r) - offset) % blocks, (2 * (pair - r) + 1 - offset) % blocks]
+    place = (pair.reshape(1), lax.axis_index("tones").reshape(1), hop_offset)
     side_alone = side.reshape(1)
     side_and_slot = jnp.stack([side, offset % 2])
     order = (user_order[:, None] == jnp.arange(users, dtype=jnp.int32)[None, :]).astype(BF16)
@@ -386,8 +387,10 @@
     own, peer, odd, pieces = {}, {}, {}, []
 
     def ready(c, first_tone, carry, after):
-        scalars = jnp.stack([first_tone + starts[c]] + order_of_blocks)
-        return prepare(channel, received, step_sizes, scalars, sizes[c], blocks, carry, after)
+        scalars = (first_tone.reshape(1),) + place
+        return prepare(
+            channel, received, step_sizes, scalars, starts[c], sizes[c], blocks, carry, after
+        )
 
     def ready_peer(c, after):
         sent = ready(c, (1 - side) * half, 8 if c == 0 else 0, after)
@@ -430,11 +433,14 @@
         jnp.concatenate([step_sizes, peer_rates], 0),
         jnp.concatenate([peer_rates, step_sizes], 0),
     )
-    early = max(chunks - 4, 0)
+    early = max(chunks - 6, 0)
     total = None
     for c in range(chunks):
         before = chain(0, False, rows, side_alone, rates, own[c], peer[c], [], [before])
         both = lax.ppermute(before, "blk", onward)
+        if early and c == early + 2:
+            total = bring_together(0, early, None, False, [before])
+            before = total
         if c > 0:
             before = complete(c - 1, [before] + pieces[-1:])
         if c + 2 < chunks:
@@ -449,9 +455,6 @@
         even, moving = done
         odd[c] = (even, lax.ppermute(moving, "blk", onward))
         before = even
-        if early and c == early + 1:
-            total = bring_together(0, early, None, False, [before])
-            before = total
     before = complete(chunks - 1, [before] + pieces[-1:])
     if early < chunks - 1:
         total = bring_together(early, chunks - 1, total, False, [before])

time: 575 us -> 568 us (0.988)
  waiting for transfers between devices: 157 us -> 144 us
  local copies, waits for them, and re-layouts: 13.2 us -> 1.4 us
  starting transfers between devices: 92.3 us -> 103 us
  Pallas kernels: 294 us -> 304 us
    all_to_all x9 -> x10, waiting for transfers between devices: 86.8 us -> 56.6 us  [complete(): lax.all_to_all(done, ('blk', 'tones'), split_axis=0, concat_axis=0, tiled...]
    ppermute x9 -> x10, waiting for transfers between devices: 24.1 us -> 39.2 us  [on_device(): odd[c] = (even, lax.ppermute(moving, 'blk', onward))]
    another operation x18 -> x0, local copies, waits for them, and re-layouts: 11.2 us -> none  [ready(): scalars = jnp.stack([first_tone + starts[c]] + order_of_blocks)]
    ppermute x18 -> x20, waiting for transfers between devices: 39.6 us -> 48.1 us  [ready_peer(): peer[c] = [lax.ppermute(value, 'blk', swap) for value in sent]]
    ppermute x9 -> x10, waiting for transfers between devices: 6.63 us -> 0.03 us  [on_device(): both = lax.ppermute(before, 'blk', onward)]
    ppermute x18 -> x20, starting transfers between devices: 19.4 us -> 25.8 us  [ready_peer(): peer[c] = [lax.ppermute(value, 'blk', swap) for value in sent]]
    pallas_call x18 -> x20, Pallas kernels: 97.2 us -> 103 us  [prepare(): pl.pallas_call(functools.partial(prepare_body, carry, blocks), out_shape=...]
    all_to_all x9 -> x10, starting transfers between devices: 45.1 us -> 49.3 us  [complete(): lax.all_to_all(done, ('blk', 'tones'), split_axis=0, concat_axis=0, tiled...]
  transfers between devices with their start and end apart: 45 -> 50, of which waited for: 21 -> 21; matrix products, arithmetic and copies ran while one was open for 2% -> 1% of each run, Pallas kernels for 48% -> 51%
where the time goes in v5:
time: 568 us; the launch traced here: 558 us
  Pallas kernels  304 us (54%)
  waiting for transfers between devices  144 us (25%)
  starting transfers between devices  103 us (18%)
    pallas_call x20, Pallas kernels, chain(): pl.pallas_call(functools.partial(chain_body, round_index, last, rows), ou...  107 us
    pallas_call x20, Pallas kernels, prepare(): pl.pallas_call(functools.partial(prepare_body, carry, blocks), out_shape=...  103 us
    all_to_all x10, waiting for transfers between devices, complete(): lax.all_to_all(done, ('blk', 'tones'), split_axis=0, concat_axis=0, tiled...  56.6 us
    pallas_call x10, Pallas kernels, finish(): pl.pallas_call(functools.partial(finish_body, count, rows), out_shape=jax...  51.9 us
    all_to_all x10, starting transfers between devices, complete(): lax.all_to_all(done, ('blk', 'tones'), split_axis=0, concat_axis=0, tiled...  49.3 us
    ppermute x20, waiting for transfers between devices, ready_peer(): peer[c] = [lax.ppermute(value, 'blk', swap) for value in sent]  48.1 us
    pallas_call x3, Pallas kernels, despread(): pl.pallas_call(functools.partial(despread_body, groups, sizes, rows, fold...  42.2 us
    ppermute x10, waiting for transfers between devices, on_device(): odd[c] = (even, lax.ppermute(moving, 'blk', onward))  39.2 us
  transfers between devices with their start and end apart: 50, of which 21 were waited for; matrix products, arithmetic and copies ran while one was open for 1% of the time, Pallas kernels for 51%

profile of v5, /device:TPU:0, one launch (start us, length us, event | category | flops | bytes accessed | tf_op | source)
XLA Modules:
  0.0 558.0 jit_solution(13260570193195828576)
XLA Ops:
  7.2 5.8 %prepare.21 = (f32[2,704,256]{2,1,0:T(8,128)}, f32[2,448,256]{2,1,0:T(8,128)}) custom-call(s32[1]{0:T(128)} %bitcast.3.base, s32[1]{0:T(128)} %bitcast.4.pair, s32[1]{0:T(128)} %bitcast.5.group, s32[8]{0:T(128)} %hop_offset.39, f32[1,2]{1,0:T(1,128)} %rates.39, f32[32,2,256,256]{3,2,1,0:T(8,128)} %chan.39, f32[32,2,448,256]{3,2,1,0:T(8,128)} %recv.39, ...), custom_call_target="tpu_custom_call" | custom-call | flops 9999999827968 | bytes 10000000000 | tf_op jit(solution)/shard_map/prepare/pallas_call | solution.py:86
  29.7 5.7 %prepare.23 = (f32[2,704,256]{2,1,0:T(8,128)}, f32[2,448,256]{2,1,0:T(8,128)}) custom-call(s32[1]{0:T(128)} %bitcast.3.base, s32[1]{0:T(128)} %bitcast.4.pair, s32[1]{0:T(128)} %bitcast.5.group, s32[8]{0:T(128)} %hop_offset.39, f32[1,2]{1,0:T(1,128)} %rates.39, f32[32,2,256,256]{3,2,1,0:T(8,128)} %chan.39, f32[32,2,448,256]{3,2,1,0:T(8,128)} %recv.39, ...), custom_call_target="tpu_custom_call" | custom-call | flops 9999999827968 | bytes 10000000000 | tf_op jit(solution)/shard_map/prepare/pallas_call | solution.py:86
  44.7 40.3 %collective-permute-done.3.refs_3_ = f32[1,448,256]{2,1,0:T(8,128)} collective-permute-done((f32[1,448,256]{2,1,0:T(8,128)}, f32[1,448,256]{2,1,0:T(8,128)}, u32[]{:S(2)}, u32[]{:S(2)}) %collective-permute-start.3) | collective-permute-done | bytes 458784 | tf_op jit(solution)/shard_map/ppermute | solution.py:397
  122.2 6.9 %chain1.11 = (f32[2,2,112,256]{3,2,1,0:T(8,128)}, f32[2,2,112,256]{3,2,1,0:T(8,128)}) custom-call(s32[1]{0:T(128)} %bitcast.side, f32[2,2]{1,0:T(2,128)} %maximum_select_fusion.rates, f32[2,704,256]{2,1,0:T(8,128)} %get-tuple-element.69.refs_5_.refs_0_.own, f32[2,704,256]{2,1,0:T(8,128)} %collective-permute-done.1.refs_1_.peer, ...), custom_call_target="tpu_custom_call" | custom-call | flops 9999999827968 | bytes 10000000000 | tf_op jit(solution)/shard_map/chain1/pallas_call | solution.py:179
  136.5 6.2 %all-to-all-done.refs_1_.refs_0_ = f32[32,8,448]{2,1,0:T(8,128)} async-done(((f32[32,8,448]{2,1,0:T(8,128)}), f32[32,8,448]{2,1,0:T(8,128)}, u32[]{:S(2)}, u32[]{:S(2)}) %all-to-all-start) | async-done | bytes 458784 | tf_op jit(solution)/shard_map/all_to_all | solution.py:408
  143.5 5.8 %finish.11.refs_0_ = f32[32,8,896]{2,1,0:T(8,128)} custom-call(s32[2]{0:T(128)} %pad_add_fusion.scalars, f32[2,2]{1,0:T(2,128)} %maximum_select_fusion.rates, f32[2,704,256]{2,1,0:T(8,128)} %get-tuple-element.69.refs_5_.refs_0_.own, f32[2,704,256]{2,1,0:T(8,128)} %collective-permute-done.1.refs_1_.peer, f32[2,2,112,256]{3,2,1,0:T(8,128)} %get-tuple-element.78.refs_2_.even, ...), custom_call_target="tpu_custom_call" | custom-call | flops 9999999827968 | bytes 10000000000 | tf_op jit(solution)/shard_map/finish/pallas_call | solution.py:236
  155.0 6.4 %all-to-all-start.1 = ((f32[32,8,896]{2,1,0:T(8,128)}), f32[32,8,896]{2,1,0:T(8,128)}, u32[]{:S(2)}, u32[]{:S(2)}) async-start(f32[32,8,896]{2,1,0:T(8,128)} %finish.11.refs_0_), calls=%async_computation.1 | async-start | bytes 1835008 | tf_op jit(solution)/shard_map/all_to_all | solution.py:408
  169.1 6.9 %chain1.12 = (f32[2,2,112,256]{3,2,1,0:T(8,128)}, f32[2,2,112,256]{3,2,1,0:T(8,128)}) custom-call(s32[1]{0:T(128)} %bitcast.side, f32[2,2]{1,0:T(2,128)} %maximum_select_fusion.rates, f32[2,704,256]{2,1,0:T(8,128)} %get-tuple-element.77.refs_5_.refs_0_.own, f32[2,704,256]{2,1,0:T(8,128)} %collective-permute-done.8.refs_1_.peer, ...), custom_call_target="tpu_custom_call" | custom-call | flops 9999999827968 | bytes 10000000000 | tf_op jit(solution)/shard_map/chain1/pallas_call | solution.py:179
  184.6 6.4 %collective-permute-done.14.odd = f32[2,2,112,256]{3,2,1,0:T(8,128)} collective-permute-done((f32[2,2,112,256]{3,2,1,0:T(8,128)}, f32[2,2,112,256]{3,2,1,0:T(8,128)}, u32[]{:S(2)}, u32[]{:S(2)}) %collective-permute-start.14) | collective-permute-done | bytes 458784 | tf_op jit(solution)/shard_map/ppermute | solution.py:456
  191.0 12.1 %all-to-all-done.1.refs_1_ = f32[32,8,896]{2,1,0:T(8,128)} async-done(((f32[32,8,896]{2,1,0:T(8,128)}), f32[32,8,896]{2,1,0:T(8,128)}, u32[]{:S(2)}, u32[]{:S(2)}) %all-to-all-start.1) | async-done | bytes 917536 | tf_op jit(solution)/shard_map/all_to_all | solution.py:408
  203.2 5.8 %finish.12.refs_0_ = f32[32,8,896]{2,1,0:T(8,128)} custom-call(s32[2]{0:T(128)} %pad_add_fusion.scalars, f32[2,2]{1,0:T(2,128)} %maximum_select_fusion.rates, f32[2,704,256]{2,1,0:T(8,128)} %get-tuple-element.77.refs_5_.refs_0_.own, f32[2,704,256]{2,1,0:T(8,128)} %collective-permute-done.8.refs_1_.peer, f32[2,2,112,256]{3,2,1,0:T(8,128)} %get-tuple-element.86.refs_2_.even, ...), custom_call_target="tpu_custom_call" | custom-call | flops 9999999827968 | bytes 10000000000 | tf_op jit(solution)/shard_map/finish/pallas_call | solution.py:236
  227.8 6.9 %chain1.13 = (f32[2,2,112,256]{3,2,1,0:T(8,128)}, f32[2,2,112,256]{3,2,1,0:T(8,128)}) custom-call(s32[1]{0:T(128)} %bitcast.side, f32[2,2]{1,0:T(2,128)} %maximum_select_fusion.rates, f32[2,704,256]{2,1,0:T(8,128)} %get-tuple-element.81.refs_5_.refs_0_.own, f32[2,704,256]{2,1,0:T(8,128)} %collective-permute-done.9.refs_1_.peer, ...), custom_call_target="tpu_custom_call" | custom-call | flops 9999999827968 | bytes 10000000000 | tf_op jit(solution)/shard_map/chain1/pallas_call | solution.py:179
  249.7 13.9 %all-to-all-done.2.refs_1_.refs_2_ = f32[32,8,896]{2,1,0:T(8,128)} async-done(((f32[32,8,896]{2,1,0:T(8,128)}), f32[32,8,896]{2,1,0:T(8,128)}, u32[]{:S(2)}, u32[]{:S(2)}) %all-to-all-start.2) | async-done | bytes 917536 | tf_op jit(solution)/shard_map/all_to_all | solution.py:408
  287.8 6.9 %chain1.14 = (f32[2,2,112,256]{3,2,1,0:T(8,128)}, f32[2,2,112,256]{3,2,1,0:T(8,128)}) custom-call(s32[1]{0:T(128)} %bitcast.side, f32[2,2]{1,0:T(2,128)} %maximum_select_fusion.rates, f32[2,704,256]{2,1,0:T(8,128)} %get-tuple-element.89.refs_5_.refs_0_.own, f32[2,704,256]{2,1,0:T(8,128)} %collective-permute-done.16.refs_1_.peer, ...), custom_call_target="tpu_custom_call" | custom-call | flops 9999999827968 | bytes 10000000000 | tf_op jit(solution)/shard_map/chain1/pallas_call | solution.py:179
  309.6 14.3 %all-to-all-done.3.refs_1_.refs_3_ = f32[32,8,896]{2,1,0:T(8,128)} async-done(((f32[32,8,896]{2,1,0:T(8,128)}), f32[32,8,896]{2,1,0:T(8,128)}, u32[]{:S(2)}, u32[]{:S(2)}) %all-to-all-start.3) | async-done | bytes 917536 | tf_op jit(solution)/shard_map/all_to_all | solution.py:408
  324.0 5.7 %finish.14.refs_0_ = f32[32,8,896]{2,1,0:T(8,128)} custom-call(s32[2]{0:T(128)} %pad_add_fusion.scalars, f32[2,2]{1,0:T(2,128)} %maximum_select_fusion.rates, f32[2,704,256]{2,1,0:T(8,128)} %get-tuple-element.89.refs_5_.refs_0_.own, f32[2,704,256]{2,1,0:T(8,128)} %collective-permute-done.16.refs_1_.peer, f32[2,2,112,256]{3,2,1,0:T(8,128)} %get-tuple-element.98.refs_2_.even, ...), custom_call_target="tpu_custom_call" | custom-call | flops 9999999827968 | bytes 10000000000 | tf_op jit(solution)/shard_map/finish/pallas_call | solution.py:236
  346.9 6.9 %chain1.15 = (f32[2,2,112,256]{3,2,1,0:T(8,128)}, f32[2,2,112,256]{3,2,1,0:T(8,128)}) custom-call(s32[1]{0:T(128)} %bitcast.side, f32[2,2]{1,0:T(2,128)} %maximum_select_fusion.rates, f32[2,704,256]{2,1,0:T(8,128)} %get-tuple-element.93.refs_5_.refs_0_.own, f32[2,704,256]{2,1,0:T(8,128)} %collective-permute-done.17.refs_1_.peer, ...), custom_call_target="tpu_custom_call" | custom-call | flops 9999999827968 | bytes 10000000000 | tf_op jit(solution)/shard_map/chain1/pallas_call | solution.py:179
  367.3 13.9 %despread.3.refs_0_.refs_5_ = f32[8,2,448,256]{3,2,1,0:T(8,128)} custom-call(s32[32]{0:T(128)} %and_select_fusion.source, bf16[2,2,224,256]{3,2,1,0:T(8,128)(2,1)} %constant.88.clone.table, f32[32,8,448]{2,1,0:T(8,128)} %all-to-all-done.refs_1_.refs_0_, f32[32,8,896]{2,1,0:T(8,128)} %all-to-all-done.1.refs_1_, f32[32,8,896]{2,1,0:T(8,128)} %all-to-all-done.2.refs_1_.refs_2_, ...), custom_call_target="tpu_custom_call" | custom-call | flops 9999999827968 | bytes 10000000000 | tf_op jit(solution)/shard_map/despread/pallas_call | solution.py:336
  384.3 5.7 %finish.15.refs_0_ = f32[32,8,896]{2,1,0:T(8,128)} custom-call(s32[2]{0:T(128)} %pad_add_fusion.scalars, f32[2,2]{1,0:T(2,128)} %maximum_select_fusion.rates, f32[2,704,256]{2,1,0:T(8,128)} %get-tuple-element.93.refs_5_.refs_0_.own, f32[2,704,256]{2,1,0:T(8,128)} %collective-permute-done.17.refs_1_.peer, f32[2,2,112,256]{3,2,1,0:T(8,128)} %get-tuple-element.102.refs_2_.even, ...), custom_call_target="tpu_custom_call" | custom-call | flops 9999999827968 | bytes 10000000000 | tf_op jit(solution)/shard_map/finish/pallas_call | solution.py:236
  405.9 6.9 %chain1.16 = (f32[2,2,112,256]{3,2,1,0:T(8,128)}, f32[2,2,112,256]{3,2,1,0:T(8,128)}) custom-call(s32[1]{0:T(128)} %bitcast.side, f32[2,2]{1,0:T(2,128)} %maximum_select_fusion.rates, f32[2,704,256]{2,1,0:T(8,128)} %get-tuple-element.101.refs_5_.refs_0_.own, f32[2,704,256]{2,1,0:T(8,128)} %collective-permute-done.24.refs_1_.peer, ...), custom_call_target="tpu_custom_call" | custom-call | flops 9999999827968 | bytes 10000000000 | tf_op jit(solution)/shard_map/chain1/pallas_call | solution.py:179
  418.8 9.4 %collective-permute-done.30.odd = f32[2,2,112,256]{3,2,1,0:T(8,128)} collective-permute-done((f32[2,2,112,256]{3,2,1,0:T(8,128)}, f32[2,2,112,256]{3,2,1,0:T(8,128)}, u32[]{:S(2)}, u32[]{:S(2)}) %collective-permute-start.30) | collective-permute-done | bytes 458784 | tf_op jit(solution)/shard_map/ppermute | solution.py:456
  511.0 7.9 %collective-permute-done.39.odd = f32[1,2,112,256]{3,2,1,0:T(8,128)S(1)} collective-permute-done((f32[1,2,112,256]{3,2,1,0:T(8,128)}, f32[1,2,112,256]{3,2,1,0:T(8,128)S(1)}, u32[]{:S(2)}, u32[]{:S(2)}) %collective-permute-start.39) | collective-permute-done | bytes 229408 | tf_op jit(solution)/shard_map/ppermute | solution.py:456
  529.6 16.8 %despread.4.refs_1_ = f32[8,2,448,256]{3,2,1,0:T(8,128)} custom-call(s32[32]{0:T(128)} %and_select_fusion.source, bf16[2,2,256,256]{3,2,1,0:T(8,128)(2,1)} %constant.89.clone.table, f32[32,8,896]{2,1,0:T(8,128)} %all-to-all-done.4.refs_1_.refs_0_, f32[32,8,896]{2,1,0:T(8,128)} %all-to-all-done.5.refs_1_, f32[32,8,896]{2,1,0:T(8,128)} %all-to-all-done.6.refs_1_.refs_2_, ...), custom_call_target="tpu_custom_call" | custom-call | flops 9999999827968 | bytes 10000000000 | tf_op jit(solution)/shard_map/despread/pallas_call | solution.py:336
  546.4 11.5 %despread.5 = f32[8,2,448,256]{3,2,1,0:T(8,128)} custom-call(s32[32]{0:T(128)} %and_select_fusion.source, bf16[2,1,96,256]{3,2,1,0:T(8,128)(2,1)} %constant.90.clone.table, f32[32,8,448]{2,1,0:T(8,128)} %all-to-all-done.9.refs_0_, f32[8,2,448,256]{3,2,1,0:T(8,128)} %despread.4.refs_1_), custom_call_target="tpu_custom_call" | custom-call | flops 9999999827968 | bytes 10000000000 | tf_op jit(solution)/shard_map/despread/pallas_call | solution.py:336
  (147 shorter events, 320.5 us)
Async XLA Ops:
  13.1 80.1 %collective-permute-start.1 = (f32[2,704,256]{2,1,0:T(8,128)}, f32[2,704,256]{2,1,0:T(8,128)}, u32[]{:S(2)}, u32[]{:S(2)}) collective-permute-start(f32[2,704,256]{2,1,0:T(8,128)} %get-tuple-element.66.refs_0_), channel_id=1, source_target_pairs={{0,8},{8,0},{16,24},{24,16},{1,9},{9,1},{17,25},{25,17},{2,10},{10... | collective-permute-start | bytes 4325384 | tf_op jit(solution)/shard_map/ppermute | solution.py:397
  13.1 108.9 %collective-permute-start.2 = (f32[2,448,256]{2,1,0:T(8,128)}, f32[2,448,256]{2,1,0:T(8,128)}, u32[]{:S(2)}, u32[]{:S(2)}) collective-permute-start(f32[2,448,256]{2,1,0:T(8,128)} %get-tuple-element.71), channel_id=1, source_target_pairs={{0,8},{8,0},{16,24},{24,16},{1,9},{9,1},{17,25},{25,17},{2,10},{10... | collective-permute-start | bytes 2752520 | tf_op jit(solution)/shard_map/ppermute | solution.py:397
  15.1 70.0 %collective-permute-start.3 = (f32[1,448,256]{2,1,0:T(8,128)}, f32[1,448,256]{2,1,0:T(8,128)}, u32[]{:S(2)}, u32[]{:S(2)}) collective-permute-start(f32[1,448,256]{2,1,0:T(8,128)} %get-tuple-element.73), channel_id=1, source_target_pairs={{0,8},{8,0},{16,24},{24,16},{1,9},{9,1},{17,25},{25,17},{2,10},{10... | collective-permute-start | bytes 1376264 | tf_op jit(solution)/shard_map/ppermute | solution.py:397
  35.4 51.7 %collective-permute-start.4 = (f32[1,2,2,112,256]{4,3,2,1,0:T(8,128)}, f32[1,2,2,112,256]{4,3,2,1,0:T(8,128)}, u32[]{:S(2)}, u32[]{:S(2)}) collective-permute-start(f32[1,2,2,112,256]{4,3,2,1,0:T(8,128)} %chain0.10.refs_0_), channel_id=1, source_target_pairs={{0,16},{8,24},{16,0},{24,8},{1,17},{9,25},{17,1},{25,9},{2,18},{10... | collective-permute-start | bytes 1376264 | tf_op jit(solution)/shard_map/ppermute | solution.py:440
  43.2 87.7 %collective-permute-start.8 = (f32[2,704,256]{2,1,0:T(8,128)}, f32[2,704,256]{2,1,0:T(8,128)}, u32[]{:S(2)}, u32[]{:S(2)}) collective-permute-start(f32[2,704,256]{2,1,0:T(8,128)} %get-tuple-element.68.refs_0_), channel_id=1, source_target_pairs={{0,8},{8,0},{16,24},{24,16},{1,9},{9,1},{17,25},{25,17},{2,10},{10... | collective-permute-start | bytes 4325384 | tf_op jit(solution)/shard_map/ppermute | solution.py:397
  85.1 83.9 %collective-permute-start.11 = (f32[2,448,256]{2,1,0:T(8,128)}, f32[2,448,256]{2,1,0:T(8,128)}, u32[]{:S(2)}, u32[]{:S(2)}) collective-permute-start(f32[2,448,256]{2,1,0:T(8,128)} %get-tuple-element.85), channel_id=1, source_target_pairs={{0,8},{8,0},{16,24},{24,16},{1,9},{9,1},{17,25},{25,17},{2,10},{10... | collective-permute-start | bytes 2752520 | tf_op jit(solution)/shard_map/ppermute | solution.py:397
  120.1 57.8 %collective-permute-start.9 = (f32[2,704,256]{2,1,0:T(8,128)}, f32[2,704,256]{2,1,0:T(8,128)}, u32[]{:S(2)}, u32[]{:S(2)}) collective-permute-start(f32[2,704,256]{2,1,0:T(8,128)} %get-tuple-element.76.refs_0_), channel_id=1, source_target_pairs={{0,8},{8,0},{16,24},{24,16},{1,9},{9,1},{17,25},{25,17},{2,10},{10... | collective-permute-start | bytes 4325384 | tf_op jit(solution)/shard_map/ppermute | solution.py:397
  122.0 105.8 %collective-permute-start.10 = (f32[2,448,256]{2,1,0:T(8,128)}, f32[2,448,256]{2,1,0:T(8,128)}, u32[]{:S(2)}, u32[]{:S(2)}) collective-permute-start(f32[2,448,256]{2,1,0:T(8,128)} %get-tuple-element.83), channel_id=1, source_target_pairs={{0,8},{8,0},{16,24},{24,16},{1,9},{9,1},{17,25},{25,17},{2,10},{10... | collective-permute-start | bytes 2752520 | tf_op jit(solution)/shard_map/ppermute | solution.py:397
  155.0 48.2 %all-to-all-start.1 = ((f32[32,8,896]{2,1,0:T(8,128)}), f32[32,8,896]{2,1,0:T(8,128)}, u32[]{:S(2)}, u32[]{:S(2)}) async-start(f32[32,8,896]{2,1,0:T(8,128)} %finish.11.refs_0_), calls=%async_computation.1 | async-start | bytes 1835008 | tf_op jit(solution)/shard_map/all_to_all | solution.py:408
  167.1 71.0 %collective-permute-start.16 = (f32[2,704,256]{2,1,0:T(8,128)}, f32[2,704,256]{2,1,0:T(8,128)}, u32[]{:S(2)}, u32[]{:S(2)}) collective-permute-start(f32[2,704,256]{2,1,0:T(8,128)} %get-tuple-element.80.refs_0_), channel_id=1, source_target_pairs={{0,8},{8,0},{16,24},{24,16},{1,9},{9,1},{17,25},{25,17},{2,10},{10... | collective-permute-start | bytes 4325384 | tf_op jit(solution)/shard_map/ppermute | solution.py:397
  168.9 118.8 %collective-permute-start.19 = (f32[2,448,256]{2,1,0:T(8,128)}, f32[2,448,256]{2,1,0:T(8,128)}, u32[]{:S(2)}, u32[]{:S(2)}) collective-permute-start(f32[2,448,256]{2,1,0:T(8,128)} %get-tuple-element.97), channel_id=1, source_target_pairs={{0,8},{8,0},{16,24},{24,16},{1,9},{9,1},{17,25},{25,17},{2,10},{10... | collective-permute-start | bytes 2752520 | tf_op jit(solution)/shard_map/ppermute | solution.py:397
  183.3 44.5 %collective-permute-start.13 = (f32[2,2,2,112,256]{4,3,2,1,0:T(8,128)}, f32[2,2,2,112,256]{4,3,2,1,0:T(8,128)}, u32[]{:S(2)}, u32[]{:S(2)}) collective-permute-start(f32[2,2,2,112,256]{4,3,2,1,0:T(8,128)} %chain0.13.refs_0_), channel_id=1, source_target_pairs={{0,16},{8,24},{16,0},{24,8},{1,17},{9,25},{17,1},{25,9},{2,18},{10... | collective-permute-start | bytes 2752520 | tf_op jit(solution)/shard_map/ppermute | solution.py:440
  214.6 48.9 %all-to-all-start.2 = ((f32[32,8,896]{2,1,0:T(8,128)}), f32[32,8,896]{2,1,0:T(8,128)}, u32[]{:S(2)}, u32[]{:S(2)}) async-start(f32[32,8,896]{2,1,0:T(8,128)} %finish.12.refs_0_), calls=%async_computation.2 | async-start | bytes 1835008 | tf_op jit(solution)/shard_map/all_to_all | solution.py:408
  225.9 72.6 %collective-permute-start.17 = (f32[2,704,256]{2,1,0:T(8,128)}, f32[2,704,256]{2,1,0:T(8,128)}, u32[]{:S(2)}, u32[]{:S(2)}) collective-permute-start(f32[2,704,256]{2,1,0:T(8,128)} %get-tuple-element.88.refs_0_), channel_id=1, source_target_pairs={{0,8},{8,0},{16,24},{24,16},{1,9},{9,1},{17,25},{25,17},{2,10},{10... | collective-permute-start | bytes 4325384 | tf_op jit(solution)/shard_map/ppermute | solution.py:397
  236.2 110.7 %collective-permute-start.18 = (f32[2,448,256]{2,1,0:T(8,128)}, f32[2,448,256]{2,1,0:T(8,128)}, u32[]{:S(2)}, u32[]{:S(2)}) collective-permute-start(f32[2,448,256]{2,1,0:T(8,128)} %get-tuple-element.95), channel_id=1, source_target_pairs={{0,8},{8,0},{16,24},{24,16},{1,9},{9,1},{17,25},{25,17},{2,10},{10... | collective-permute-start | bytes 2752520 | tf_op jit(solution)/shard_map/ppermute | solution.py:397
  275.0 49.0 %all-to-all-start.3 = ((f32[32,8,896]{2,1,0:T(8,128)}), f32[32,8,896]{2,1,0:T(8,128)}, u32[]{:S(2)}, u32[]{:S(2)}) async-start(f32[32,8,896]{2,1,0:T(8,128)} %finish.13.refs_0_), calls=%async_computation.3 | async-start | bytes 1835008 | tf_op jit(solution)/shard_map/all_to_all | solution.py:408
  285.9 73.5 %collective-permute-start.24 = (f32[2,704,256]{2,1,0:T(8,128)}, f32[2,704,256]{2,1,0:T(8,128)}, u32[]{:S(2)}, u32[]{:S(2)}) collective-permute-start(f32[2,704,256]{2,1,0:T(8,128)} %get-tuple-element.92.refs_0_), channel_id=1, source_target_pairs={{0,8},{8,0},{16,24},{24,16},{1,9},{9,1},{17,25},{25,17},{2,10},{10... | collective-permute-start | bytes 4325384 | tf_op jit(solution)/shard_map/ppermute | solution.py:397
  306.3 99.6 %collective-permute-start.27 = (f32[2,448,256]{2,1,0:T(8,128)}, f32[2,448,256]{2,1,0:T(8,128)}, u32[]{:S(2)}, u32[]{:S(2)}) collective-permute-start(f32[2,448,256]{2,1,0:T(8,128)} %get-tuple-element.109), channel_id=1, source_target_pairs={{0,8},{8,0},{16,24},{24,16},{1,9},{9,1},{17,25},{25,17},{2,10},{10... | collective-permute-start | bytes 2752520 | tf_op jit(solution)/shard_map/ppermute | solution.py:397
  334.0 50.3 %all-to-all-start.4 = ((f32[32,8,896]{2,1,0:T(8,128)}), f32[32,8,896]{2,1,0:T(8,128)}, u32[]{:S(2)}, u32[]{:S(2)}) async-start(f32[32,8,896]{2,1,0:T(8,128)} %finish.14.refs_0_), calls=%async_computation.4 | async-start | bytes 1835008 | tf_op jit(solution)/shard_map/all_to_all | solution.py:408
  345.0 69.4 %collective-permute-start.25 = (f32[1,704,256]{2,1,0:T(8,128)}, f32[1,704,256]{2,1,0:T(8,128)}, u32[]{:S(2)}, u32[]{:S(2)}) collective-permute-start(f32[1,704,256]{2,1,0:T(8,128)} %get-tuple-element.100.refs_0_), channel_id=1, source_target_pairs={{0,8},{8,0},{16,24},{24,16},{1,9},{9,1},{17,25},{25,17},{2,10},{10... | collective-permute-start | bytes 2162696 | tf_op jit(solution)/shard_map/ppermute | solution.py:397
  355.2 93.8 %collective-permute-start.26 = (f32[1,448,256]{2,1,0:T(8,128)}, f32[1,448,256]{2,1,0:T(8,128)}, u32[]{:S(2)}, u32[]{:S(2)}) collective-permute-start(f32[1,448,256]{2,1,0:T(8,128)} %get-tuple-element.107), channel_id=1, source_target_pairs={{0,8},{8,0},{16,24},{24,16},{1,9},{9,1},{17,25},{25,17},{2,10},{10... | collective-permute-start | bytes 1376264 | tf_op jit(solution)/shard_map/ppermute | solution.py:397
  404.0 51.5 %collective-permute-start.32 = (f32[1,704,256]{2,1,0:T(8,128)}, f32[1,704,256]{2,1,0:T(8,128)}, u32[]{:S(2)}, u32[]{:S(2)}) collective-permute-start(f32[1,704,256]{2,1,0:T(8,128)} %get-tuple-element.104.refs_0_), channel_id=1, source_target_pairs={{0,8},{8,0},{16,24},{24,16},{1,9},{9,1},{17,25},{25,17},{2,10},{10... | collective-permute-start | bytes 2162696 | tf_op jit(solution)/shard_map/ppermute | solution.py:397
  418.6 61.5 %collective-permute-start.35 = (f32[1,448,256]{2,1,0:T(8,128)}, f32[1,448,256]{2,1,0:T(8,128)}, u32[]{:S(2)}, u32[]{:S(2)}) collective-permute-start(f32[1,448,256]{2,1,0:T(8,128)} %get-tuple-element.120), channel_id=1, source_target_pairs={{0,8},{8,0},{16,24},{24,16},{1,9},{9,1},{17,25},{25,17},{2,10},{10... | collective-permute-start | bytes 1376264 | tf_op jit(solution)/shard_map/ppermute | solution.py:397
  455.0 49.8 %collective-permute-start.34 = (f32[1,448,256]{2,1,0:T(8,128)}, f32[1,448,256]{2,1,0:T(8,128)}, u32[]{:S(2)}, u32[]{:S(2)}) collective-permute-start(f32[1,448,256]{2,1,0:T(8,128)} %get-tuple-element.118), channel_id=1, source_target_pairs={{0,8},{8,0},{16,24},{24,16},{1,9},{9,1},{17,25},{25,17},{2,10},{10... | collective-permute-start | bytes 1376264 | tf_op jit(solution)/shard_map/ppermute | solution.py:397
  (31 other events, 637.2 us)

commit v6 on v5

--- a/solution.py
+++ b/solution.py
@@ -265,54 +265,49 @@
     if not first:
         total = refs[len(sizes)]
     out, tones_first, symbols_first = refs[-3:]
-    items = out.shape[0]
     tones = sum(sizes)
-    pair = pl.program_id(0)
-    part = pl.program_id(1)
-
-    def turn(slot):
-        block = 2 * pair + slot
-
-        def gather(group, carry):
-            position = source[block * groups + group]
-            for side in range(2):
-                place = (group * 2 + side) * tones * 2
-                src = (2 * position + side) * groups + group
-                for piece, size in zip(pieces, sizes):
-                    for tone in range(2 * size):
-                        lane = (tone * 2 + slot) * rows
-                        tones_first[place + tone, :, :rows] = piece[src, :, lane : lane + rows]
-                    place = place + 2 * size
-            return carry
-
-        lax.fori_loop(0, groups, gather, 0)
-        for item in range(items):
-            value = tones_first[:, item, :]
-            here = slice((slot * items + item) * rows, (slot * items + item + 1) * rows)
-            if folded:
-                high = value.astype(BF16).astype(F32)
-                joined = jnp.concatenate([high, high, value - high], 0)
-                symbols_first[0, here] = joined.T[:rows].astype(BF16)
-            else:
-                high, low = split(value.T[:rows])
-                symbols_first[0, here] = high
-                symbols_first[1, here] = low
-
-    @pl.when(part == 0)
+    length = out.shape[3]
+    blocks = tones_first.shape[0]
+    item = pl.program_id(0)
+
+    @pl.when(item == 0)
     def _():
-        for slot in range(2):
-            turn(slot)
-
+        for block in range(blocks):
+
+            def gather(group, carry):
+                position = source[block * groups + group]
+                for side in range(2):
+                    place = (group * 2 + side) * tones * 2
+                    src = (2 * position + side) * groups + group
+                    for piece, size in zip(pieces, sizes):
+                        for tone in range(2 * size):
+                            lane = (tone * 2 + block % 2) * rows
+                            tones_first[block, place + tone, :, :rows] = piece[src, :, lane : lane + rows]
+                        place = place + 2 * size
+                return carry
+
+            lax.fori_loop(0, groups, gather, 0)
+
+    for block in range(blocks):
+        value = tones_first[block, :, item, :]
+        here = slice(block * rows, (block + 1) * rows)
+        if folded:
+            high = value.astype(BF16).astype(F32)
+            joined = jnp.concatenate([high, high, value - high], 0)
+            symbols_first[0, here] = joined.T[:rows].astype(BF16)
+        else:
+            high, low = split(value.T[:rows])
+            symbols_first[0, here] = high
+            symbols_first[1, here] = low
     if folded:
-        result = dot(symbols_first[0], table[part, 0], (1, 0))
+        result = dot(symbols_first[0], table[0], (1, 0))
     else:
-        result = dot3((symbols_first[0], symbols_first[1]), (table[part, 0], table[part, 1]), (1, 0))
-    for slot in range(2):
-        for item in range(items):
-            value = result[(slot * items + item) * rows : (slot * items + item + 1) * rows]
-            if not first:
-                value = value + total[item, 0, slot * rows : (slot + 1) * rows, :]
-            out[item, 0, slot * rows : (slot + 1) * rows, :] = jnp.tanh(value) if last else value
+        result = dot3((symbols_first[0], symbols_first[1]), (table[0], table[1]), (1, 0))
+    for part in range(2):
+        value = result[:, part * length : (part + 1) * length]
+        if not first:
+            value = value + total[0, part]
+        out[0, part] = jnp.tanh(value) if last else value
 
 
 def despread(pieces, starts, groups, half, blocks, rows, source, total, last, after):
@@ -324,29 +319,30 @@
     index = (np.arange(groups * 2)[:, None] * half + local[None, :]).reshape(-1)
     angle = 2.0 * np.pi / length * (index[:, None] * np.arange(length)[None, :] % length)
     cosine, sine = np.cos(angle) / np.sqrt(length), np.sin(angle) / np.sqrt(length)
-    table = np.stack([np.stack([cosine, -sine], 1), np.stack([sine, cosine], 1)])
-    table = table.reshape(2, 1, 2 * len(index), length)
+    real, imag = np.concatenate([cosine, sine], 1), np.concatenate([-sine, cosine], 1)
+    table = np.stack([real, imag], 1).reshape(1, 2 * len(index), 2 * length)
     high = table.astype(ml_dtypes.bfloat16)
     low = (table - high.astype(np.float64)).astype(ml_dtypes.bfloat16)
-    depth = table.shape[2]
+    depth = table.shape[1]
     folded = 3 * depth <= 256
-    table = np.concatenate([high, low, high], 2) if folded else np.concatenate([high, low], 1)
-    block_spec = pl.BlockSpec((items, 1, 2 * rows, length), lambda i, part, s: (0, part, i, 0))
+    table = np.concatenate([high, low, high], 1) if folded else np.concatenate([high, low], 0)
+    symbols = blocks * rows
+    block_spec = pl.BlockSpec((1, 2, symbols, length), lambda i, s: (i, 0, 0, 0))
     totals = [] if total is None else [total]
     return pl.pallas_call(
         functools.partial(despread_body, groups, sizes, rows, folded, total is None, last),
-        out_shape=jax.ShapeDtypeStruct((items, 2, blocks * rows, length), F32),
+        out_shape=jax.ShapeDtypeStruct((items, 2, symbols, length), F32),
         grid_spec=pltpu.PrefetchScalarGridSpec(
             num_scalar_prefetch=1,
-            grid=(blocks // 2, 2),
-            in_specs=[pl.BlockSpec(table.shape, lambda i, part, s: (0, 0, 0, 0))]
-            + [pl.BlockSpec(piece.shape, lambda i, part, s: (0, 0, 0)) for piece in pieces]
+            grid=(items,),
+            in_specs=[pl.BlockSpec(table.shape, lambda i, s: (0, 0, 0))]
+            + [pl.BlockSpec(piece.shape, lambda i, s: (0, 0, 0)) for piece in pieces]
             + [block_spec] * len(totals)
             + [ANY] * len(after),
             out_specs=block_spec,
             scratch_shapes=[
-                pltpu.VMEM((depth, items, lanes), F32),
-                pltpu.VMEM((table.shape[1], 2 * items * rows, table.shape[2]), BF16),
+                pltpu.VMEM((blocks, depth, items, lanes), F32),
+                pltpu.VMEM((table.shape[0], symbols, table.shape[1]), BF16),
             ],
         ),
         compiler_params=pltpu.CompilerParams(vmem_limit_bytes=VMEM_LIMIT),
@@ -433,20 +429,26 @@
         jnp.concatenate([step_sizes, peer_rates], 0),
         jnp.concatenate([peer_rates, step_sizes], 0),
     )
-    early = max(chunks - 6, 0)
-    total = None
+    ahead = {c: [c + 1] for c in range(chunks - 1)}
+    parts = {}
+    if chunks > 8:
+        for c in (chunks - 2, chunks - 1):
+            ahead[c - 1].remove(c)
+            ahead[c - 4].append(c)
+        parts = {chunks - 4: chunks - 6, chunks - 2: chunks - 4}
+    begin, total = 0, None
     for c in range(chunks):
         before = chain(0, False, rows, side_alone, rates, own[c], peer[c], [], [before])
         both = lax.ppermute(before, "blk", onward)
-        if early and c == early + 2:
-            total = bring_together(0, early, None, False, [before])
-            before = total
+        if c in parts:
+            total = bring_together(begin, parts[c], total, False, [before])
+            begin, before = parts[c], total
         if c > 0:
             before = complete(c - 1, [before] + pieces[-1:])
         if c + 2 < chunks:
             before = ready_peer(c + 2, [before])
-        if c + 1 < chunks:
-            before = ready_own(c + 1, [before])
+        for other in ahead.get(c, []):
+            before = ready_own(other, [before])
         for r in range(1, pairs):
             done = chain(r, r == pairs - 1, rows, side_alone, rates, own[c], peer[c], [both], [before])
             if r < pairs - 1:
@@ -456,8 +458,8 @@
         odd[c] = (even, lax.ppermute(moving, "blk", onward))
         before = even
     before = complete(chunks - 1, [before] + pieces[-1:])
-    if early < chunks - 1:
-        total = bring_together(early, chunks - 1, total, False, [before])
+    if begin < chunks - 1:
+        total = bring_together(begin, chunks - 1, total, False, [before])
     return bring_together(chunks - 1, chunks, total, True, [])
 
 

time: 568 us -> 570 us (level)
  waiting for transfers between devices: 144 us -> 127 us
  Pallas kernels: 304 us -> 318 us
    ppermute x20, waiting for transfers between devices: 48.1 us -> 32 us  [ready_peer(): peer[c] = [lax.ppermute(value, 'blk', swap) for value in sent]]
    pallas_call x3 -> x4, Pallas kernels: 42.2 us -> 55.5 us  [despread(): pl.pallas_call(functools.partial(despread_body, groups, sizes, rows, fold...]
    ppermute x10, waiting for transfers between devices: 39.2 us -> 32.7 us  [on_device(): odd[c] = (even, lax.ppermute(moving, 'blk', onward))]
  transfers between devices with their start and end apart: 50 -> 50, of which waited for: 21 -> 20; matrix products, arithmetic and copies ran while one was open for 1% -> 1% of each run, Pallas kernels for 51% -> 53%
where the time goes in v6:
time: 570 us; the launch traced here: 559 us
  Pallas kernels  318 us (56%)
  waiting for transfers between devices  127 us (22%)
  starting transfers between devices  108 us (19%)
    pallas_call x20, Pallas kernels, chain(): pl.pallas_call(functools.partial(chain_body, round_index, last, rows), ou...  107 us
    pallas_call x20, Pallas kernels, prepare(): pl.pallas_call(functools.partial(prepare_body, carry, blocks), out_shape=...  103 us
    all_to_all x10, waiting for transfers between devices, complete(): lax.all_to_all(done, ('blk', 'tones'), split_axis=0, concat_axis=0, tiled...  60.8 us
    pallas_call x4, Pallas kernels, despread(): pl.pallas_call(functools.partial(despread_body, groups, sizes, rows, fold...  55.5 us
    pallas_call x10, Pallas kernels, finish(): pl.pallas_call(functools.partial(finish_body, count, rows), out_shape=jax...  51.4 us
    all_to_all x10, starting transfers between devices, complete(): lax.all_to_all(done, ('blk', 'tones'), split_axis=0, concat_axis=0, tiled...  50.7 us
    ppermute x10, waiting for transfers between devices, on_device(): odd[c] = (even, lax.ppermute(moving, 'blk', onward))  32.7 us
    ppermute x20, waiting for transfers between devices, ready_peer(): peer[c] = [lax.ppermute(value, 'blk', swap) for value in sent]  32 us
  transfers between devices with their start and end apart: 50, of which 20 were waited for; matrix products, arithmetic and copies ran while one was open for 1% of the time, Pallas kernels for 53%

profile of v6, /device:TPU:0, one launch (start us, length us, event | category | flops | bytes accessed | tf_op | source)
XLA Modules:
  0.0 559.4 jit_solution(5152452182585280369)
XLA Ops:
  7.3 5.8 %prepare.21 = (f32[2,704,256]{2,1,0:T(8,128)}, f32[2,448,256]{2,1,0:T(8,128)}) custom-call(s32[1]{0:T(128)} %bitcast.3.base, s32[1]{0:T(128)} %bitcast.4.pair, s32[1]{0:T(128)} %bitcast.5.group, s32[8]{0:T(128)} %hop_offset.39, f32[1,2]{1,0:T(1,128)} %rates.39, f32[32,2,256,256]{3,2,1,0:T(8,128)} %chan.39, f32[32,2,448,256]{3,2,1,0:T(8,128)} %recv.39, ...), custom_call_target="tpu_custom_call" | custom-call | flops 9999999827968 | bytes 10000000000 | tf_op jit(solution)/shard_map/prepare/pallas_call | solution.py:86
  53.2 12.3 %collective-permute-done.4.refs_1_.peer = f32[2,704,256]{2,1,0:T(8,128)} collective-permute-done((f32[2,704,256]{2,1,0:T(8,128)}, f32[2,704,256]{2,1,0:T(8,128)}, u32[]{:S(2)}, u32[]{:S(2)}) %collective-permute-start.4) | collective-permute-done | bytes 1441824 | tf_op jit(solution)/shard_map/ppermute | solution.py:393
  95.9 6.9 %chain1.11 = (f32[2,2,112,256]{3,2,1,0:T(8,128)}, f32[2,2,112,256]{3,2,1,0:T(8,128)}) custom-call(s32[1]{0:T(128)} %bitcast.side, f32[2,2]{1,0:T(2,128)} %maximum_select_fusion.rates, f32[2,704,256]{2,1,0:T(8,128)} %get-tuple-element.71.refs_5_.refs_0_.own, f32[2,704,256]{2,1,0:T(8,128)} %collective-permute-done.4.refs_1_.peer, ...), custom_call_target="tpu_custom_call" | custom-call | flops 9999999827968 | bytes 10000000000 | tf_op jit(solution)/shard_map/chain1/pallas_call | solution.py:179
  104.6 15.6 %collective-permute-done.5.refs_1_.peer = f32[2,704,256]{2,1,0:T(8,128)} collective-permute-done((f32[2,704,256]{2,1,0:T(8,128)}, f32[2,704,256]{2,1,0:T(8,128)}, u32[]{:S(2)}, u32[]{:S(2)}) %collective-permute-start.5) | collective-permute-done | bytes 1441824 | tf_op jit(solution)/shard_map/ppermute | solution.py:393
  127.8 15.1 %all-to-all-done.refs_1_.refs_0_ = f32[32,8,448]{2,1,0:T(8,128)} async-done(((f32[32,8,448]{2,1,0:T(8,128)}), f32[32,8,448]{2,1,0:T(8,128)}, u32[]{:S(2)}, u32[]{:S(2)}) %all-to-all-start) | async-done | bytes 458784 | tf_op jit(solution)/shard_map/all_to_all | solution.py:404
  142.8 5.8 %finish.11.refs_0_ = f32[32,8,896]{2,1,0:T(8,128)} custom-call(s32[2]{0:T(128)} %pad_add_fusion.scalars, f32[2,2]{1,0:T(2,128)} %maximum_select_fusion.rates, f32[2,704,256]{2,1,0:T(8,128)} %get-tuple-element.71.refs_5_.refs_0_.own, f32[2,704,256]{2,1,0:T(8,128)} %collective-permute-done.4.refs_1_.peer, f32[2,2,112,256]{3,2,1,0:T(8,128)} %get-tuple-element.80.refs_2_.even, ...), custom_call_target="tpu_custom_call" | custom-call | flops 9999999827968 | bytes 10000000000 | tf_op jit(solution)/shard_map/finish/pallas_call | solution.py:236
  167.2 6.9 %chain1.12 = (f32[2,2,112,256]{3,2,1,0:T(8,128)}, f32[2,2,112,256]{3,2,1,0:T(8,128)}) custom-call(s32[1]{0:T(128)} %bitcast.side, f32[2,2]{1,0:T(2,128)} %maximum_select_fusion.rates, f32[2,704,256]{2,1,0:T(8,128)} %get-tuple-element.75.refs_5_.refs_0_.own, f32[2,704,256]{2,1,0:T(8,128)} %collective-permute-done.5.refs_1_.peer, ...), custom_call_target="tpu_custom_call" | custom-call | flops 9999999827968 | bytes 10000000000 | tf_op jit(solution)/shard_map/chain1/pallas_call | solution.py:179
  189.1 14.1 %all-to-all-done.1.refs_1_ = f32[32,8,896]{2,1,0:T(8,128)} async-done(((f32[32,8,896]{2,1,0:T(8,128)}), f32[32,8,896]{2,1,0:T(8,128)}, u32[]{:S(2)}, u32[]{:S(2)}) %all-to-all-start.1) | async-done | bytes 917536 | tf_op jit(solution)/shard_map/all_to_all | solution.py:404
  220.1 5.8 %prepare.30 = (f32[2,704,256]{2,1,0:T(8,128)}, f32[2,448,256]{2,1,0:T(8,128)}) custom-call(s32[1]{0:T(128)} %bitcast.7.base, s32[1]{0:T(128)} %bitcast.4.pair, s32[1]{0:T(128)} %bitcast.5.group, s32[8]{0:T(128)} %hop_offset.39, f32[1,2]{1,0:T(1,128)} %rates.39, f32[32,2,256,256]{3,2,1,0:T(8,128)} %chan.39, f32[32,2,448,256]{3,2,1,0:T(8,128)} %recv.39, ...), custom_call_target="tpu_custom_call" | custom-call | flops 9999999827968 | bytes 10000000000 | tf_op jit(solution)/shard_map/prepare/pallas_call | solution.py:86
  227.8 6.9 %chain1.13 = (f32[2,2,112,256]{3,2,1,0:T(8,128)}, f32[2,2,112,256]{3,2,1,0:T(8,128)}) custom-call(s32[1]{0:T(128)} %bitcast.side, f32[2,2]{1,0:T(2,128)} %maximum_select_fusion.rates, f32[2,704,256]{2,1,0:T(8,128)} %get-tuple-element.83.refs_5_.refs_0_.own, f32[2,704,256]{2,1,0:T(8,128)} %collective-permute-done.12.refs_1_.peer, ...), custom_call_target="tpu_custom_call" | custom-call | flops 9999999827968 | bytes 10000000000 | tf_op jit(solution)/shard_map/chain1/pallas_call | solution.py:179
  249.7 13.9 %all-to-all-done.2.refs_1_.refs_2_ = f32[32,8,896]{2,1,0:T(8,128)} async-done(((f32[32,8,896]{2,1,0:T(8,128)}), f32[32,8,896]{2,1,0:T(8,128)}, u32[]{:S(2)}, u32[]{:S(2)}) %all-to-all-start.2) | async-done | bytes 917536 | tf_op jit(solution)/shard_map/all_to_all | solution.py:404
  263.6 5.8 %finish.13.refs_0_ = f32[32,8,896]{2,1,0:T(8,128)} custom-call(s32[2]{0:T(128)} %pad_add_fusion.scalars, f32[2,2]{1,0:T(2,128)} %maximum_select_fusion.rates, f32[2,704,256]{2,1,0:T(8,128)} %get-tuple-element.83.refs_5_.refs_0_.own, f32[2,704,256]{2,1,0:T(8,128)} %collective-permute-done.12.refs_1_.peer, f32[2,2,112,256]{3,2,1,0:T(8,128)} %get-tuple-element.92.refs_2_.even, ...), custom_call_target="tpu_custom_call" | custom-call | flops 9999999827968 | bytes 10000000000 | tf_op jit(solution)/shard_map/finish/pallas_call | solution.py:236
  292.1 6.9 %chain1.14 = (f32[2,2,112,256]{3,2,1,0:T(8,128)}, f32[2,2,112,256]{3,2,1,0:T(8,128)}) custom-call(s32[1]{0:T(128)} %bitcast.side, f32[2,2]{1,0:T(2,128)} %maximum_select_fusion.rates, f32[2,704,256]{2,1,0:T(8,128)} %get-tuple-element.87.refs_5_.refs_0_.own, f32[2,704,256]{2,1,0:T(8,128)} %collective-permute-done.13.refs_1_.peer, ...), custom_call_target="tpu_custom_call" | custom-call | flops 9999999827968 | bytes 10000000000 | tf_op jit(solution)/shard_map/chain1/pallas_call | solution.py:179
  313.7 10.3 %all-to-all-done.3.refs_1_.refs_3_ = f32[32,8,896]{2,1,0:T(8,128)} async-done(((f32[32,8,896]{2,1,0:T(8,128)}), f32[32,8,896]{2,1,0:T(8,128)}, u32[]{:S(2)}, u32[]{:S(2)}) %all-to-all-start.3) | async-done | bytes 917536 | tf_op jit(solution)/shard_map/all_to_all | solution.py:404
  351.3 6.9 %chain1.15 = (f32[2,2,112,256]{3,2,1,0:T(8,128)}, f32[2,2,112,256]{3,2,1,0:T(8,128)}) custom-call(s32[1]{0:T(128)} %bitcast.side, f32[2,2]{1,0:T(2,128)} %maximum_select_fusion.rates, f32[2,704,256]{2,1,0:T(8,128)} %get-tuple-element.95.refs_0_.own, f32[2,704,256]{2,1,0:T(8,128)} %collective-permute-done.20.refs_1_.peer, ...), custom_call_target="tpu_custom_call" | custom-call | flops 9999999827968 | bytes 10000000000 | tf_op jit(solution)/shard_map/chain1/pallas_call | solution.py:179
  368.8 13.8 %despread.4.refs_0_.refs_2_ = f32[8,2,448,256]{3,2,1,0:T(8,128)} custom-call(s32[32]{0:T(128)} %and_select_fusion.source, bf16[2,224,512]{2,1,0:T(8,128)(2,1)} %constant.90.clone.table, f32[32,8,448]{2,1,0:T(8,128)} %all-to-all-done.refs_1_.refs_0_, f32[32,8,896]{2,1,0:T(8,128)} %all-to-all-done.1.refs_1_, f32[32,8,896]{2,1,0:T(8,128)} %all-to-all-done.2.refs_1_.refs_2_, ...), custom_call_target="tpu_custom_call" | custom-call | flops 9999999827968 | bytes 10000000000 | tf_op jit(solution)/shard_map/despread/pallas_call | solution.py:332
  406.0 6.9 %chain1.16 = (f32[2,2,112,256]{3,2,1,0:T(8,128)}, f32[2,2,112,256]{3,2,1,0:T(8,128)}) custom-call(s32[1]{0:T(128)} %bitcast.side, f32[2,2]{1,0:T(2,128)} %maximum_select_fusion.rates, f32[2,704,256]{2,1,0:T(8,128)} %get-tuple-element.100.refs_0_.own, f32[2,704,256]{2,1,0:T(8,128)} %collective-permute-done.21.refs_1_.peer, ...), custom_call_target="tpu_custom_call" | custom-call | flops 9999999827968 | bytes 10000000000 | tf_op jit(solution)/shard_map/chain1/pallas_call | solution.py:179
  418.8 9.5 %collective-permute-done.27.odd = f32[2,2,112,256]{3,2,1,0:T(8,128)} collective-permute-done((f32[2,2,112,256]{3,2,1,0:T(8,128)}, f32[2,2,112,256]{3,2,1,0:T(8,128)}, u32[]{:S(2)}, u32[]{:S(2)}) %collective-permute-start.27) | collective-permute-done | bytes 458784 | tf_op jit(solution)/shard_map/ppermute | solution.py:458
  428.3 5.8 %finish.16.refs_0_ = f32[32,8,896]{2,1,0:T(8,128)} custom-call(s32[2]{0:T(128)} %pad_add_fusion.scalars, f32[2,2]{1,0:T(2,128)} %maximum_select_fusion.rates, f32[2,704,256]{2,1,0:T(8,128)} %get-tuple-element.100.refs_0_.own, f32[2,704,256]{2,1,0:T(8,128)} %collective-permute-done.21.refs_1_.peer, f32[2,2,112,256]{3,2,1,0:T(8,128)} %get-tuple-element.110.refs_2_.even, ...), custom_call_target="tpu_custom_call" | custom-call | flops 9999999827968 | bytes 10000000000 | tf_op jit(solution)/shard_map/finish/pallas_call | solution.py:236
  455.4 14.5 %despread.5.refs_0_.refs_3_ = f32[8,2,448,256]{3,2,1,0:T(8,128)} custom-call(s32[32]{0:T(128)} %and_select_fusion.source, bf16[2,128,512]{2,1,0:T(8,128)(2,1)} %constant.91.clone.table, f32[32,8,896]{2,1,0:T(8,128)} %all-to-all-done.4.refs_1_.refs_0_, f32[32,8,896]{2,1,0:T(8,128)} %all-to-all-done.5.refs_1_, f32[8,2,448,256]{3,2,1,0:T(8,128)} %despread.4.refs_0_.refs_2_, ...), custom_call_target="tpu_custom_call" | custom-call | flops 9999999827968 | bytes 10000000000 | tf_op jit(solution)/shard_map/despread/pallas_call | solution.py:332
  474.1 6.2 %all-to-all-start.7 = ((f32[32,8,448]{2,1,0:T(8,128)}), f32[32,8,448]{2,1,0:T(8,128)}, u32[]{:S(2)}, u32[]{:S(2)}) async-start(f32[32,8,448]{2,1,0:T(8,128)} %finish.17.refs_5_), calls=%async_computation.7 | async-start | bytes 1048576 | tf_op jit(solution)/shard_map/all_to_all | solution.py:404
  511.3 7.9 %collective-permute-done.39.odd = f32[1,2,112,256]{3,2,1,0:T(8,128)S(1)} collective-permute-done((f32[1,2,112,256]{3,2,1,0:T(8,128)}, f32[1,2,112,256]{3,2,1,0:T(8,128)S(1)}, u32[]{:S(2)}, u32[]{:S(2)}) %collective-permute-start.39) | collective-permute-done | bytes 229408 | tf_op jit(solution)/shard_map/ppermute | solution.py:458
  529.7 14.4 %despread.6.refs_1_ = f32[8,2,448,256]{3,2,1,0:T(8,128)} custom-call(s32[32]{0:T(128)} %and_select_fusion.source, bf16[2,128,512]{2,1,0:T(8,128)(2,1)} %constant.92.clone.table, f32[32,8,896]{2,1,0:T(8,128)} %all-to-all-done.6.refs_1_.refs_0_, f32[32,8,448]{2,1,0:T(8,128)} %all-to-all-done.7.refs_1_, f32[32,8,448]{2,1,0:T(8,128)} %all-to-all-done.8.refs_1_.refs_2_, ...), custom_call_target="tpu_custom_call" | custom-call | flops 9999999827968 | bytes 10000000000 | tf_op jit(solution)/shard_map/despread/pallas_call | solution.py:332
  546.1 12.8 %despread.7 = f32[8,2,448,256]{3,2,1,0:T(8,128)} custom-call(s32[32]{0:T(128)} %and_select_fusion.source, bf16[1,96,512]{2,1,0:T(8,128)(2,1)} %constant.93.clone.table, f32[32,8,448]{2,1,0:T(8,128)} %all-to-all-done.9.refs_0_, f32[8,2,448,256]{3,2,1,0:T(8,128)} %despread.6.refs_1_), custom_call_target="tpu_custom_call" | custom-call | flops 9999999827968 | bytes 10000000000 | tf_op jit(solution)/shard_map/despread/pallas_call | solution.py:332
  (148 shorter events, 325.9 us)
Async XLA Ops:
  13.1 52.3 %collective-permute-start.4 = (f32[2,704,256]{2,1,0:T(8,128)}, f32[2,704,256]{2,1,0:T(8,128)}, u32[]{:S(2)}, u32[]{:S(2)}) collective-permute-start(f32[2,704,256]{2,1,0:T(8,128)} %get-tuple-element.66.refs_0_), channel_id=1, source_target_pairs={{0,8},{8,0},{16,24},{24,16},{1,9},{9,1},{17,25},{25,17},{2,10},{10... | collective-permute-start | bytes 4325384 | tf_op jit(solution)/shard_map/ppermute | solution.py:393
  15.1 80.6 %collective-permute-start.7 = (f32[2,448,256]{2,1,0:T(8,128)}, f32[2,448,256]{2,1,0:T(8,128)}, u32[]{:S(2)}, u32[]{:S(2)}) collective-permute-start(f32[2,448,256]{2,1,0:T(8,128)} %get-tuple-element.79), channel_id=1, source_target_pairs={{0,8},{8,0},{16,24},{24,16},{1,9},{9,1},{17,25},{25,17},{2,10},{10... | collective-permute-start | bytes 2752520 | tf_op jit(solution)/shard_map/ppermute | solution.py:393
  43.2 77.0 %collective-permute-start.5 = (f32[2,704,256]{2,1,0:T(8,128)}, f32[2,704,256]{2,1,0:T(8,128)}, u32[]{:S(2)}, u32[]{:S(2)}) collective-permute-start(f32[2,704,256]{2,1,0:T(8,128)} %get-tuple-element.70.refs_0_), channel_id=1, source_target_pairs={{0,8},{8,0},{16,24},{24,16},{1,9},{9,1},{17,25},{25,17},{2,10},{10... | collective-permute-start | bytes 4325384 | tf_op jit(solution)/shard_map/ppermute | solution.py:393
  44.7 122.3 %collective-permute-start.6 = (f32[2,448,256]{2,1,0:T(8,128)}, f32[2,448,256]{2,1,0:T(8,128)}, u32[]{:S(2)}, u32[]{:S(2)}) collective-permute-start(f32[2,448,256]{2,1,0:T(8,128)} %get-tuple-element.77), channel_id=1, source_target_pairs={{0,8},{8,0},{16,24},{24,16},{1,9},{9,1},{17,25},{25,17},{2,10},{10... | collective-permute-start | bytes 2752520 | tf_op jit(solution)/shard_map/ppermute | solution.py:393
  82.9 59.9 %all-to-all-start = ((f32[32,8,448]{2,1,0:T(8,128)}), f32[32,8,448]{2,1,0:T(8,128)}, u32[]{:S(2)}, u32[]{:S(2)}) async-start(f32[32,8,448]{2,1,0:T(8,128)} %finish.10.refs_0_), calls=%async_computation | async-start | bytes 1048576 | tf_op jit(solution)/shard_map/all_to_all | solution.py:404
  93.8 84.0 %collective-permute-start.12 = (f32[2,704,256]{2,1,0:T(8,128)}, f32[2,704,256]{2,1,0:T(8,128)}, u32[]{:S(2)}, u32[]{:S(2)}) collective-permute-start(f32[2,704,256]{2,1,0:T(8,128)} %get-tuple-element.74.refs_0_), channel_id=1, source_target_pairs={{0,8},{8,0},{16,24},{24,16},{1,9},{9,1},{17,25},{25,17},{2,10},{10... | collective-permute-start | bytes 4325384 | tf_op jit(solution)/shard_map/ppermute | solution.py:393
  95.7 132.1 %collective-permute-start.15 = (f32[2,448,256]{2,1,0:T(8,128)}, f32[2,448,256]{2,1,0:T(8,128)}, u32[]{:S(2)}, u32[]{:S(2)}) collective-permute-start(f32[2,448,256]{2,1,0:T(8,128)} %get-tuple-element.91), channel_id=1, source_target_pairs={{0,8},{8,0},{16,24},{24,16},{1,9},{9,1},{17,25},{25,17},{2,10},{10... | collective-permute-start | bytes 2752520 | tf_op jit(solution)/shard_map/ppermute | solution.py:393
  154.2 49.0 %all-to-all-start.1 = ((f32[32,8,896]{2,1,0:T(8,128)}), f32[32,8,896]{2,1,0:T(8,128)}, u32[]{:S(2)}, u32[]{:S(2)}) async-start(f32[32,8,896]{2,1,0:T(8,128)} %finish.11.refs_0_), calls=%async_computation.1 | async-start | bytes 1835008 | tf_op jit(solution)/shard_map/all_to_all | solution.py:404
  165.2 73.0 %collective-permute-start.13 = (f32[2,704,256]{2,1,0:T(8,128)}, f32[2,704,256]{2,1,0:T(8,128)}, u32[]{:S(2)}, u32[]{:S(2)}) collective-permute-start(f32[2,704,256]{2,1,0:T(8,128)} %get-tuple-element.82.refs_0_), channel_id=1, source_target_pairs={{0,8},{8,0},{16,24},{24,16},{1,9},{9,1},{17,25},{25,17},{2,10},{10... | collective-permute-start | bytes 4325384 | tf_op jit(solution)/shard_map/ppermute | solution.py:393
  167.0 125.1 %collective-permute-start.14 = (f32[2,448,256]{2,1,0:T(8,128)}, f32[2,448,256]{2,1,0:T(8,128)}, u32[]{:S(2)}, u32[]{:S(2)}) collective-permute-start(f32[2,448,256]{2,1,0:T(8,128)} %get-tuple-element.89), channel_id=1, source_target_pairs={{0,8},{8,0},{16,24},{24,16},{1,9},{9,1},{17,25},{25,17},{2,10},{10... | collective-permute-start | bytes 2752520 | tf_op jit(solution)/shard_map/ppermute | solution.py:393
  214.6 49.0 %all-to-all-start.2 = ((f32[32,8,896]{2,1,0:T(8,128)}), f32[32,8,896]{2,1,0:T(8,128)}, u32[]{:S(2)}, u32[]{:S(2)}) async-start(f32[32,8,896]{2,1,0:T(8,128)} %finish.12.refs_0_), calls=%async_computation.2 | async-start | bytes 1835008 | tf_op jit(solution)/shard_map/all_to_all | solution.py:404
  225.9 74.6 %collective-permute-start.20 = (f32[2,704,256]{2,1,0:T(8,128)}, f32[2,704,256]{2,1,0:T(8,128)}, u32[]{:S(2)}, u32[]{:S(2)}) collective-permute-start(f32[2,704,256]{2,1,0:T(8,128)} %get-tuple-element.86.refs_0_), channel_id=1, source_target_pairs={{0,8},{8,0},{16,24},{24,16},{1,9},{9,1},{17,25},{25,17},{2,10},{10... | collective-permute-start | bytes 4325384 | tf_op jit(solution)/shard_map/ppermute | solution.py:393
  243.6 48.5 %collective-permute-start.17 = (f32[2,2,2,112,256]{4,3,2,1,0:T(8,128)}, f32[2,2,2,112,256]{4,3,2,1,0:T(8,128)}, u32[]{:S(2)}, u32[]{:S(2)}) collective-permute-start(f32[2,2,2,112,256]{4,3,2,1,0:T(8,128)} %chain0.14.refs_0_), channel_id=1, source_target_pairs={{0,16},{8,24},{16,0},{24,8},{1,17},{9,25},{17,1},{25,9},{2,18},{10... | collective-permute-start | bytes 2752520 | tf_op jit(solution)/shard_map/ppermute | solution.py:442
  245.7 105.6 %collective-permute-start.23 = (f32[2,448,256]{2,1,0:T(8,128)}, f32[2,448,256]{2,1,0:T(8,128)}, u32[]{:S(2)}, u32[]{:S(2)}) collective-permute-start(f32[2,448,256]{2,1,0:T(8,128)} %get-tuple-element.105), channel_id=1, source_target_pairs={{0,8},{8,0},{16,24},{24,16},{1,9},{9,1},{17,25},{25,17},{2,10},{10... | collective-permute-start | bytes 2752520 | tf_op jit(solution)/shard_map/ppermute | solution.py:393
  275.0 49.0 %all-to-all-start.3 = ((f32[32,8,896]{2,1,0:T(8,128)}), f32[32,8,896]{2,1,0:T(8,128)}, u32[]{:S(2)}, u32[]{:S(2)}) async-start(f32[32,8,896]{2,1,0:T(8,128)} %finish.13.refs_0_), calls=%async_computation.3 | async-start | bytes 1835008 | tf_op jit(solution)/shard_map/all_to_all | solution.py:404
  285.9 73.8 %collective-permute-start.21 = (f32[2,704,256]{2,1,0:T(8,128)}, f32[2,704,256]{2,1,0:T(8,128)}, u32[]{:S(2)}, u32[]{:S(2)}) collective-permute-start(f32[2,704,256]{2,1,0:T(8,128)} %get-tuple-element.94.refs_0_), channel_id=1, source_target_pairs={{0,8},{8,0},{16,24},{24,16},{1,9},{9,1},{17,25},{25,17},{2,10},{10... | collective-permute-start | bytes 4325384 | tf_op jit(solution)/shard_map/ppermute | solution.py:393
  305.9 45.4 %collective-permute-start.24 = (f32[2,2,2,112,256]{4,3,2,1,0:T(8,128)}, f32[2,2,2,112,256]{4,3,2,1,0:T(8,128)}, u32[]{:S(2)}, u32[]{:S(2)}) collective-permute-start(f32[2,2,2,112,256]{4,3,2,1,0:T(8,128)} %chain0.15.refs_0_), channel_id=1, source_target_pairs={{0,16},{8,24},{16,0},{24,8},{1,17},{9,25},{17,1},{25,9},{2,18},{10... | collective-permute-start | bytes 2752520 | tf_op jit(solution)/shard_map/ppermute | solution.py:442
  306.5 99.5 %collective-permute-start.22 = (f32[2,448,256]{2,1,0:T(8,128)}, f32[2,448,256]{2,1,0:T(8,128)}, u32[]{:S(2)}, u32[]{:S(2)}) collective-permute-start(f32[2,448,256]{2,1,0:T(8,128)} %get-tuple-element.103), channel_id=1, source_target_pairs={{0,8},{8,0},{16,24},{24,16},{1,9},{9,1},{17,25},{25,17},{2,10},{10... | collective-permute-start | bytes 2752520 | tf_op jit(solution)/shard_map/ppermute | solution.py:393
  334.1 50.3 %all-to-all-start.4 = ((f32[32,8,896]{2,1,0:T(8,128)}), f32[32,8,896]{2,1,0:T(8,128)}, u32[]{:S(2)}, u32[]{:S(2)}) async-start(f32[32,8,896]{2,1,0:T(8,128)} %finish.14.refs_0_), calls=%async_computation.4 | async-start | bytes 1835008 | tf_op jit(solution)/shard_map/all_to_all | solution.py:404
  345.0 69.3 %collective-permute-start.28 = (f32[1,704,256]{2,1,0:T(8,128)}, f32[1,704,256]{2,1,0:T(8,128)}, u32[]{:S(2)}, u32[]{:S(2)}) collective-permute-start(f32[1,704,256]{2,1,0:T(8,128)} %get-tuple-element.99.refs_0_), channel_id=1, source_target_pairs={{0,8},{8,0},{16,24},{24,16},{1,9},{9,1},{17,25},{25,17},{2,10},{10... | collective-permute-start | bytes 2162696 | tf_op jit(solution)/shard_map/ppermute | solution.py:393
  367.3 77.4 %collective-permute-start.33 = (f32[1,448,256]{2,1,0:T(8,128)}, f32[1,448,256]{2,1,0:T(8,128)}, u32[]{:S(2)}, u32[]{:S(2)}) collective-permute-start(f32[1,448,256]{2,1,0:T(8,128)} %get-tuple-element.118), channel_id=1, source_target_pairs={{0,8},{8,0},{16,24},{24,16},{1,9},{9,1},{17,25},{25,17},{2,10},{10... | collective-permute-start | bytes 1376264 | tf_op jit(solution)/shard_map/ppermute | solution.py:393
  404.1 46.7 %collective-permute-start.31 = (f32[1,704,256]{2,1,0:T(8,128)}, f32[1,704,256]{2,1,0:T(8,128)}, u32[]{:S(2)}, u32[]{:S(2)}) collective-permute-start(f32[1,704,256]{2,1,0:T(8,128)} %get-tuple-element.108.refs_0_), channel_id=1, source_target_pairs={{0,8},{8,0},{16,24},{24,16},{1,9},{9,1},{17,25},{25,17},{2,10},{10... | collective-permute-start | bytes 2162696 | tf_op jit(solution)/shard_map/ppermute | solution.py:393
  418.6 61.7 %collective-permute-start.32 = (f32[1,448,256]{2,1,0:T(8,128)}, f32[1,448,256]{2,1,0:T(8,128)}, u32[]{:S(2)}, u32[]{:S(2)}) collective-permute-start(f32[1,448,256]{2,1,0:T(8,128)} %get-tuple-element.116), channel_id=1, source_target_pairs={{0,8},{8,0},{16,24},{24,16},{1,9},{9,1},{17,25},{25,17},{2,10},{10... | collective-permute-start | bytes 1376264 | tf_op jit(solution)/shard_map/ppermute | solution.py:393
  455.1 50.0 %collective-permute-start.30 = (f32[1,448,256]{2,1,0:T(8,128)}, f32[1,448,256]{2,1,0:T(8,128)}, u32[]{:S(2)}, u32[]{:S(2)}) collective-permute-start(f32[1,448,256]{2,1,0:T(8,128)} %get-tuple-element.114), channel_id=1, source_target_pairs={{0,8},{8,0},{16,24},{24,16},{1,9},{9,1},{17,25},{25,17},{2,10},{10... | collective-permute-start | bytes 1376264 | tf_op jit(solution)/shard_map/ppermute | solution.py:393
  (31 other events, 675.0 us)

commit v7 on v6

--- a/solution.py
+++ b/solution.py
@@ -264,30 +264,46 @@
     pieces = refs[: len(sizes)]
     if not first:
         total = refs[len(sizes)]
-    out, tones_first, symbols_first = refs[-3:]
+    out, tones_first, symbols_first, held, arrived, left = refs[-6:]
     tones = sum(sizes)
-    length = out.shape[3]
+    items, _, _, length = held.shape
     blocks = tones_first.shape[0]
-    item = pl.program_id(0)
-
-    @pl.when(item == 0)
-    def _():
-        for block in range(blocks):
-
-            def gather(group, carry):
-                position = source[block * groups + group]
-                for side in range(2):
-                    place = (group * 2 + side) * tones * 2
-                    src = (2 * position + side) * groups + group
-                    for piece, size in zip(pieces, sizes):
-                        for tone in range(2 * size):
-                            lane = (tone * 2 + block % 2) * rows
-                            tones_first[block, place + tone, :, :rows] = piece[src, :, lane : lane + rows]
-                        place = place + 2 * size
-                return carry
-
-            lax.fori_loop(0, groups, gather, 0)
-
+
+    def fetch(item):
+        return pltpu.make_async_copy(total.at[item], held.at[item], arrived.at[item])
+
+    def store(item):
+        return pltpu.make_async_copy(held.at[item], out.at[item], left.at[item])
+
+    if not first:
+        for item in range(items):
+            fetch(item).start()
+    for block in range(blocks):
+
+        def gather(group, carry):
+            position = source[block * groups + group]
+            for side in range(2):
+                place = (group * 2 + side) * tones * 2
+                src = (2 * position + side) * groups + group
+                for piece, size in zip(pieces, sizes):
+                    for tone in range(2 * size):
+                        lane = (tone * 2 + block % 2) * rows
+                        tones_first[block, place + tone, :, :rows] = piece[src, :, lane : lane + rows]
+                    place = place + 2 * size
+            return carry
+
+        lax.fori_loop(0, groups, gather, 0)
+
+    for item in range(items):
+        despread_item(rows, folded, first, last, item, table, tones_first, symbols_first, held, fetch)
+        store(item).start()
+    for item in range(items):
+        store(item).wait()
+
+
+def despread_item(rows, folded, first, last, item, table, tones_first, symbols_first, held, fetch):
+    length = held.shape[3]
+    blocks = tones_first.shape[0]
     for block in range(blocks):
         value = tones_first[block, :, item, :]
         here = slice(block * rows, (block + 1) * rows)
@@ -303,11 +319,13 @@
         result = dot(symbols_first[0], table[0], (1, 0))
     else:
         result = dot3((symbols_first[0], symbols_first[1]), (table[0], table[1]), (1, 0))
+    if not first:
+        fetch(item).wait()
     for part in range(2):
         value = result[:, part * length : (part + 1) * length]
         if not first:
-            value = value + total[0, part]
-        out[0, part] = jnp.tanh(value) if last else value
+            value = value + held[item, part]
+        held[item, part] = jnp.tanh(value) if last else value
 
 
 def despread(pieces, starts, groups, half, blocks, rows, source, total, last, after):
@@ -327,22 +345,24 @@
     folded = 3 * depth <= 256
     table = np.concatenate([high, low, high], 1) if folded else np.concatenate([high, low], 0)
     symbols = blocks * rows
-    block_spec = pl.BlockSpec((1, 2, symbols, length), lambda i, s: (i, 0, 0, 0))
     totals = [] if total is None else [total]
     return pl.pallas_call(
         functools.partial(despread_body, groups, sizes, rows, folded, total is None, last),
         out_shape=jax.ShapeDtypeStruct((items, 2, symbols, length), F32),
         grid_spec=pltpu.PrefetchScalarGridSpec(
             num_scalar_prefetch=1,
-            grid=(items,),
+            grid=(1,),
             in_specs=[pl.BlockSpec(table.shape, lambda i, s: (0, 0, 0))]
             + [pl.BlockSpec(piece.shape, lambda i, s: (0, 0, 0)) for piece in pieces]
-            + [block_spec] * len(totals)
+            + [ANY] * len(totals)
             + [ANY] * len(after),
-            out_specs=block_spec,
+            out_specs=ANY,
             scratch_shapes=[
                 pltpu.VMEM((blocks, depth, items, lanes), F32),
                 pltpu.VMEM((table.shape[0], symbols, table.shape[1]), BF16),
+                pltpu.VMEM((items, 2, symbols, length), F32),
+                pltpu.SemaphoreType.DMA((items,)),
+                pltpu.SemaphoreType.DMA((items,)),
             ],
         ),
         compiler_params=pltpu.CompilerParams(vmem_limit_bytes=VMEM_LIMIT),
@@ -434,8 +454,8 @@
     if chunks > 8:
         for c in (chunks - 2, chunks - 1):
             ahead[c - 1].remove(c)
-            ahead[c - 4].append(c)
-        parts = {chunks - 4: chunks - 6, chunks - 2: chunks - 4}
+            ahead[c - 5].append(c)
+        parts = {chunks - 5: chunks - 7}
     begin, total = 0, None
     for c in range(chunks):
         before = chain(0, False, rows, side_alone, rates, own[c], peer[c], [], [before])
@@ -444,13 +464,14 @@
             total = bring_together(begin, parts[c], total, False, [before])
             begin, before = parts[c], total
         if c > 0:
-            before = complete(c - 1, [before] + pieces[-1:])
+            before = complete(c - 1, [before] + ([] if c >= chunks - 2 else pieces[-1:]))
         if c + 2 < chunks:
             before = ready_peer(c + 2, [before])
         for other in ahead.get(c, []):
             before = ready_own(other, [before])
         for r in range(1, pairs):
-            done = chain(r, r == pairs - 1, rows, side_alone, rates, own[c], peer[c], [both], [before])
+            after = [before] + (pieces[-2:-1] if c >= chunks - 2 else [])
+            done = chain(r, r == pairs - 1, rows, side_alone, rates, own[c], peer[c], [both], after)
             if r < pairs - 1:
                 both = lax.ppermute(done, "blk", onward)
                 before = done

time: 570 us -> 560 us (0.982)
  Pallas kernels: 318 us -> 299 us
  waiting for transfers between devices: 127 us -> 144 us
  starting transfers between devices: 108 us -> 100 us
    pallas_call x4 -> x3, Pallas kernels: 55.5 us -> 37.6 us  [despread(): pl.pallas_call(functools.partial(despread_body, groups, sizes, rows, fold...]
    ppermute x20, waiting for transfers between devices: 32 us -> 45.2 us  [ready_peer(): peer[c] = [lax.ppermute(value, 'blk', swap) for value in sent]]
    ppermute x10, waiting for transfers between devices: 32.7 us -> 41.9 us  [on_device(): odd[c] = (even, lax.ppermute(moving, 'blk', onward))]
    ppermute x10, starting transfers between devices: 14.7 us -> 8.59 us  [on_device(): both = lax.ppermute(before, 'blk', onward)]
  transfers between devices with their start and end apart: 50 -> 50, of which waited for: 20 -> 20; matrix products, arithmetic and copies ran while one was open for 1% -> 1% of each run, Pallas kernels for 53% -> 51%
where the time goes in v7:
time: 560 us; the launch traced here: 550 us
  Pallas kernels  299 us (53%)
  waiting for transfers between devices  144 us (26%)
  starting transfers between devices  100 us (18%)
    pallas_call x20, Pallas kernels, chain(): pl.pallas_call(functools.partial(chain_body, round_index, last, rows), ou...  107 us
    pallas_call x20, Pallas kernels, prepare(): pl.pallas_call(functools.partial(prepare_body, carry, blocks), out_shape=...  103 us
    all_to_all x10, waiting for transfers between devices, complete(): lax.all_to_all(done, ('blk', 'tones'), split_axis=0, concat_axis=0, tiled...  56.1 us
    pallas_call x10, Pallas kernels, finish(): pl.pallas_call(functools.partial(finish_body, count, rows), out_shape=jax...  51.4 us
    all_to_all x10, starting transfers between devices, complete(): lax.all_to_all(done, ('blk', 'tones'), split_axis=0, concat_axis=0, tiled...  50 us
    ppermute x20, waiting for transfers between devices, ready_peer(): peer[c] = [lax.ppermute(value, 'blk', swap) for value in sent]  45.2 us
    ppermute x10, waiting for transfers between devices, on_device(): odd[c] = (even, lax.ppermute(moving, 'blk', onward))  41.9 us
    pallas_call x3, Pallas kernels, despread(): pl.pallas_call(functools.partial(despread_body, groups, sizes, rows, fold...  37.6 us
  transfers between devices with their start and end apart: 50, of which 20 were waited for; matrix products, arithmetic and copies ran while one was open for 1% of the time, Pallas kernels for 51%

profile of v7, /device:TPU:0, one launch (start us, length us, event | category | flops | bytes accessed | tf_op | source)
XLA Modules:
  0.0 549.7 jit_solution(2787831573120725900)
XLA Ops:
  7.2 5.8 %prepare.21 = (f32[2,704,256]{2,1,0:T(8,128)}, f32[2,448,256]{2,1,0:T(8,128)}) custom-call(s32[1]{0:T(128)} %bitcast.3.base, s32[1]{0:T(128)} %bitcast.4.pair, s32[1]{0:T(128)} %bitcast.5.group, s32[8]{0:T(128)} %hop_offset.39, f32[1,2]{1,0:T(1,128)} %rates.39, f32[32,2,256,256]{3,2,1,0:T(8,128)} %chan.39, f32[32,2,448,256]{3,2,1,0:T(8,128)} %recv.39, ...), custom_call_target="tpu_custom_call" | custom-call | flops 9999999827968 | bytes 10000000000 | tf_op jit(solution)/shard_map/prepare/pallas_call | solution.py:86
  44.7 40.4 %collective-permute-done.3.refs_3_ = f32[1,448,256]{2,1,0:T(8,128)} collective-permute-done((f32[1,448,256]{2,1,0:T(8,128)}, f32[1,448,256]{2,1,0:T(8,128)}, u32[]{:S(2)}, u32[]{:S(2)}) %collective-permute-start.3) | collective-permute-done | bytes 458784 | tf_op jit(solution)/shard_map/ppermute | solution.py:413
  122.4 6.9 %chain1.11 = (f32[2,2,112,256]{3,2,1,0:T(8,128)}, f32[2,2,112,256]{3,2,1,0:T(8,128)}) custom-call(s32[1]{0:T(128)} %bitcast.side, f32[2,2]{1,0:T(2,128)} %maximum_select_fusion.rates, f32[2,704,256]{2,1,0:T(8,128)} %get-tuple-element.69.refs_5_.refs_0_.own, f32[2,704,256]{2,1,0:T(8,128)} %collective-permute-done.1.refs_1_.peer, ...), custom_call_target="tpu_custom_call" | custom-call | flops 9999999827968 | bytes 10000000000 | tf_op jit(solution)/shard_map/chain1/pallas_call | solution.py:179
  136.8 6.0 %all-to-all-done.refs_1_.refs_0_ = f32[32,8,448]{2,1,0:T(8,128)} async-done(((f32[32,8,448]{2,1,0:T(8,128)}), f32[32,8,448]{2,1,0:T(8,128)}, u32[]{:S(2)}, u32[]{:S(2)}) %all-to-all-start) | async-done | bytes 458784 | tf_op jit(solution)/shard_map/all_to_all | solution.py:424
  155.1 6.2 %all-to-all-start.1 = ((f32[32,8,896]{2,1,0:T(8,128)}), f32[32,8,896]{2,1,0:T(8,128)}, u32[]{:S(2)}, u32[]{:S(2)}) async-start(f32[32,8,896]{2,1,0:T(8,128)} %finish.11.refs_0_), calls=%async_computation.1 | async-start | bytes 1835008 | tf_op jit(solution)/shard_map/all_to_all | solution.py:424
  169.1 6.9 %chain1.12 = (f32[2,2,112,256]{3,2,1,0:T(8,128)}, f32[2,2,112,256]{3,2,1,0:T(8,128)}) custom-call(s32[1]{0:T(128)} %bitcast.side, f32[2,2]{1,0:T(2,128)} %maximum_select_fusion.rates, f32[2,704,256]{2,1,0:T(8,128)} %get-tuple-element.77.refs_5_.refs_0_.own, f32[2,704,256]{2,1,0:T(8,128)} %collective-permute-done.8.refs_1_.peer, ...), custom_call_target="tpu_custom_call" | custom-call | flops 9999999827968 | bytes 10000000000 | tf_op jit(solution)/shard_map/chain1/pallas_call | solution.py:179
  184.6 6.4 %collective-permute-done.14.odd = f32[2,2,112,256]{3,2,1,0:T(8,128)} collective-permute-done((f32[2,2,112,256]{3,2,1,0:T(8,128)}, f32[2,2,112,256]{3,2,1,0:T(8,128)}, u32[]{:S(2)}, u32[]{:S(2)}) %collective-permute-start.14) | collective-permute-done | bytes 458784 | tf_op jit(solution)/shard_map/ppermute | solution.py:479
  191.0 12.2 %all-to-all-done.1.refs_1_ = f32[32,8,896]{2,1,0:T(8,128)} async-done(((f32[32,8,896]{2,1,0:T(8,128)}), f32[32,8,896]{2,1,0:T(8,128)}, u32[]{:S(2)}, u32[]{:S(2)}) %all-to-all-start.1) | async-done | bytes 917536 | tf_op jit(solution)/shard_map/all_to_all | solution.py:424
  203.2 5.7 %finish.12.refs_0_ = f32[32,8,896]{2,1,0:T(8,128)} custom-call(s32[2]{0:T(128)} %pad_add_fusion.scalars, f32[2,2]{1,0:T(2,128)} %maximum_select_fusion.rates, f32[2,704,256]{2,1,0:T(8,128)} %get-tuple-element.77.refs_5_.refs_0_.own, f32[2,704,256]{2,1,0:T(8,128)} %collective-permute-done.8.refs_1_.peer, f32[2,2,112,256]{3,2,1,0:T(8,128)} %get-tuple-element.86.refs_2_.even, ...), custom_call_target="tpu_custom_call" | custom-call | flops 9999999827968 | bytes 10000000000 | tf_op jit(solution)/shard_map/finish/pallas_call | solution.py:236
  231.8 6.9 %chain1.13 = (f32[2,2,112,256]{3,2,1,0:T(8,128)}, f32[2,2,112,256]{3,2,1,0:T(8,128)}) custom-call(s32[1]{0:T(128)} %bitcast.side, f32[2,2]{1,0:T(2,128)} %maximum_select_fusion.rates, f32[2,704,256]{2,1,0:T(8,128)} %get-tuple-element.81.refs_5_.refs_0_.own, f32[2,704,256]{2,1,0:T(8,128)} %collective-permute-done.9.refs_1_.peer, ...), custom_call_target="tpu_custom_call" | custom-call | flops 9999999827968 | bytes 10000000000 | tf_op jit(solution)/shard_map/chain1/pallas_call | solution.py:179
  247.5 5.9 %collective-permute-done.15.odd = f32[2,2,112,256]{3,2,1,0:T(8,128)} collective-permute-done((f32[2,2,112,256]{3,2,1,0:T(8,128)}, f32[2,2,112,256]{3,2,1,0:T(8,128)}, u32[]{:S(2)}, u32[]{:S(2)}) %collective-permute-start.15) | collective-permute-done | bytes 458784 | tf_op jit(solution)/shard_map/ppermute | solution.py:479
  253.4 10.2 %all-to-all-done.2.refs_1_.refs_2_ = f32[32,8,896]{2,1,0:T(8,128)} async-done(((f32[32,8,896]{2,1,0:T(8,128)}), f32[32,8,896]{2,1,0:T(8,128)}, u32[]{:S(2)}, u32[]{:S(2)}) %all-to-all-start.2) | async-done | bytes 917536 | tf_op jit(solution)/shard_map/all_to_all | solution.py:424
  263.6 5.8 %finish.13.refs_0_ = f32[32,8,896]{2,1,0:T(8,128)} custom-call(s32[2]{0:T(128)} %pad_add_fusion.scalars, f32[2,2]{1,0:T(2,128)} %maximum_select_fusion.rates, f32[2,704,256]{2,1,0:T(8,128)} %get-tuple-element.81.refs_5_.refs_0_.own, f32[2,704,256]{2,1,0:T(8,128)} %collective-permute-done.9.refs_1_.peer, f32[2,2,112,256]{3,2,1,0:T(8,128)} %get-tuple-element.91.refs_2_.even, ...), custom_call_target="tpu_custom_call" | custom-call | flops 9999999827968 | bytes 10000000000 | tf_op jit(solution)/shard_map/finish/pallas_call | solution.py:236
  292.3 6.9 %chain1.14 = (f32[2,2,112,256]{3,2,1,0:T(8,128)}, f32[2,2,112,256]{3,2,1,0:T(8,128)}) custom-call(s32[1]{0:T(128)} %bitcast.side, f32[2,2]{1,0:T(2,128)} %maximum_select_fusion.rates, f32[2,704,256]{2,1,0:T(8,128)} %get-tuple-element.89.refs_0_.own, f32[2,704,256]{2,1,0:T(8,128)} %collective-permute-done.16.refs_1_.peer, ...), custom_call_target="tpu_custom_call" | custom-call | flops 9999999827968 | bytes 10000000000 | tf_op jit(solution)/shard_map/chain1/pallas_call | solution.py:179
  306.8 10.0 %despread.3.refs_0_.refs_6_ = f32[8,2,448,256]{3,2,1,0:T(8,128)} custom-call(s32[32]{0:T(128)} %and_select_fusion.source, bf16[2,160,512]{2,1,0:T(8,128)(2,1)} %constant.88.clone.table, f32[32,8,448]{2,1,0:T(8,128)} %all-to-all-done.refs_1_.refs_0_, f32[32,8,896]{2,1,0:T(8,128)} %all-to-all-done.1.refs_1_, f32[32,8,896]{2,1,0:T(8,128)} %all-to-all-done.2.refs_1_.refs_2_, ...), custom_call_target="tpu_custom_call" | custom-call | flops 9999999827968 | bytes 10000000000 | tf_op jit(solution)/shard_map/despread/pallas_call | solution.py:349
  316.9 7.1 %all-to-all-done.3.refs_1_.refs_0_ = f32[32,8,896]{2,1,0:T(8,128)} async-done(((f32[32,8,896]{2,1,0:T(8,128)}), f32[32,8,896]{2,1,0:T(8,128)}, u32[]{:S(2)}, u32[]{:S(2)}) %all-to-all-start.3) | async-done | bytes 917536 | tf_op jit(solution)/shard_map/all_to_all | solution.py:424
  347.1 6.9 %chain1.15 = (f32[2,2,112,256]{3,2,1,0:T(8,128)}, f32[2,2,112,256]{3,2,1,0:T(8,128)}) custom-call(s32[1]{0:T(128)} %bitcast.side, f32[2,2]{1,0:T(2,128)} %maximum_select_fusion.rates, f32[2,704,256]{2,1,0:T(8,128)} %get-tuple-element.94.refs_0_.own, f32[2,704,256]{2,1,0:T(8,128)} %collective-permute-done.20.refs_1_.peer, ...), custom_call_target="tpu_custom_call" | custom-call | flops 9999999827968 | bytes 10000000000 | tf_op jit(solution)/shard_map/chain1/pallas_call | solution.py:179
  369.0 15.4 %all-to-all-done.4.refs_1_ = f32[32,8,896]{2,1,0:T(8,128)} async-done(((f32[32,8,896]{2,1,0:T(8,128)}), f32[32,8,896]{2,1,0:T(8,128)}, u32[]{:S(2)}, u32[]{:S(2)}) %all-to-all-start.4) | async-done | bytes 917536 | tf_op jit(solution)/shard_map/all_to_all | solution.py:424
  405.9 6.9 %chain1.16 = (f32[2,2,112,256]{3,2,1,0:T(8,128)}, f32[2,2,112,256]{3,2,1,0:T(8,128)}) custom-call(s32[1]{0:T(128)} %bitcast.side, f32[2,2]{1,0:T(2,128)} %maximum_select_fusion.rates, f32[2,704,256]{2,1,0:T(8,128)} %get-tuple-element.101.refs_5_.refs_0_.own, f32[2,704,256]{2,1,0:T(8,128)} %collective-permute-done.21.refs_1_.peer, ...), custom_call_target="tpu_custom_call" | custom-call | flops 9999999827968 | bytes 10000000000 | tf_op jit(solution)/shard_map/chain1/pallas_call | solution.py:179
  418.7 9.5 %collective-permute-done.27.odd = f32[2,2,112,256]{3,2,1,0:T(8,128)} collective-permute-done((f32[2,2,112,256]{3,2,1,0:T(8,128)}, f32[2,2,112,256]{3,2,1,0:T(8,128)}, u32[]{:S(2)}, u32[]{:S(2)}) %collective-permute-start.27) | collective-permute-done | bytes 458784 | tf_op jit(solution)/shard_map/ppermute | solution.py:479
  482.0 5.8 %collective-permute-done.38.odd = f32[1,2,112,256]{3,2,1,0:T(8,128)} collective-permute-done((f32[1,2,112,256]{3,2,1,0:T(8,128)}, f32[1,2,112,256]{3,2,1,0:T(8,128)}, u32[]{:S(2)}, u32[]{:S(2)}) %collective-permute-start.38) | collective-permute-done | bytes 229408 | tf_op jit(solution)/shard_map/ppermute | solution.py:479
  502.9 7.9 %collective-permute-done.39.odd = f32[1,2,112,256]{3,2,1,0:T(8,128)S(1)} collective-permute-done((f32[1,2,112,256]{3,2,1,0:T(8,128)}, f32[1,2,112,256]{3,2,1,0:T(8,128)S(1)}, u32[]{:S(2)}, u32[]{:S(2)}) %collective-permute-start.39) | collective-permute-done | bytes 229408 | tf_op jit(solution)/shard_map/ppermute | solution.py:479
  521.6 18.6 %despread.4.refs_1_ = f32[8,2,448,256]{3,2,1,0:T(8,128)} custom-call(s32[32]{0:T(128)} %and_select_fusion.source, bf16[2,320,512]{2,1,0:T(8,128)(2,1)} %constant.89.clone.table, f32[32,8,896]{2,1,0:T(8,128)} %all-to-all-done.3.refs_1_.refs_0_, f32[32,8,896]{2,1,0:T(8,128)} %all-to-all-done.4.refs_1_, f32[32,8,896]{2,1,0:T(8,128)} %all-to-all-done.5.refs_1_.refs_2_, ...), custom_call_target="tpu_custom_call" | custom-call | flops 9999999827968 | bytes 10000000000 | tf_op jit(solution)/shard_map/despread/pallas_call | solution.py:349
  540.2 9.0 %despread.5 = f32[8,2,448,256]{3,2,1,0:T(8,128)} custom-call(s32[32]{0:T(128)} %and_select_fusion.source, bf16[1,96,512]{2,1,0:T(8,128)(2,1)} %constant.90.clone.table, f32[32,8,448]{2,1,0:T(8,128)} %all-to-all-done.9.refs_0_, f32[8,2,448,256]{3,2,1,0:T(8,128)} %despread.4.refs_1_), custom_call_target="tpu_custom_call" | custom-call | flops 9999999827968 | bytes 10000000000 | tf_op jit(solution)/shard_map/despread/pallas_call | solution.py:349
  (147 shorter events, 317.8 us)
Async XLA Ops:
  13.1 80.1 %collective-permute-start.1 = (f32[2,704,256]{2,1,0:T(8,128)}, f32[2,704,256]{2,1,0:T(8,128)}, u32[]{:S(2)}, u32[]{:S(2)}) collective-permute-start(f32[2,704,256]{2,1,0:T(8,128)} %get-tuple-element.66.refs_0_), channel_id=1, source_target_pairs={{0,8},{8,0},{16,24},{24,16},{1,9},{9,1},{17,25},{25,17},{2,10},{10... | collective-permute-start | bytes 4325384 | tf_op jit(solution)/shard_map/ppermute | solution.py:413
  13.1 109.2 %collective-permute-start.2 = (f32[2,448,256]{2,1,0:T(8,128)}, f32[2,448,256]{2,1,0:T(8,128)}, u32[]{:S(2)}, u32[]{:S(2)}) collective-permute-start(f32[2,448,256]{2,1,0:T(8,128)} %get-tuple-element.71), channel_id=1, source_target_pairs={{0,8},{8,0},{16,24},{24,16},{1,9},{9,1},{17,25},{25,17},{2,10},{10... | collective-permute-start | bytes 2752520 | tf_op jit(solution)/shard_map/ppermute | solution.py:413
  15.1 70.0 %collective-permute-start.3 = (f32[1,448,256]{2,1,0:T(8,128)}, f32[1,448,256]{2,1,0:T(8,128)}, u32[]{:S(2)}, u32[]{:S(2)}) collective-permute-start(f32[1,448,256]{2,1,0:T(8,128)} %get-tuple-element.73), channel_id=1, source_target_pairs={{0,8},{8,0},{16,24},{24,16},{1,9},{9,1},{17,25},{25,17},{2,10},{10... | collective-permute-start | bytes 1376264 | tf_op jit(solution)/shard_map/ppermute | solution.py:413
  35.4 51.8 %collective-permute-start.4 = (f32[1,2,2,112,256]{4,3,2,1,0:T(8,128)}, f32[1,2,2,112,256]{4,3,2,1,0:T(8,128)}, u32[]{:S(2)}, u32[]{:S(2)}) collective-permute-start(f32[1,2,2,112,256]{4,3,2,1,0:T(8,128)} %chain0.10.refs_0_), channel_id=1, source_target_pairs={{0,16},{8,24},{16,0},{24,8},{1,17},{9,25},{17,1},{25,9},{2,18},{10... | collective-permute-start | bytes 1376264 | tf_op jit(solution)/shard_map/ppermute | solution.py:462
  43.3 87.9 %collective-permute-start.8 = (f32[2,704,256]{2,1,0:T(8,128)}, f32[2,704,256]{2,1,0:T(8,128)}, u32[]{:S(2)}, u32[]{:S(2)}) collective-permute-start(f32[2,704,256]{2,1,0:T(8,128)} %get-tuple-element.68.refs_0_), channel_id=1, source_target_pairs={{0,8},{8,0},{16,24},{24,16},{1,9},{9,1},{17,25},{25,17},{2,10},{10... | collective-permute-start | bytes 4325384 | tf_op jit(solution)/shard_map/ppermute | solution.py:413
  85.1 83.9 %collective-permute-start.11 = (f32[2,448,256]{2,1,0:T(8,128)}, f32[2,448,256]{2,1,0:T(8,128)}, u32[]{:S(2)}, u32[]{:S(2)}) collective-permute-start(f32[2,448,256]{2,1,0:T(8,128)} %get-tuple-element.85), channel_id=1, source_target_pairs={{0,8},{8,0},{16,24},{24,16},{1,9},{9,1},{17,25},{25,17},{2,10},{10... | collective-permute-start | bytes 2752520 | tf_op jit(solution)/shard_map/ppermute | solution.py:413
  120.4 57.5 %collective-permute-start.9 = (f32[2,704,256]{2,1,0:T(8,128)}, f32[2,704,256]{2,1,0:T(8,128)}, u32[]{:S(2)}, u32[]{:S(2)}) collective-permute-start(f32[2,704,256]{2,1,0:T(8,128)} %get-tuple-element.76.refs_0_), channel_id=1, source_target_pairs={{0,8},{8,0},{16,24},{24,16},{1,9},{9,1},{17,25},{25,17},{2,10},{10... | collective-permute-start | bytes 4325384 | tf_op jit(solution)/shard_map/ppermute | solution.py:413
  122.3 109.5 %collective-permute-start.10 = (f32[2,448,256]{2,1,0:T(8,128)}, f32[2,448,256]{2,1,0:T(8,128)}, u32[]{:S(2)}, u32[]{:S(2)}) collective-permute-start(f32[2,448,256]{2,1,0:T(8,128)} %get-tuple-element.83), channel_id=1, source_target_pairs={{0,8},{8,0},{16,24},{24,16},{1,9},{9,1},{17,25},{25,17},{2,10},{10... | collective-permute-start | bytes 2752520 | tf_op jit(solution)/shard_map/ppermute | solution.py:413
  155.1 48.1 %all-to-all-start.1 = ((f32[32,8,896]{2,1,0:T(8,128)}), f32[32,8,896]{2,1,0:T(8,128)}, u32[]{:S(2)}, u32[]{:S(2)}) async-start(f32[32,8,896]{2,1,0:T(8,128)} %finish.11.refs_0_), calls=%async_computation.1 | async-start | bytes 1835008 | tf_op jit(solution)/shard_map/all_to_all | solution.py:424
  167.1 73.1 %collective-permute-start.16 = (f32[2,704,256]{2,1,0:T(8,128)}, f32[2,704,256]{2,1,0:T(8,128)}, u32[]{:S(2)}, u32[]{:S(2)}) collective-permute-start(f32[2,704,256]{2,1,0:T(8,128)} %get-tuple-element.80.refs_0_), channel_id=1, source_target_pairs={{0,8},{8,0},{16,24},{24,16},{1,9},{9,1},{17,25},{25,17},{2,10},{10... | collective-permute-start | bytes 4325384 | tf_op jit(solution)/shard_map/ppermute | solution.py:413
  169.0 123.3 %collective-permute-start.17 = (f32[2,448,256]{2,1,0:T(8,128)}, f32[2,448,256]{2,1,0:T(8,128)}, u32[]{:S(2)}, u32[]{:S(2)}) collective-permute-start(f32[2,448,256]{2,1,0:T(8,128)} %get-tuple-element.97), channel_id=1, source_target_pairs={{0,8},{8,0},{16,24},{24,16},{1,9},{9,1},{17,25},{25,17},{2,10},{10... | collective-permute-start | bytes 2752520 | tf_op jit(solution)/shard_map/ppermute | solution.py:413
  183.3 48.5 %collective-permute-start.13 = (f32[2,2,2,112,256]{4,3,2,1,0:T(8,128)}, f32[2,2,2,112,256]{4,3,2,1,0:T(8,128)}, u32[]{:S(2)}, u32[]{:S(2)}) collective-permute-start(f32[2,2,2,112,256]{4,3,2,1,0:T(8,128)} %chain0.13.refs_0_), channel_id=1, source_target_pairs={{0,16},{8,24},{16,0},{24,8},{1,17},{9,25},{17,1},{25,9},{2,18},{10... | collective-permute-start | bytes 2752520 | tf_op jit(solution)/shard_map/ppermute | solution.py:462
  214.6 49.0 %all-to-all-start.2 = ((f32[32,8,896]{2,1,0:T(8,128)}), f32[32,8,896]{2,1,0:T(8,128)}, u32[]{:S(2)}, u32[]{:S(2)}) async-start(f32[32,8,896]{2,1,0:T(8,128)} %finish.12.refs_0_), calls=%async_computation.2 | async-start | bytes 1835008 | tf_op jit(solution)/shard_map/all_to_all | solution.py:424
  225.6 75.7 %collective-permute-start.20 = (f32[2,704,256]{2,1,0:T(8,128)}, f32[2,704,256]{2,1,0:T(8,128)}, u32[]{:S(2)}, u32[]{:S(2)}) collective-permute-start(f32[2,704,256]{2,1,0:T(8,128)} %get-tuple-element.88.refs_0_), channel_id=1, source_target_pairs={{0,8},{8,0},{16,24},{24,16},{1,9},{9,1},{17,25},{25,17},{2,10},{10... | collective-permute-start | bytes 4325384 | tf_op jit(solution)/shard_map/ppermute | solution.py:413
  246.2 100.9 %collective-permute-start.23 = (f32[2,448,256]{2,1,0:T(8,128)}, f32[2,448,256]{2,1,0:T(8,128)}, u32[]{:S(2)}, u32[]{:S(2)}) collective-permute-start(f32[2,448,256]{2,1,0:T(8,128)} %get-tuple-element.105), channel_id=1, source_target_pairs={{0,8},{8,0},{16,24},{24,16},{1,9},{9,1},{17,25},{25,17},{2,10},{10... | collective-permute-start | bytes 2752520 | tf_op jit(solution)/shard_map/ppermute | solution.py:413
  275.1 48.9 %all-to-all-start.3 = ((f32[32,8,896]{2,1,0:T(8,128)}), f32[32,8,896]{2,1,0:T(8,128)}, u32[]{:S(2)}, u32[]{:S(2)}) async-start(f32[32,8,896]{2,1,0:T(8,128)} %finish.13.refs_0_), calls=%async_computation.3 | async-start | bytes 1835008 | tf_op jit(solution)/shard_map/all_to_all | solution.py:424
  286.0 73.3 %collective-permute-start.21 = (f32[2,704,256]{2,1,0:T(8,128)}, f32[2,704,256]{2,1,0:T(8,128)}, u32[]{:S(2)}, u32[]{:S(2)}) collective-permute-start(f32[2,704,256]{2,1,0:T(8,128)} %get-tuple-element.93.refs_0_), channel_id=1, source_target_pairs={{0,8},{8,0},{16,24},{24,16},{1,9},{9,1},{17,25},{25,17},{2,10},{10... | collective-permute-start | bytes 4325384 | tf_op jit(solution)/shard_map/ppermute | solution.py:413
  300.6 105.3 %collective-permute-start.22 = (f32[2,448,256]{2,1,0:T(8,128)}, f32[2,448,256]{2,1,0:T(8,128)}, u32[]{:S(2)}, u32[]{:S(2)}) collective-permute-start(f32[2,448,256]{2,1,0:T(8,128)} %get-tuple-element.103), channel_id=1, source_target_pairs={{0,8},{8,0},{16,24},{24,16},{1,9},{9,1},{17,25},{25,17},{2,10},{10... | collective-permute-start | bytes 2752520 | tf_op jit(solution)/shard_map/ppermute | solution.py:413
  334.0 50.4 %all-to-all-start.4 = ((f32[32,8,896]{2,1,0:T(8,128)}), f32[32,8,896]{2,1,0:T(8,128)}, u32[]{:S(2)}, u32[]{:S(2)}) async-start(f32[32,8,896]{2,1,0:T(8,128)} %finish.14.refs_0_), calls=%async_computation.4 | async-start | bytes 1835008 | tf_op jit(solution)/shard_map/all_to_all | solution.py:424
  345.2 69.6 %collective-permute-start.28 = (f32[1,704,256]{2,1,0:T(8,128)}, f32[1,704,256]{2,1,0:T(8,128)}, u32[]{:S(2)}, u32[]{:S(2)}) collective-permute-start(f32[1,704,256]{2,1,0:T(8,128)} %get-tuple-element.100.refs_0_), channel_id=1, source_target_pairs={{0,8},{8,0},{16,24},{24,16},{1,9},{9,1},{17,25},{25,17},{2,10},{10... | collective-permute-start | bytes 2162696 | tf_op jit(solution)/shard_map/ppermute | solution.py:413
  367.3 77.3 %collective-permute-start.33 = (f32[1,448,256]{2,1,0:T(8,128)}, f32[1,448,256]{2,1,0:T(8,128)}, u32[]{:S(2)}, u32[]{:S(2)}) collective-permute-start(f32[1,448,256]{2,1,0:T(8,128)} %get-tuple-element.118), channel_id=1, source_target_pairs={{0,8},{8,0},{16,24},{24,16},{1,9},{9,1},{17,25},{25,17},{2,10},{10... | collective-permute-start | bytes 1376264 | tf_op jit(solution)/shard_map/ppermute | solution.py:413
  404.0 47.2 %collective-permute-start.31 = (f32[1,704,256]{2,1,0:T(8,128)}, f32[1,704,256]{2,1,0:T(8,128)}, u32[]{:S(2)}, u32[]{:S(2)}) collective-permute-start(f32[1,704,256]{2,1,0:T(8,128)} %get-tuple-element.108.refs_0_), channel_id=1, source_target_pairs={{0,8},{8,0},{16,24},{24,16},{1,9},{9,1},{17,25},{25,17},{2,10},{10... | collective-permute-start | bytes 2162696 | tf_op jit(solution)/shard_map/ppermute | solution.py:413
  414.2 57.0 %collective-permute-start.32 = (f32[1,448,256]{2,1,0:T(8,128)}, f32[1,448,256]{2,1,0:T(8,128)}, u32[]{:S(2)}, u32[]{:S(2)}) collective-permute-start(f32[1,448,256]{2,1,0:T(8,128)} %get-tuple-element.116), channel_id=1, source_target_pairs={{0,8},{8,0},{16,24},{24,16},{1,9},{9,1},{17,25},{25,17},{2,10},{10... | collective-permute-start | bytes 1376264 | tf_op jit(solution)/shard_map/ppermute | solution.py:413
  444.6 52.0 %collective-permute-start.30 = (f32[1,448,256]{2,1,0:T(8,128)}, f32[1,448,256]{2,1,0:T(8,128)}, u32[]{:S(2)}, u32[]{:S(2)}) collective-permute-start(f32[1,448,256]{2,1,0:T(8,128)} %get-tuple-element.114), channel_id=1, source_target_pairs={{0,8},{8,0},{16,24},{24,16},{1,9},{9,1},{17,25},{25,17},{2,10},{10... | collective-permute-start | bytes 1376264 | tf_op jit(solution)/shard_map/ppermute | solution.py:413
  (31 other events, 623.3 us)

commit v8 on v7

--- a/solution.py
+++ b/solution.py
@@ -258,6 +258,19 @@
         cost_estimate=HEAVY,
         name="finish",
     )(scalars, rates, own[0], peer[0], even, odd, order, *after)
+
+
+def held_back(value, after):
+    return pl.pallas_call(
+        lambda *refs: None,
+        out_shape=jax.ShapeDtypeStruct(value.shape, value.dtype),
+        in_specs=[ANY] * (1 + len(after)),
+        out_specs=ANY,
+        input_output_aliases={0: 0},
+        compiler_params=pltpu.CompilerParams(vmem_limit_bytes=VMEM_LIMIT),
+        cost_estimate=HEAVY,
+        name="held_back",
+    )(value, *after)
 
 
 def despread_body(groups, sizes, rows, folded, first, last, source, table, *refs):
@@ -400,7 +413,7 @@
     begins = (jnp.arange(blocks, dtype=jnp.int32)[:, None] + hop_offset[None, :]) % blocks
     source = jnp.where(begins % 2 == 0, begins // 2 + pairs - 1, begins // 2) % pairs
 
-    own, peer, odd, pieces = {}, {}, {}, []
+    own, peer, later, odd, pieces = {}, {}, {}, {}, []
 
     def ready(c, first_tone, carry, after):
         scalars = (first_tone.reshape(1),) + place
@@ -410,8 +423,16 @@
 
     def ready_peer(c, after):
         sent = ready(c, (1 - side) * half, 8 if c == 0 else 0, after)
-        peer[c] = [lax.ppermute(value, "blk", swap) for value in sent]
+        peer[c] = [lax.ppermute(sent[0], "blk", swap)]
+        later[c] = sent[1:]
         return sent[0]
+
+    def send_later(c, after):
+        for value in later[c]:
+            value = held_back(value, after)
+            peer[c].append(lax.ppermute(value, "blk", swap))
+            after = [value]
+        return after[0]
 
     def ready_own(c, after):
         own[c] = ready(c, side * half, 0, after)
@@ -440,6 +461,7 @@
         )
 
     before = ready_peer(0, [])
+    before = send_later(0, [before])
     if chunks > 1:
         before = ready_peer(1, [before])
     before = ready_own(0, [before])
@@ -455,7 +477,7 @@
         for c in (chunks - 2, chunks - 1):
             ahead[c - 1].remove(c)
             ahead[c - 5].append(c)
-        parts = {chunks - 5: chunks - 7}
+        parts = {chunks - 5: chunks - 7, chunks - 4: chunks - 6}
     begin, total = 0, None
     for c in range(chunks):
         before = chain(0, False, rows, side_alone, rates, own[c], peer[c], [], [before])
@@ -465,6 +487,8 @@
             begin, before = parts[c], total
         if c > 0:
             before = complete(c - 1, [before] + ([] if c >= chunks - 2 else pieces[-1:]))
+        if c + 1 < chunks:
+            before = send_later(c + 1, [before])
         if c + 2 < chunks:
             before = ready_peer(c + 2, [before])
         for other in ahead.get(c, []):

time: 560 us -> 551 us (0.984)
  waiting for transfers between devices: 144 us -> 124 us
  Pallas kernels: 299 us -> 306 us
  starting transfers between devices: 100 us -> 106 us
    all_to_all x10, waiting for transfers between devices: 56.1 us -> 7.06 us  [complete(): lax.all_to_all(done, ('blk', 'tones'), split_axis=0, concat_axis=0, tiled...]
    ppermute x20, waiting for transfers between devices: 45.2 us -> 93.6 us  [the longest x10 93.5 us: ready_peer(): peer[c] = [lax.ppermute(sent[0], 'blk', swap)]]
    ppermute x10, waiting for transfers between devices: 41.9 us -> 22.9 us  [on_device(): odd[c] = (even, lax.ppermute(moving, 'blk', onward))]
    ppermute x10, starting transfers between devices: 8.59 us -> 16.5 us  [on_device(): both = lax.ppermute(before, 'blk', onward)]
    pallas_call x3 -> x4, Pallas kernels: 37.6 us -> 44.2 us  [despread(): pl.pallas_call(functools.partial(despread_body, groups, sizes, rows, fold...]
  transfers between devices with their start and end apart: 50 -> 50, of which waited for: 20 -> 15; matrix products, arithmetic and copies ran while one was open for 1% -> 1% of each run, Pallas kernels for 51% -> 53%
where the time goes in v8:
time: 551 us; the launch traced here: 542 us
  Pallas kernels  306 us (56%)
  waiting for transfers between devices  124 us (23%)
  starting transfers between devices  106 us (19%)
    pallas_call x20, Pallas kernels, chain(): pl.pallas_call(functools.partial(chain_body, round_index, last, rows), ou...  107 us
    pallas_call x20, Pallas kernels, prepare(): pl.pallas_call(functools.partial(prepare_body, carry, blocks), out_shape=...  103 us
    ppermute x10, waiting for transfers between devices, ready_peer(): peer[c] = [lax.ppermute(sent[0], 'blk', swap)]  93.5 us
    pallas_call x10, Pallas kernels, finish(): pl.pallas_call(functools.partial(finish_body, count, rows), out_shape=jax...  51.2 us
    all_to_all x10, starting transfers between devices, complete(): lax.all_to_all(done, ('blk', 'tones'), split_axis=0, concat_axis=0, tiled...  49 us
    pallas_call x4, Pallas kernels, despread(): pl.pallas_call(functools.partial(despread_body, groups, sizes, rows, fold...  44.2 us
    ppermute x10, waiting for transfers between devices, on_device(): odd[c] = (even, lax.ppermute(moving, 'blk', onward))  22.9 us
    ppermute x10, starting transfers between devices, send_later(): peer[c].append(lax.ppermute(value, 'blk', swap))  17 us
  transfers between devices with their start and end apart: 50, of which 15 were waited for; matrix products, arithmetic and copies ran while one was open for 1% of the time, Pallas kernels for 53%

profile of v8, /device:TPU:0, one launch (start us, length us, event | category | flops | bytes accessed | tf_op | source)
XLA Modules:
  0.0 541.5 jit_solution(5149361797253887104)
XLA Ops:
  7.3 5.8 %prepare.21 = (f32[2,704,256]{2,1,0:T(8,128)}, f32[2,448,256]{2,1,0:T(8,128)}) custom-call(s32[1]{0:T(128)} %bitcast.3.base, s32[1]{0:T(128)} %bitcast.4.pair, s32[1]{0:T(128)} %bitcast.5.group, s32[8]{0:T(128)} %hop_offset.39, f32[1,2]{1,0:T(1,128)} %rates.39, f32[32,2,256,256]{3,2,1,0:T(8,128)} %chan.39, f32[32,2,448,256]{3,2,1,0:T(8,128)} %recv.39, ...), custom_call_target="tpu_custom_call" | custom-call | flops 9999999827968 | bytes 10000000000 | tf_op jit(solution)/shard_map/prepare/pallas_call | solution.py:86
  49.7 15.7 %collective-permute-done.4.refs_1_.peer = f32[2,704,256]{2,1,0:T(8,128)} collective-permute-done((f32[2,704,256]{2,1,0:T(8,128)}, f32[2,704,256]{2,1,0:T(8,128)}, u32[]{:S(2)}, u32[]{:S(2)}) %collective-permute-start.4) | collective-permute-done | bytes 1441824 | tf_op jit(solution)/shard_map/ppermute | solution.py:426
  90.2 5.8 %prepare.26 = (f32[2,704,256]{2,1,0:T(8,128)}, f32[2,448,256]{2,1,0:T(8,128)}) custom-call(s32[1]{0:T(128)} %bitcast.7.base, s32[1]{0:T(128)} %bitcast.4.pair, s32[1]{0:T(128)} %bitcast.5.group, s32[8]{0:T(128)} %hop_offset.39, f32[1,2]{1,0:T(1,128)} %rates.39, f32[32,2,256,256]{3,2,1,0:T(8,128)} %chan.39, f32[32,2,448,256]{3,2,1,0:T(8,128)} %recv.39, ...), custom_call_target="tpu_custom_call" | custom-call | flops 9999999827968 | bytes 10000000000 | tf_op jit(solution)/shard_map/prepare/pallas_call | solution.py:86
  96.0 6.9 %chain1.11 = (f32[2,2,112,256]{3,2,1,0:T(8,128)}, f32[2,2,112,256]{3,2,1,0:T(8,128)}) custom-call(s32[1]{0:T(128)} %bitcast.side, f32[2,2]{1,0:T(2,128)} %maximum_select_fusion.rates, f32[2,704,256]{2,1,0:T(8,128)} %get-tuple-element.73.refs_5_.refs_0_.own, f32[2,704,256]{2,1,0:T(8,128)} %collective-permute-done.4.refs_1_.peer, ...), custom_call_target="tpu_custom_call" | custom-call | flops 9999999827968 | bytes 10000000000 | tf_op jit(solution)/shard_map/chain1/pallas_call | solution.py:179
  104.8 15.5 %collective-permute-done.8.refs_1_.peer = f32[2,704,256]{2,1,0:T(8,128)} collective-permute-done((f32[2,704,256]{2,1,0:T(8,128)}, f32[2,704,256]{2,1,0:T(8,128)}, u32[]{:S(2)}, u32[]{:S(2)}) %collective-permute-start.8) | collective-permute-done | bytes 1441824 | tf_op jit(solution)/shard_map/ppermute | solution.py:426
  127.7 5.7 %finish.11.refs_1_ = f32[32,8,896]{2,1,0:T(8,128)} custom-call(s32[2]{0:T(128)} %pad_add_fusion.scalars, f32[2,2]{1,0:T(2,128)} %maximum_select_fusion.rates, f32[2,704,256]{2,1,0:T(8,128)} %get-tuple-element.73.refs_5_.refs_0_.own, f32[2,704,256]{2,1,0:T(8,128)} %collective-permute-done.4.refs_1_.peer, f32[2,2,112,256]{3,2,1,0:T(8,128)} %get-tuple-element.80.refs_2_.even, ...), custom_call_target="tpu_custom_call" | custom-call | flops 9999999827968 | bytes 10000000000 | tf_op jit(solution)/shard_map/finish/pallas_call | solution.py:236
  152.2 6.9 %chain1.12 = (f32[2,2,112,256]{3,2,1,0:T(8,128)}, f32[2,2,112,256]{3,2,1,0:T(8,128)}) custom-call(s32[1]{0:T(128)} %bitcast.side, f32[2,2]{1,0:T(2,128)} %maximum_select_fusion.rates, f32[2,704,256]{2,1,0:T(8,128)} %get-tuple-element.79.refs_5_.refs_0_.own, f32[2,704,256]{2,1,0:T(8,128)} %collective-permute-done.8.refs_1_.peer, ...), custom_call_target="tpu_custom_call" | custom-call | flops 9999999827968 | bytes 10000000000 | tf_op jit(solution)/shard_map/chain1/pallas_call | solution.py:179
  161.0 18.5 %collective-permute-done.12.refs_1_.peer = f32[2,704,256]{2,1,0:T(8,128)} collective-permute-done((f32[2,704,256]{2,1,0:T(8,128)}, f32[2,704,256]{2,1,0:T(8,128)}, u32[]{:S(2)}, u32[]{:S(2)}) %collective-permute-start.12) | collective-permute-done | bytes 1441824 | tf_op jit(solution)/shard_map/ppermute | solution.py:426
  187.1 5.7 %finish.12.refs_1_ = f32[32,8,896]{2,1,0:T(8,128)} custom-call(s32[2]{0:T(128)} %pad_add_fusion.scalars, f32[2,2]{1,0:T(2,128)} %maximum_select_fusion.rates, f32[2,704,256]{2,1,0:T(8,128)} %get-tuple-element.79.refs_5_.refs_0_.own, f32[2,704,256]{2,1,0:T(8,128)} %collective-permute-done.8.refs_1_.peer, f32[2,2,112,256]{3,2,1,0:T(8,128)} %get-tuple-element.86.refs_2_.even, ...), custom_call_target="tpu_custom_call" | custom-call | flops 9999999827968 | bytes 10000000000 | tf_op jit(solution)/shard_map/finish/pallas_call | solution.py:236
  216.1 6.9 %chain1.13 = (f32[2,2,112,256]{3,2,1,0:T(8,128)}, f32[2,2,112,256]{3,2,1,0:T(8,128)}) custom-call(s32[1]{0:T(128)} %bitcast.side, f32[2,2]{1,0:T(2,128)} %maximum_select_fusion.rates, f32[2,704,256]{2,1,0:T(8,128)} %get-tuple-element.85.refs_5_.refs_0_.own, f32[2,704,256]{2,1,0:T(8,128)} %collective-permute-done.12.refs_1_.peer, ...), custom_call_target="tpu_custom_call" | custom-call | flops 9999999827968 | bytes 10000000000 | tf_op jit(solution)/shard_map/chain1/pallas_call | solution.py:179
  224.9 15.0 %collective-permute-done.16.refs_1_.peer = f32[2,704,256]{2,1,0:T(8,128)} collective-permute-done((f32[2,704,256]{2,1,0:T(8,128)}, f32[2,704,256]{2,1,0:T(8,128)}, u32[]{:S(2)}, u32[]{:S(2)}) %collective-permute-start.16) | collective-permute-done | bytes 1441824 | tf_op jit(solution)/shard_map/ppermute | solution.py:426
  247.5 5.7 %finish.13.refs_1_ = f32[32,8,896]{2,1,0:T(8,128)} custom-call(s32[2]{0:T(128)} %pad_add_fusion.scalars, f32[2,2]{1,0:T(2,128)} %maximum_select_fusion.rates, f32[2,704,256]{2,1,0:T(8,128)} %get-tuple-element.85.refs_5_.refs_0_.own, f32[2,704,256]{2,1,0:T(8,128)} %collective-permute-done.12.refs_1_.peer, f32[2,2,112,256]{3,2,1,0:T(8,128)} %get-tuple-element.93.refs_2_.even, ...), custom_call_target="tpu_custom_call" | custom-call | flops 9999999827968 | bytes 10000000000 | tf_op jit(solution)/shard_map/finish/pallas_call | solution.py:236
  276.3 6.9 %chain1.14 = (f32[2,2,112,256]{3,2,1,0:T(8,128)}, f32[2,2,112,256]{3,2,1,0:T(8,128)}) custom-call(s32[1]{0:T(128)} %bitcast.side, f32[2,2]{1,0:T(2,128)} %maximum_select_fusion.rates, f32[2,704,256]{2,1,0:T(8,128)} %get-tuple-element.91.refs_0_.own, f32[2,704,256]{2,1,0:T(8,128)} %collective-permute-done.16.refs_1_.peer, ...), custom_call_target="tpu_custom_call" | custom-call | flops 9999999827968 | bytes 10000000000 | tf_op jit(solution)/shard_map/chain1/pallas_call | solution.py:179
  285.1 15.3 %collective-permute-done.20.refs_1_.peer = f32[2,704,256]{2,1,0:T(8,128)} collective-permute-done((f32[2,704,256]{2,1,0:T(8,128)}, f32[2,704,256]{2,1,0:T(8,128)}, u32[]{:S(2)}, u32[]{:S(2)}) %collective-permute-start.20) | collective-permute-done | bytes 1441824 | tf_op jit(solution)/shard_map/ppermute | solution.py:426
  307.9 10.0 %despread.4.refs_0_.refs_1_ = f32[8,2,448,256]{3,2,1,0:T(8,128)} custom-call(s32[32]{0:T(128)} %and_select_fusion.source, bf16[2,160,512]{2,1,0:T(8,128)(2,1)} %constant.90.clone.table, f32[32,8,448]{2,1,0:T(8,128)} %all-to-all-done.refs_1_.refs_0_, f32[32,8,896]{2,1,0:T(8,128)} %all-to-all-done.1.refs_1_, f32[32,8,896]{2,1,0:T(8,128)} %all-to-all-done.2.refs_1_.refs_2_, ...), custom_call_target="tpu_custom_call" | custom-call | flops 9999999827968 | bytes 10000000000 | tf_op jit(solution)/shard_map/despread/pallas_call | solution.py:362
  317.9 5.7 %finish.14.refs_1_ = f32[32,8,896]{2,1,0:T(8,128)} custom-call(s32[2]{0:T(128)} %pad_add_fusion.scalars, f32[2,2]{1,0:T(2,128)} %maximum_select_fusion.rates, f32[2,704,256]{2,1,0:T(8,128)} %get-tuple-element.91.refs_0_.own, f32[2,704,256]{2,1,0:T(8,128)} %collective-permute-done.16.refs_1_.peer, f32[2,2,112,256]{3,2,1,0:T(8,128)} %get-tuple-element.100.refs_2_.even, ...), custom_call_target="tpu_custom_call" | custom-call | flops 9999999827968 | bytes 10000000000 | tf_op jit(solution)/shard_map/finish/pallas_call | solution.py:236
  341.0 6.9 %chain1.15 = (f32[2,2,112,256]{3,2,1,0:T(8,128)}, f32[2,2,112,256]{3,2,1,0:T(8,128)}) custom-call(s32[1]{0:T(128)} %bitcast.side, f32[2,2]{1,0:T(2,128)} %maximum_select_fusion.rates, f32[2,704,256]{2,1,0:T(8,128)} %get-tuple-element.96.refs_0_.own, f32[2,704,256]{2,1,0:T(8,128)} %collective-permute-done.20.refs_1_.peer, ...), custom_call_target="tpu_custom_call" | custom-call | flops 9999999827968 | bytes 10000000000 | tf_op jit(solution)/shard_map/chain1/pallas_call | solution.py:179
  349.8 11.0 %collective-permute-done.24.refs_1_.peer = f32[2,704,256]{2,1,0:T(8,128)} collective-permute-done((f32[2,704,256]{2,1,0:T(8,128)}, f32[2,704,256]{2,1,0:T(8,128)}, u32[]{:S(2)}, u32[]{:S(2)}) %collective-permute-start.24) | collective-permute-done | bytes 1441824 | tf_op jit(solution)/shard_map/ppermute | solution.py:426
  368.3 10.5 %despread.5.refs_0_.refs_5_ = f32[8,2,448,256]{3,2,1,0:T(8,128)} custom-call(s32[32]{0:T(128)} %and_select_fusion.source, bf16[1,192,512]{2,1,0:T(8,128)(2,1)} %constant.91.clone.table, f32[32,8,896]{2,1,0:T(8,128)} %all-to-all-done.3.refs_1_.refs_0_, f32[8,2,448,256]{3,2,1,0:T(8,128)} %despread.4.refs_0_.refs_1_, f32[2,2,2,112,256]{4,3,2,1,0:T(8,128)} %chain0.16.refs_2_), custom_call_target="tpu_custom_call" | custom-call | flops 9999999827968 | bytes 10000000000 | tf_op jit(solution)/shard_map/despread/pallas_call | solution.py:362
  400.6 6.9 %chain1.16 = (f32[2,2,112,256]{3,2,1,0:T(8,128)}, f32[2,2,112,256]{3,2,1,0:T(8,128)}) custom-call(s32[1]{0:T(128)} %bitcast.side, f32[2,2]{1,0:T(2,128)} %maximum_select_fusion.rates, f32[2,704,256]{2,1,0:T(8,128)} %get-tuple-element.105.refs_5_.refs_0_.own, f32[2,704,256]{2,1,0:T(8,128)} %collective-permute-done.24.refs_1_.peer, ...), custom_call_target="tpu_custom_call" | custom-call | flops 9999999827968 | bytes 10000000000 | tf_op jit(solution)/shard_map/chain1/pallas_call | solution.py:179
  413.3 8.9 %collective-permute-done.27.odd = f32[2,2,112,256]{3,2,1,0:T(8,128)} collective-permute-done((f32[2,2,112,256]{3,2,1,0:T(8,128)}, f32[2,2,112,256]{3,2,1,0:T(8,128)}, u32[]{:S(2)}, u32[]{:S(2)}) %collective-permute-start.27) | collective-permute-done | bytes 458784 | tf_op jit(solution)/shard_map/ppermute | solution.py:503
  497.4 7.9 %collective-permute-done.39.odd = f32[1,2,112,256]{3,2,1,0:T(8,128)S(1)} collective-permute-done((f32[1,2,112,256]{3,2,1,0:T(8,128)}, f32[1,2,112,256]{3,2,1,0:T(8,128)S(1)}, u32[]{:S(2)}, u32[]{:S(2)}) %collective-permute-start.39) | collective-permute-done | bytes 229408 | tf_op jit(solution)/shard_map/ppermute | solution.py:503
  516.0 14.7 %despread.6.refs_1_ = f32[8,2,448,256]{3,2,1,0:T(8,128)} custom-call(s32[32]{0:T(128)} %and_select_fusion.source, bf16[2,256,512]{2,1,0:T(8,128)(2,1)} %constant.92.clone.table, f32[32,8,896]{2,1,0:T(8,128)} %all-to-all-done.4.refs_1_.refs_0_, f32[32,8,896]{2,1,0:T(8,128)} %all-to-all-done.5.refs_1_, f32[32,8,896]{2,1,0:T(8,128)} %all-to-all-done.6.refs_6_.refs_2_, ...), custom_call_target="tpu_custom_call" | custom-call | flops 9999999827968 | bytes 10000000000 | tf_op jit(solution)/shard_map/despread/pallas_call | solution.py:362
  532.3 9.0 %despread.7 = f32[8,2,448,256]{3,2,1,0:T(8,128)} custom-call(s32[32]{0:T(128)} %and_select_fusion.source, bf16[1,96,512]{2,1,0:T(8,128)(2,1)} %constant.93.clone.table, f32[32,8,448]{2,1,0:T(8,128)} %all-to-all-done.9.refs_0_, f32[8,2,448,256]{3,2,1,0:T(8,128)} %despread.6.refs_1_), custom_call_target="tpu_custom_call" | custom-call | flops 9999999827968 | bytes 10000000000 | tf_op jit(solution)/shard_map/despread/pallas_call | solution.py:362
  (158 shorter events, 311.1 us)
Async XLA Ops:
  7.3 37.9 %collective-permute-start.1 = (f32[1,448,256]{2,1,0:T(8,128)}, f32[1,448,256]{2,1,0:T(8,128)}, u32[]{:S(2)}, u32[]{:S(2)}) collective-permute-start(f32[1,448,256]{2,1,0:T(8,128)} %held_back.10.refs_0_), channel_id=1, source_target_pairs={{0,8},{8,0},{16,24},{24,16},{1,9},{9,1},{17,25},{25,17},{2,10},{10... | collective-permute-start | bytes 1376264 | tf_op jit(solution)/shard_map/ppermute | solution.py:433
  13.1 52.3 %collective-permute-start.4 = (f32[2,704,256]{2,1,0:T(8,128)}, f32[2,704,256]{2,1,0:T(8,128)}, u32[]{:S(2)}, u32[]{:S(2)}) collective-permute-start(f32[2,704,256]{2,1,0:T(8,128)} %get-tuple-element.68.refs_0_), channel_id=1, source_target_pairs={{0,8},{8,0},{16,24},{24,16},{1,9},{9,1},{17,25},{25,17},{2,10},{10... | collective-permute-start | bytes 4325384 | tf_op jit(solution)/shard_map/ppermute | solution.py:426
  31.8 64.2 %collective-permute-start.5 = (f32[2,448,256]{2,1,0:T(8,128)}, f32[2,448,256]{2,1,0:T(8,128)}, u32[]{:S(2)}, u32[]{:S(2)}) collective-permute-start(f32[2,448,256]{2,1,0:T(8,128)} %held_back.11.refs_0_), channel_id=1, source_target_pairs={{0,8},{8,0},{16,24},{24,16},{1,9},{9,1},{17,25},{25,17},{2,10},{10... | collective-permute-start | bytes 2752520 | tf_op jit(solution)/shard_map/ppermute | solution.py:433
  39.0 81.3 %collective-permute-start.8 = (f32[2,704,256]{2,1,0:T(8,128)}, f32[2,704,256]{2,1,0:T(8,128)}, u32[]{:S(2)}, u32[]{:S(2)}) collective-permute-start(f32[2,704,256]{2,1,0:T(8,128)} %get-tuple-element.72.refs_0_), channel_id=1, source_target_pairs={{0,8},{8,0},{16,24},{24,16},{1,9},{9,1},{17,25},{25,17},{2,10},{10... | collective-permute-start | bytes 4325384 | tf_op jit(solution)/shard_map/ppermute | solution.py:426
  77.2 50.5 %all-to-all-start = ((f32[32,8,448]{2,1,0:T(8,128)}), f32[32,8,448]{2,1,0:T(8,128)}, u32[]{:S(2)}, u32[]{:S(2)}) async-start(f32[32,8,448]{2,1,0:T(8,128)} %finish.10.refs_1_), calls=%async_computation | async-start | bytes 1048576 | tf_op jit(solution)/shard_map/all_to_all | solution.py:445
  82.4 69.8 %collective-permute-start.9 = (f32[2,448,256]{2,1,0:T(8,128)}, f32[2,448,256]{2,1,0:T(8,128)}, u32[]{:S(2)}, u32[]{:S(2)}) collective-permute-start(f32[2,448,256]{2,1,0:T(8,128)} %held_back.12.refs_0_), channel_id=1, source_target_pairs={{0,8},{8,0},{16,24},{24,16},{1,9},{9,1},{17,25},{25,17},{2,10},{10... | collective-permute-start | bytes 2752520 | tf_op jit(solution)/shard_map/ppermute | solution.py:433
  90.1 89.5 %collective-permute-start.12 = (f32[2,704,256]{2,1,0:T(8,128)}, f32[2,704,256]{2,1,0:T(8,128)}, u32[]{:S(2)}, u32[]{:S(2)}) collective-permute-start(f32[2,704,256]{2,1,0:T(8,128)} %get-tuple-element.78.refs_0_), channel_id=1, source_target_pairs={{0,8},{8,0},{16,24},{24,16},{1,9},{9,1},{17,25},{25,17},{2,10},{10... | collective-permute-start | bytes 4325384 | tf_op jit(solution)/shard_map/ppermute | solution.py:426
  133.5 53.6 %all-to-all-start.1 = ((f32[32,8,896]{2,1,0:T(8,128)}), f32[32,8,896]{2,1,0:T(8,128)}, u32[]{:S(2)}, u32[]{:S(2)}) async-start(f32[32,8,896]{2,1,0:T(8,128)} %finish.11.refs_1_), calls=%async_computation.1 | async-start | bytes 1835008 | tf_op jit(solution)/shard_map/all_to_all | solution.py:445
  138.7 77.4 %collective-permute-start.13 = (f32[2,448,256]{2,1,0:T(8,128)}, f32[2,448,256]{2,1,0:T(8,128)}, u32[]{:S(2)}, u32[]{:S(2)}) collective-permute-start(f32[2,448,256]{2,1,0:T(8,128)} %held_back.13.refs_0_), channel_id=1, source_target_pairs={{0,8},{8,0},{16,24},{24,16},{1,9},{9,1},{17,25},{25,17},{2,10},{10... | collective-permute-start | bytes 2752520 | tf_op jit(solution)/shard_map/ppermute | solution.py:433
  146.4 93.6 %collective-permute-start.16 = (f32[2,704,256]{2,1,0:T(8,128)}, f32[2,704,256]{2,1,0:T(8,128)}, u32[]{:S(2)}, u32[]{:S(2)}) collective-permute-start(f32[2,704,256]{2,1,0:T(8,128)} %get-tuple-element.84.refs_0_), channel_id=1, source_target_pairs={{0,8},{8,0},{16,24},{24,16},{1,9},{9,1},{17,25},{25,17},{2,10},{10... | collective-permute-start | bytes 4325384 | tf_op jit(solution)/shard_map/ppermute | solution.py:426
  192.8 54.7 %all-to-all-start.2 = ((f32[32,8,896]{2,1,0:T(8,128)}), f32[32,8,896]{2,1,0:T(8,128)}, u32[]{:S(2)}, u32[]{:S(2)}) async-start(f32[32,8,896]{2,1,0:T(8,128)} %finish.12.refs_1_), calls=%async_computation.2 | async-start | bytes 1835008 | tf_op jit(solution)/shard_map/all_to_all | solution.py:445
  198.3 78.0 %collective-permute-start.17 = (f32[2,448,256]{2,1,0:T(8,128)}, f32[2,448,256]{2,1,0:T(8,128)}, u32[]{:S(2)}, u32[]{:S(2)}) collective-permute-start(f32[2,448,256]{2,1,0:T(8,128)} %held_back.14.refs_0_), channel_id=1, source_target_pairs={{0,8},{8,0},{16,24},{24,16},{1,9},{9,1},{17,25},{25,17},{2,10},{10... | collective-permute-start | bytes 2752520 | tf_op jit(solution)/shard_map/ppermute | solution.py:433
  205.9 94.4 %collective-permute-start.20 = (f32[2,704,256]{2,1,0:T(8,128)}, f32[2,704,256]{2,1,0:T(8,128)}, u32[]{:S(2)}, u32[]{:S(2)}) collective-permute-start(f32[2,704,256]{2,1,0:T(8,128)} %get-tuple-element.90.refs_0_), channel_id=1, source_target_pairs={{0,8},{8,0},{16,24},{24,16},{1,9},{9,1},{17,25},{25,17},{2,10},{10... | collective-permute-start | bytes 4325384 | tf_op jit(solution)/shard_map/ppermute | solution.py:426
  253.2 64.7 %all-to-all-start.3 = ((f32[32,8,896]{2,1,0:T(8,128)}), f32[32,8,896]{2,1,0:T(8,128)}, u32[]{:S(2)}, u32[]{:S(2)}) async-start(f32[32,8,896]{2,1,0:T(8,128)} %finish.13.refs_1_), calls=%async_computation.3 | async-start | bytes 1835008 | tf_op jit(solution)/shard_map/all_to_all | solution.py:445
  258.4 82.6 %collective-permute-start.21 = (f32[2,448,256]{2,1,0:T(8,128)}, f32[2,448,256]{2,1,0:T(8,128)}, u32[]{:S(2)}, u32[]{:S(2)}) collective-permute-start(f32[2,448,256]{2,1,0:T(8,128)} %held_back.15.refs_0_), channel_id=1, source_target_pairs={{0,8},{8,0},{16,24},{24,16},{1,9},{9,1},{17,25},{25,17},{2,10},{10... | collective-permute-start | bytes 2752520 | tf_op jit(solution)/shard_map/ppermute | solution.py:433
  266.1 94.7 %collective-permute-start.24 = (f32[2,704,256]{2,1,0:T(8,128)}, f32[2,704,256]{2,1,0:T(8,128)}, u32[]{:S(2)}, u32[]{:S(2)}) collective-permute-start(f32[2,704,256]{2,1,0:T(8,128)} %get-tuple-element.95.refs_0_), channel_id=1, source_target_pairs={{0,8},{8,0},{16,24},{24,16},{1,9},{9,1},{17,25},{25,17},{2,10},{10... | collective-permute-start | bytes 4325384 | tf_op jit(solution)/shard_map/ppermute | solution.py:426
  283.2 34.7 %collective-permute-start.19 = (f32[2,2,112,256]{3,2,1,0:T(8,128)}, f32[2,2,112,256]{3,2,1,0:T(8,128)}, u32[]{:S(2)}, u32[]{:S(2)}) collective-permute-start(f32[2,2,112,256]{3,2,1,0:T(8,128)} %get-tuple-element.101), channel_id=1, source_target_pairs={{0,16},{8,24},{16,0},{24,8},{1,17},{9,25},{17,1},{25,9},{2,18},{10... | collective-permute-start | bytes 1376264 | tf_op jit(solution)/shard_map/ppermute | solution.py:503
  305.8 35.2 %collective-permute-start.22 = (f32[2,2,2,112,256]{4,3,2,1,0:T(8,128)}, f32[2,2,2,112,256]{4,3,2,1,0:T(8,128)}, u32[]{:S(2)}, u32[]{:S(2)}) collective-permute-start(f32[2,2,2,112,256]{4,3,2,1,0:T(8,128)} %chain0.15.refs_3_), channel_id=1, source_target_pairs={{0,16},{8,24},{16,0},{24,8},{1,17},{9,25},{17,1},{25,9},{2,18},{10... | collective-permute-start | bytes 2752520 | tf_op jit(solution)/shard_map/ppermute | solution.py:484
  323.7 55.0 %all-to-all-start.4 = ((f32[32,8,896]{2,1,0:T(8,128)}), f32[32,8,896]{2,1,0:T(8,128)}, u32[]{:S(2)}, u32[]{:S(2)}) async-start(f32[32,8,896]{2,1,0:T(8,128)} %finish.14.refs_1_), calls=%async_computation.4 | async-start | bytes 1835008 | tf_op jit(solution)/shard_map/all_to_all | solution.py:445
  328.9 71.7 %collective-permute-start.25 = (f32[2,448,256]{2,1,0:T(8,128)}, f32[2,448,256]{2,1,0:T(8,128)}, u32[]{:S(2)}, u32[]{:S(2)}) collective-permute-start(f32[2,448,256]{2,1,0:T(8,128)} %held_back.16.refs_0_), channel_id=1, source_target_pairs={{0,8},{8,0},{16,24},{24,16},{1,9},{9,1},{17,25},{25,17},{2,10},{10... | collective-permute-start | bytes 2752520 | tf_op jit(solution)/shard_map/ppermute | solution.py:433
  335.2 74.1 %collective-permute-start.28 = (f32[1,704,256]{2,1,0:T(8,128)}, f32[1,704,256]{2,1,0:T(8,128)}, u32[]{:S(2)}, u32[]{:S(2)}) collective-permute-start(f32[1,704,256]{2,1,0:T(8,128)} %get-tuple-element.104.refs_0_), channel_id=1, source_target_pairs={{0,8},{8,0},{16,24},{24,16},{1,9},{9,1},{17,25},{25,17},{2,10},{10... | collective-permute-start | bytes 2162696 | tf_op jit(solution)/shard_map/ppermute | solution.py:426
  384.5 37.7 %all-to-all-start.5 = ((f32[32,8,896]{2,1,0:T(8,128)}), f32[32,8,896]{2,1,0:T(8,128)}, u32[]{:S(2)}, u32[]{:S(2)}) async-start(f32[32,8,896]{2,1,0:T(8,128)} %finish.15.refs_1_), calls=%async_computation.5 | async-start | bytes 1835008 | tf_op jit(solution)/shard_map/all_to_all | solution.py:445
  389.9 49.6 %collective-permute-start.30 = (f32[1,448,256]{2,1,0:T(8,128)}, f32[1,448,256]{2,1,0:T(8,128)}, u32[]{:S(2)}, u32[]{:S(2)}) collective-permute-start(f32[1,448,256]{2,1,0:T(8,128)} %held_back.17.refs_0_), channel_id=1, source_target_pairs={{0,8},{8,0},{16,24},{24,16},{1,9},{9,1},{17,25},{25,17},{2,10},{10... | collective-permute-start | bytes 1376264 | tf_op jit(solution)/shard_map/ppermute | solution.py:433
  396.1 49.6 %collective-permute-start.33 = (f32[1,704,256]{2,1,0:T(8,128)}, f32[1,704,256]{2,1,0:T(8,128)}, u32[]{:S(2)}, u32[]{:S(2)}) collective-permute-start(f32[1,704,256]{2,1,0:T(8,128)} %get-tuple-element.110.refs_0_), channel_id=1, source_target_pairs={{0,8},{8,0},{16,24},{24,16},{1,9},{9,1},{17,25},{25,17},{2,10},{10... | collective-permute-start | bytes 2162696 | tf_op jit(solution)/shard_map/ppermute | solution.py:426
  (31 other events, 643.2 us)

commit v9 on v8

--- a/solution.py
+++ b/solution.py
@@ -474,17 +474,14 @@
     ahead = {c: [c + 1] for c in range(chunks - 1)}
     parts = {}
     if chunks > 8:
-        for c in (chunks - 2, chunks - 1):
+        for c in range(chunks - 3, chunks):
             ahead[c - 1].remove(c)
             ahead[c - 5].append(c)
-        parts = {chunks - 5: chunks - 7, chunks - 4: chunks - 6}
+        parts = {chunks - 5: chunks - 6}
     begin, total = 0, None
     for c in range(chunks):
         before = chain(0, False, rows, side_alone, rates, own[c], peer[c], [], [before])
         both = lax.ppermute(before, "blk", onward)
-        if c in parts:
-            total = bring_together(begin, parts[c], total, False, [before])
-            begin, before = parts[c], total
         if c > 0:
             before = complete(c - 1, [before] + ([] if c >= chunks - 2 else pieces[-1:]))
         if c + 1 < chunks:
@@ -502,6 +499,9 @@
         even, moving = done
         odd[c] = (even, lax.ppermute(moving, "blk", onward))
         before = even
+        if c in parts:
+            total = bring_together(begin, parts[c], total, False, [before])
+            begin, before = parts[c], total
     before = complete(chunks - 1, [before] + pieces[-1:])
     if begin < chunks - 1:
         total = bring_together(begin, chunks - 1, total, False, [before])

time: 551 us -> 550 us (level)
  Pallas kernels: 306 us -> 297 us
  starting transfers between devices: 106 us -> 112 us
    ppermute x10, waiting for transfers between devices: 22.9 us -> 9.12 us  [on_device(): odd[c] = (even, lax.ppermute(moving, 'blk', onward))]
    ppermute x10, waiting for transfers between devices: 93.5 us -> 104 us  [ready_peer(): peer[c] = [lax.ppermute(sent[0], 'blk', swap)]]
    pallas_call x4 -> x3, Pallas kernels: 44.2 us -> 35.2 us  [despread(): pl.pallas_call(functools.partial(despread_body, groups, sizes, rows, fold...]
    ppermute x10, waiting for transfers between devices: 0.03 us -> 6.14 us  [on_device(): both = lax.ppermute(before, 'blk', onward)]
  transfers between devices with their start and end apart: 50 -> 50, of which waited for: 15 -> 16; matrix products, arithmetic and copies ran while one was open for 1% -> 1% of each run, Pallas kernels for 53% -> 52%
where the time goes in v9:
time: 550 us; the launch traced here: 540 us
  Pallas kernels  297 us (54%)
  waiting for transfers between devices  124 us (23%)
  starting transfers between devices  112 us (20%)
    pallas_call x20, Pallas kernels, chain(): pl.pallas_call(functools.partial(chain_body, round_index, last, rows), ou...  107 us
    ppermute x10, waiting for transfers between devices, ready_peer(): peer[c] = [lax.ppermute(sent[0], 'blk', swap)]  104 us
    pallas_call x20, Pallas kernels, prepare(): pl.pallas_call(functools.partial(prepare_body, carry, blocks), out_shape=...  103 us
    pallas_call x10, Pallas kernels, finish(): pl.pallas_call(functools.partial(finish_body, count, rows), out_shape=jax...  51.3 us
    all_to_all x10, starting transfers between devices, complete(): lax.all_to_all(done, ('blk', 'tones'), split_axis=0, concat_axis=0, tiled...  51.1 us
    pallas_call x3, Pallas kernels, despread(): pl.pallas_call(functools.partial(despread_body, groups, sizes, rows, fold...  35.2 us
    ppermute x10, starting transfers between devices, on_device(): both = lax.ppermute(before, 'blk', onward)  21.1 us
    ppermute x10, starting transfers between devices, send_later(): peer[c].append(lax.ppermute(value, 'blk', swap))  16.9 us
  transfers between devices with their start and end apart: 50, of which 16 were waited for; matrix products, arithmetic and copies ran while one was open for 1% of the time, Pallas kernels for 52%

profile of v9, /device:TPU:0, one launch (start us, length us, event | category | flops | bytes accessed | tf_op | source)
XLA Modules:
  0.0 540.0 jit_solution(4117118006794800635)
XLA Ops:
  7.3 5.8 %prepare.21 = (f32[2,704,256]{2,1,0:T(8,128)}, f32[2,448,256]{2,1,0:T(8,128)}) custom-call(s32[1]{0:T(128)} %bitcast.3.base, s32[1]{0:T(128)} %bitcast.4.pair, s32[1]{0:T(128)} %bitcast.5.group, s32[8]{0:T(128)} %hop_offset.39, f32[1,2]{1,0:T(1,128)} %rates.39, f32[32,2,256,256]{3,2,1,0:T(8,128)} %chan.39, f32[32,2,448,256]{3,2,1,0:T(8,128)} %recv.39, ...), custom_call_target="tpu_custom_call" | custom-call | flops 9999999827968 | bytes 10000000000 | tf_op jit(solution)/shard_map/prepare/pallas_call | solution.py:86
  49.8 15.6 %collective-permute-done.4.refs_1_.peer = f32[2,704,256]{2,1,0:T(8,128)} collective-permute-done((f32[2,704,256]{2,1,0:T(8,128)}, f32[2,704,256]{2,1,0:T(8,128)}, u32[]{:S(2)}, u32[]{:S(2)}) %collective-permute-start.4) | collective-permute-done | bytes 1441824 | tf_op jit(solution)/shard_map/ppermute | solution.py:426
  96.2 6.9 %chain1.11 = (f32[2,2,112,256]{3,2,1,0:T(8,128)}, f32[2,2,112,256]{3,2,1,0:T(8,128)}) custom-call(s32[1]{0:T(128)} %bitcast.side, f32[2,2]{1,0:T(2,128)} %maximum_select_fusion.rates, f32[2,704,256]{2,1,0:T(8,128)} %get-tuple-element.73.refs_5_.refs_0_.own, f32[2,704,256]{2,1,0:T(8,128)} %collective-permute-done.4.refs_1_.peer, ...), custom_call_target="tpu_custom_call" | custom-call | flops 9999999827968 | bytes 10000000000 | tf_op jit(solution)/shard_map/chain1/pallas_call | solution.py:179
  105.0 15.2 %collective-permute-done.8.refs_1_.peer = f32[2,704,256]{2,1,0:T(8,128)} collective-permute-done((f32[2,704,256]{2,1,0:T(8,128)}, f32[2,704,256]{2,1,0:T(8,128)}, u32[]{:S(2)}, u32[]{:S(2)}) %collective-permute-start.8) | collective-permute-done | bytes 1441824 | tf_op jit(solution)/shard_map/ppermute | solution.py:426
  127.7 5.7 %finish.11.refs_1_ = f32[32,8,896]{2,1,0:T(8,128)} custom-call(s32[2]{0:T(128)} %pad_add_fusion.scalars, f32[2,2]{1,0:T(2,128)} %maximum_select_fusion.rates, f32[2,704,256]{2,1,0:T(8,128)} %get-tuple-element.73.refs_5_.refs_0_.own, f32[2,704,256]{2,1,0:T(8,128)} %collective-permute-done.4.refs_1_.peer, f32[2,2,112,256]{3,2,1,0:T(8,128)} %get-tuple-element.80.refs_2_.even, ...), custom_call_target="tpu_custom_call" | custom-call | flops 9999999827968 | bytes 10000000000 | tf_op jit(solution)/shard_map/finish/pallas_call | solution.py:236
  156.5 6.9 %chain1.12 = (f32[2,2,112,256]{3,2,1,0:T(8,128)}, f32[2,2,112,256]{3,2,1,0:T(8,128)}) custom-call(s32[1]{0:T(128)} %bitcast.side, f32[2,2]{1,0:T(2,128)} %maximum_select_fusion.rates, f32[2,704,256]{2,1,0:T(8,128)} %get-tuple-element.79.refs_5_.refs_0_.own, f32[2,704,256]{2,1,0:T(8,128)} %collective-permute-done.8.refs_1_.peer, ...), custom_call_target="tpu_custom_call" | custom-call | flops 9999999827968 | bytes 10000000000 | tf_op jit(solution)/shard_map/chain1/pallas_call | solution.py:179
  165.3 14.2 %collective-permute-done.12.refs_1_.peer = f32[2,704,256]{2,1,0:T(8,128)} collective-permute-done((f32[2,704,256]{2,1,0:T(8,128)}, f32[2,704,256]{2,1,0:T(8,128)}, u32[]{:S(2)}, u32[]{:S(2)}) %collective-permute-start.12) | collective-permute-done | bytes 1441824 | tf_op jit(solution)/shard_map/ppermute | solution.py:426
  187.1 5.7 %finish.12.refs_1_ = f32[32,8,896]{2,1,0:T(8,128)} custom-call(s32[2]{0:T(128)} %pad_add_fusion.scalars, f32[2,2]{1,0:T(2,128)} %maximum_select_fusion.rates, f32[2,704,256]{2,1,0:T(8,128)} %get-tuple-element.79.refs_5_.refs_0_.own, f32[2,704,256]{2,1,0:T(8,128)} %collective-permute-done.8.refs_1_.peer, f32[2,2,112,256]{3,2,1,0:T(8,128)} %get-tuple-element.87.refs_2_.even, ...), custom_call_target="tpu_custom_call" | custom-call | flops 9999999827968 | bytes 10000000000 | tf_op jit(solution)/shard_map/finish/pallas_call | solution.py:236
  205.8 5.7 %prepare.31 = (f32[2,704,256]{2,1,0:T(8,128)}, f32[2,448,256]{2,1,0:T(8,128)}) custom-call(s32[1]{0:T(128)} %bitcast.7.base, s32[1]{0:T(128)} %bitcast.4.pair, s32[1]{0:T(128)} %bitcast.5.group, s32[8]{0:T(128)} %hop_offset.39, f32[1,2]{1,0:T(1,128)} %rates.39, f32[32,2,256,256]{3,2,1,0:T(8,128)} %chan.39, f32[32,2,448,256]{3,2,1,0:T(8,128)} %recv.39, ...), custom_call_target="tpu_custom_call" | custom-call | flops 9999999827968 | bytes 10000000000 | tf_op jit(solution)/shard_map/prepare/pallas_call | solution.py:86
  216.0 6.9 %chain1.13 = (f32[2,2,112,256]{3,2,1,0:T(8,128)}, f32[2,2,112,256]{3,2,1,0:T(8,128)}) custom-call(s32[1]{0:T(128)} %bitcast.side, f32[2,2]{1,0:T(2,128)} %maximum_select_fusion.rates, f32[2,704,256]{2,1,0:T(8,128)} %get-tuple-element.85.refs_0_.own, f32[2,704,256]{2,1,0:T(8,128)} %collective-permute-done.12.refs_1_.peer, ...), custom_call_target="tpu_custom_call" | custom-call | flops 9999999827968 | bytes 10000000000 | tf_op jit(solution)/shard_map/chain1/pallas_call | solution.py:179
  224.7 15.2 %collective-permute-done.16.refs_1_.peer = f32[2,704,256]{2,1,0:T(8,128)} collective-permute-done((f32[2,704,256]{2,1,0:T(8,128)}, f32[2,704,256]{2,1,0:T(8,128)}, u32[]{:S(2)}, u32[]{:S(2)}) %collective-permute-start.16) | collective-permute-done | bytes 1441824 | tf_op jit(solution)/shard_map/ppermute | solution.py:426
  276.4 6.9 %chain1.14 = (f32[2,2,112,256]{3,2,1,0:T(8,128)}, f32[2,2,112,256]{3,2,1,0:T(8,128)}) custom-call(s32[1]{0:T(128)} %bitcast.side, f32[2,2]{1,0:T(2,128)} %maximum_select_fusion.rates, f32[2,704,256]{2,1,0:T(8,128)} %get-tuple-element.92.refs_0_.own, f32[2,704,256]{2,1,0:T(8,128)} %collective-permute-done.16.refs_1_.peer, ...), custom_call_target="tpu_custom_call" | custom-call | flops 9999999827968 | bytes 10000000000 | tf_op jit(solution)/shard_map/chain1/pallas_call | solution.py:179
  285.1 15.2 %collective-permute-done.20.refs_1_.peer = f32[2,704,256]{2,1,0:T(8,128)} collective-permute-done((f32[2,704,256]{2,1,0:T(8,128)}, f32[2,704,256]{2,1,0:T(8,128)}, u32[]{:S(2)}, u32[]{:S(2)}) %collective-permute-start.20) | collective-permute-done | bytes 1441824 | tf_op jit(solution)/shard_map/ppermute | solution.py:426
  307.9 5.7 %finish.14.refs_1_ = f32[32,8,896]{2,1,0:T(8,128)} custom-call(s32[2]{0:T(128)} %pad_add_fusion.scalars, f32[2,2]{1,0:T(2,128)} %maximum_select_fusion.rates, f32[2,704,256]{2,1,0:T(8,128)} %get-tuple-element.92.refs_0_.own, f32[2,704,256]{2,1,0:T(8,128)} %collective-permute-done.16.refs_1_.peer, f32[2,2,112,256]{3,2,1,0:T(8,128)} %get-tuple-element.101.refs_2_.even, ...), custom_call_target="tpu_custom_call" | custom-call | flops 9999999827968 | bytes 10000000000 | tf_op jit(solution)/shard_map/finish/pallas_call | solution.py:236
  331.3 6.9 %chain1.15 = (f32[2,2,112,256]{3,2,1,0:T(8,128)}, f32[2,2,112,256]{3,2,1,0:T(8,128)}) custom-call(s32[1]{0:T(128)} %bitcast.side, f32[2,2]{1,0:T(2,128)} %maximum_select_fusion.rates, f32[2,704,256]{2,1,0:T(8,128)} %get-tuple-element.97.refs_0_.own, f32[2,704,256]{2,1,0:T(8,128)} %collective-permute-done.20.refs_1_.peer, ...), custom_call_target="tpu_custom_call" | custom-call | flops 9999999827968 | bytes 10000000000 | tf_op jit(solution)/shard_map/chain1/pallas_call | solution.py:179
  340.0 11.4 %despread.3.refs_2_.refs_5_ = f32[8,2,448,256]{3,2,1,0:T(8,128)} custom-call(s32[32]{0:T(128)} %and_select_fusion.source, bf16[2,224,512]{2,1,0:T(8,128)(2,1)} %constant.88.clone.table, f32[32,8,448]{2,1,0:T(8,128)} %all-to-all-done.refs_1_.refs_0_, f32[32,8,896]{2,1,0:T(8,128)} %all-to-all-done.1.refs_1_, f32[32,8,896]{2,1,0:T(8,128)} %all-to-all-done.2.refs_1_.refs_2_, ...), custom_call_target="tpu_custom_call" | custom-call | flops 9999999827968 | bytes 10000000000 | tf_op jit(solution)/shard_map/despread/pallas_call | solution.py:362
  351.4 9.3 %collective-permute-done.24.refs_1_.peer = f32[2,704,256]{2,1,0:T(8,128)} collective-permute-done((f32[2,704,256]{2,1,0:T(8,128)}, f32[2,704,256]{2,1,0:T(8,128)}, u32[]{:S(2)}, u32[]{:S(2)}) %collective-permute-start.24) | collective-permute-done | bytes 1441824 | tf_op jit(solution)/shard_map/ppermute | solution.py:426
  368.3 5.7 %finish.15.refs_1_ = f32[32,8,896]{2,1,0:T(8,128)} custom-call(s32[2]{0:T(128)} %pad_add_fusion.scalars, f32[2,2]{1,0:T(2,128)} %maximum_select_fusion.rates, f32[2,704,256]{2,1,0:T(8,128)} %get-tuple-element.97.refs_0_.own, f32[2,704,256]{2,1,0:T(8,128)} %collective-permute-done.20.refs_1_.peer, f32[2,2,112,256]{3,2,1,0:T(8,128)} %get-tuple-element.107.refs_4_.even, ...), custom_call_target="tpu_custom_call" | custom-call | flops 9999999827968 | bytes 10000000000 | tf_op jit(solution)/shard_map/finish/pallas_call | solution.py:236
  385.7 6.1 %collective-permute-done.26.refs_4_ = f32[2,2,2,112,256]{4,3,2,1,0:T(8,128)} collective-permute-done((f32[2,2,2,112,256]{4,3,2,1,0:T(8,128)}, f32[2,2,2,112,256]{4,3,2,1,0:T(8,128)}, u32[]{:S(2)}, u32[]{:S(2)}) %collective-permute-start.26) | collective-permute-done | bytes 917536 | tf_op jit(solution)/shard_map/ppermute | solution.py:484
  391.8 6.9 %chain1.16 = (f32[2,2,112,256]{3,2,1,0:T(8,128)}, f32[2,2,112,256]{3,2,1,0:T(8,128)}) custom-call(s32[1]{0:T(128)} %bitcast.side, f32[2,2]{1,0:T(2,128)} %maximum_select_fusion.rates, f32[2,704,256]{2,1,0:T(8,128)} %get-tuple-element.106.refs_5_.refs_0_.own, f32[2,704,256]{2,1,0:T(8,128)} %collective-permute-done.24.refs_1_.peer, ...), custom_call_target="tpu_custom_call" | custom-call | flops 9999999827968 | bytes 10000000000 | tf_op jit(solution)/shard_map/chain1/pallas_call | solution.py:179
  462.9 9.8 %collective-permute-done.29.refs_1_.peer = f32[1,704,256]{2,1,0:T(8,128)} collective-permute-done((f32[1,704,256]{2,1,0:T(8,128)}, f32[1,704,256]{2,1,0:T(8,128)}, u32[]{:S(2)}, u32[]{:S(2)}) %collective-permute-start.29) | collective-permute-done | bytes 720928 | tf_op jit(solution)/shard_map/ppermute | solution.py:426
  495.6 7.9 %collective-permute-done.39.odd = f32[1,2,112,256]{3,2,1,0:T(8,128)S(1)} collective-permute-done((f32[1,2,112,256]{3,2,1,0:T(8,128)}, f32[1,2,112,256]{3,2,1,0:T(8,128)S(1)}, u32[]{:S(2)}, u32[]{:S(2)}) %collective-permute-start.39) | collective-permute-done | bytes 229408 | tf_op jit(solution)/shard_map/ppermute | solution.py:500
  514.3 14.8 %despread.4.refs_1_ = f32[8,2,448,256]{3,2,1,0:T(8,128)} custom-call(s32[32]{0:T(128)} %and_select_fusion.source, bf16[2,256,512]{2,1,0:T(8,128)(2,1)} %constant.89.clone.table, f32[32,8,896]{2,1,0:T(8,128)} %all-to-all-done.4.refs_1_.refs_0_, f32[32,8,896]{2,1,0:T(8,128)} %all-to-all-done.5.refs_1_, f32[32,8,896]{2,1,0:T(8,128)} %all-to-all-done.6.refs_6_.refs_2_, ...), custom_call_target="tpu_custom_call" | custom-call | flops 9999999827968 | bytes 10000000000 | tf_op jit(solution)/shard_map/despread/pallas_call | solution.py:362
  530.6 9.0 %despread.5 = f32[8,2,448,256]{3,2,1,0:T(8,128)} custom-call(s32[32]{0:T(128)} %and_select_fusion.source, bf16[1,96,512]{2,1,0:T(8,128)(2,1)} %constant.90.clone.table, f32[32,8,448]{2,1,0:T(8,128)} %all-to-all-done.9.refs_0_, f32[8,2,448,256]{3,2,1,0:T(8,128)} %despread.4.refs_1_), custom_call_target="tpu_custom_call" | custom-call | flops 9999999827968 | bytes 10000000000 | tf_op jit(solution)/shard_map/despread/pallas_call | solution.py:362
  (157 shorter events, 317.7 us)
Async XLA Ops:
  7.3 38.0 %collective-permute-start.1 = (f32[1,448,256]{2,1,0:T(8,128)}, f32[1,448,256]{2,1,0:T(8,128)}, u32[]{:S(2)}, u32[]{:S(2)}) collective-permute-start(f32[1,448,256]{2,1,0:T(8,128)} %held_back.10.refs_0_), channel_id=1, source_target_pairs={{0,8},{8,0},{16,24},{24,16},{1,9},{9,1},{17,25},{25,17},{2,10},{10... | collective-permute-start | bytes 1376264 | tf_op jit(solution)/shard_map/ppermute | solution.py:433
  13.1 52.3 %collective-permute-start.4 = (f32[2,704,256]{2,1,0:T(8,128)}, f32[2,704,256]{2,1,0:T(8,128)}, u32[]{:S(2)}, u32[]{:S(2)}) collective-permute-start(f32[2,704,256]{2,1,0:T(8,128)} %get-tuple-element.68.refs_0_), channel_id=1, source_target_pairs={{0,8},{8,0},{16,24},{24,16},{1,9},{9,1},{17,25},{25,17},{2,10},{10... | collective-permute-start | bytes 4325384 | tf_op jit(solution)/shard_map/ppermute | solution.py:426
  31.9 64.4 %collective-permute-start.5 = (f32[2,448,256]{2,1,0:T(8,128)}, f32[2,448,256]{2,1,0:T(8,128)}, u32[]{:S(2)}, u32[]{:S(2)}) collective-permute-start(f32[2,448,256]{2,1,0:T(8,128)} %held_back.11.refs_0_), channel_id=1, source_target_pairs={{0,8},{8,0},{16,24},{24,16},{1,9},{9,1},{17,25},{25,17},{2,10},{10... | collective-permute-start | bytes 2752520 | tf_op jit(solution)/shard_map/ppermute | solution.py:433
  39.0 81.2 %collective-permute-start.8 = (f32[2,704,256]{2,1,0:T(8,128)}, f32[2,704,256]{2,1,0:T(8,128)}, u32[]{:S(2)}, u32[]{:S(2)}) collective-permute-start(f32[2,704,256]{2,1,0:T(8,128)} %get-tuple-element.72.refs_0_), channel_id=1, source_target_pairs={{0,8},{8,0},{16,24},{24,16},{1,9},{9,1},{17,25},{25,17},{2,10},{10... | collective-permute-start | bytes 4325384 | tf_op jit(solution)/shard_map/ppermute | solution.py:426
  77.2 50.5 %all-to-all-start = ((f32[32,8,448]{2,1,0:T(8,128)}), f32[32,8,448]{2,1,0:T(8,128)}, u32[]{:S(2)}, u32[]{:S(2)}) async-start(f32[32,8,448]{2,1,0:T(8,128)} %finish.10.refs_1_), calls=%async_computation | async-start | bytes 1048576 | tf_op jit(solution)/shard_map/all_to_all | solution.py:445
  82.8 73.8 %collective-permute-start.9 = (f32[2,448,256]{2,1,0:T(8,128)}, f32[2,448,256]{2,1,0:T(8,128)}, u32[]{:S(2)}, u32[]{:S(2)}) collective-permute-start(f32[2,448,256]{2,1,0:T(8,128)} %held_back.12.refs_0_), channel_id=1, source_target_pairs={{0,8},{8,0},{16,24},{24,16},{1,9},{9,1},{17,25},{25,17},{2,10},{10... | collective-permute-start | bytes 2752520 | tf_op jit(solution)/shard_map/ppermute | solution.py:433
  90.4 89.2 %collective-permute-start.12 = (f32[2,704,256]{2,1,0:T(8,128)}, f32[2,704,256]{2,1,0:T(8,128)}, u32[]{:S(2)}, u32[]{:S(2)}) collective-permute-start(f32[2,704,256]{2,1,0:T(8,128)} %get-tuple-element.78.refs_0_), channel_id=1, source_target_pairs={{0,8},{8,0},{16,24},{24,16},{1,9},{9,1},{17,25},{25,17},{2,10},{10... | collective-permute-start | bytes 4325384 | tf_op jit(solution)/shard_map/ppermute | solution.py:426
  133.5 53.6 %all-to-all-start.1 = ((f32[32,8,896]{2,1,0:T(8,128)}), f32[32,8,896]{2,1,0:T(8,128)}, u32[]{:S(2)}, u32[]{:S(2)}) async-start(f32[32,8,896]{2,1,0:T(8,128)} %finish.11.refs_1_), calls=%async_computation.1 | async-start | bytes 1835008 | tf_op jit(solution)/shard_map/all_to_all | solution.py:445
  138.7 77.2 %collective-permute-start.13 = (f32[2,448,256]{2,1,0:T(8,128)}, f32[2,448,256]{2,1,0:T(8,128)}, u32[]{:S(2)}, u32[]{:S(2)}) collective-permute-start(f32[2,448,256]{2,1,0:T(8,128)} %held_back.13.refs_0_), channel_id=1, source_target_pairs={{0,8},{8,0},{16,24},{24,16},{1,9},{9,1},{17,25},{25,17},{2,10},{10... | collective-permute-start | bytes 2752520 | tf_op jit(solution)/shard_map/ppermute | solution.py:433
  146.3 93.6 %collective-permute-start.16 = (f32[2,704,256]{2,1,0:T(8,128)}, f32[2,704,256]{2,1,0:T(8,128)}, u32[]{:S(2)}, u32[]{:S(2)}) collective-permute-start(f32[2,704,256]{2,1,0:T(8,128)} %get-tuple-element.84.refs_0_), channel_id=1, source_target_pairs={{0,8},{8,0},{16,24},{24,16},{1,9},{9,1},{17,25},{25,17},{2,10},{10... | collective-permute-start | bytes 4325384 | tf_op jit(solution)/shard_map/ppermute | solution.py:426
  192.8 54.7 %all-to-all-start.2 = ((f32[32,8,896]{2,1,0:T(8,128)}), f32[32,8,896]{2,1,0:T(8,128)}, u32[]{:S(2)}, u32[]{:S(2)}) async-start(f32[32,8,896]{2,1,0:T(8,128)} %finish.12.refs_1_), calls=%async_computation.2 | async-start | bytes 1835008 | tf_op jit(solution)/shard_map/all_to_all | solution.py:445
  198.1 78.3 %collective-permute-start.17 = (f32[2,448,256]{2,1,0:T(8,128)}, f32[2,448,256]{2,1,0:T(8,128)}, u32[]{:S(2)}, u32[]{:S(2)}) collective-permute-start(f32[2,448,256]{2,1,0:T(8,128)} %held_back.14.refs_0_), channel_id=1, source_target_pairs={{0,8},{8,0},{16,24},{24,16},{1,9},{9,1},{17,25},{25,17},{2,10},{10... | collective-permute-start | bytes 2752520 | tf_op jit(solution)/shard_map/ppermute | solution.py:433
  205.7 94.6 %collective-permute-start.20 = (f32[2,704,256]{2,1,0:T(8,128)}, f32[2,704,256]{2,1,0:T(8,128)}, u32[]{:S(2)}, u32[]{:S(2)}) collective-permute-start(f32[2,704,256]{2,1,0:T(8,128)} %get-tuple-element.91.refs_0_), channel_id=1, source_target_pairs={{0,8},{8,0},{16,24},{24,16},{1,9},{9,1},{17,25},{25,17},{2,10},{10... | collective-permute-start | bytes 4325384 | tf_op jit(solution)/shard_map/ppermute | solution.py:426
  253.2 54.6 %all-to-all-start.3 = ((f32[32,8,896]{2,1,0:T(8,128)}), f32[32,8,896]{2,1,0:T(8,128)}, u32[]{:S(2)}, u32[]{:S(2)}) async-start(f32[32,8,896]{2,1,0:T(8,128)} %finish.13.refs_1_), calls=%async_computation.3 | async-start | bytes 1835008 | tf_op jit(solution)/shard_map/all_to_all | solution.py:445
  258.5 72.7 %collective-permute-start.21 = (f32[2,448,256]{2,1,0:T(8,128)}, f32[2,448,256]{2,1,0:T(8,128)}, u32[]{:S(2)}, u32[]{:S(2)}) collective-permute-start(f32[2,448,256]{2,1,0:T(8,128)} %held_back.15.refs_0_), channel_id=1, source_target_pairs={{0,8},{8,0},{16,24},{24,16},{1,9},{9,1},{17,25},{25,17},{2,10},{10... | collective-permute-start | bytes 2752520 | tf_op jit(solution)/shard_map/ppermute | solution.py:433
  266.1 94.6 %collective-permute-start.24 = (f32[2,704,256]{2,1,0:T(8,128)}, f32[2,704,256]{2,1,0:T(8,128)}, u32[]{:S(2)}, u32[]{:S(2)}) collective-permute-start(f32[2,704,256]{2,1,0:T(8,128)} %get-tuple-element.96.refs_0_), channel_id=1, source_target_pairs={{0,8},{8,0},{16,24},{24,16},{1,9},{9,1},{17,25},{25,17},{2,10},{10... | collective-permute-start | bytes 4325384 | tf_op jit(solution)/shard_map/ppermute | solution.py:426
  313.6 54.7 %all-to-all-start.4 = ((f32[32,8,896]{2,1,0:T(8,128)}), f32[32,8,896]{2,1,0:T(8,128)}, u32[]{:S(2)}, u32[]{:S(2)}) async-start(f32[32,8,896]{2,1,0:T(8,128)} %finish.14.refs_1_), calls=%async_computation.4 | async-start | bytes 1835008 | tf_op jit(solution)/shard_map/all_to_all | solution.py:445
  319.1 66.6 %collective-permute-start.25 = (f32[2,448,256]{2,1,0:T(8,128)}, f32[2,448,256]{2,1,0:T(8,128)}, u32[]{:S(2)}, u32[]{:S(2)}) collective-permute-start(f32[2,448,256]{2,1,0:T(8,128)} %held_back.16.refs_0_), channel_id=1, source_target_pairs={{0,8},{8,0},{16,24},{24,16},{1,9},{9,1},{17,25},{25,17},{2,10},{10... | collective-permute-start | bytes 2752520 | tf_op jit(solution)/shard_map/ppermute | solution.py:433
  325.4 80.2 %collective-permute-start.28 = (f32[1,704,256]{2,1,0:T(8,128)}, f32[1,704,256]{2,1,0:T(8,128)}, u32[]{:S(2)}, u32[]{:S(2)}) collective-permute-start(f32[1,704,256]{2,1,0:T(8,128)} %get-tuple-element.105.refs_0_), channel_id=1, source_target_pairs={{0,8},{8,0},{16,24},{24,16},{1,9},{9,1},{17,25},{25,17},{2,10},{10... | collective-permute-start | bytes 2162696 | tf_op jit(solution)/shard_map/ppermute | solution.py:426
  374.0 37.6 %all-to-all-start.5 = ((f32[32,8,896]{2,1,0:T(8,128)}), f32[32,8,896]{2,1,0:T(8,128)}, u32[]{:S(2)}, u32[]{:S(2)}) async-start(f32[32,8,896]{2,1,0:T(8,128)} %finish.15.refs_1_), calls=%async_computation.5 | async-start | bytes 1835008 | tf_op jit(solution)/shard_map/all_to_all | solution.py:445
  379.2 49.6 %collective-permute-start.30 = (f32[1,448,256]{2,1,0:T(8,128)}, f32[1,448,256]{2,1,0:T(8,128)}, u32[]{:S(2)}, u32[]{:S(2)}) collective-permute-start(f32[1,448,256]{2,1,0:T(8,128)} %held_back.17.refs_0_), channel_id=1, source_target_pairs={{0,8},{8,0},{16,24},{24,16},{1,9},{9,1},{17,25},{25,17},{2,10},{10... | collective-permute-start | bytes 1376264 | tf_op jit(solution)/shard_map/ppermute | solution.py:433
  385.5 52.9 %collective-permute-start.33 = (f32[1,704,256]{2,1,0:T(8,128)}, f32[1,704,256]{2,1,0:T(8,128)}, u32[]{:S(2)}, u32[]{:S(2)}) collective-permute-start(f32[1,704,256]{2,1,0:T(8,128)} %get-tuple-element.111.refs_5_), channel_id=1, source_target_pairs={{0,8},{8,0},{16,24},{24,16},{1,9},{9,1},{17,25},{25,17},{2,10},{10... | collective-permute-start | bytes 2162696 | tf_op jit(solution)/shard_map/ppermute | solution.py:426
  428.4 44.3 %collective-permute-start.29 = (f32[1,704,256]{2,1,0:T(8,128)}, f32[1,704,256]{2,1,0:T(8,128)}, u32[]{:S(2)}, u32[]{:S(2)}) collective-permute-start(f32[1,704,256]{2,1,0:T(8,128)} %get-tuple-element.114.refs_5_), channel_id=1, source_target_pairs={{0,8},{8,0},{16,24},{24,16},{1,9},{9,1},{17,25},{25,17},{2,10},{10... | collective-permute-start | bytes 2162696 | tf_op jit(solution)/shard_map/ppermute | solution.py:426
  449.6 39.8 %collective-permute-start.34 = (f32[1,448,256]{2,1,0:T(8,128)}, f32[1,448,256]{2,1,0:T(8,128)}, u32[]{:S(2)}, u32[]{:S(2)}) collective-permute-start(f32[1,448,256]{2,1,0:T(8,128)} %held_back.19.refs_5_), channel_id=1, source_target_pairs={{0,8},{8,0},{16,24},{24,16},{1,9},{9,1},{17,25},{25,17},{2,10},{10... | collective-permute-start | bytes 1376264 | tf_op jit(solution)/shard_map/ppermute | solution.py:433
  (31 other events, 626.1 us)

commit v10 on v9

--- a/solution.py
+++ b/solution.py
@@ -400,7 +400,7 @@
     swap = [(p, p ^ 1) for p in range(blocks)]
     onward = [(p, (p + 2) % blocks) for p in range(blocks)]
 
-    doubles = max((half - 4) // 2, 0)
+    doubles = max((half - 2) // 2, 0)
     sizes = [1] + [2] * doubles + [1] * (half - 1 - 2 * doubles)
     starts = [sum(sizes[:c]) for c in range(len(sizes))]
     chunks = len(sizes)
@@ -477,7 +477,7 @@
         for c in range(chunks - 3, chunks):
             ahead[c - 1].remove(c)
             ahead[c - 5].append(c)
-        parts = {chunks - 5: chunks - 6}
+        parts = {chunks - 4: chunks - 5}
     begin, total = 0, None
     for c in range(chunks):
         before = chain(0, False, rows, side_alone, rates, own[c], peer[c], [], [before])

time: 550 us -> 551 us (level)
  waiting for transfers between devices: 124 us -> 153 us
  starting transfers between devices: 112 us -> 98.6 us
  Pallas kernels: 297 us -> 284 us
    ppermute x10 -> x9, waiting for transfers between devices: 6.14 us -> 19.1 us  [on_device(): both = lax.ppermute(before, 'blk', onward)]
    all_to_all x10 -> x9, waiting for transfers between devices: 5.24 us -> 12 us  [complete(): lax.all_to_all(done, ('blk', 'tones'), split_axis=0, concat_axis=0, tiled...]
    all_to_all x10 -> x9, starting transfers between devices: 51.1 us -> 44.5 us  [complete(): lax.all_to_all(done, ('blk', 'tones'), split_axis=0, concat_axis=0, tiled...]
    pallas_call x20 -> x18, Pallas kernels: 103 us -> 97.1 us  [prepare(): pl.pallas_call(functools.partial(prepare_body, carry, blocks), out_shape=...]
    ppermute x10 -> x9, waiting for transfers between devices: 104 us -> 110 us  [ready_peer(): peer[c] = [lax.ppermute(sent[0], 'blk', swap)]]
    pallas_call x20 -> x18, Pallas kernels: 107 us -> 103 us  [chain(): pl.pallas_call(functools.partial(chain_body, round_index, last, rows), ou...]
    pallas_call x10 -> x9, Pallas kernels: 51.3 us -> 48.7 us  [finish(): pl.pallas_call(functools.partial(finish_body, count, rows), out_shape=jax...]
    ppermute x10 -> x9, starting transfers between devices: 21.1 us -> 18.7 us  [on_device(): both = lax.ppermute(before, 'blk', onward)]
  transfers between devices with their start and end apart: 50 -> 45, of which waited for: 16 -> 17; matrix products, arithmetic and copies ran while one was open for 1% -> 1% of each run, Pallas kernels for 52% -> 49%
where the time goes in v10:
time: 551 us; the launch traced here: 542 us
  Pallas kernels  284 us (52%)
  waiting for transfers between devices  153 us (28%)
  starting transfers between devices  98.6 us (18%)
    ppermute x9, waiting for transfers between devices, ready_peer(): peer[c] = [lax.ppermute(sent[0], 'blk', swap)]  110 us
    pallas_call x18, Pallas kernels, chain(): pl.pallas_call(functools.partial(chain_body, round_index, last, rows), ou...  103 us
    pallas_call x18, Pallas kernels, prepare(): pl.pallas_call(functools.partial(prepare_body, carry, blocks), out_shape=...  97.1 us
    pallas_call x9, Pallas kernels, finish(): pl.pallas_call(functools.partial(finish_body, count, rows), out_shape=jax...  48.7 us
    all_to_all x9, starting transfers between devices, complete(): lax.all_to_all(done, ('blk', 'tones'), split_axis=0, concat_axis=0, tiled...  44.5 us
    pallas_call x3, Pallas kernels, despread(): pl.pallas_call(functools.partial(despread_body, groups, sizes, rows, fold...  35.1 us
    ppermute x9, waiting for transfers between devices, on_device(): both = lax.ppermute(before, 'blk', onward)  19.1 us
    ppermute x9, starting transfers between devices, on_device(): both = lax.ppermute(before, 'blk', onward)  18.7 us
  transfers between devices with their start and end apart: 45, of which 17 were waited for; matrix products, arithmetic and copies ran while one was open for 1% of the time, Pallas kernels for 49%

profile of v10, /device:TPU:0, one launch (start us, length us, event | category | flops | bytes accessed | tf_op | source)
XLA Modules:
  0.0 541.8 jit_solution(17926599893220776921)
XLA Ops:
  7.3 5.8 %prepare.19 = (f32[2,704,256]{2,1,0:T(8,128)}, f32[2,448,256]{2,1,0:T(8,128)}) custom-call(s32[1]{0:T(128)} %bitcast.3.base, s32[1]{0:T(128)} %bitcast.4.pair, s32[1]{0:T(128)} %bitcast.5.group, s32[8]{0:T(128)} %hop_offset.35, f32[1,2]{1,0:T(1,128)} %rates.35, f32[32,2,256,256]{3,2,1,0:T(8,128)} %chan.35, f32[32,2,448,256]{3,2,1,0:T(8,128)} %recv.35, ...), custom_call_target="tpu_custom_call" | custom-call | flops 9999999827968 | bytes 10000000000 | tf_op jit(solution)/shard_map/prepare/pallas_call | solution.py:86
  49.8 15.7 %collective-permute-done.4.refs_1_.peer = f32[2,704,256]{2,1,0:T(8,128)} collective-permute-done((f32[2,704,256]{2,1,0:T(8,128)}, f32[2,704,256]{2,1,0:T(8,128)}, u32[]{:S(2)}, u32[]{:S(2)}) %collective-permute-start.4) | collective-permute-done | bytes 1441824 | tf_op jit(solution)/shard_map/ppermute | solution.py:426
  101.7 6.9 %chain1.10 = (f32[2,2,112,256]{3,2,1,0:T(8,128)}, f32[2,2,112,256]{3,2,1,0:T(8,128)}) custom-call(s32[1]{0:T(128)} %bitcast.side, f32[2,2]{1,0:T(2,128)} %maximum_select_fusion.rates, f32[2,704,256]{2,1,0:T(8,128)} %get-tuple-element.67.refs_5_.refs_0_.own, f32[2,704,256]{2,1,0:T(8,128)} %collective-permute-done.4.refs_1_.peer, ...), custom_call_target="tpu_custom_call" | custom-call | flops 9999999827968 | bytes 10000000000 | tf_op jit(solution)/shard_map/chain1/pallas_call | solution.py:179
  110.5 9.7 %collective-permute-done.8.refs_1_.peer = f32[2,704,256]{2,1,0:T(8,128)} collective-permute-done((f32[2,704,256]{2,1,0:T(8,128)}, f32[2,704,256]{2,1,0:T(8,128)}, u32[]{:S(2)}, u32[]{:S(2)}) %collective-permute-start.8) | collective-permute-done | bytes 1441824 | tf_op jit(solution)/shard_map/ppermute | solution.py:426
  158.3 6.9 %chain1.11 = (f32[2,2,112,256]{3,2,1,0:T(8,128)}, f32[2,2,112,256]{3,2,1,0:T(8,128)}) custom-call(s32[1]{0:T(128)} %bitcast.side, f32[2,2]{1,0:T(2,128)} %maximum_select_fusion.rates, f32[2,704,256]{2,1,0:T(8,128)} %get-tuple-element.73.refs_0_.own, f32[2,704,256]{2,1,0:T(8,128)} %collective-permute-done.8.refs_1_.peer, ...), custom_call_target="tpu_custom_call" | custom-call | flops 9999999827968 | bytes 10000000000 | tf_op jit(solution)/shard_map/chain1/pallas_call | solution.py:179
  167.0 12.5 %collective-permute-done.12.refs_1_.peer = f32[2,704,256]{2,1,0:T(8,128)} collective-permute-done((f32[2,704,256]{2,1,0:T(8,128)}, f32[2,704,256]{2,1,0:T(8,128)}, u32[]{:S(2)}, u32[]{:S(2)}) %collective-permute-start.12) | collective-permute-done | bytes 1441824 | tf_op jit(solution)/shard_map/ppermute | solution.py:426
  187.1 5.7 %finish.11.refs_1_ = f32[32,8,896]{2,1,0:T(8,128)} custom-call(s32[2]{0:T(128)} %pad_add_fusion.scalars, f32[2,2]{1,0:T(2,128)} %maximum_select_fusion.rates, f32[2,704,256]{2,1,0:T(8,128)} %get-tuple-element.73.refs_0_.own, f32[2,704,256]{2,1,0:T(8,128)} %collective-permute-done.8.refs_1_.peer, f32[2,2,112,256]{3,2,1,0:T(8,128)} %get-tuple-element.82.refs_2_.even, ...), custom_call_target="tpu_custom_call" | custom-call | flops 9999999827968 | bytes 10000000000 | tf_op jit(solution)/shard_map/finish/pallas_call | solution.py:236
  215.9 6.9 %chain1.12 = (f32[2,2,112,256]{3,2,1,0:T(8,128)}, f32[2,2,112,256]{3,2,1,0:T(8,128)}) custom-call(s32[1]{0:T(128)} %bitcast.side, f32[2,2]{1,0:T(2,128)} %maximum_select_fusion.rates, f32[2,704,256]{2,1,0:T(8,128)} %get-tuple-element.80.refs_0_.own, f32[2,704,256]{2,1,0:T(8,128)} %collective-permute-done.12.refs_1_.peer, ...), custom_call_target="tpu_custom_call" | custom-call | flops 9999999827968 | bytes 10000000000 | tf_op jit(solution)/shard_map/chain1/pallas_call | solution.py:179
  224.7 15.3 %collective-permute-done.16.refs_1_.peer = f32[2,704,256]{2,1,0:T(8,128)} collective-permute-done((f32[2,704,256]{2,1,0:T(8,128)}, f32[2,704,256]{2,1,0:T(8,128)}, u32[]{:S(2)}, u32[]{:S(2)}) %collective-permute-start.16) | collective-permute-done | bytes 1441824 | tf_op jit(solution)/shard_map/ppermute | solution.py:426
  247.5 5.8 %finish.12.refs_1_ = f32[32,8,896]{2,1,0:T(8,128)} custom-call(s32[2]{0:T(128)} %pad_add_fusion.scalars, f32[2,2]{1,0:T(2,128)} %maximum_select_fusion.rates, f32[2,704,256]{2,1,0:T(8,128)} %get-tuple-element.80.refs_0_.own, f32[2,704,256]{2,1,0:T(8,128)} %collective-permute-done.12.refs_1_.peer, f32[2,2,112,256]{3,2,1,0:T(8,128)} %get-tuple-element.89.refs_2_.even, ...), custom_call_target="tpu_custom_call" | custom-call | flops 9999999827968 | bytes 10000000000 | tf_op jit(solution)/shard_map/finish/pallas_call | solution.py:236
  272.1 6.9 %chain1.13 = (f32[2,2,112,256]{3,2,1,0:T(8,128)}, f32[2,2,112,256]{3,2,1,0:T(8,128)}) custom-call(s32[1]{0:T(128)} %bitcast.side, f32[2,2]{1,0:T(2,128)} %maximum_select_fusion.rates, f32[2,704,256]{2,1,0:T(8,128)} %get-tuple-element.85.refs_0_.own, f32[2,704,256]{2,1,0:T(8,128)} %collective-permute-done.16.refs_1_.peer, ...), custom_call_target="tpu_custom_call" | custom-call | flops 9999999827968 | bytes 10000000000 | tf_op jit(solution)/shard_map/chain1/pallas_call | solution.py:179
  280.8 19.6 %collective-permute-done.20.refs_1_.peer = f32[2,704,256]{2,1,0:T(8,128)} collective-permute-done((f32[2,704,256]{2,1,0:T(8,128)}, f32[2,704,256]{2,1,0:T(8,128)}, u32[]{:S(2)}, u32[]{:S(2)}) %collective-permute-start.20) | collective-permute-done | bytes 1441824 | tf_op jit(solution)/shard_map/ppermute | solution.py:426
  331.3 6.9 %chain1.14 = (f32[2,2,112,256]{3,2,1,0:T(8,128)}, f32[2,2,112,256]{3,2,1,0:T(8,128)}) custom-call(s32[1]{0:T(128)} %bitcast.side, f32[2,2]{1,0:T(2,128)} %maximum_select_fusion.rates, f32[2,704,256]{2,1,0:T(8,128)} %get-tuple-element.94.refs_5_.refs_0_.own, f32[2,704,256]{2,1,0:T(8,128)} %collective-permute-done.20.refs_1_.peer, ...), custom_call_target="tpu_custom_call" | custom-call | flops 9999999827968 | bytes 10000000000 | tf_op jit(solution)/shard_map/chain1/pallas_call | solution.py:179
  339.8 11.4 %despread.3.refs_2_.refs_4_ = f32[8,2,448,256]{3,2,1,0:T(8,128)} custom-call(s32[32]{0:T(128)} %and_select_fusion.source, bf16[2,224,512]{2,1,0:T(8,128)(2,1)} %constant.88.clone.table, f32[32,8,448]{2,1,0:T(8,128)} %all-to-all-done.refs_1_.refs_0_, f32[32,8,896]{2,1,0:T(8,128)} %all-to-all-done.1.refs_1_, f32[32,8,896]{2,1,0:T(8,128)} %all-to-all-done.2.refs_1_.refs_2_, ...), custom_call_target="tpu_custom_call" | custom-call | flops 9999999827968 | bytes 10000000000 | tf_op jit(solution)/shard_map/despread/pallas_call | solution.py:362
  351.3 9.5 %collective-permute-done.24.refs_1_.peer = f32[2,704,256]{2,1,0:T(8,128)} collective-permute-done((f32[2,704,256]{2,1,0:T(8,128)}, f32[2,704,256]{2,1,0:T(8,128)}, u32[]{:S(2)}, u32[]{:S(2)}) %collective-permute-start.24) | collective-permute-done | bytes 1441824 | tf_op jit(solution)/shard_map/ppermute | solution.py:426
  385.9 5.7 %collective-permute-done.27.refs_4_ = f32[2,2,2,112,256]{4,3,2,1,0:T(8,128)} collective-permute-done((f32[2,2,2,112,256]{4,3,2,1,0:T(8,128)}, f32[2,2,2,112,256]{4,3,2,1,0:T(8,128)}, u32[]{:S(2)}, u32[]{:S(2)}) %collective-permute-start.27) | collective-permute-done | bytes 917536 | tf_op jit(solution)/shard_map/ppermute | solution.py:484
  391.6 6.9 %chain1.15 = (f32[2,2,112,256]{3,2,1,0:T(8,128)}, f32[2,2,112,256]{3,2,1,0:T(8,128)}) custom-call(s32[1]{0:T(128)} %bitcast.side, f32[2,2]{1,0:T(2,128)} %maximum_select_fusion.rates, f32[2,704,256]{2,1,0:T(8,128)} %get-tuple-element.74.refs_5_.refs_0_.own, f32[2,704,256]{2,1,0:T(8,128)} %collective-permute-done.24.refs_1_.peer, ...), custom_call_target="tpu_custom_call" | custom-call | flops 9999999827968 | bytes 10000000000 | tf_op jit(solution)/shard_map/chain1/pallas_call | solution.py:179
  400.2 20.9 %collective-permute-done.29.refs_1_.peer = f32[2,704,256]{2,1,0:T(8,128)} collective-permute-done((f32[2,704,256]{2,1,0:T(8,128)}, f32[2,704,256]{2,1,0:T(8,128)}, u32[]{:S(2)}, u32[]{:S(2)}) %collective-permute-start.29) | collective-permute-done | bytes 1441824 | tf_op jit(solution)/shard_map/ppermute | solution.py:426
  443.3 8.7 %collective-permute-done.32.refs_4_ = f32[2,2,2,112,256]{4,3,2,1,0:T(8,128)} collective-permute-done((f32[2,2,2,112,256]{4,3,2,1,0:T(8,128)}, f32[2,2,2,112,256]{4,3,2,1,0:T(8,128)}, u32[]{:S(2)}, u32[]{:S(2)}) %collective-permute-start.32) | collective-permute-done | bytes 917536 | tf_op jit(solution)/shard_map/ppermute | solution.py:484
  452.0 6.9 %chain1.16 = (f32[2,2,112,256]{3,2,1,0:T(8,128)}, f32[2,2,112,256]{3,2,1,0:T(8,128)}) custom-call(s32[1]{0:T(128)} %bitcast.side, f32[2,2]{1,0:T(2,128)} %maximum_select_fusion.rates, f32[2,704,256]{2,1,0:T(8,128)} %get-tuple-element.81.refs_5_.refs_0_.own, f32[2,704,256]{2,1,0:T(8,128)} %collective-permute-done.29.refs_1_.peer, ...), custom_call_target="tpu_custom_call" | custom-call | flops 9999999827968 | bytes 10000000000 | tf_op jit(solution)/shard_map/chain1/pallas_call | solution.py:179
  490.0 9.3 %collective-permute-done.35.odd = f32[1,2,112,256]{3,2,1,0:T(8,128)S(1)} collective-permute-done((f32[1,2,112,256]{3,2,1,0:T(8,128)}, f32[1,2,112,256]{3,2,1,0:T(8,128)S(1)}, u32[]{:S(2)}, u32[]{:S(2)}) %collective-permute-start.35) | collective-permute-done | bytes 229408 | tf_op jit(solution)/shard_map/ppermute | solution.py:500
  499.3 9.2 %all-to-all-done.7.refs_1_.refs_3_ = f32[32,8,896]{2,1,0:T(8,128)} async-done(((f32[32,8,896]{2,1,0:T(8,128)}), f32[32,8,896]{2,1,0:T(8,128)}, u32[]{:S(2)}, u32[]{:S(2)}) %all-to-all-start.7) | async-done | bytes 917536 | tf_op jit(solution)/shard_map/all_to_all | solution.py:445
  516.3 14.7 %despread.4.refs_1_ = f32[8,2,448,256]{3,2,1,0:T(8,128)} custom-call(s32[32]{0:T(128)} %and_select_fusion.source, bf16[2,256,512]{2,1,0:T(8,128)(2,1)} %constant.89.clone.table, f32[32,8,896]{2,1,0:T(8,128)} %all-to-all-done.4.refs_1_.refs_0_, f32[32,8,896]{2,1,0:T(8,128)} %all-to-all-done.5.refs_6_.refs_1_, f32[32,8,896]{2,1,0:T(8,128)} %all-to-all-done.6.refs_6_.refs_2_, ...), custom_call_target="tpu_custom_call" | custom-call | flops 9999999827968 | bytes 10000000000 | tf_op jit(solution)/shard_map/despread/pallas_call | solution.py:362
  532.6 9.0 %despread.5 = f32[8,2,448,256]{3,2,1,0:T(8,128)} custom-call(s32[32]{0:T(128)} %and_select_fusion.source, bf16[1,96,512]{2,1,0:T(8,128)(2,1)} %constant.90.clone.table, f32[32,8,448]{2,1,0:T(8,128)} %all-to-all-done.8.refs_0_, f32[8,2,448,256]{3,2,1,0:T(8,128)} %despread.4.refs_1_), custom_call_target="tpu_custom_call" | custom-call | flops 9999999827968 | bytes 10000000000 | tf_op jit(solution)/shard_map/despread/pallas_call | solution.py:362
  (141 shorter events, 302.8 us)
Async XLA Ops:
  7.3 38.0 %collective-permute-start.1 = (f32[1,448,256]{2,1,0:T(8,128)}, f32[1,448,256]{2,1,0:T(8,128)}, u32[]{:S(2)}, u32[]{:S(2)}) collective-permute-start(f32[1,448,256]{2,1,0:T(8,128)} %held_back.9.refs_0_), channel_id=1, source_target_pairs={{0,8},{8,0},{16,24},{24,16},{1,9},{9,1},{17,25},{25,17},{2,10},{10... | collective-permute-start | bytes 1376264 | tf_op jit(solution)/shard_map/ppermute | solution.py:433
  13.1 52.4 %collective-permute-start.4 = (f32[2,704,256]{2,1,0:T(8,128)}, f32[2,704,256]{2,1,0:T(8,128)}, u32[]{:S(2)}, u32[]{:S(2)}) collective-permute-start(f32[2,704,256]{2,1,0:T(8,128)} %get-tuple-element.62.refs_0_), channel_id=1, source_target_pairs={{0,8},{8,0},{16,24},{24,16},{1,9},{9,1},{17,25},{25,17},{2,10},{10... | collective-permute-start | bytes 4325384 | tf_op jit(solution)/shard_map/ppermute | solution.py:426
  31.9 69.8 %collective-permute-start.5 = (f32[2,448,256]{2,1,0:T(8,128)}, f32[2,448,256]{2,1,0:T(8,128)}, u32[]{:S(2)}, u32[]{:S(2)}) collective-permute-start(f32[2,448,256]{2,1,0:T(8,128)} %held_back.10.refs_0_), channel_id=1, source_target_pairs={{0,8},{8,0},{16,24},{24,16},{1,9},{9,1},{17,25},{25,17},{2,10},{10... | collective-permute-start | bytes 2752520 | tf_op jit(solution)/shard_map/ppermute | solution.py:433
  39.0 81.2 %collective-permute-start.8 = (f32[2,704,256]{2,1,0:T(8,128)}, f32[2,704,256]{2,1,0:T(8,128)}, u32[]{:S(2)}, u32[]{:S(2)}) collective-permute-start(f32[2,704,256]{2,1,0:T(8,128)} %get-tuple-element.66.refs_0_), channel_id=1, source_target_pairs={{0,8},{8,0},{16,24},{24,16},{1,9},{9,1},{17,25},{25,17},{2,10},{10... | collective-permute-start | bytes 4325384 | tf_op jit(solution)/shard_map/ppermute | solution.py:426
  77.2 50.6 %all-to-all-start = ((f32[32,8,448]{2,1,0:T(8,128)}), f32[32,8,448]{2,1,0:T(8,128)}, u32[]{:S(2)}, u32[]{:S(2)}) async-start(f32[32,8,448]{2,1,0:T(8,128)} %finish.9.refs_1_), calls=%async_computation | async-start | bytes 1048576 | tf_op jit(solution)/shard_map/all_to_all | solution.py:445
  82.5 75.7 %collective-permute-start.9 = (f32[2,448,256]{2,1,0:T(8,128)}, f32[2,448,256]{2,1,0:T(8,128)}, u32[]{:S(2)}, u32[]{:S(2)}) collective-permute-start(f32[2,448,256]{2,1,0:T(8,128)} %held_back.11.refs_0_), channel_id=1, source_target_pairs={{0,8},{8,0},{16,24},{24,16},{1,9},{9,1},{17,25},{25,17},{2,10},{10... | collective-permute-start | bytes 2752520 | tf_op jit(solution)/shard_map/ppermute | solution.py:433
  90.2 89.4 %collective-permute-start.12 = (f32[2,704,256]{2,1,0:T(8,128)}, f32[2,704,256]{2,1,0:T(8,128)}, u32[]{:S(2)}, u32[]{:S(2)}) collective-permute-start(f32[2,704,256]{2,1,0:T(8,128)} %get-tuple-element.72.refs_0_), channel_id=1, source_target_pairs={{0,8},{8,0},{16,24},{24,16},{1,9},{9,1},{17,25},{25,17},{2,10},{10... | collective-permute-start | bytes 4325384 | tf_op jit(solution)/shard_map/ppermute | solution.py:426
  133.5 53.6 %all-to-all-start.1 = ((f32[32,8,896]{2,1,0:T(8,128)}), f32[32,8,896]{2,1,0:T(8,128)}, u32[]{:S(2)}, u32[]{:S(2)}) async-start(f32[32,8,896]{2,1,0:T(8,128)} %finish.10.refs_1_), calls=%async_computation.1 | async-start | bytes 1835008 | tf_op jit(solution)/shard_map/all_to_all | solution.py:445
  139.1 76.8 %collective-permute-start.13 = (f32[2,448,256]{2,1,0:T(8,128)}, f32[2,448,256]{2,1,0:T(8,128)}, u32[]{:S(2)}, u32[]{:S(2)}) collective-permute-start(f32[2,448,256]{2,1,0:T(8,128)} %held_back.12.refs_0_), channel_id=1, source_target_pairs={{0,8},{8,0},{16,24},{24,16},{1,9},{9,1},{17,25},{25,17},{2,10},{10... | collective-permute-start | bytes 2752520 | tf_op jit(solution)/shard_map/ppermute | solution.py:433
  146.8 93.2 %collective-permute-start.16 = (f32[2,704,256]{2,1,0:T(8,128)}, f32[2,704,256]{2,1,0:T(8,128)}, u32[]{:S(2)}, u32[]{:S(2)}) collective-permute-start(f32[2,704,256]{2,1,0:T(8,128)} %get-tuple-element.79.refs_0_), channel_id=1, source_target_pairs={{0,8},{8,0},{16,24},{24,16},{1,9},{9,1},{17,25},{25,17},{2,10},{10... | collective-permute-start | bytes 4325384 | tf_op jit(solution)/shard_map/ppermute | solution.py:426
  192.9 54.6 %all-to-all-start.2 = ((f32[32,8,896]{2,1,0:T(8,128)}), f32[32,8,896]{2,1,0:T(8,128)}, u32[]{:S(2)}, u32[]{:S(2)}) async-start(f32[32,8,896]{2,1,0:T(8,128)} %finish.11.refs_1_), calls=%async_computation.2 | async-start | bytes 1835008 | tf_op jit(solution)/shard_map/all_to_all | solution.py:445
  198.1 74.0 %collective-permute-start.17 = (f32[2,448,256]{2,1,0:T(8,128)}, f32[2,448,256]{2,1,0:T(8,128)}, u32[]{:S(2)}, u32[]{:S(2)}) collective-permute-start(f32[2,448,256]{2,1,0:T(8,128)} %held_back.13.refs_0_), channel_id=1, source_target_pairs={{0,8},{8,0},{16,24},{24,16},{1,9},{9,1},{17,25},{25,17},{2,10},{10... | collective-permute-start | bytes 2752520 | tf_op jit(solution)/shard_map/ppermute | solution.py:433
  205.7 94.7 %collective-permute-start.20 = (f32[2,704,256]{2,1,0:T(8,128)}, f32[2,704,256]{2,1,0:T(8,128)}, u32[]{:S(2)}, u32[]{:S(2)}) collective-permute-start(f32[2,704,256]{2,1,0:T(8,128)} %get-tuple-element.84.refs_0_), channel_id=1, source_target_pairs={{0,8},{8,0},{16,24},{24,16},{1,9},{9,1},{17,25},{25,17},{2,10},{10... | collective-permute-start | bytes 4325384 | tf_op jit(solution)/shard_map/ppermute | solution.py:426
  253.3 54.6 %all-to-all-start.3 = ((f32[32,8,896]{2,1,0:T(8,128)}), f32[32,8,896]{2,1,0:T(8,128)}, u32[]{:S(2)}, u32[]{:S(2)}) async-start(f32[32,8,896]{2,1,0:T(8,128)} %finish.12.refs_1_), calls=%async_computation.3 | async-start | bytes 1835008 | tf_op jit(solution)/shard_map/all_to_all | solution.py:445
  258.6 68.1 %collective-permute-start.21 = (f32[2,448,256]{2,1,0:T(8,128)}, f32[2,448,256]{2,1,0:T(8,128)}, u32[]{:S(2)}, u32[]{:S(2)}) collective-permute-start(f32[2,448,256]{2,1,0:T(8,128)} %held_back.14.refs_0_), channel_id=1, source_target_pairs={{0,8},{8,0},{16,24},{24,16},{1,9},{9,1},{17,25},{25,17},{2,10},{10... | collective-permute-start | bytes 2752520 | tf_op jit(solution)/shard_map/ppermute | solution.py:433
  266.2 94.5 %collective-permute-start.24 = (f32[2,704,256]{2,1,0:T(8,128)}, f32[2,704,256]{2,1,0:T(8,128)}, u32[]{:S(2)}, u32[]{:S(2)}) collective-permute-start(f32[2,704,256]{2,1,0:T(8,128)} %get-tuple-element.93.refs_0_), channel_id=1, source_target_pairs={{0,8},{8,0},{16,24},{24,16},{1,9},{9,1},{17,25},{25,17},{2,10},{10... | collective-permute-start | bytes 4325384 | tf_op jit(solution)/shard_map/ppermute | solution.py:426
  313.6 54.7 %all-to-all-start.4 = ((f32[32,8,896]{2,1,0:T(8,128)}), f32[32,8,896]{2,1,0:T(8,128)}, u32[]{:S(2)}, u32[]{:S(2)}) async-start(f32[32,8,896]{2,1,0:T(8,128)} %finish.13.refs_1_), calls=%async_computation.4 | async-start | bytes 1835008 | tf_op jit(solution)/shard_map/all_to_all | solution.py:445
  318.9 67.0 %collective-permute-start.26 = (f32[2,448,256]{2,1,0:T(8,128)}, f32[2,448,256]{2,1,0:T(8,128)}, u32[]{:S(2)}, u32[]{:S(2)}) collective-permute-start(f32[2,448,256]{2,1,0:T(8,128)} %held_back.15.refs_0_), channel_id=1, source_target_pairs={{0,8},{8,0},{16,24},{24,16},{1,9},{9,1},{17,25},{25,17},{2,10},{10... | collective-permute-start | bytes 2752520 | tf_op jit(solution)/shard_map/ppermute | solution.py:433
  326.5 94.6 %collective-permute-start.29 = (f32[2,704,256]{2,1,0:T(8,128)}, f32[2,704,256]{2,1,0:T(8,128)}, u32[]{:S(2)}, u32[]{:S(2)}) collective-permute-start(f32[2,704,256]{2,1,0:T(8,128)} %get-tuple-element.99.refs_5_), channel_id=1, source_target_pairs={{0,8},{8,0},{16,24},{24,16},{1,9},{9,1},{17,25},{25,17},{2,10},{10... | collective-permute-start | bytes 4325384 | tf_op jit(solution)/shard_map/ppermute | solution.py:426
  374.0 61.9 %all-to-all-start.5 = ((f32[32,8,896]{2,1,0:T(8,128)}), f32[32,8,896]{2,1,0:T(8,128)}, u32[]{:S(2)}, u32[]{:S(2)}) async-start(f32[32,8,896]{2,1,0:T(8,128)} %finish.14.refs_1_), calls=%async_computation.5 | async-start | bytes 1835008 | tf_op jit(solution)/shard_map/all_to_all | solution.py:445
  379.5 63.8 %collective-permute-start.31 = (f32[2,448,256]{2,1,0:T(8,128)}, f32[2,448,256]{2,1,0:T(8,128)}, u32[]{:S(2)}, u32[]{:S(2)}) collective-permute-start(f32[2,448,256]{2,1,0:T(8,128)} %held_back.16.refs_0_), channel_id=1, source_target_pairs={{0,8},{8,0},{16,24},{24,16},{1,9},{9,1},{17,25},{25,17},{2,10},{10... | collective-permute-start | bytes 2752520 | tf_op jit(solution)/shard_map/ppermute | solution.py:433
  385.7 80.3 %collective-permute-start.25 = (f32[1,704,256]{2,1,0:T(8,128)}, f32[1,704,256]{2,1,0:T(8,128)}, u32[]{:S(2)}, u32[]{:S(2)}) collective-permute-start(f32[1,704,256]{2,1,0:T(8,128)} %get-tuple-element.102.refs_5_), channel_id=1, source_target_pairs={{0,8},{8,0},{16,24},{24,16},{1,9},{9,1},{17,25},{25,17},{2,10},{10... | collective-permute-start | bytes 2162696 | tf_op jit(solution)/shard_map/ppermute | solution.py:426
  434.4 49.4 %collective-permute-start.30 = (f32[1,448,256]{2,1,0:T(8,128)}, f32[1,448,256]{2,1,0:T(8,128)}, u32[]{:S(2)}, u32[]{:S(2)}) collective-permute-start(f32[1,448,256]{2,1,0:T(8,128)} %held_back.17.refs_5_), channel_id=1, source_target_pairs={{0,8},{8,0},{16,24},{24,16},{1,9},{9,1},{17,25},{25,17},{2,10},{10... | collective-permute-start | bytes 1376264 | tf_op jit(solution)/shard_map/ppermute | solution.py:433
  435.9 42.9 %all-to-all-start.6 = ((f32[32,8,896]{2,1,0:T(8,128)}), f32[32,8,896]{2,1,0:T(8,128)}, u32[]{:S(2)}, u32[]{:S(2)}) async-start(f32[32,8,896]{2,1,0:T(8,128)} %finish.15.refs_1_), calls=%async_computation.6 | async-start | bytes 1835008 | tf_op jit(solution)/shard_map/all_to_all | solution.py:445
  (26 other events, 534.0 us)

commit v11 on v9

--- a/solution.py
+++ b/solution.py
@@ -305,7 +305,7 @@
                     place = place + 2 * size
             return carry
 
-        lax.fori_loop(0, groups, gather, 0)
+        lax.fori_loop(0, groups, gather, 0, unroll=folded)
 
     for item in range(items):
         despread_item(rows, folded, first, last, item, table, tones_first, symbols_first, held, fetch)

time: 550 us -> 548 us (level)
  no operation moved by 1% of the time
where the time goes in v11:
time: 548 us; the launch traced here: 539 us
  Pallas kernels  296 us (54%)
  waiting for transfers between devices  124 us (23%)
  starting transfers between devices  112 us (20%)
    pallas_call x20, Pallas kernels, chain(): pl.pallas_call(functools.partial(chain_body, round_index, last, rows), ou...  107 us
    ppermute x10, waiting for transfers between devices, ready_peer(): peer[c] = [lax.ppermute(sent[0], 'blk', swap)]  104 us
    pallas_call x20, Pallas kernels, prepare(): pl.pallas_call(functools.partial(prepare_body, carry, blocks), out_shape=...  103 us
    pallas_call x10, Pallas kernels, finish(): pl.pallas_call(functools.partial(finish_body, count, rows), out_shape=jax...  51.3 us
    all_to_all x10, starting transfers between devices, complete(): lax.all_to_all(done, ('blk', 'tones'), split_axis=0, concat_axis=0, tiled...  51.1 us
    pallas_call x3, Pallas kernels, despread(): pl.pallas_call(functools.partial(despread_body, groups, sizes, rows, fold...  34 us
    ppermute x10, starting transfers between devices, on_device(): both = lax.ppermute(before, 'blk', onward)  21.1 us
    ppermute x10, starting transfers between devices, send_later(): peer[c].append(lax.ppermute(value, 'blk', swap))  16.9 us
  transfers between devices with their start and end apart: 50, of which 16 were waited for; matrix products, arithmetic and copies ran while one was open for 1% of the time, Pallas kernels for 52%

profile of v11, /device:TPU:0, one launch (start us, length us, event | category | flops | bytes accessed | tf_op | source)
XLA Modules:
  0.0 538.8 jit_solution(12830582319886414284)
XLA Ops:
  7.3 5.8 %prepare.21 = (f32[2,704,256]{2,1,0:T(8,128)}, f32[2,448,256]{2,1,0:T(8,128)}) custom-call(s32[1]{0:T(128)} %bitcast.3.base, s32[1]{0:T(128)} %bitcast.4.pair, s32[1]{0:T(128)} %bitcast.5.group, s32[8]{0:T(128)} %hop_offset.39, f32[1,2]{1,0:T(1,128)} %rates.39, f32[32,2,256,256]{3,2,1,0:T(8,128)} %chan.39, f32[32,2,448,256]{3,2,1,0:T(8,128)} %recv.39, ...), custom_call_target="tpu_custom_call" | custom-call | flops 9999999827968 | bytes 10000000000 | tf_op jit(solution)/shard_map/prepare/pallas_call | solution.py:86
  49.8 15.6 %collective-permute-done.4.refs_1_.peer = f32[2,704,256]{2,1,0:T(8,128)} collective-permute-done((f32[2,704,256]{2,1,0:T(8,128)}, f32[2,704,256]{2,1,0:T(8,128)}, u32[]{:S(2)}, u32[]{:S(2)}) %collective-permute-start.4) | collective-permute-done | bytes 1441824 | tf_op jit(solution)/shard_map/ppermute | solution.py:426
  96.2 6.9 %chain1.11 = (f32[2,2,112,256]{3,2,1,0:T(8,128)}, f32[2,2,112,256]{3,2,1,0:T(8,128)}) custom-call(s32[1]{0:T(128)} %bitcast.side, f32[2,2]{1,0:T(2,128)} %maximum_select_fusion.rates, f32[2,704,256]{2,1,0:T(8,128)} %get-tuple-element.73.refs_5_.refs_0_.own, f32[2,704,256]{2,1,0:T(8,128)} %collective-permute-done.4.refs_1_.peer, ...), custom_call_target="tpu_custom_call" | custom-call | flops 9999999827968 | bytes 10000000000 | tf_op jit(solution)/shard_map/chain1/pallas_call | solution.py:179
  105.0 15.2 %collective-permute-done.8.refs_1_.peer = f32[2,704,256]{2,1,0:T(8,128)} collective-permute-done((f32[2,704,256]{2,1,0:T(8,128)}, f32[2,704,256]{2,1,0:T(8,128)}, u32[]{:S(2)}, u32[]{:S(2)}) %collective-permute-start.8) | collective-permute-done | bytes 1441824 | tf_op jit(solution)/shard_map/ppermute | solution.py:426
  127.7 5.7 %finish.11.refs_1_ = f32[32,8,896]{2,1,0:T(8,128)} custom-call(s32[2]{0:T(128)} %pad_add_fusion.scalars, f32[2,2]{1,0:T(2,128)} %maximum_select_fusion.rates, f32[2,704,256]{2,1,0:T(8,128)} %get-tuple-element.73.refs_5_.refs_0_.own, f32[2,704,256]{2,1,0:T(8,128)} %collective-permute-done.4.refs_1_.peer, f32[2,2,112,256]{3,2,1,0:T(8,128)} %get-tuple-element.80.refs_2_.even, ...), custom_call_target="tpu_custom_call" | custom-call | flops 9999999827968 | bytes 10000000000 | tf_op jit(solution)/shard_map/finish/pallas_call | solution.py:236
  156.5 6.9 %chain1.12 = (f32[2,2,112,256]{3,2,1,0:T(8,128)}, f32[2,2,112,256]{3,2,1,0:T(8,128)}) custom-call(s32[1]{0:T(128)} %bitcast.side, f32[2,2]{1,0:T(2,128)} %maximum_select_fusion.rates, f32[2,704,256]{2,1,0:T(8,128)} %get-tuple-element.79.refs_5_.refs_0_.own, f32[2,704,256]{2,1,0:T(8,128)} %collective-permute-done.8.refs_1_.peer, ...), custom_call_target="tpu_custom_call" | custom-call | flops 9999999827968 | bytes 10000000000 | tf_op jit(solution)/shard_map/chain1/pallas_call | solution.py:179
  165.3 14.2 %collective-permute-done.12.refs_1_.peer = f32[2,704,256]{2,1,0:T(8,128)} collective-permute-done((f32[2,704,256]{2,1,0:T(8,128)}, f32[2,704,256]{2,1,0:T(8,128)}, u32[]{:S(2)}, u32[]{:S(2)}) %collective-permute-start.12) | collective-permute-done | bytes 1441824 | tf_op jit(solution)/shard_map/ppermute | solution.py:426
  187.1 5.7 %finish.12.refs_1_ = f32[32,8,896]{2,1,0:T(8,128)} custom-call(s32[2]{0:T(128)} %pad_add_fusion.scalars, f32[2,2]{1,0:T(2,128)} %maximum_select_fusion.rates, f32[2,704,256]{2,1,0:T(8,128)} %get-tuple-element.79.refs_5_.refs_0_.own, f32[2,704,256]{2,1,0:T(8,128)} %collective-permute-done.8.refs_1_.peer, f32[2,2,112,256]{3,2,1,0:T(8,128)} %get-tuple-element.87.refs_2_.even, ...), custom_call_target="tpu_custom_call" | custom-call | flops 9999999827968 | bytes 10000000000 | tf_op jit(solution)/shard_map/finish/pallas_call | solution.py:236
  205.8 5.7 %prepare.31 = (f32[2,704,256]{2,1,0:T(8,128)}, f32[2,448,256]{2,1,0:T(8,128)}) custom-call(s32[1]{0:T(128)} %bitcast.7.base, s32[1]{0:T(128)} %bitcast.4.pair, s32[1]{0:T(128)} %bitcast.5.group, s32[8]{0:T(128)} %hop_offset.39, f32[1,2]{1,0:T(1,128)} %rates.39, f32[32,2,256,256]{3,2,1,0:T(8,128)} %chan.39, f32[32,2,448,256]{3,2,1,0:T(8,128)} %recv.39, ...), custom_call_target="tpu_custom_call" | custom-call | flops 9999999827968 | bytes 10000000000 | tf_op jit(solution)/shard_map/prepare/pallas_call | solution.py:86
  216.0 6.9 %chain1.13 = (f32[2,2,112,256]{3,2,1,0:T(8,128)}, f32[2,2,112,256]{3,2,1,0:T(8,128)}) custom-call(s32[1]{0:T(128)} %bitcast.side, f32[2,2]{1,0:T(2,128)} %maximum_select_fusion.rates, f32[2,704,256]{2,1,0:T(8,128)} %get-tuple-element.85.refs_0_.own, f32[2,704,256]{2,1,0:T(8,128)} %collective-permute-done.12.refs_1_.peer, ...), custom_call_target="tpu_custom_call" | custom-call | flops 9999999827968 | bytes 10000000000 | tf_op jit(solution)/shard_map/chain1/pallas_call | solution.py:179
  224.7 15.2 %collective-permute-done.16.refs_1_.peer = f32[2,704,256]{2,1,0:T(8,128)} collective-permute-done((f32[2,704,256]{2,1,0:T(8,128)}, f32[2,704,256]{2,1,0:T(8,128)}, u32[]{:S(2)}, u32[]{:S(2)}) %collective-permute-start.16) | collective-permute-done | bytes 1441824 | tf_op jit(solution)/shard_map/ppermute | solution.py:426
  276.4 6.9 %chain1.14 = (f32[2,2,112,256]{3,2,1,0:T(8,128)}, f32[2,2,112,256]{3,2,1,0:T(8,128)}) custom-call(s32[1]{0:T(128)} %bitcast.side, f32[2,2]{1,0:T(2,128)} %maximum_select_fusion.rates, f32[2,704,256]{2,1,0:T(8,128)} %get-tuple-element.92.refs_0_.own, f32[2,704,256]{2,1,0:T(8,128)} %collective-permute-done.16.refs_1_.peer, ...), custom_call_target="tpu_custom_call" | custom-call | flops 9999999827968 | bytes 10000000000 | tf_op jit(solution)/shard_map/chain1/pallas_call | solution.py:179
  285.1 15.2 %collective-permute-done.20.refs_1_.peer = f32[2,704,256]{2,1,0:T(8,128)} collective-permute-done((f32[2,704,256]{2,1,0:T(8,128)}, f32[2,704,256]{2,1,0:T(8,128)}, u32[]{:S(2)}, u32[]{:S(2)}) %collective-permute-start.20) | collective-permute-done | bytes 1441824 | tf_op jit(solution)/shard_map/ppermute | solution.py:426
  307.9 5.7 %finish.14.refs_1_ = f32[32,8,896]{2,1,0:T(8,128)} custom-call(s32[2]{0:T(128)} %pad_add_fusion.scalars, f32[2,2]{1,0:T(2,128)} %maximum_select_fusion.rates, f32[2,704,256]{2,1,0:T(8,128)} %get-tuple-element.92.refs_0_.own, f32[2,704,256]{2,1,0:T(8,128)} %collective-permute-done.16.refs_1_.peer, f32[2,2,112,256]{3,2,1,0:T(8,128)} %get-tuple-element.101.refs_2_.even, ...), custom_call_target="tpu_custom_call" | custom-call | flops 9999999827968 | bytes 10000000000 | tf_op jit(solution)/shard_map/finish/pallas_call | solution.py:236
  331.3 6.9 %chain1.15 = (f32[2,2,112,256]{3,2,1,0:T(8,128)}, f32[2,2,112,256]{3,2,1,0:T(8,128)}) custom-call(s32[1]{0:T(128)} %bitcast.side, f32[2,2]{1,0:T(2,128)} %maximum_select_fusion.rates, f32[2,704,256]{2,1,0:T(8,128)} %get-tuple-element.97.refs_0_.own, f32[2,704,256]{2,1,0:T(8,128)} %collective-permute-done.20.refs_1_.peer, ...), custom_call_target="tpu_custom_call" | custom-call | flops 9999999827968 | bytes 10000000000 | tf_op jit(solution)/shard_map/chain1/pallas_call | solution.py:179
  340.0 11.4 %despread.3.refs_2_.refs_5_ = f32[8,2,448,256]{3,2,1,0:T(8,128)} custom-call(s32[32]{0:T(128)} %and_select_fusion.source, bf16[2,224,512]{2,1,0:T(8,128)(2,1)} %constant.88.clone.table, f32[32,8,448]{2,1,0:T(8,128)} %all-to-all-done.refs_1_.refs_0_, f32[32,8,896]{2,1,0:T(8,128)} %all-to-all-done.1.refs_1_, f32[32,8,896]{2,1,0:T(8,128)} %all-to-all-done.2.refs_1_.refs_2_, ...), custom_call_target="tpu_custom_call" | custom-call | flops 9999999827968 | bytes 10000000000 | tf_op jit(solution)/shard_map/despread/pallas_call | solution.py:362
  351.4 9.3 %collective-permute-done.24.refs_1_.peer = f32[2,704,256]{2,1,0:T(8,128)} collective-permute-done((f32[2,704,256]{2,1,0:T(8,128)}, f32[2,704,256]{2,1,0:T(8,128)}, u32[]{:S(2)}, u32[]{:S(2)}) %collective-permute-start.24) | collective-permute-done | bytes 1441824 | tf_op jit(solution)/shard_map/ppermute | solution.py:426
  368.3 5.7 %finish.15.refs_1_ = f32[32,8,896]{2,1,0:T(8,128)} custom-call(s32[2]{0:T(128)} %pad_add_fusion.scalars, f32[2,2]{1,0:T(2,128)} %maximum_select_fusion.rates, f32[2,704,256]{2,1,0:T(8,128)} %get-tuple-element.97.refs_0_.own, f32[2,704,256]{2,1,0:T(8,128)} %collective-permute-done.20.refs_1_.peer, f32[2,2,112,256]{3,2,1,0:T(8,128)} %get-tuple-element.107.refs_4_.even, ...), custom_call_target="tpu_custom_call" | custom-call | flops 9999999827968 | bytes 10000000000 | tf_op jit(solution)/shard_map/finish/pallas_call | solution.py:236
  385.7 6.1 %collective-permute-done.26.refs_4_ = f32[2,2,2,112,256]{4,3,2,1,0:T(8,128)} collective-permute-done((f32[2,2,2,112,256]{4,3,2,1,0:T(8,128)}, f32[2,2,2,112,256]{4,3,2,1,0:T(8,128)}, u32[]{:S(2)}, u32[]{:S(2)}) %collective-permute-start.26) | collective-permute-done | bytes 917536 | tf_op jit(solution)/shard_map/ppermute | solution.py:484
  391.8 6.9 %chain1.16 = (f32[2,2,112,256]{3,2,1,0:T(8,128)}, f32[2,2,112,256]{3,2,1,0:T(8,128)}) custom-call(s32[1]{0:T(128)} %bitcast.side, f32[2,2]{1,0:T(2,128)} %maximum_select_fusion.rates, f32[2,704,256]{2,1,0:T(8,128)} %get-tuple-element.106.refs_5_.refs_0_.own, f32[2,704,256]{2,1,0:T(8,128)} %collective-permute-done.24.refs_1_.peer, ...), custom_call_target="tpu_custom_call" | custom-call | flops 9999999827968 | bytes 10000000000 | tf_op jit(solution)/shard_map/chain1/pallas_call | solution.py:179
  462.9 9.8 %collective-permute-done.29.refs_1_.peer = f32[1,704,256]{2,1,0:T(8,128)} collective-permute-done((f32[1,704,256]{2,1,0:T(8,128)}, f32[1,704,256]{2,1,0:T(8,128)}, u32[]{:S(2)}, u32[]{:S(2)}) %collective-permute-start.29) | collective-permute-done | bytes 720928 | tf_op jit(solution)/shard_map/ppermute | solution.py:426
  495.6 7.9 %collective-permute-done.39.odd = f32[1,2,112,256]{3,2,1,0:T(8,128)S(1)} collective-permute-done((f32[1,2,112,256]{3,2,1,0:T(8,128)}, f32[1,2,112,256]{3,2,1,0:T(8,128)S(1)}, u32[]{:S(2)}, u32[]{:S(2)}) %collective-permute-start.39) | collective-permute-done | bytes 229408 | tf_op jit(solution)/shard_map/ppermute | solution.py:500
  514.3 14.8 %despread.4.refs_1_ = f32[8,2,448,256]{3,2,1,0:T(8,128)} custom-call(s32[32]{0:T(128)} %and_select_fusion.source, bf16[2,256,512]{2,1,0:T(8,128)(2,1)} %constant.89.clone.table, f32[32,8,896]{2,1,0:T(8,128)} %all-to-all-done.4.refs_1_.refs_0_, f32[32,8,896]{2,1,0:T(8,128)} %all-to-all-done.5.refs_1_, f32[32,8,896]{2,1,0:T(8,128)} %all-to-all-done.6.refs_6_.refs_2_, ...), custom_call_target="tpu_custom_call" | custom-call | flops 9999999827968 | bytes 10000000000 | tf_op jit(solution)/shard_map/despread/pallas_call | solution.py:362
  530.6 7.8 %despread.5 = f32[8,2,448,256]{3,2,1,0:T(8,128)} custom-call(s32[32]{0:T(128)} %and_select_fusion.source, bf16[1,96,512]{2,1,0:T(8,128)(2,1)} %constant.90.clone.table, f32[32,8,448]{2,1,0:T(8,128)} %all-to-all-done.9.refs_0_, f32[8,2,448,256]{3,2,1,0:T(8,128)} %despread.4.refs_1_), custom_call_target="tpu_custom_call" | custom-call | flops 9999999827968 | bytes 10000000000 | tf_op jit(solution)/shard_map/despread/pallas_call | solution.py:362
  (157 shorter events, 317.7 us)
Async XLA Ops:
  7.3 38.0 %collective-permute-start.1 = (f32[1,448,256]{2,1,0:T(8,128)}, f32[1,448,256]{2,1,0:T(8,128)}, u32[]{:S(2)}, u32[]{:S(2)}) collective-permute-start(f32[1,448,256]{2,1,0:T(8,128)} %held_back.10.refs_0_), channel_id=1, source_target_pairs={{0,8},{8,0},{16,24},{24,16},{1,9},{9,1},{17,25},{25,17},{2,10},{10... | collective-permute-start | bytes 1376264 | tf_op jit(solution)/shard_map/ppermute | solution.py:433
  13.1 52.3 %collective-permute-start.4 = (f32[2,704,256]{2,1,0:T(8,128)}, f32[2,704,256]{2,1,0:T(8,128)}, u32[]{:S(2)}, u32[]{:S(2)}) collective-permute-start(f32[2,704,256]{2,1,0:T(8,128)} %get-tuple-element.68.refs_0_), channel_id=1, source_target_pairs={{0,8},{8,0},{16,24},{24,16},{1,9},{9,1},{17,25},{25,17},{2,10},{10... | collective-permute-start | bytes 4325384 | tf_op jit(solution)/shard_map/ppermute | solution.py:426
  31.9 64.4 %collective-permute-start.5 = (f32[2,448,256]{2,1,0:T(8,128)}, f32[2,448,256]{2,1,0:T(8,128)}, u32[]{:S(2)}, u32[]{:S(2)}) collective-permute-start(f32[2,448,256]{2,1,0:T(8,128)} %held_back.11.refs_0_), channel_id=1, source_target_pairs={{0,8},{8,0},{16,24},{24,16},{1,9},{9,1},{17,25},{25,17},{2,10},{10... | collective-permute-start | bytes 2752520 | tf_op jit(solution)/shard_map/ppermute | solution.py:433
  39.0 81.2 %collective-permute-start.8 = (f32[2,704,256]{2,1,0:T(8,128)}, f32[2,704,256]{2,1,0:T(8,128)}, u32[]{:S(2)}, u32[]{:S(2)}) collective-permute-start(f32[2,704,256]{2,1,0:T(8,128)} %get-tuple-element.72.refs_0_), channel_id=1, source_target_pairs={{0,8},{8,0},{16,24},{24,16},{1,9},{9,1},{17,25},{25,17},{2,10},{10... | collective-permute-start | bytes 4325384 | tf_op jit(solution)/shard_map/ppermute | solution.py:426
  77.2 50.5 %all-to-all-start = ((f32[32,8,448]{2,1,0:T(8,128)}), f32[32,8,448]{2,1,0:T(8,128)}, u32[]{:S(2)}, u32[]{:S(2)}) async-start(f32[32,8,448]{2,1,0:T(8,128)} %finish.10.refs_1_), calls=%async_computation | async-start | bytes 1048576 | tf_op jit(solution)/shard_map/all_to_all | solution.py:445
  82.8 73.8 %collective-permute-start.9 = (f32[2,448,256]{2,1,0:T(8,128)}, f32[2,448,256]{2,1,0:T(8,128)}, u32[]{:S(2)}, u32[]{:S(2)}) collective-permute-start(f32[2,448,256]{2,1,0:T(8,128)} %held_back.12.refs_0_), channel_id=1, source_target_pairs={{0,8},{8,0},{16,24},{24,16},{1,9},{9,1},{17,25},{25,17},{2,10},{10... | collective-permute-start | bytes 2752520 | tf_op jit(solution)/shard_map/ppermute | solution.py:433
  90.4 89.2 %collective-permute-start.12 = (f32[2,704,256]{2,1,0:T(8,128)}, f32[2,704,256]{2,1,0:T(8,128)}, u32[]{:S(2)}, u32[]{:S(2)}) collective-permute-start(f32[2,704,256]{2,1,0:T(8,128)} %get-tuple-element.78.refs_0_), channel_id=1, source_target_pairs={{0,8},{8,0},{16,24},{24,16},{1,9},{9,1},{17,25},{25,17},{2,10},{10... | collective-permute-start | bytes 4325384 | tf_op jit(solution)/shard_map/ppermute | solution.py:426
  133.5 53.6 %all-to-all-start.1 = ((f32[32,8,896]{2,1,0:T(8,128)}), f32[32,8,896]{2,1,0:T(8,128)}, u32[]{:S(2)}, u32[]{:S(2)}) async-start(f32[32,8,896]{2,1,0:T(8,128)} %finish.11.refs_1_), calls=%async_computation.1 | async-start | bytes 1835008 | tf_op jit(solution)/shard_map/all_to_all | solution.py:445
  138.7 77.2 %collective-permute-start.13 = (f32[2,448,256]{2,1,0:T(8,128)}, f32[2,448,256]{2,1,0:T(8,128)}, u32[]{:S(2)}, u32[]{:S(2)}) collective-permute-start(f32[2,448,256]{2,1,0:T(8,128)} %held_back.13.refs_0_), channel_id=1, source_target_pairs={{0,8},{8,0},{16,24},{24,16},{1,9},{9,1},{17,25},{25,17},{2,10},{10... | collective-permute-start | bytes 2752520 | tf_op jit(solution)/shard_map/ppermute | solution.py:433
  146.3 93.6 %collective-permute-start.16 = (f32[2,704,256]{2,1,0:T(8,128)}, f32[2,704,256]{2,1,0:T(8,128)}, u32[]{:S(2)}, u32[]{:S(2)}) collective-permute-start(f32[2,704,256]{2,1,0:T(8,128)} %get-tuple-element.84.refs_0_), channel_id=1, source_target_pairs={{0,8},{8,0},{16,24},{24,16},{1,9},{9,1},{17,25},{25,17},{2,10},{10... | collective-permute-start | bytes 4325384 | tf_op jit(solution)/shard_map/ppermute | solution.py:426
  192.8 54.7 %all-to-all-start.2 = ((f32[32,8,896]{2,1,0:T(8,128)}), f32[32,8,896]{2,1,0:T(8,128)}, u32[]{:S(2)}, u32[]{:S(2)}) async-start(f32[32,8,896]{2,1,0:T(8,128)} %finish.12.refs_1_), calls=%async_computation.2 | async-start | bytes 1835008 | tf_op jit(solution)/shard_map/all_to_all | solution.py:445
  198.1 78.3 %collective-permute-start.17 = (f32[2,448,256]{2,1,0:T(8,128)}, f32[2,448,256]{2,1,0:T(8,128)}, u32[]{:S(2)}, u32[]{:S(2)}) collective-permute-start(f32[2,448,256]{2,1,0:T(8,128)} %held_back.14.refs_0_), channel_id=1, source_target_pairs={{0,8},{8,0},{16,24},{24,16},{1,9},{9,1},{17,25},{25,17},{2,10},{10... | collective-permute-start | bytes 2752520 | tf_op jit(solution)/shard_map/ppermute | solution.py:433
  205.7 94.6 %collective-permute-start.20 = (f32[2,704,256]{2,1,0:T(8,128)}, f32[2,704,256]{2,1,0:T(8,128)}, u32[]{:S(2)}, u32[]{:S(2)}) collective-permute-start(f32[2,704,256]{2,1,0:T(8,128)} %get-tuple-element.91.refs_0_), channel_id=1, source_target_pairs={{0,8},{8,0},{16,24},{24,16},{1,9},{9,1},{17,25},{25,17},{2,10},{10... | collective-permute-start | bytes 4325384 | tf_op jit(solution)/shard_map/ppermute | solution.py:426
  253.2 54.6 %all-to-all-start.3 = ((f32[32,8,896]{2,1,0:T(8,128)}), f32[32,8,896]{2,1,0:T(8,128)}, u32[]{:S(2)}, u32[]{:S(2)}) async-start(f32[32,8,896]{2,1,0:T(8,128)} %finish.13.refs_1_), calls=%async_computation.3 | async-start | bytes 1835008 | tf_op jit(solution)/shard_map/all_to_all | solution.py:445
  258.5 72.7 %collective-permute-start.21 = (f32[2,448,256]{2,1,0:T(8,128)}, f32[2,448,256]{2,1,0:T(8,128)}, u32[]{:S(2)}, u32[]{:S(2)}) collective-permute-start(f32[2,448,256]{2,1,0:T(8,128)} %held_back.15.refs_0_), channel_id=1, source_target_pairs={{0,8},{8,0},{16,24},{24,16},{1,9},{9,1},{17,25},{25,17},{2,10},{10... | collective-permute-start | bytes 2752520 | tf_op jit(solution)/shard_map/ppermute | solution.py:433
  266.1 94.6 %collective-permute-start.24 = (f32[2,704,256]{2,1,0:T(8,128)}, f32[2,704,256]{2,1,0:T(8,128)}, u32[]{:S(2)}, u32[]{:S(2)}) collective-permute-start(f32[2,704,256]{2,1,0:T(8,128)} %get-tuple-element.96.refs_0_), channel_id=1, source_target_pairs={{0,8},{8,0},{16,24},{24,16},{1,9},{9,1},{17,25},{25,17},{2,10},{10... | collective-permute-start | bytes 4325384 | tf_op jit(solution)/shard_map/ppermute | solution.py:426
  313.6 54.7 %all-to-all-start.4 = ((f32[32,8,896]{2,1,0:T(8,128)}), f32[32,8,896]{2,1,0:T(8,128)}, u32[]{:S(2)}, u32[]{:S(2)}) async-start(f32[32,8,896]{2,1,0:T(8,128)} %finish.14.refs_1_), calls=%async_computation.4 | async-start | bytes 1835008 | tf_op jit(solution)/shard_map/all_to_all | solution.py:445
  319.1 66.6 %collective-permute-start.25 = (f32[2,448,256]{2,1,0:T(8,128)}, f32[2,448,256]{2,1,0:T(8,128)}, u32[]{:S(2)}, u32[]{:S(2)}) collective-permute-start(f32[2,448,256]{2,1,0:T(8,128)} %held_back.16.refs_0_), channel_id=1, source_target_pairs={{0,8},{8,0},{16,24},{24,16},{1,9},{9,1},{17,25},{25,17},{2,10},{10... | collective-permute-start | bytes 2752520 | tf_op jit(solution)/shard_map/ppermute | solution.py:433
  325.4 80.2 %collective-permute-start.28 = (f32[1,704,256]{2,1,0:T(8,128)}, f32[1,704,256]{2,1,0:T(8,128)}, u32[]{:S(2)}, u32[]{:S(2)}) collective-permute-start(f32[1,704,256]{2,1,0:T(8,128)} %get-tuple-element.105.refs_0_), channel_id=1, source_target_pairs={{0,8},{8,0},{16,24},{24,16},{1,9},{9,1},{17,25},{25,17},{2,10},{10... | collective-permute-start | bytes 2162696 | tf_op jit(solution)/shard_map/ppermute | solution.py:426
  374.0 37.6 %all-to-all-start.5 = ((f32[32,8,896]{2,1,0:T(8,128)}), f32[32,8,896]{2,1,0:T(8,128)}, u32[]{:S(2)}, u32[]{:S(2)}) async-start(f32[32,8,896]{2,1,0:T(8,128)} %finish.15.refs_1_), calls=%async_computation.5 | async-start | bytes 1835008 | tf_op jit(solution)/shard_map/all_to_all | solution.py:445
  379.2 49.6 %collective-permute-start.30 = (f32[1,448,256]{2,1,0:T(8,128)}, f32[1,448,256]{2,1,0:T(8,128)}, u32[]{:S(2)}, u32[]{:S(2)}) collective-permute-start(f32[1,448,256]{2,1,0:T(8,128)} %held_back.17.refs_0_), channel_id=1, source_target_pairs={{0,8},{8,0},{16,24},{24,16},{1,9},{9,1},{17,25},{25,17},{2,10},{10... | collective-permute-start | bytes 1376264 | tf_op jit(solution)/shard_map/ppermute | solution.py:433
  385.5 52.9 %collective-permute-start.33 = (f32[1,704,256]{2,1,0:T(8,128)}, f32[1,704,256]{2,1,0:T(8,128)}, u32[]{:S(2)}, u32[]{:S(2)}) collective-permute-start(f32[1,704,256]{2,1,0:T(8,128)} %get-tuple-element.111.refs_5_), channel_id=1, source_target_pairs={{0,8},{8,0},{16,24},{24,16},{1,9},{9,1},{17,25},{25,17},{2,10},{10... | collective-permute-start | bytes 2162696 | tf_op jit(solution)/shard_map/ppermute | solution.py:426
  428.4 44.3 %collective-permute-start.29 = (f32[1,704,256]{2,1,0:T(8,128)}, f32[1,704,256]{2,1,0:T(8,128)}, u32[]{:S(2)}, u32[]{:S(2)}) collective-permute-start(f32[1,704,256]{2,1,0:T(8,128)} %get-tuple-element.114.refs_5_), channel_id=1, source_target_pairs={{0,8},{8,0},{16,24},{24,16},{1,9},{9,1},{17,25},{25,17},{2,10},{10... | collective-permute-start | bytes 2162696 | tf_op jit(solution)/shard_map/ppermute | solution.py:426
  449.6 39.8 %collective-permute-start.34 = (f32[1,448,256]{2,1,0:T(8,128)}, f32[1,448,256]{2,1,0:T(8,128)}, u32[]{:S(2)}, u32[]{:S(2)}) collective-permute-start(f32[1,448,256]{2,1,0:T(8,128)} %held_back.19.refs_5_), channel_id=1, source_target_pairs={{0,8},{8,0},{16,24},{24,16},{1,9},{9,1},{17,25},{25,17},{2,10},{10... | collective-permute-start | bytes 1376264 | tf_op jit(solution)/shard_map/ppermute | solution.py:433
  (31 other events, 626.1 us)
